TPU v7x, 32 devices: a whole 2x2x4 slice. The times are simulated.
32 devices in a mesh: rep: 2 (over y), gx: 8 (over z, x), gy: 2 (over core).
Axes of the slice: x: 2, y: 2, z: 4, core: 2. Of those that a mesh axis runs over, the one named last changes fastest.
Arguments:
- hidden_in: bfloat16 [2, 32, 16384], P(None, ('rep', 'gy'), 'gx'), parts along dimension 1, may hold values from -180 to 180
- norm_gain: bfloat16 [16384], P('gx'), may hold values from 0.099609375 to 1.8984375
- query_weight: bfloat16 [16384, 8192], P('gx', 'gy'), may hold values from -0.046875 to 0.046875
- key_weight: bfloat16 [16384, 512], P('gx', 'gy'), may hold values from -0.046875 to 0.046875
- value_weight: bfloat16 [16384, 512], P('gx', 'gy'), may hold values from -0.046875 to 0.046875
- out_weight: bfloat16 [8192, 16384], P('gy', 'gx'), may hold values from -0.0625 to 0.0625
- cache_keys: bfloat16 [32, 384, 512], P(('rep', 'gx', 'gy')), parts along dimension 0, may hold values from -400 to 400
- cache_values: bfloat16 [32, 384, 512], P(('rep', 'gx', 'gy')), parts along dimension 0, may hold values from -12 to 12
- lengths: int32 [32], P(('rep', 'gx', 'gy')), parts along dimension 0, may hold values from 48 to 384, as said below
- positions: int32 [32], P(('rep', 'gx', 'gy')), parts along dimension 0, may hold values from 48 to 4479, as said below
Outputs:
- attention_out: bfloat16 [2, 32, 16384], P(None, ('rep', 'gy'), 'gx'), parts along dimension 1
- new_keys: bfloat16 [2, 32, 512], P(None, ('rep', 'gx', 'gy')), parts along dimension 1
- new_values: bfloat16 [2, 32, 512], P(None, ('rep', 'gx', 'gy')), parts along dimension 1
There are 2 independent parts, one for each index of `rep`. A program takes and returns all parts, laid end to end along the dimension named above; an argument that names none is the same for every part. Nothing has to cross between parts.
Inputs may be any that keep to these rules, and one draw needn't show every extreme that they name: Sequence b's cached tokens fill its slots 0 to lengths[b] - 1; in every draw some sequence fills all 384 slots. positions[b] is never below the sequence's cached length; step t's token stands at positions[b] + t.
All inputs are finite; a program needn't handle non-finite values.
Results may differ from a plain program's by a relative error of at most 0.012.
Values may be sent and summed in bfloat16 or wider, within the bound.
No kernel may reach another device: no remote copies, remote signals or barrier semaphores. Data moves between devices by JAX's collectives and lax.ppermute only.
A program may use at most 128 MiB of HBM per device.

v0:
```python
from functools import partial
import math

import jax
import jax.numpy as jnp
from jax import lax
from jax.sharding import PartitionSpec as P

HD = 128


epsilon = 1e-05
rope_theta = 500000.0


def rope_frequencies(head_size):
    index = jnp.arange(head_size // 2).astype(jnp.float32)
    frequency = jnp.exp(-math.log(rope_theta) * 2.0 * index / head_size)
    wavelength = 2.0 * math.pi / frequency
    smooth = (8192.0 / wavelength - 1.0) / 3.0
    blended = (1.0 - smooth) * frequency / 8.0 + smooth * frequency
    adjusted = jnp.where(wavelength > 8192.0, frequency / 8.0, blended)
    return jnp.where(wavelength < 2048.0, frequency, adjusted)


def rotate(values, places):
    frequency = rope_frequencies(values.shape[-1])
    angle = places.astype(jnp.float32)[..., None] * frequency
    cosine = jnp.cos(angle)[..., None, :]
    sine = jnp.sin(angle)[..., None, :]
    half = values.shape[-1] // 2
    lower = values[..., :half]
    upper = values[..., half:]
    return jnp.concatenate([lower * cosine - upper * sine, upper * cosine + lower * sine], axis=-1)


def attend_local(queries, cached_keys, cached_values, fresh_keys, fresh_values, length, start_step):
    query_count, heads, head_size = queries.shape
    kv_heads = cached_keys.shape[1] // head_size
    group = heads // kv_heads
    grouped = queries.reshape(query_count, kv_heads, group, head_size)
    stored_keys = cached_keys.reshape(-1, kv_heads, head_size)
    stored_values = cached_values.reshape(-1, kv_heads, head_size)
    recent_keys = fresh_keys.reshape(-1, kv_heads, head_size)
    recent_values = fresh_values.reshape(-1, kv_heads, head_size)
    factor = 1.0 / math.sqrt(head_size)
    cache_scores = (
        jnp.einsum("skgd,ckd->skgc", grouped, stored_keys, preferred_element_type=jnp.float32)
        * factor
    )
    live = jnp.arange(stored_keys.shape[0]) < length
    cache_scores = jnp.where(live[None, None, None, :], cache_scores, -jnp.inf)
    fresh_scores = (
        jnp.einsum("skgd,tkd->skgt", grouped, recent_keys, preferred_element_type=jnp.float32)
        * factor
    )
    seen = (
        jnp.arange(recent_keys.shape[0])[None, :] <= (start_step + jnp.arange(query_count))[:, None]
    )
    fresh_scores = jnp.where(seen[:, None, None, :], fresh_scores, -jnp.inf)
    top = jnp.maximum(jnp.max(cache_scores, axis=-1), jnp.max(fresh_scores, axis=-1))
    cache_exp = jnp.exp(cache_scores - top[..., None])
    fresh_exp = jnp.exp(fresh_scores - top[..., None])
    total = jnp.sum(cache_exp, axis=-1) + jnp.sum(fresh_exp, axis=-1)
    cache_weight = (cache_exp / total[..., None]).astype(jnp.bfloat16)
    fresh_weight = (fresh_exp / total[..., None]).astype(jnp.bfloat16)
    mixed = jnp.einsum(
        "skgc,ckd->skgd", cache_weight, stored_values, preferred_element_type=jnp.float32
    )
    mixed = mixed + jnp.einsum(
        "skgt,tkd->skgd", fresh_weight, recent_values, preferred_element_type=jnp.float32
    )
    return mixed.reshape(query_count, heads * head_size).astype(jnp.bfloat16)


def body(
    hidden_in,
    norm_gain,
    query_weight,
    key_weight,
    value_weight,
    out_weight,
    cache_keys,
    cache_values,
    lengths,
    positions,
):
    step_total = hidden_in.shape[0]
    gathered = lax.all_gather(hidden_in, "gy", axis=1, tiled=True)
    activations = gathered.astype(jnp.float32)
    square_sums = lax.psum(jnp.sum(activations * activations, axis=-1), "gx")
    gx_count = lax.axis_size("gx")
    full_width = activations.shape[-1] * gx_count
    inverse_rms = lax.rsqrt(square_sums / full_width + epsilon)
    scaled = (activations * norm_gain.astype(jnp.float32)).astype(jnp.bfloat16)
    seq_total = gathered.shape[1]
    per_block = seq_total // gx_count
    block_start = lax.axis_index("gx") * per_block
    pair_cols = key_weight.shape[1]
    groups = (0, step_total)
    start_step, step_count = groups
    flat_rows = jnp.transpose(scaled, (1, 0, 2)).reshape(seq_total * step_count, -1)
    local_rows = per_block * step_count
    piece = flat_rows
    query_part = lax.psum_scatter(
        jnp.dot(piece, query_weight, preferred_element_type=jnp.float32),
        "gx",
        scatter_dimension=0,
        tiled=True,
    )
    piece = flat_rows
    pair_part = lax.psum_scatter(
        jnp.concatenate(
            [
                jnp.dot(piece, key_weight, preferred_element_type=jnp.float32),
                jnp.dot(piece, value_weight, preferred_element_type=jnp.float32),
            ],
            axis=1,
        ),
        "gx",
        scatter_dimension=0,
        tiled=True,
    )
    key_part = pair_part[:, :pair_cols]
    value_part = pair_part[:, pair_cols:]
    rms_rows = jnp.transpose(inverse_rms)
    rms_rows = lax.dynamic_slice_in_dim(rms_rows, block_start, per_block, 0).reshape(local_rows, 1)

    def by_heads(projected):
        return (projected * rms_rows).reshape(per_block, step_count, -1, HD)

    queries = lax.all_to_all(by_heads(query_part), "gy", split_axis=0, concat_axis=2, tiled=True)
    keys_now = lax.all_to_all(by_heads(key_part), "gy", split_axis=0, concat_axis=2, tiled=True)
    values_now = lax.all_to_all(by_heads(value_part), "gy", split_axis=0, concat_axis=2, tiled=True)
    places = positions[:, None] + (start_step + jnp.arange(step_count))[None, :]
    queries = rotate(queries, places).astype(jnp.bfloat16)
    owned = queries.shape[0]
    keys_now = rotate(keys_now, places).astype(jnp.bfloat16).reshape(owned, step_count, -1)
    values_now = values_now.astype(jnp.bfloat16).reshape(owned, step_count, -1)
    queries, keys_now, values_now = (queries, keys_now, values_now)
    attend = partial(attend_local, start_step=start_step)
    context = jax.vmap(attend)(queries, cache_keys, cache_values, keys_now, values_now, lengths)
    halves = lax.all_to_all(context, "gy", split_axis=2, concat_axis=0, tiled=True)
    piece = lax.all_gather(halves, "gx", axis=0, tiled=True)
    rows_here = piece.shape[0]
    product = jnp.dot(
        piece.reshape(rows_here * step_count, -1), out_weight, preferred_element_type=jnp.float32
    )
    partial_out = product.reshape(rows_here, step_count, -1)
    summed = lax.psum_scatter(partial_out, "gy", scatter_dimension=0, tiled=True)
    outputs = jnp.transpose(summed, (1, 0, 2)).astype(jnp.bfloat16)
    new_keys = jnp.transpose(keys_now, (1, 0, 2))
    new_values = jnp.transpose(values_now, (1, 0, 2))
    return (outputs, new_keys, new_values)


def solution(mesh):
    in_specs = (
        P(None, ("rep", "gy"), "gx"),
        P("gx"),
        P("gx", "gy"),
        P("gx", "gy"),
        P("gx", "gy"),
        P("gy", "gx"),
        P(("rep", "gx", "gy"), None, None),
        P(("rep", "gx", "gy"), None, None),
        P(("rep", "gx", "gy")),
        P(("rep", "gx", "gy")),
    )
    out_specs = (
        P(None, ("rep", "gy"), "gx"),
        P(None, ("rep", "gx", "gy"), None),
        P(None, ("rep", "gx", "gy"), None),
    )
    return jax.shard_map(body, mesh=mesh, in_specs=in_specs, out_specs=out_specs, check_vma=False)
```

profile of v0, /device:TPU:0, one launch (start us, length us, event | category | flops | bytes accessed | tf_op | source)
XLA Modules:
  0.0 246.0 jit_solution(7141140896583419036)
XLA Ops:
  7.2 0.0 copy-start
  7.2 0.0 copy-start.3
  7.2 0.0 copy-start.1
  7.2 0.0 copy-start.2
  7.2 0.0 all-reduce.5.cloned.1.call-start
  7.3 0.8 convert_element_type.107
  8.1 2.3 all_gather.6
  10.4 0.1 fusion.12
  10.5 0.1 copy.42
  10.7 0.1 reshape.295
  10.7 0.0 copy-done
  10.8 0.3 fusion.32
  11.0 1.5 fusion.31
  12.5 9.6 %fusion.30 = f32[32,4096]{1,0:T(8,128)} fusion(bf16[32,2048]{1,0:T(8,128)(2,1)S(1)} %reshape.295, bf16[2048,4096]{1,0:T(8,128)(2,1)} %param.12), kind=kOutput, calls=%fused_computation.61 | convolution fusion | flops 536870912 | bytes 17432576 | tf_op jit(solution)/shard_map/dot_general | solution.py:106
  22.1 0.6 pad_maximum_fusion
  22.8 0.0 all-reduce.5.cloned.1.call-update
  22.8 23.3 %psum.7 = f32[2,16]{1,0:T(2,128)S(1)} all-reduce(f32[2,16]{1,0:T(2,128)S(1)} %get-tuple-element.5), channel_id=1, replica_groups=mesh['rep'=2,'gx'=8,'gy'=2] {'gx'}, use_global_device_ids=true, to_apply=%region_2.0 | all-reduce | flops 32 | bytes 256 | tf_op jit(solution)/shard_map/psum | solution.py:91
  46.1 0.1 dynamic-slice_bitcast_fusion
  47.4 0.1 copy.43
  47.5 0.1 mul.172
  47.6 0.0 copy-done.1
  47.6 0.1 reshape.297
  47.7 0.0 copy-done.2
  47.7 0.1 reshape.300
  47.8 0.0 copy-done.3
  47.9 0.6 dynamic-slice.4
  49.1 0.1 multiply_cosine_fusion
  49.2 49.4 %all-reduce.5.cloned.1.call-done = (f32[32,4096]{1,0:T(8,128)}, f32[32,512]{1,0:T(8,128)}) async-done(((f32[32,4096]{1,0:T(8,128)}, f32[32,512]{1,0:T(8,128)}), (f32[32,4096]{1,0:T(8,128)}, f32[32,512]{1,0:T(8,128)})) %all-reduce.5.cloned.1.call-update) | async-done | bytes 589840
  98.6 1.0 fusion.19
  99.6 0.6 copy.66
  100.3 0.8 dynamic-slice_multiply_fusion.2
  101.0 0.8 dynamic-slice_multiply_fusion.1
  101.8 0.6 copy.50
  102.4 3.7 %all_to_all.63 = f32[2,2,2,128]{3,1,2,0:T(2,128)S(1)} all-to-all(f32[2,2,2,128]{3,1,2,0:T(2,128)S(1)} %copy.48), channel_id=1, replica_groups=mesh['rep'=2,'gx'=8,'gy'=2] {'gy'}, dimensions={0} | all-to-all | bytes 8192 | tf_op jit(solution)/shard_map/all_to_all | solution.py:133
  106.1 3.3 %all-to-all-start = ((f32[2,2,32,128]{3,2,1,0:T(8,128)}), f32[2,2,32,128]{3,2,1,0:T(8,128)S(1)}, u32[]{:S(2)}, u32[]{:S(2)}) async-start(f32[2,2,32,128]{3,2,1,0:T(8,128)} %bitcast.55), calls=%async_computation | async-start | bytes 131072 | tf_op jit(solution)/shard_map/all_to_all | solution.py:132
  109.4 0.1 subtract_convert_fusion.1
  109.5 1.3 all-to-all-done
  110.8 3.2 %all-to-all-start.2 = ((bf16[2,2,2,128]{3,1,2,0:T(2,128)(2,1)}), bf16[2,2,2,128]{3,1,2,0:T(2,128)(2,1)S(1)}, u32[]{:S(2)}, u32[]{:S(2)}) async-start(bf16[2,2,2,128]{3,1,2,0:T(2,128)(2,1)} %copy.50), calls=%async_computation.2 | async-start | bytes 4096 | tf_op jit(solution)/shard_map/all_to_all | solution.py:134
  114.0 0.2 reduce-scatter.2.cloned.1.call-start
  114.3 0.1 subtract_convert_fusion
  114.4 0.4 fusion.28
  114.7 0.3 fusion.29
  115.1 0.2 fusion.15
  115.3 0.2 convolution_bitcast_fusion
  115.5 0.0 all-to-all-done.2
  115.6 0.2 fusion.6
  115.8 6.8 %copy.52 = bf16[1,2,8192]{1,0,2:T(2,128)(2,1)} copy(bf16[1,2,8192]{2,1,0:T(2,128)(2,1)S(1)} %convert_element_type.120) | data formatting | bytes 65536 | tf_op jit(solution)/shard_map/vmap()/convert_element_type | solution.py:73
  122.6 0.5 broadcast.181
  123.1 45.2 %reduce.4 = bf16[8192,2]{1,0:T(8,128)(2,1)S(1)} reduce(bf16[8192,1,2]{2,1,0:T(2,128)(2,1)} %bitcast.97, bf16[]{:T(256)} %broadcast.181), dimensions={1}, to_apply=%bitcast.84.reduce_sub_computation | reduce | bytes 65538
  168.3 3.2 %reshape.311 = bf16[2,2,4096]{2,1,0:T(2,128)(2,1)S(1)} reshape(bf16[8192,2]{1,0:T(8,128)(2,1)S(1)} %reduce.4) | data formatting | bytes 65536
  171.6 3.7 %all_to_all.64 = bf16[2,2,4096]{2,1,0:T(2,128)(2,1)S(1)} all-to-all(bf16[2,2,4096]{2,1,0:T(2,128)(2,1)S(1)} %reshape.311), channel_id=1, replica_groups=mesh['rep'=2,'gx'=8,'gy'=2] {'gy'}, dimensions={0} | all-to-all | bytes 65536 | tf_op jit(solution)/shard_map/all_to_all | solution.py:143
  175.3 6.2 %reshape.312 = bf16[8192,1,2]{2,1,0:T(2,128)(2,1)} reshape(bf16[2,2,4096]{2,1,0:T(2,128)(2,1)S(1)} %all_to_all.64) | data formatting | bytes 65536
  181.5 8.1 %copy.53 = bf16[1,2,8192]{2,1,0:T(2,128)(2,1)S(1)} copy(bf16[1,2,8192]{1,0,2:T(2,128)(2,1)} %bitcast.98) | data formatting | bytes 65536 | tf_op jit(solution)/shard_map/all_to_all | solution.py:143
  189.6 31.0 %all-gather = bf16[16,1,2,4096]{3,2,1,0:T(2,128)(2,1)S(1)} all-gather(bf16[2,1,2,4096]{3,2,1,0:T(2,128)(2,1)S(1)} %copy.54), channel_id=2, replica_groups=mesh['rep'=2,'gx'=8,'gy'=2] {'gx'}, dimensions={0}, use_global_device_ids=true | all-gather | bytes 294912 | tf_op jit(solution)/shard_map/all_gather | solution.py:144
  220.6 9.5 %fusion = f32[16,2,2048]{2,0,1:T(8,128)} fusion(bf16[4096,2048]{1,0:T(8,128)(2,1)} %param.15, bf16[16,1,2,4096]{3,2,1,0:T(2,128)(2,1)S(1)} %all-gather), kind=kOutput, calls=%fused_computation | convolution fusion | flops 536870912 | bytes 17301504 | tf_op jit(solution)/shard_map/dot_general | solution.py:146
  230.1 0.0 reduce-scatter.2.cloned.1.call-update
  230.2 0.7 maximum_bitcast_fusion.2
  230.8 6.2 %reduce-scatter.2.cloned.1.call-done = f32[8,2,2048]{2,0,1:T(8,128)} async-done(((f32[16,2,2048]{2,0,1:T(8,128)}), f32[8,2,2048]{2,0,1:T(8,128)}) %reduce-scatter.2.cloned.1.call-update) | async-done | bytes 131088 | tf_op jit(solution)/shard_map/reduce_scatter | solution.py:150
  237.0 1.5 convert_bitcast_fusion
  238.6 0.6 copy.90
  (16 shorter events, 0.2 us)
Async XLA Ops:
  7.2 3.6 %copy-start = (bf16[2048,256]{1,0:T(8,128)(2,1)S(1)}, bf16[2048,256]{1,0:T(8,128)(2,1)}, u32[]{:S(2)}) copy-start(bf16[2048,256]{1,0:T(8,128)(2,1)} %param.14) | copy-start | bytes 3145732
  7.2 40.7 %copy-start.3 = (u32[32]{0:T(128)S(1)}, u32[32]{0:T(128)}, u32[]{:S(2)}) copy-start(u32[32]{0:T(128)} %constant.54) | copy-start | bytes 388
  7.2 40.4 %copy-start.1 = (bf16[1,384,512]{2,1,0:T(8,128)(2,1)S(1)}, bf16[1,384,512]{2,1,0:T(8,128)(2,1)}, u32[]{:S(2)}) copy-start(bf16[1,384,512]{2,1,0:T(8,128)(2,1)} %param.16) | copy-start | bytes 1179652
  7.2 40.5 %copy-start.2 = (bf16[1,384,512]{2,1,0:T(8,128)(2,1)S(1)}, bf16[1,384,512]{2,1,0:T(8,128)(2,1)}, u32[]{:S(2)}) copy-start(bf16[1,384,512]{2,1,0:T(8,128)(2,1)} %param.17) | copy-start | bytes 1179652
  7.2 91.4 %all-reduce.5.cloned.1.call-start = ((), (), s32[]{:S(2)}) async-start(), calls=%async_computation.6 | async-start | bytes 1179648
  106.1 4.7 %all-to-all-start = ((f32[2,2,32,128]{3,2,1,0:T(8,128)}), f32[2,2,32,128]{3,2,1,0:T(8,128)S(1)}, u32[]{:S(2)}, u32[]{:S(2)}) async-start(f32[2,2,32,128]{3,2,1,0:T(8,128)} %bitcast.55), calls=%async_computation | async-start | bytes 131072 | tf_op jit(solution)/shard_map/all_to_all | solution.py:132
  110.8 4.7 %all-to-all-start.2 = ((bf16[2,2,2,128]{3,1,2,0:T(2,128)(2,1)}), bf16[2,2,2,128]{3,1,2,0:T(2,128)(2,1)S(1)}, u32[]{:S(2)}, u32[]{:S(2)}) async-start(bf16[2,2,2,128]{3,1,2,0:T(2,128)(2,1)} %copy.50), calls=%async_computation.2 | async-start | bytes 4096 | tf_op jit(solution)/shard_map/all_to_all | solution.py:134
  114.0 123.0 %reduce-scatter.2.cloned.1.call-start = ((), (), s32[]{:S(2)}) async-start(), calls=%async_computation.5 | async-start | bytes 393216 | tf_op jit(solution)/shard_map/reduce_scatter | solution.py:150
Sparse Core Ops, SparseCore 0:
  22.9 75.6 all-reduce.4
  230.3 6.7 reduce-scatter.1
where the time goes:
time: 247 us; the launch traced here: 246 us
  blocking collectives  64 us (26%)
  waiting for transfers between devices  57 us (23%)
  other arithmetic  52 us (21%)
  local copies, waits for them, and re-layouts  28 us (11%)
  matrix products  22 us (9%)
  between operations  16.3 us (7%)
  starting transfers between devices  6.78 us (3%)
    unnamed x3, waiting for transfers between devices  49.4 us
    unnamed x2, other arithmetic  46.2 us
    all_gather x1, blocking collectives, body(): piece = lax.all_gather(halves, 'gx', axis=0, tiled=True)  31 us
    psum x1, blocking collectives, body(): square_sums = lax.psum(jnp.sum(activations * activations, axis=-1), 'gx')  23.3 us
    unnamed x14, local copies, waits for them, and re-layouts  11.7 us
    dot_general x1, matrix products, body(): jnp.dot(piece, query_weight, preferred_element_type=jnp.float32)  9.58 us
    dot_general x1, matrix products, body(): jnp.dot(piece.reshape(rows_here * step_count, -1), out_weight, preferred_...  9.5 us
    all_to_all x3, local copies, waits for them, and re-layouts, body(): lax.all_to_all(context, 'gy', split_axis=2, concat_axis=0, tiled=True)  8.15 us
  transfers between devices with their start and end apart: 4, of which 3 were waited for; matrix products, arithmetic and copies ran while one was open for 1% of the time, Pallas kernels for 0%

commit v1 on v0

v1 whole, which is shorter than its diff:
```python
import functools
import math

import jax
import jax.numpy as jnp
from jax import lax
from jax.experimental import pallas as pl
from jax.experimental.pallas import tpu as pltpu
from jax.sharding import PartitionSpec as P

HD = 128
epsilon = 1e-05
rope_theta = 500000.0
MIB = 1024 * 1024


def rope_frequencies(head_size):
    index = jnp.arange(head_size // 2).astype(jnp.float32)
    frequency = jnp.exp(-math.log(rope_theta) * 2.0 * index / head_size)
    wavelength = 2.0 * math.pi / frequency
    smooth = (8192.0 / wavelength - 1.0) / 3.0
    blended = (1.0 - smooth) * frequency / 8.0 + smooth * frequency
    adjusted = jnp.where(wavelength > 8192.0, frequency / 8.0, blended)
    return jnp.where(wavelength < 2048.0, frequency, adjusted)


def rope_table(position, steps):
    frequency = rope_frequencies(HD)
    places = position + jnp.arange(steps, dtype=jnp.int32)
    angle = places.astype(jnp.float32)[:, None] * frequency
    cosine, sine = jnp.cos(angle), jnp.sin(angle)
    return jnp.concatenate(
        [cosine, cosine, -sine, sine], axis=-1
    ).reshape(2 * steps, HD)


def project_kernel(steps, pitch, chunk, x_ref, gain_ref, wq_ref, wk_ref, wv_ref, out_ref,
                   wq_buf, wk_buf, wv_buf, rows_buf, sems):
    q_cols = wq_ref.shape[1]
    kv_cols = wk_ref.shape[1]
    chunks = q_cols // chunk
    copies = []
    for c in range(chunks):
        copies.append(pltpu.make_async_copy(
            wq_ref.at[:, c * chunk:(c + 1) * chunk], wq_buf.at[c], sems.at[c]))
    copies.append(pltpu.make_async_copy(wk_ref, wk_buf, sems.at[chunks]))
    copies.append(pltpu.make_async_copy(wv_ref, wv_buf, sems.at[chunks + 1]))
    for copy in copies:
        copy.start()

    total_rows = x_ref.shape[0]
    half_seqs = total_rows // (2 * steps)
    stride = steps * pitch

    def spread(head, block):
        for g in range(2):
            for t in range(steps):
                first = (g * steps + t) * half_seqs
                start = (g * half_seqs * steps + t) * pitch + head
                rows_buf[pl.ds(start, half_seqs, stride=stride), :] = block[first:first + half_seqs, :]

    x = x_ref[...].astype(jnp.float32)
    scaled = (x * gain_ref[...].astype(jnp.float32)).astype(jnp.bfloat16)
    squares = jnp.sum(x * x, axis=-1, keepdims=True)
    high = squares.astype(jnp.bfloat16).astype(jnp.float32)
    low = squares - high
    heads = (q_cols + 2 * kv_cols) // HD
    spread(heads, jnp.broadcast_to(high, (total_rows, HD)))
    spread(heads + 1, jnp.broadcast_to(low, (total_rows, HD)))
    for spare in range(heads + 2, pitch):
        spread(spare, jnp.zeros((total_rows, HD), jnp.float32))

    def multiply(weights, first_head):
        product = jnp.dot(scaled, weights, preferred_element_type=jnp.float32)
        for i in range(product.shape[1] // HD):
            spread(first_head + i, product[:, i * HD:(i + 1) * HD])

    for c in range(chunks):
        copies[c].wait()
        multiply(wq_buf[c], c * chunk // HD)
    copies[chunks].wait()
    multiply(wk_buf[...], q_cols // HD)
    copies[chunks + 1].wait()
    multiply(wv_buf[...], (q_cols + kv_cols) // HD)
    out_ref[...] = rows_buf[...].reshape(out_ref.shape).astype(jnp.bfloat16)


def project(x, gain, wq, wk, wv, steps, pitch):
    total_rows, depth = x.shape
    q_cols, kv_cols = wq.shape[1], wk.shape[1]
    seqs = total_rows // steps
    chunk = 512
    vmem = pl.BlockSpec(memory_space=pltpu.VMEM)
    hbm = pl.BlockSpec(memory_space=pl.ANY)
    return pl.pallas_call(
        functools.partial(project_kernel, steps, pitch, chunk),
        out_shape=jax.ShapeDtypeStruct((seqs, steps * pitch, HD), jnp.bfloat16),
        in_specs=[vmem, vmem, hbm, hbm, hbm],
        out_specs=vmem,
        scratch_shapes=[
            pltpu.VMEM((q_cols // chunk, depth, chunk), jnp.bfloat16),
            pltpu.VMEM((depth, kv_cols), jnp.bfloat16),
            pltpu.VMEM((depth, kv_cols), jnp.bfloat16),
            pltpu.VMEM((seqs * steps * pitch, HD), jnp.float32),
            pltpu.SemaphoreType.DMA((q_cols // chunk + 2,)),
        ],
        compiler_params=pltpu.CompilerParams(vmem_limit_bytes=32 * MIB),
        cost_estimate=pl.CostEstimate(
            flops=2 * total_rows * depth * (q_cols + 2 * kv_cols),
            bytes_accessed=2 * depth * (q_cols + 2 * kv_cols), transcendentals=0),
        name="project",
    )(x, gain, wq, wk, wv)


def attend_kernel(steps, pitch, width, length_ref, parts_ref, table_ref, keys_ref, values_ref,
                  context_ref, new_keys_ref, new_values_ref):
    devices = parts_ref.shape[0]
    kv_heads = keys_ref.shape[1] // HD
    half_kv = kv_heads // 2
    half_heads = context_ref.shape[1] // steps
    group = half_heads // half_kv
    slots = keys_ref.shape[0]
    factor = 1.0 / math.sqrt(HD)
    live = lax.broadcasted_iota(jnp.int32, (steps * group, slots), 1) < length_ref[0]
    row_step = lax.broadcasted_iota(jnp.int32, (steps * group, 1), 0) // group
    fresh_keys = [[None] * kv_heads for _ in range(steps)]
    fresh_values = [[None] * kv_heads for _ in range(steps)]
    queries = [[None] * kv_heads for _ in range(steps)]
    for g in range(2):
        total = parts_ref[g].astype(jnp.float32)
        for i in range(1, devices // 2):
            total = total + parts_ref[2 * i + g].astype(jnp.float32)
        for t in range(steps):
            rows = total[t * pitch:(t + 1) * pitch]
            first_k = half_heads
            first_v = first_k + half_kv
            first_s = first_v + half_kv
            squares = rows[first_s:first_s + 1] + rows[first_s + 1:first_s + 2]
            rows = rows * lax.rsqrt(squares / width + epsilon)
            cosine = table_ref[2 * t:2 * t + 1, :]
            sine = table_ref[2 * t + 1:2 * t + 2, :]
            turned = rows * cosine + pltpu.roll(rows, HD // 2, 1) * sine
            turned = turned.astype(jnp.bfloat16)
            plain = rows.astype(jnp.bfloat16)
            for k in range(half_kv):
                head = g * half_kv + k
                queries[t][head] = turned[k * group:(k + 1) * group]
                fresh_keys[t][head] = turned[first_k + k:first_k + k + 1].astype(jnp.float32)
                fresh_values[t][head] = plain[first_v + k:first_v + k + 1].astype(jnp.float32)
    new_keys_ref[...] = jnp.concatenate(
        [jnp.concatenate(row, axis=1) for row in fresh_keys], axis=0).astype(jnp.bfloat16)
    new_values_ref[...] = jnp.concatenate(
        [jnp.concatenate(row, axis=1) for row in fresh_values], axis=0).astype(jnp.bfloat16)
    for head in range(kv_heads):
        columns = slice(head * HD, (head + 1) * HD)
        query = jnp.concatenate([queries[t][head] for t in range(steps)], axis=0)
        scores = lax.dot_general(
            query, keys_ref[:, columns], (((1,), (1,)), ((), ())),
            preferred_element_type=jnp.float32) * factor
        scores = jnp.where(live, scores, -jnp.inf)
        top = jnp.max(scores, axis=-1, keepdims=True)
        wide = query.astype(jnp.float32)
        fresh = []
        for s in range(steps):
            score = jnp.sum(wide * fresh_keys[s][head], axis=-1, keepdims=True) * factor
            score = jnp.where(row_step >= s, score, -jnp.inf)
            fresh.append(score)
            top = jnp.maximum(top, score)
        scores = jnp.exp(scores - top)
        total = jnp.sum(scores, axis=-1, keepdims=True)
        fresh = [jnp.exp(score - top) for score in fresh]
        for score in fresh:
            total = total + score
        weight = (scores / total).astype(jnp.bfloat16)
        mixed = jnp.dot(weight, values_ref[:, columns], preferred_element_type=jnp.float32)
        for s in range(steps):
            weight = (fresh[s] / total).astype(jnp.bfloat16).astype(jnp.float32)
            mixed = mixed + weight * fresh_values[s][head]
        mixed = mixed.astype(jnp.bfloat16)
        g, k = head // half_kv, head % half_kv
        for t in range(steps):
            piece = mixed[t * group:(t + 1) * group]
            first = t * half_heads + k * group
            for i in range(devices // 2):
                context_ref[2 * i + g, first:first + group, :] = piece


def attend(length, parts, table, keys, values, steps, pitch, width, half_heads):
    devices = parts.shape[0]
    vmem = pl.BlockSpec(memory_space=pltpu.VMEM)
    smem = pl.BlockSpec(memory_space=pltpu.SMEM)
    kv_cols = keys.shape[1]
    return pl.pallas_call(
        functools.partial(attend_kernel, steps, pitch, width),
        out_shape=(
            jax.ShapeDtypeStruct((devices, steps * half_heads, HD), jnp.bfloat16),
            jax.ShapeDtypeStruct((steps, kv_cols), jnp.bfloat16),
            jax.ShapeDtypeStruct((steps, kv_cols), jnp.bfloat16),
        ),
        in_specs=[smem, vmem, vmem, vmem, vmem],
        out_specs=(vmem, vmem, vmem),
        compiler_params=pltpu.CompilerParams(vmem_limit_bytes=16 * MIB),
        name="attend",
    )(length, parts, table, keys, values)


def output_kernel(steps, chunk, side_ref, context_ref, weight_ref, mine_ref, other_ref,
                  weight_buf, wide_buf, rows_buf, sems):
    devices, per_device, _ = context_ref.shape
    heads = per_device // steps
    half_seqs = devices // 2
    columns = weight_ref.shape[1]
    chunks = columns // chunk
    copies = [pltpu.make_async_copy(
        weight_ref.at[:, c * chunk:(c + 1) * chunk], weight_buf.at[c], sems.at[c])
        for c in range(chunks)]
    for copy in copies:
        copy.start()
    wide_buf[...] = context_ref[...].astype(jnp.float32).reshape(wide_buf.shape)
    for h in range(heads):
        pieces = []
        for g in range(2):
            for t in range(steps):
                start = (g * half_seqs * steps + t) * heads + h
                pieces.append(wide_buf[pl.ds(start, half_seqs, stride=per_device), :])
        rows_buf[:, h * HD:(h + 1) * HD] = jnp.concatenate(pieces, axis=0).astype(jnp.bfloat16)
    rows = rows_buf[...]
    side = side_ref[0]
    half = rows.shape[0] // 2
    for c in range(chunks):
        copies[c].wait()
        product = jnp.dot(rows, weight_buf[c], preferred_element_type=jnp.float32)
        lower, upper = product[:half], product[half:]
        span = slice(c * chunk, (c + 1) * chunk)
        mine_ref[:, span] = jnp.where(side == 0, lower, upper)
        other_ref[:, span] = jnp.where(side == 0, upper, lower).astype(jnp.bfloat16)


def output(side, context, weight, steps):
    devices, per_device, _ = context.shape
    depth, columns = weight.shape
    chunk = min(columns, 256)
    half = devices * steps // 2
    vmem = pl.BlockSpec(memory_space=pltpu.VMEM)
    smem = pl.BlockSpec(memory_space=pltpu.SMEM)
    hbm = pl.BlockSpec(memory_space=pl.ANY)
    return pl.pallas_call(
        functools.partial(output_kernel, steps, chunk),
        out_shape=(
            jax.ShapeDtypeStruct((half, columns), jnp.float32),
            jax.ShapeDtypeStruct((half, columns), jnp.bfloat16),
        ),
        in_specs=[smem, vmem, hbm],
        out_specs=(vmem, vmem),
        scratch_shapes=[
            pltpu.VMEM((columns // chunk, depth, chunk), jnp.bfloat16),
            pltpu.VMEM((devices * per_device, HD), jnp.float32),
            pltpu.VMEM((devices * steps, depth), jnp.bfloat16),
            pltpu.SemaphoreType.DMA((columns // chunk,)),
        ],
        compiler_params=pltpu.CompilerParams(vmem_limit_bytes=32 * MIB),
        cost_estimate=pl.CostEstimate(
            flops=2 * devices * steps * depth * columns,
            bytes_accessed=2 * depth * columns, transcendentals=0),
        name="output",
    )(side, context, weight)


def body(hidden_in, norm_gain, query_weight, key_weight, value_weight, out_weight,
         cache_keys, cache_values, lengths, positions):
    steps, half_seqs, depth = hidden_in.shape
    gx_count = lax.axis_size("gx")
    half_heads = query_weight.shape[1] // HD
    heads_here = half_heads + 2 * key_weight.shape[1] // HD
    pitch = -(-(heads_here + 2) // 8) * 8
    x = lax.all_gather(hidden_in.reshape(steps * half_seqs, depth), "gy", axis=0, tiled=True)
    parts = project(x, norm_gain[None, :], query_weight, key_weight, value_weight, steps, pitch)
    parts = lax.all_to_all(parts, ("gx", "gy"), split_axis=0, concat_axis=0, tiled=True)
    table = rope_table(positions[0], steps)
    context, new_keys, new_values = attend(
        lengths, parts, table, cache_keys[0], cache_values[0],
        steps, pitch, depth * gx_count, half_heads)
    context = lax.all_to_all(context, ("gx", "gy"), split_axis=0, concat_axis=0, tiled=True)
    side = lax.axis_index("gy").astype(jnp.int32).reshape(1)
    mine, other = output(side, context, out_weight, steps)
    other = lax.ppermute(other, "gy", [(0, 1), (1, 0)])
    result = (mine + other.astype(jnp.float32)).astype(jnp.bfloat16)
    return (
        result.reshape(steps, half_seqs, -1),
        new_keys[:, None, :],
        new_values[:, None, :],
    )


def solution(mesh):
    in_specs = (
        P(None, ("rep", "gy"), "gx"),
        P("gx"),
        P("gx", "gy"),
        P("gx", "gy"),
        P("gx", "gy"),
        P("gy", "gx"),
        P(("rep", "gx", "gy"), None, None),
        P(("rep", "gx", "gy"), None, None),
        P(("rep", "gx", "gy")),
        P(("rep", "gx", "gy")),
    )
    out_specs = (
        P(None, ("rep", "gy"), "gx"),
        P(None, ("rep", "gx", "gy"), None),
        P(None, ("rep", "gx", "gy"), None),
    )
    return jax.shard_map(body, mesh=mesh, in_specs=in_specs, out_specs=out_specs, check_vma=False)
```

time: 247 us -> 70.7 us (0.29)
  blocking collectives: 64 us -> 2.21 us
  other arithmetic: 52 us -> 0.85 us
  waiting for transfers between devices: 57 us -> 20.8 us
  matrix products: 22 us -> 0 us
  Pallas kernels: 0 us -> 18.7 us
  between operations: 16.3 us -> 1.99 us
  local copies, waits for them, and re-layouts: 28 us -> 14.7 us
  starting transfers between devices: 6.78 us -> 10.9 us
    unnamed x3 -> x0, waiting for transfers between devices: 49.4 us -> none
    unnamed x2 -> x0, other arithmetic: 46.2 us -> none
    all_gather x2 -> x1, blocking collectives: 33.3 us -> 2.21 us  [body(): lax.all_gather(hidden_in.reshape(steps * half_seqs, depth), 'gy', axis=0,...]
    psum x1 -> x0, blocking collectives: 23.3 us -> none  [body(): square_sums = lax.psum(jnp.sum(activations * activations, axis=-1), 'gx')]
    dot_general x8 -> x0, matrix products: 22 us -> none  [the longest x1 9.58 us: body(): jnp.dot(piece, query_weight, preferred_element_type=jnp.float32)]
    pallas_call x0 -> x3, Pallas kernels: none -> 18.7 us  [the longest x1 8.37 us: project(): pl.pallas_call(functools.partial(project_kernel, steps, pitch, chunk), ou...]
    all_to_all x2, waiting for transfers between devices: 1.32 us -> 19.6 us  [the longest x1 10 us: body(): lax.all_to_all(context, ('gx', 'gy'), split_axis=0, concat_axis=0, tiled=...]
    all_to_all x4 -> x0, local copies, waits for them, and re-layouts: 8.15 us -> none  [the longest x3 8.15 us: body(): lax.all_to_all(context, 'gy', split_axis=2, concat_axis=0, tiled=True)]
  transfers between devices with their start and end apart: 4 -> 3, of which waited for: 3 -> 3; matrix products, arithmetic and copies ran while one was open for 1% -> 0% of each run, Pallas kernels for 0% -> 0%
where the time goes in v1:
time: 70.7 us; the launch traced here: 70.1 us
  waiting for transfers between devices  20.8 us (29%)
  Pallas kernels  18.7 us (26%)
  local copies, waits for them, and re-layouts  14.7 us (21%)
  starting transfers between devices  10.9 us (15%)
  blocking collectives  2.21 us (3%)
  between operations  1.99 us (3%)
  other arithmetic  0.85 us (1%)
    unnamed x12, local copies, waits for them, and re-layouts  14 us
    all_to_all x1, waiting for transfers between devices, body(): lax.all_to_all(context, ('gx', 'gy'), split_axis=0, concat_axis=0, tiled=...  10 us
    all_to_all x1, waiting for transfers between devices, body(): lax.all_to_all(parts, ('gx', 'gy'), split_axis=0, concat_axis=0, tiled=True)  9.57 us
    pallas_call x1, Pallas kernels, project(): pl.pallas_call(functools.partial(project_kernel, steps, pitch, chunk), ou...  8.37 us
    pallas_call x1, Pallas kernels, output(): pl.pallas_call(functools.partial(output_kernel, steps, chunk), out_shape=...  8.13 us
    all_to_all x1, starting transfers between devices, body(): lax.all_to_all(parts, ('gx', 'gy'), split_axis=0, concat_axis=0, tiled=True)  7.27 us
    all_to_all x1, starting transfers between devices, body(): lax.all_to_all(context, ('gx', 'gy'), split_axis=0, concat_axis=0, tiled=...  3.53 us
    all_gather x1, blocking collectives, body(): lax.all_gather(hidden_in.reshape(steps * half_seqs, depth), 'gy', axis=0,...  2.21 us
  transfers between devices with their start and end apart: 3, of which 3 were waited for; matrix products, arithmetic and copies ran while one was open for 0% of the time, Pallas kernels for 0%

profile of v1, /device:TPU:0, one launch (start us, length us, event | category | flops | bytes accessed | tf_op | source)
XLA Modules:
  0.0 70.1 jit_solution(6067362223942774727)
XLA Ops:
  0.6 2.2 %all_gather.3.x_ref = bf16[32,2048]{1,0:T(8,128)(2,1)S(1)} all-gather(bf16[16,2048]{1,0:T(8,128)(2,1)} %bitcast.12), channel_id=1, replica_groups=mesh['rep'=2,'gx'=8,'gy'=2] {'gy'}, dimensions={0}, use_global_device_ids=true | all-gather | bytes 196608 | tf_op jit(solution)/shard_map/all_gather | solution.py:276
  2.8 0.7 broadcast_in_dim.11.gain_ref
  3.5 0.0 copy-start.1
  3.5 5.8 %copy-done.1 = bf16[2048,4096]{1,0:T(8,128)(2,1)S(1)} copy-done((bf16[2048,4096]{1,0:T(8,128)(2,1)S(1)}, bf16[2048,4096]{1,0:T(8,128)(2,1)}, u32[]{:S(2)}) %copy-start.1) | copy-done | bytes 16777240
  9.3 0.0 copy-start.2
  9.3 1.2 %copy-done.2 = bf16[2048,256]{1,0:T(8,128)(2,1)S(1)} copy-done((bf16[2048,256]{1,0:T(8,128)(2,1)S(1)}, bf16[2048,256]{1,0:T(8,128)(2,1)}, u32[]{:S(2)}) %copy-start.2) | copy-done | bytes 1048600
  10.5 0.0 copy-start.3
  10.5 1.2 %copy-done.3 = bf16[2048,256]{1,0:T(8,128)(2,1)S(1)} copy-done((bf16[2048,256]{1,0:T(8,128)(2,1)S(1)}, bf16[2048,256]{1,0:T(8,128)(2,1)}, u32[]{:S(2)}) %copy-start.3) | copy-done | bytes 1048600
  11.8 0.0 copy-start.4
  11.8 0.0 copy-start.5
  11.8 8.4 %project.1 = bf16[16,80,128]{2,1,0:T(8,128)(2,1)} custom-call(bf16[32,2048]{1,0:T(8,128)(2,1)S(1)} %all_gather.3.x_ref, bf16[1,2048]{1,0:T(2,128)(2,1)S(1)} %broadcast_in_dim.11.gain_ref, bf16[2048,4096]{1,0:T(8,128)(2,1)S(1)} %copy-done.1, bf16[2048,256]{1,0:T(8,128)(2,1)S(1)} %copy-done.2, bf16[2048,256]{1,0:T(8,128)(2,1)S(1)} %copy-done.3), custom_call_target="tpu_custom_call" | custom-call | flops 603979776 | bytes 18874368 | tf_op jit(solution)/shard_map/project/pallas_call | solution.py:95
  20.1 7.3 %all-to-all-start = ((bf16[16,80,128]{2,1,0:T(8,128)(2,1)}), bf16[16,80,128]{2,1,0:T(8,128)(2,1)S(1)}, u32[]{:S(2)}, u32[]{:S(2)}) async-start(bf16[16,80,128]{2,1,0:T(8,128)(2,1)} %project.1), calls=%async_computation | async-start | bytes 655360 | tf_op jit(solution)/shard_map/all_to_all | solution.py:278
  28.7 0.1 multiply_cosine_fusion
  28.9 0.1 pad_maximum_fusion
  28.9 9.6 %all-to-all-done.parts_ref = bf16[16,80,128]{2,1,0:T(8,128)(2,1)S(1)} async-done(((bf16[16,80,128]{2,1,0:T(8,128)(2,1)}), bf16[16,80,128]{2,1,0:T(8,128)(2,1)S(1)}, u32[]{:S(2)}, u32[]{:S(2)}) %all-to-all-start) | async-done | bytes 327712 | tf_op jit(solution)/shard_map/all_to_all | solution.py:278
  38.5 0.0 copy-done.4
  38.5 0.0 copy-done.5
  38.5 2.2 %attend.1 = (bf16[16,64,128]{2,1,0:T(8,128)(2,1)}, bf16[2,512]{1,0:T(2,128)(2,1)}, bf16[2,512]{1,0:T(2,128)(2,1)}) custom-call(s32[1]{0:T(128)S(6)} %copy.13.length_ref, bf16[16,80,128]{2,1,0:T(8,128)(2,1)S(1)} %all-to-all-done.parts_ref, f32[4,128]{1,0:T(4,128)S(1)} %reshape.46.table_ref, bf16[384,512]{1,0:T(8,128)(2,1)S(1)} %bitcast.10, ...), custom_call_target="tpu_custom_call" | custom-call | tf_op jit(solution)/shard_map/attend/pallas_call | solution.py:193
  40.7 3.5 %all-to-all-start.1 = ((bf16[16,64,128]{2,1,0:T(8,128)(2,1)}), bf16[16,64,128]{2,1,0:T(8,128)(2,1)S(1)}, u32[]{:S(2)}, u32[]{:S(2)}) async-start(bf16[16,64,128]{2,1,0:T(8,128)(2,1)} %get-tuple-element.8), calls=%async_computation.1 | async-start | bytes 524288 | tf_op jit(solution)/shard_map/all_to_all | solution.py:283
  44.3 10.0 %all-to-all-done.1.context_ref = bf16[16,64,128]{2,1,0:T(8,128)(2,1)S(1)} async-done(((bf16[16,64,128]{2,1,0:T(8,128)(2,1)}), bf16[16,64,128]{2,1,0:T(8,128)(2,1)S(1)}, u32[]{:S(2)}, u32[]{:S(2)}) %all-to-all-start.1) | async-done | bytes 262176 | tf_op jit(solution)/shard_map/all_to_all | solution.py:283
  54.3 0.0 copy-start
  54.3 5.8 %copy-done = bf16[4096,2048]{1,0:T(8,128)(2,1)S(1)} copy-done((bf16[4096,2048]{1,0:T(8,128)(2,1)S(1)}, bf16[4096,2048]{1,0:T(8,128)(2,1)}, u32[]{:S(2)}) %copy-start) | copy-done | bytes 16777240
  60.0 8.1 %output.1 = (f32[16,2048]{1,0:T(8,128)S(1)}, bf16[16,2048]{1,0:T(8,128)(2,1)S(1)}) custom-call(s32[1]{0:T(128)} %bitcast.side_ref, bf16[16,64,128]{2,1,0:T(8,128)(2,1)S(1)} %all-to-all-done.1.context_ref, bf16[4096,2048]{1,0:T(8,128)(2,1)S(1)} %copy-done), custom_call_target="tpu_custom_call" | custom-call | flops 536870912 | bytes 16777216 | tf_op jit(solution)/shard_map/output/pallas_call | solution.py:247
  68.2 0.1 collective-permute-start
  68.3 1.2 %collective-permute-done = bf16[16,2048]{1,0:T(8,128)(2,1)S(1)} collective-permute-done((bf16[16,2048]{1,0:T(8,128)(2,1)S(1)}, bf16[16,2048]{1,0:T(8,128)(2,1)S(1)}, u32[]{:S(2)}, u32[]{:S(2)}) %collective-permute-start) | collective-permute-done | bytes 65568 | tf_op jit(solution)/shard_map/ppermute | solution.py:286
  69.5 0.6 fusion
  (3 shorter events, 0.0 us)
Async XLA Ops:
  3.5 5.8 %copy-start.1 = (bf16[2048,4096]{1,0:T(8,128)(2,1)S(1)}, bf16[2048,4096]{1,0:T(8,128)(2,1)}, u32[]{:S(2)}) copy-start(bf16[2048,4096]{1,0:T(8,128)(2,1)} %wq_ref.1) | copy-start | bytes 50331652
  9.3 1.2 %copy-start.2 = (bf16[2048,256]{1,0:T(8,128)(2,1)S(1)}, bf16[2048,256]{1,0:T(8,128)(2,1)}, u32[]{:S(2)}) copy-start(bf16[2048,256]{1,0:T(8,128)(2,1)} %wk_ref.1) | copy-start | bytes 3145732
  10.5 1.2 %copy-start.3 = (bf16[2048,256]{1,0:T(8,128)(2,1)S(1)}, bf16[2048,256]{1,0:T(8,128)(2,1)}, u32[]{:S(2)}) copy-start(bf16[2048,256]{1,0:T(8,128)(2,1)} %wv_ref.1) | copy-start | bytes 3145732
  11.8 26.8 %copy-start.4 = (bf16[1,384,512]{2,1,0:T(8,128)(2,1)S(1)}, bf16[1,384,512]{2,1,0:T(8,128)(2,1)}, u32[]{:S(2)}) copy-start(bf16[1,384,512]{2,1,0:T(8,128)(2,1)} %param.16) | copy-start | bytes 1179652
  11.8 26.8 %copy-start.5 = (bf16[1,384,512]{2,1,0:T(8,128)(2,1)S(1)}, bf16[1,384,512]{2,1,0:T(8,128)(2,1)}, u32[]{:S(2)}) copy-start(bf16[1,384,512]{2,1,0:T(8,128)(2,1)} %param.17) | copy-start | bytes 1179652
  20.1 18.4 %all-to-all-start = ((bf16[16,80,128]{2,1,0:T(8,128)(2,1)}), bf16[16,80,128]{2,1,0:T(8,128)(2,1)S(1)}, u32[]{:S(2)}, u32[]{:S(2)}) async-start(bf16[16,80,128]{2,1,0:T(8,128)(2,1)} %project.1), calls=%async_computation | async-start | bytes 655360 | tf_op jit(solution)/shard_map/all_to_all | solution.py:278
  40.7 13.5 %all-to-all-start.1 = ((bf16[16,64,128]{2,1,0:T(8,128)(2,1)}), bf16[16,64,128]{2,1,0:T(8,128)(2,1)S(1)}, u32[]{:S(2)}, u32[]{:S(2)}) async-start(bf16[16,64,128]{2,1,0:T(8,128)(2,1)} %get-tuple-element.8), calls=%async_computation.1 | async-start | bytes 524288 | tf_op jit(solution)/shard_map/all_to_all | solution.py:283
  54.3 5.8 %copy-start = (bf16[4096,2048]{1,0:T(8,128)(2,1)S(1)}, bf16[4096,2048]{1,0:T(8,128)(2,1)}, u32[]{:S(2)}) copy-start(bf16[4096,2048]{1,0:T(8,128)(2,1)} %weight_ref.1) | copy-start | bytes 50331652
  68.2 1.3 %collective-permute-start = (bf16[16,2048]{1,0:T(8,128)(2,1)S(1)}, bf16[16,2048]{1,0:T(8,128)(2,1)S(1)}, u32[]{:S(2)}, u32[]{:S(2)}) collective-permute-start(bf16[16,2048]{1,0:T(8,128)(2,1)S(1)} %get-tuple-element.10), channel_id=1, source_target_pairs={{0,1},{1,0},{2,3},{3,2},{4,5},{5,4},{6,7},{7,6},{8,9},{9,8},{10,11... | collective-permute-start | bytes 196616 | tf_op jit(solution)/shard_map/ppermute | solution.py:286

commit v2 on v1

v2 whole, which is shorter than its diff:
```python
import functools
import math

import jax
import jax.numpy as jnp
from jax import lax
from jax.experimental import pallas as pl
from jax.experimental.pallas import tpu as pltpu
from jax.sharding import PartitionSpec as P

HD = 128
epsilon = 1e-05
rope_theta = 500000.0
MIB = 1024 * 1024


def rope_frequencies(head_size):
    index = jnp.arange(head_size // 2).astype(jnp.float32)
    frequency = jnp.exp(-math.log(rope_theta) * 2.0 * index / head_size)
    wavelength = 2.0 * math.pi / frequency
    smooth = (8192.0 / wavelength - 1.0) / 3.0
    blended = (1.0 - smooth) * frequency / 8.0 + smooth * frequency
    adjusted = jnp.where(wavelength > 8192.0, frequency / 8.0, blended)
    return jnp.where(wavelength < 2048.0, frequency, adjusted)


def rope_table(position, steps):
    frequency = rope_frequencies(HD)
    places = position + jnp.arange(steps, dtype=jnp.int32)
    angle = places.astype(jnp.float32)[:, None] * frequency
    cosine, sine = jnp.cos(angle), jnp.sin(angle)
    return jnp.concatenate(
        [cosine, cosine, -sine, sine], axis=-1
    ).reshape(2 * steps, HD)


def project_kernel(steps, pitch, chunk, place_ref, mine_ref, other_ref, gain_ref, wq_ref, wk_ref, wv_ref,
                   *rest):
    out_refs, (wq_buf, wk_buf, wv_buf, rows_buf, sems) = rest[:-5], rest[-5:]
    q_cols = wq_ref.shape[1]
    kv_cols = wk_ref.shape[1]
    chunks = q_cols // chunk
    copies = [pltpu.make_async_copy(wk_ref, wk_buf, sems.at[chunks]),
              pltpu.make_async_copy(wv_ref, wv_buf, sems.at[chunks + 1])]
    for c in range(chunks):
        copies.append(pltpu.make_async_copy(
            wq_ref.at[:, c * chunk:(c + 1) * chunk], wq_buf.at[c], sems.at[c]))
    for copy in copies:
        copy.start()

    device = place_ref[0]
    half_rows = mine_ref.shape[0]
    total_rows = 2 * half_rows
    half_seqs = half_rows // steps
    stride = steps * pitch

    def spread(head, block):
        for g in range(2):
            for t in range(steps):
                first = (g * steps + t) * half_seqs
                start = (g * half_seqs * steps + t) * pitch + head
                rows_buf[pl.ds(start, half_seqs, stride=stride), :] = block[first:first + half_seqs, :]

    low_side = device % 2 == 0
    mine = mine_ref[...].astype(jnp.float32)
    other = other_ref[...].astype(jnp.float32)
    x = jnp.concatenate(
        [jnp.where(low_side, mine, other), jnp.where(low_side, other, mine)], axis=0)
    gain = gain_ref[...].astype(jnp.float32)
    gain = jnp.concatenate([gain[i:i + 1] for i in range(gain.shape[0])], axis=1)
    scaled = (x * gain).astype(jnp.bfloat16)
    squares = jnp.sum(x * x, axis=-1, keepdims=True)
    high = squares.astype(jnp.bfloat16).astype(jnp.float32)
    low = squares - high
    heads = (q_cols + 2 * kv_cols) // HD
    spread(heads, jnp.broadcast_to(high, (total_rows, HD)))
    spread(heads + 1, jnp.broadcast_to(low, (total_rows, HD)))
    for spare in range(heads + 2, pitch):
        spread(spare, jnp.zeros((total_rows, HD), jnp.float32))

    def multiply(weights, first_head):
        product = jnp.dot(scaled, weights, preferred_element_type=jnp.float32)
        for i in range(product.shape[1] // HD):
            spread(first_head + i, product[:, i * HD:(i + 1) * HD])

    copies[0].wait()
    multiply(wk_buf[...], q_cols // HD)
    copies[1].wait()
    multiply(wv_buf[...], (q_cols + kv_cols) // HD)
    for c in range(chunks):
        copies[2 + c].wait()
        multiply(wq_buf[c], c * chunk // HD)
    if len(out_refs) == 1:
        out_refs[0][...] = rows_buf[...].reshape(out_refs[0].shape).astype(jnp.bfloat16)
    else:
        for k, out_ref in enumerate(out_refs):
            start = pl.multiple_of((device ^ k) * stride, 8)
            out_ref[...] = rows_buf[pl.ds(start, stride), :].astype(jnp.bfloat16)


def project(place, mine, other, gain, wq, wk, wv, steps, pitch, direct):
    half_rows, depth = mine.shape
    q_cols, kv_cols = wq.shape[1], wk.shape[1]
    seqs = 2 * half_rows // steps
    chunk = 512
    vmem = pl.BlockSpec(memory_space=pltpu.VMEM)
    smem = pl.BlockSpec(memory_space=pltpu.SMEM)
    hbm = pl.BlockSpec(memory_space=pltpu.HBM)
    if direct:
        out_shape = (jax.ShapeDtypeStruct((steps * pitch, HD), jnp.bfloat16),) * seqs
    else:
        out_shape = (jax.ShapeDtypeStruct((seqs, steps * pitch, HD), jnp.bfloat16),)
    return pl.pallas_call(
        functools.partial(project_kernel, steps, pitch, chunk),
        out_shape=out_shape,
        in_specs=[smem, vmem, vmem, vmem, hbm, hbm, hbm],
        out_specs=(vmem,) * len(out_shape),
        scratch_shapes=[
            pltpu.VMEM((q_cols // chunk, depth, chunk), jnp.bfloat16),
            pltpu.VMEM((depth, kv_cols), jnp.bfloat16),
            pltpu.VMEM((depth, kv_cols), jnp.bfloat16),
            pltpu.VMEM((seqs * steps * pitch, HD), jnp.float32),
            pltpu.SemaphoreType.DMA((q_cols // chunk + 2,)),
        ],
        compiler_params=pltpu.CompilerParams(vmem_limit_bytes=44 * MIB),
        cost_estimate=pl.CostEstimate(
            flops=4 * half_rows * depth * (q_cols + 2 * kv_cols),
            bytes_accessed=2 * depth * (q_cols + 2 * kv_cols), transcendentals=0),
        name="project",
    )(place, mine, other, gain, wq, wk, wv)


def attend_kernel(steps, pitch, width, direct, place_ref, length_ref, table_ref, keys_ref, values_ref, *rest):
    part_refs, (same_ref, cross_ref, new_keys_ref, new_values_ref) = rest[:-4], rest[-4:]
    kv_heads = keys_ref.shape[1] // HD
    half_kv = kv_heads // 2
    half_heads = same_ref.shape[0] // steps
    low_side = place_ref[0] % 2 == 0
    if direct:
        same, cross = [
            functools.reduce(jnp.add, [ref[...].astype(jnp.float32) for ref in part_refs[i::2]])
            for i in range(2)]
    else:
        parts_ref = part_refs[0]
        even, odd = [
            functools.reduce(jnp.add, [
                parts_ref[i].astype(jnp.float32) for i in range(g, parts_ref.shape[0], 2)])
            for g in range(2)]
        same, cross = jnp.where(low_side, even, odd), jnp.where(low_side, odd, even)
    halves = [jnp.where(low_side, same, cross), jnp.where(low_side, cross, same)]
    group = half_heads // half_kv
    slots = keys_ref.shape[0]
    factor = 1.0 / math.sqrt(HD)
    live = lax.broadcasted_iota(jnp.int32, (steps * group, slots), 1) < length_ref[0]
    row_step = lax.broadcasted_iota(jnp.int32, (steps * group, 1), 0) // group
    fresh_keys = [[None] * kv_heads for _ in range(steps)]
    fresh_values = [[None] * kv_heads for _ in range(steps)]
    queries = [[None] * kv_heads for _ in range(steps)]
    for g in range(2):
        for t in range(steps):
            rows = halves[g][t * pitch:(t + 1) * pitch]
            first_k = half_heads
            first_v = first_k + half_kv
            first_s = first_v + half_kv
            squares = rows[first_s:first_s + 1] + rows[first_s + 1:first_s + 2]
            rows = rows * lax.rsqrt(squares / width + epsilon)
            cosine = table_ref[2 * t:2 * t + 1, :]
            sine = table_ref[2 * t + 1:2 * t + 2, :]
            turned = rows * cosine + pltpu.roll(rows, HD // 2, 1) * sine
            turned = turned.astype(jnp.bfloat16)
            plain = rows.astype(jnp.bfloat16)
            for k in range(half_kv):
                head = g * half_kv + k
                queries[t][head] = turned[k * group:(k + 1) * group]
                fresh_keys[t][head] = turned[first_k + k:first_k + k + 1].astype(jnp.float32)
                fresh_values[t][head] = plain[first_v + k:first_v + k + 1].astype(jnp.float32)
    new_keys_ref[...] = jnp.concatenate(
        [jnp.concatenate(row, axis=1) for row in fresh_keys], axis=0).astype(jnp.bfloat16)
    new_values_ref[...] = jnp.concatenate(
        [jnp.concatenate(row, axis=1) for row in fresh_values], axis=0).astype(jnp.bfloat16)
    contexts = [[], []]
    for head in range(kv_heads):
        columns = slice(head * HD, (head + 1) * HD)
        query = jnp.concatenate([queries[t][head] for t in range(steps)], axis=0)
        scores = lax.dot_general(
            query, keys_ref[:, columns], (((1,), (1,)), ((), ())),
            preferred_element_type=jnp.float32) * factor
        scores = jnp.where(live, scores, -jnp.inf)
        top = jnp.max(scores, axis=-1, keepdims=True)
        wide = query.astype(jnp.float32)
        fresh = []
        for s in range(steps):
            score = jnp.sum(wide * fresh_keys[s][head], axis=-1, keepdims=True) * factor
            score = jnp.where(row_step >= s, score, -jnp.inf)
            fresh.append(score)
            top = jnp.maximum(top, score)
        scores = jnp.exp(scores - top)
        total = jnp.sum(scores, axis=-1, keepdims=True)
        fresh = [jnp.exp(score - top) for score in fresh]
        for score in fresh:
            total = total + score
        weight = (scores / total).astype(jnp.bfloat16)
        mixed = jnp.dot(weight, values_ref[:, columns], preferred_element_type=jnp.float32)
        for s in range(steps):
            weight = (fresh[s] / total).astype(jnp.bfloat16).astype(jnp.float32)
            mixed = mixed + weight * fresh_values[s][head]
        contexts[head // half_kv].append(mixed)
    rows = [
        jnp.concatenate([half[k][t * group:(t + 1) * group] for t in range(steps) for k in range(half_kv)], axis=0)
        for half in contexts]
    same_ref[...] = jnp.where(low_side, rows[0], rows[1]).astype(jnp.bfloat16)
    cross_ref[...] = jnp.where(low_side, rows[1], rows[0]).astype(jnp.bfloat16)


def attend(place, length, parts, table, keys, values, steps, pitch, width, half_heads, direct):
    vmem = pl.BlockSpec(memory_space=pltpu.VMEM)
    smem = pl.BlockSpec(memory_space=pltpu.SMEM)
    kv_cols = keys.shape[1]
    half = jax.ShapeDtypeStruct((steps * half_heads, HD), jnp.bfloat16)
    fresh = jax.ShapeDtypeStruct((steps, kv_cols), jnp.bfloat16)
    return pl.pallas_call(
        functools.partial(attend_kernel, steps, pitch, width, direct),
        out_shape=(half, half, fresh, fresh),
        in_specs=[smem, smem, vmem, vmem, vmem] + [vmem] * len(parts),
        out_specs=(vmem,) * 4,
        compiler_params=pltpu.CompilerParams(vmem_limit_bytes=16 * MIB),
        name="attend",
    )(place, length, table, keys, values, *parts)


def output_kernel(steps, chunk, place_ref, weight_ref, *rest):
    context_refs, (mine_ref, other_ref, wide_buf, rows_buf) = rest[:-4], rest[-4:]
    device = place_ref[0]
    heads = weight_ref.shape[0] // HD
    per_device = steps * heads
    devices = wide_buf.shape[0] // per_device
    half_seqs = devices // 2
    columns = weight_ref.shape[1]
    if len(context_refs) == 1:
        wide_buf[...] = context_refs[0][...].astype(jnp.float32).reshape(wide_buf.shape)
    else:
        for k, ref in enumerate(context_refs):
            start = pl.multiple_of((device ^ k) * per_device, 8)
            wide_buf[pl.ds(start, per_device), :] = ref[...].astype(jnp.float32)
    for h in range(heads):
        pieces = []
        for g in range(2):
            for t in range(steps):
                start = (g * half_seqs * steps + t) * heads + h
                pieces.append(wide_buf[pl.ds(start, half_seqs, stride=per_device), :])
        rows_buf[:, h * HD:(h + 1) * HD] = jnp.concatenate(pieces, axis=0).astype(jnp.bfloat16)
    rows = rows_buf[...]
    low_side = device % 2 == 0
    half = rows.shape[0] // 2
    for c in range(columns // chunk):
        span = slice(c * chunk, (c + 1) * chunk)
        product = jnp.dot(rows, weight_ref[:, span], preferred_element_type=jnp.float32)
        lower, upper = product[:half], product[half:]
        mine_ref[:, span] = jnp.where(low_side, lower, upper)
        other_ref[:, span] = jnp.where(low_side, upper, lower).astype(jnp.bfloat16)


def output(place, contexts, weight, devices, steps):
    depth, columns = weight.shape
    chunk = min(columns, 512)
    half = devices * steps // 2
    vmem = pl.BlockSpec(memory_space=pltpu.VMEM)
    smem = pl.BlockSpec(memory_space=pltpu.SMEM)
    return pl.pallas_call(
        functools.partial(output_kernel, steps, chunk),
        out_shape=(
            jax.ShapeDtypeStruct((half, columns), jnp.float32),
            jax.ShapeDtypeStruct((half, columns), jnp.bfloat16),
        ),
        in_specs=[smem, vmem] + [vmem] * len(contexts),
        out_specs=(vmem, vmem),
        scratch_shapes=[
            pltpu.VMEM((devices * steps * depth // HD, HD), jnp.float32),
            pltpu.VMEM((devices * steps, depth), jnp.bfloat16),
        ],
        compiler_params=pltpu.CompilerParams(vmem_limit_bytes=24 * MIB),
        cost_estimate=pl.CostEstimate(
            flops=2 * devices * steps * depth * columns,
            bytes_accessed=2 * depth * columns, transcendentals=0),
        name="output",
    )(place, weight, *contexts)


def body(hidden_in, norm_gain, query_weight, key_weight, value_weight, out_weight,
         cache_keys, cache_values, lengths, positions):
    steps, half_seqs, depth = hidden_in.shape
    both = ("gx", "gy")
    devices = lax.axis_size(both)
    direct = devices <= 16 and devices & (devices - 1) == 0
    half_heads = query_weight.shape[1] // HD
    heads_here = half_heads + 2 * key_weight.shape[1] // HD
    pitch = -(-(heads_here + 2) // 8) * 8
    place = lax.axis_index(both).astype(jnp.int32).reshape(1)
    swap = [(0, 1), (1, 0)]

    def partner(array, k):
        if k == 0:
            return array
        return lax.ppermute(array, both, [(i, i ^ k) for i in range(devices)])

    def to_all(array):
        return lax.all_to_all(array, both, split_axis=0, concat_axis=0, tiled=True)

    mine = hidden_in.reshape(steps * half_seqs, depth)
    other = lax.ppermute(mine, "gy", swap)
    parts = project(place, mine, other, norm_gain.reshape(-1, HD), query_weight, key_weight,
                    value_weight, steps, pitch, direct)

    if direct:
        parts = [partner(part, k) for k, part in enumerate(parts)]
    else:
        parts = [to_all(parts[0])]
    table = rope_table(positions[0], steps)
    same, cross, new_keys, new_values = attend(
        place, lengths, parts, table, cache_keys[0], cache_values[0],
        steps, pitch, depth * lax.axis_size("gx"), half_heads, direct)
    if direct:
        contexts = [partner(cross if k % 2 else same, k) for k in range(devices)]
    else:
        pair = jnp.where(place[0] % 2 == 0, jnp.stack([same, cross]), jnp.stack([cross, same]))
        contexts = [to_all(jnp.tile(pair, (devices // 2, 1, 1)))]
    mine, other = output(place, contexts, out_weight, devices, steps)
    other = lax.ppermute(other, "gy", swap)
    result = (mine + other.astype(jnp.float32)).astype(jnp.bfloat16)
    return (
        result.reshape(steps, half_seqs, -1),
        new_keys[:, None, :],
        new_values[:, None, :],
    )


def solution(mesh):
    in_specs = (
        P(None, ("rep", "gy"), "gx"),
        P("gx"),
        P("gx", "gy"),
        P("gx", "gy"),
        P("gx", "gy"),
        P("gy", "gx"),
        P(("rep", "gx", "gy"), None, None),
        P(("rep", "gx", "gy"), None, None),
        P(("rep", "gx", "gy")),
        P(("rep", "gx", "gy")),
    )
    out_specs = (
        P(None, ("rep", "gy"), "gx"),
        P(None, ("rep", "gx", "gy"), None),
        P(None, ("rep", "gx", "gy"), None),
    )
    return jax.shard_map(body, mesh=mesh, in_specs=in_specs, out_specs=out_specs, check_vma=False)
```

time: 70.7 us -> 77.5 us (1.096)
  starting transfers between devices: 10.9 us -> 44.3 us
  waiting for transfers between devices: 20.8 us -> 8.41 us
  Pallas kernels: 18.7 us -> 11.9 us
  local copies, waits for them, and re-layouts: 14.7 us -> 9.77 us
  blocking collectives: 2.21 us -> 0 us
    ppermute x1 -> x32, starting transfers between devices: 0.07 us -> 44.3 us  [the longest x30 43.6 us: partner(): return lax.ppermute(array, both, [(i, i ^ k) for i in range(devices)])]
    all_to_all x2 -> x0, waiting for transfers between devices: 19.6 us -> none  [the longest x1 10 us: body(): lax.all_to_all(context, ('gx', 'gy'), split_axis=0, concat_axis=0, tiled=...]
    all_to_all x2 -> x0, starting transfers between devices: 10.8 us -> none  [the longest x1 7.27 us: body(): lax.all_to_all(parts, ('gx', 'gy'), split_axis=0, concat_axis=0, tiled=True)]
    ppermute x1 -> x32, waiting for transfers between devices: 1.24 us -> 8.41 us  [the longest x30 6.83 us: partner(): return lax.ppermute(array, both, [(i, i ^ k) for i in range(devices)])]
    pallas_call x1, Pallas kernels: 8.13 us -> 3.12 us  [output(): pl.pallas_call(functools.partial(output_kernel, steps, chunk), out_shape=...]
    unnamed x12 -> x14, local copies, waits for them, and re-layouts: 14 us -> 9.75 us
    all_gather x1 -> x0, blocking collectives: 2.21 us -> none  [body(): lax.all_gather(hidden_in.reshape(steps * half_seqs, depth), 'gy', axis=0,...]
    pallas_call x1, Pallas kernels: 8.37 us -> 6.79 us  [project(): pl.pallas_call(functools.partial(project_kernel, steps, pitch, chunk), ou...]
  transfers between devices with their start and end apart: 3 -> 32, of which waited for: 3 -> 6; matrix products, arithmetic and copies ran while one was open for 0% -> 0% of each run, Pallas kernels for 0% -> 0%
where the time goes in v2:
time: 77.5 us; the launch traced here: 77.2 us
  starting transfers between devices  44.3 us (57%)
  Pallas kernels  11.9 us (15%)
  local copies, waits for them, and re-layouts  9.77 us (13%)
  waiting for transfers between devices  8.41 us (11%)
  between operations  2.04 us (3%)
  other arithmetic  0.85 us (1%)
    ppermute x30, starting transfers between devices, partner(): return lax.ppermute(array, both, [(i, i ^ k) for i in range(devices)])  43.6 us
    unnamed x14, local copies, waits for them, and re-layouts  9.75 us
    ppermute x30, waiting for transfers between devices, partner(): return lax.ppermute(array, both, [(i, i ^ k) for i in range(devices)])  6.83 us
    pallas_call x1, Pallas kernels, project(): pl.pallas_call(functools.partial(project_kernel, steps, pitch, chunk), ou...  6.79 us
    pallas_call x1, Pallas kernels, output(): pl.pallas_call(functools.partial(output_kernel, steps, chunk), out_shape=...  3.12 us
    pallas_call x1, Pallas kernels, attend(): pl.pallas_call(functools.partial(attend_kernel, steps, pitch, width, dire...  1.97 us
  transfers between devices with their start and end apart: 32, of which 6 were waited for; matrix products, arithmetic and copies ran while one was open for 0% of the time, Pallas kernels for 0%

profile of v2, /device:TPU:0, one launch (start us, length us, event | category | flops | bytes accessed | tf_op | source)
XLA Modules:
  0.0 77.2 jit_solution(4657634726632401419)
XLA Ops:
  0.6 0.5 collective-permute-start
  1.8 0.4 collective-permute-done.other_ref
  2.3 1.2 %copy-done.1 = bf16[2048,256]{1,0:T(8,128)(2,1)S(1)} copy-done((bf16[2048,256]{1,0:T(8,128)(2,1)S(1)}, bf16[2048,256]{1,0:T(8,128)(2,1)}, u32[]{:S(2)}) %copy-start.1) | copy-done | bytes 1048600
  3.5 1.2 %copy-done.2 = bf16[2048,256]{1,0:T(8,128)(2,1)S(1)} copy-done((bf16[2048,256]{1,0:T(8,128)(2,1)S(1)}, bf16[2048,256]{1,0:T(8,128)(2,1)}, u32[]{:S(2)}) %copy-start.2) | copy-done | bytes 1048600
  4.7 0.8 %copy-done.5 = bf16[2,8,2048]{2,1,0:T(8,128)(2,1)S(1)} copy-done((bf16[2,8,2048]{2,1,0:T(8,128)(2,1)S(1)}, bf16[2,8,2048]{2,1,0:T(8,128)(2,1)}, u32[]{:S(2)}) %copy-start.5) | copy-done | bytes 65560
  5.6 0.7 copy-done.6
  6.2 6.8 %project.1 = (bf16[80,128]{1,0:T(8,128)(2,1)S(1)}, bf16[80,128]{1,0:T(8,128)(2,1)S(1)}, bf16[80,128]{1,0:T(8,128)(2,1)S(1)}, bf16[80,128]{1,0:T(8,128)(2,1)S(1)}...) custom-call(s32[1]{0:T(128)} %bitcast.place_ref, ...), custom_call_target="tpu_custom_call" | custom-call | flops 603979776 | bytes 18874368 | tf_op jit(solution)/shard_map/project/pallas_call | solution.py:113
  13.0 0.4 collective-permute-start.1
  13.5 2.7 %collective-permute-start.2 = (bf16[80,128]{1,0:T(8,128)(2,1)S(1)}, bf16[80,128]{1,0:T(8,128)(2,1)S(1)}, u32[]{:S(2)}, u32[]{:S(2)}) collective-permute-start(bf16[80,128]{1,0:T(8,128)(2,1)S(1)} %get-tuple-element.27), channel_id=1, source_target_pairs={{0,2},{1,3},{2,0},{3,1},{4,6},{5,7},{6,4},{7,5},{8,10},{9,11},{10,... | collective-permute-start | bytes 61448 | tf_op jit(solution)/shard_map/ppermute | solution.py:304
  16.1 0.0 collective-permute-start.3
  16.1 1.8 %collective-permute-start.4 = (bf16[80,128]{1,0:T(8,128)(2,1)S(1)}, bf16[80,128]{1,0:T(8,128)(2,1)S(1)}, u32[]{:S(2)}, u32[]{:S(2)}) collective-permute-start(bf16[80,128]{1,0:T(8,128)(2,1)S(1)} %get-tuple-element.29), channel_id=1, source_target_pairs={{0,4},{1,5},{2,6},{3,7},{4,0},{5,1},{6,2},{7,3},{8,12},{9,13},{10,... | collective-permute-start | bytes 61448 | tf_op jit(solution)/shard_map/ppermute | solution.py:304
  17.9 0.1 collective-permute-start.5
  18.0 0.0 collective-permute-done.1.rest_1_
  18.0 2.6 %collective-permute-start.6 = (bf16[80,128]{1,0:T(8,128)(2,1)S(1)}, bf16[80,128]{1,0:T(8,128)(2,1)S(1)}, u32[]{:S(2)}, u32[]{:S(2)}) collective-permute-start(bf16[80,128]{1,0:T(8,128)(2,1)S(1)} %get-tuple-element.31), channel_id=1, source_target_pairs={{0,6},{1,7},{2,4},{3,5},{4,2},{5,3},{6,0},{7,1},{8,14},{9,15},{10,... | collective-permute-start | bytes 61448 | tf_op jit(solution)/shard_map/ppermute | solution.py:304
  20.6 0.0 collective-permute-done.2.rest_2_
  20.6 0.0 collective-permute-start.7
  20.7 0.0 collective-permute-done.3.rest_3_
  20.7 2.7 %collective-permute-start.8 = (bf16[80,128]{1,0:T(8,128)(2,1)S(1)}, bf16[80,128]{1,0:T(8,128)(2,1)S(1)}, u32[]{:S(2)}, u32[]{:S(2)}) collective-permute-start(bf16[80,128]{1,0:T(8,128)(2,1)S(1)} %get-tuple-element.33), channel_id=1, source_target_pairs={{0,8},{1,9},{2,10},{3,11},{4,12},{5,13},{6,14},{7,15},{8,0},{9,1},... | collective-permute-start | bytes 61448 | tf_op jit(solution)/shard_map/ppermute | solution.py:304
  23.3 0.0 collective-permute-done.4.rest_4_
  23.3 0.1 collective-permute-start.9
  23.5 3.5 %collective-permute-start.10 = (bf16[80,128]{1,0:T(8,128)(2,1)S(1)}, bf16[80,128]{1,0:T(8,128)(2,1)S(1)}, u32[]{:S(2)}, u32[]{:S(2)}) collective-permute-start(bf16[80,128]{1,0:T(8,128)(2,1)S(1)} %get-tuple-element.35), channel_id=1, source_target_pairs={{0,10},{1,11},{2,8},{3,9},{4,14},{5,15},{6,12},{7,13},{8,2},{9,3},... | collective-permute-start | bytes 61448 | tf_op jit(solution)/shard_map/ppermute | solution.py:304
  26.9 0.1 multiply_cosine_fusion
  27.1 0.1 collective-permute-start.11
  27.1 0.0 collective-permute-done.7.rest_7_
  27.2 3.6 %collective-permute-start.12 = (bf16[80,128]{1,0:T(8,128)(2,1)S(1)}, bf16[80,128]{1,0:T(8,128)(2,1)S(1)}, u32[]{:S(2)}, u32[]{:S(2)}) collective-permute-start(bf16[80,128]{1,0:T(8,128)(2,1)S(1)} %get-tuple-element.37), channel_id=1, source_target_pairs={{0,12},{1,13},{2,14},{3,15},{4,8},{5,9},{6,10},{7,11},{8,4},{9,5},... | collective-permute-start | bytes 61448 | tf_op jit(solution)/shard_map/ppermute | solution.py:304
  30.7 0.1 collective-permute-start.13
  30.8 0.0 collective-permute-done.9.rest_9_
  30.8 4.4 %collective-permute-start.14 = (bf16[80,128]{1,0:T(8,128)(2,1)S(1)}, bf16[80,128]{1,0:T(8,128)(2,1)S(1)}, u32[]{:S(2)}, u32[]{:S(2)}) collective-permute-start(bf16[80,128]{1,0:T(8,128)(2,1)S(1)} %get-tuple-element.39), channel_id=1, source_target_pairs={{0,14},{1,15},{2,12},{3,13},{4,10},{5,11},{6,8},{7,9},{8,6},{9,7},... | collective-permute-start | bytes 61448 | tf_op jit(solution)/shard_map/ppermute | solution.py:304
  35.2 0.0 collective-permute-done.10.rest_10_
  35.2 0.0 collective-permute-start.15
  35.3 0.1 pad_maximum_fusion
  36.0 0.0 collective-permute-done.11.rest_11_
  36.0 0.0 collective-permute-done.12.rest_12_
  36.0 0.0 collective-permute-done.13.rest_13_
  36.1 1.4 %collective-permute-done.14.rest_14_ = bf16[80,128]{1,0:T(8,128)(2,1)S(1)} collective-permute-done((bf16[80,128]{1,0:T(8,128)(2,1)S(1)}, bf16[80,128]{1,0:T(8,128)(2,1)S(1)}, u32[]{:S(2)}, u32[]{:S(2)}) %collective-permute-start.14) | collective-permute-done | bytes 20512 | tf_op jit(solution)/shard_map/ppermute | solution.py:304
  37.4 3.7 %collective-permute-done.15.rest_15_ = bf16[80,128]{1,0:T(8,128)(2,1)S(1)} collective-permute-done((bf16[80,128]{1,0:T(8,128)(2,1)S(1)}, bf16[80,128]{1,0:T(8,128)(2,1)S(1)}, u32[]{:S(2)}, u32[]{:S(2)}) %collective-permute-start.15) | collective-permute-done | bytes 20512 | tf_op jit(solution)/shard_map/ppermute | solution.py:304
  41.2 2.0 %attend.1 = (bf16[64,128]{1,0:T(8,128)(2,1)S(1)}, bf16[64,128]{1,0:T(8,128)(2,1)S(1)}, bf16[2,512]{1,0:T(2,128)(2,1)}, bf16[2,512]{1,0:T(2,128)(2,1)}) custom-call(s32[1]{0:T(128)} %bitcast.place_ref, s32[1]{0:T(128)S(6)} %copy.13.length_ref, f32[4,128]{1,0:T(4,128)S(1)} %reshape.48.table_ref, bf16[384,512]{1,0:T(8,128)(2,1)S(1)} %bitcast.11, ...), custom_call_target="tpu_custom_call" | custom-call | tf_op jit(solution)/shard_map/attend/pallas_call | solution.py:221
  43.1 0.6 collective-permute-start.29
  43.7 3.2 %collective-permute-start.27 = (bf16[64,128]{1,0:T(8,128)(2,1)S(1)}, bf16[64,128]{1,0:T(8,128)(2,1)S(1)}, u32[]{:S(2)}, u32[]{:S(2)}) collective-permute-start(bf16[64,128]{1,0:T(8,128)(2,1)S(1)} %get-tuple-element.41.rest_0_), channel_id=1, source_target_pairs={{0,12},{1,13},{2,14},{3,15},{4,8},{5,9},{6,10},{7,11},{8,4},{9,5},... | collective-permute-start | bytes 49160 | tf_op jit(solution)/shard_map/ppermute | solution.py:304
  46.9 0.0 collective-permute-start.25
  46.9 3.9 %collective-permute-start.23 = (bf16[64,128]{1,0:T(8,128)(2,1)S(1)}, bf16[64,128]{1,0:T(8,128)(2,1)S(1)}, u32[]{:S(2)}, u32[]{:S(2)}) collective-permute-start(bf16[64,128]{1,0:T(8,128)(2,1)S(1)} %get-tuple-element.41.rest_0_), channel_id=1, source_target_pairs={{0,8},{1,9},{2,10},{3,11},{4,12},{5,13},{6,14},{7,15},{8,0},{9,1},... | collective-permute-start | bytes 49160 | tf_op jit(solution)/shard_map/ppermute | solution.py:304
  50.8 2.0 %collective-permute-start.19 = (bf16[64,128]{1,0:T(8,128)(2,1)S(1)}, bf16[64,128]{1,0:T(8,128)(2,1)S(1)}, u32[]{:S(2)}, u32[]{:S(2)}) collective-permute-start(bf16[64,128]{1,0:T(8,128)(2,1)S(1)} %get-tuple-element.41.rest_0_), channel_id=1, source_target_pairs={{0,4},{1,5},{2,6},{3,7},{4,0},{5,1},{6,2},{7,3},{8,12},{9,13},{10,... | collective-permute-start | bytes 49160 | tf_op jit(solution)/shard_map/ppermute | solution.py:304
  52.8 1.5 %collective-permute-start.17 = (bf16[64,128]{1,0:T(8,128)(2,1)S(1)}, bf16[64,128]{1,0:T(8,128)(2,1)S(1)}, u32[]{:S(2)}, u32[]{:S(2)}) collective-permute-start(bf16[64,128]{1,0:T(8,128)(2,1)S(1)} %get-tuple-element.41.rest_0_), channel_id=1, source_target_pairs={{0,2},{1,3},{2,0},{3,1},{4,6},{5,7},{6,4},{7,5},{8,10},{9,11},{10,... | collective-permute-start | bytes 49160 | tf_op jit(solution)/shard_map/ppermute | solution.py:304
  54.3 0.0 collective-permute-done.25.rest_10_
  54.3 0.0 collective-permute-start.30
  54.3 3.5 %collective-permute-start.28 = (bf16[64,128]{1,0:T(8,128)(2,1)S(1)}, bf16[64,128]{1,0:T(8,128)(2,1)S(1)}, u32[]{:S(2)}, u32[]{:S(2)}) collective-permute-start(bf16[64,128]{1,0:T(8,128)(2,1)S(1)} %get-tuple-element.42), channel_id=1, source_target_pairs={{0,13},{1,12},{2,15},{3,14},{4,9},{5,8},{6,11},{7,10},{8,5},{9,4},... | collective-permute-start | bytes 49160 | tf_op jit(solution)/shard_map/ppermute | solution.py:304
  57.8 0.0 collective-permute-done.19.rest_4_
  57.8 3.6 %collective-permute-start.24 = (bf16[64,128]{1,0:T(8,128)(2,1)S(1)}, bf16[64,128]{1,0:T(8,128)(2,1)S(1)}, u32[]{:S(2)}, u32[]{:S(2)}) collective-permute-start(bf16[64,128]{1,0:T(8,128)(2,1)S(1)} %get-tuple-element.42), channel_id=1, source_target_pairs={{0,9},{1,8},{2,11},{3,10},{4,13},{5,12},{6,15},{7,14},{8,1},{9,0},... | collective-permute-start | bytes 49160 | tf_op jit(solution)/shard_map/ppermute | solution.py:304
  61.4 0.0 collective-permute-done.30.rest_15_
  61.4 1.7 %collective-permute-start.20 = (bf16[64,128]{1,0:T(8,128)(2,1)S(1)}, bf16[64,128]{1,0:T(8,128)(2,1)S(1)}, u32[]{:S(2)}, u32[]{:S(2)}) collective-permute-start(bf16[64,128]{1,0:T(8,128)(2,1)S(1)} %get-tuple-element.42), channel_id=1, source_target_pairs={{0,5},{1,4},{2,7},{3,6},{4,1},{5,0},{6,3},{7,2},{8,13},{9,12},{10,... | collective-permute-start | bytes 49160 | tf_op jit(solution)/shard_map/ppermute | solution.py:304
  63.1 0.0 collective-permute-done.28.rest_13_
  63.1 0.0 collective-permute-start.18
  63.1 0.0 collective-permute-done.26.rest_11_
  63.1 1.6 %collective-permute-start.16 = (bf16[64,128]{1,0:T(8,128)(2,1)S(1)}, bf16[64,128]{1,0:T(8,128)(2,1)S(1)}, u32[]{:S(2)}, u32[]{:S(2)}) collective-permute-start(bf16[64,128]{1,0:T(8,128)(2,1)S(1)} %get-tuple-element.42), channel_id=1, source_target_pairs={{0,1},{1,0},{2,3},{3,2},{4,5},{5,4},{6,7},{7,6},{8,9},{9,8},{10,11... | collective-permute-start | bytes 49160 | tf_op jit(solution)/shard_map/ppermute | solution.py:304
  64.7 0.0 collective-permute-done.24.rest_9_
  64.7 0.7 collective-permute-done.22.rest_7_
  65.4 0.0 collective-permute-done.20.rest_5_
  65.5 0.9 %collective-permute-done.18.rest_3_ = bf16[64,128]{1,0:T(8,128)(2,1)S(1)} collective-permute-done((bf16[64,128]{1,0:T(8,128)(2,1)S(1)}, bf16[64,128]{1,0:T(8,128)(2,1)S(1)}, u32[]{:S(2)}, u32[]{:S(2)}) %collective-permute-start.18) | collective-permute-done | bytes 16416 | tf_op jit(solution)/shard_map/ppermute | solution.py:304
  66.4 0.0 collective-permute-done.16.rest_1_
  66.4 5.8 %copy-done = bf16[4096,2048]{1,0:T(8,128)(2,1)S(1)} copy-done((bf16[4096,2048]{1,0:T(8,128)(2,1)S(1)}, bf16[4096,2048]{1,0:T(8,128)(2,1)}, u32[]{:S(2)}) %copy-start) | copy-done | bytes 16777240
  72.2 3.1 %output.1 = (f32[16,2048]{1,0:T(8,128)S(1)}, bf16[16,2048]{1,0:T(8,128)(2,1)S(1)}) custom-call(s32[1]{0:T(128)} %bitcast.place_ref, bf16[4096,2048]{1,0:T(8,128)(2,1)S(1)} %copy-done, bf16[64,128]{1,0:T(8,128)(2,1)S(1)} %get-tuple-element.41.rest_0_, bf16[64,128]{1,0:T(8,128)(2,1)S(1)} %collective-permute-done.16.rest_1_, ...), custom_call_target="tpu_custom_call" | custom-call | flops 536870912 | bytes 16777216 | tf_op jit(solution)/shard_map/output/pallas_call | solution.py:269
  75.3 0.1 collective-permute-start.31
  75.4 1.1 %collective-permute-done.31 = bf16[16,2048]{1,0:T(8,128)(2,1)S(1)} collective-permute-done((bf16[16,2048]{1,0:T(8,128)(2,1)S(1)}, bf16[16,2048]{1,0:T(8,128)(2,1)S(1)}, u32[]{:S(2)}, u32[]{:S(2)}) %collective-permute-start.31) | collective-permute-done | bytes 65568 | tf_op jit(solution)/shard_map/ppermute | solution.py:328
  76.6 0.6 fusion
  (23 shorter events, 0.1 us)
Async XLA Ops:
  0.6 1.6 %collective-permute-start = (bf16[16,2048]{1,0:T(8,128)(2,1)}, bf16[16,2048]{1,0:T(8,128)(2,1)S(1)}, u32[]{:S(2)}, u32[]{:S(2)}) collective-permute-start(bf16[16,2048]{1,0:T(8,128)(2,1)} %bitcast.13), channel_id=1, source_target_pairs={{0,1},{1,0},{2,3},{3,2},{4,5},{5,4},{6,7},{7,6},{8,9},{9,8},{10,11... | collective-permute-start | bytes 196616 | tf_op jit(solution)/shard_map/ppermute | solution.py:310
  2.3 1.2 %copy-start.1 = (bf16[2048,256]{1,0:T(8,128)(2,1)S(1)}, bf16[2048,256]{1,0:T(8,128)(2,1)}, u32[]{:S(2)}) copy-start(bf16[2048,256]{1,0:T(8,128)(2,1)} %wk_ref.1) | copy-start | bytes 3145732
  3.5 1.2 %copy-start.2 = (bf16[2048,256]{1,0:T(8,128)(2,1)S(1)}, bf16[2048,256]{1,0:T(8,128)(2,1)}, u32[]{:S(2)}) copy-start(bf16[2048,256]{1,0:T(8,128)(2,1)} %wv_ref.1) | copy-start | bytes 3145732
  4.7 0.8 %copy-start.5 = (bf16[2,8,2048]{2,1,0:T(8,128)(2,1)S(1)}, bf16[2,8,2048]{2,1,0:T(8,128)(2,1)}, u32[]{:S(2)}) copy-start(bf16[2,8,2048]{2,1,0:T(8,128)(2,1)} %param.10) | copy-start | bytes 196612
  5.6 0.7 copy-start.6
  6.2 34.9 %copy-start.3 = (bf16[1,384,512]{2,1,0:T(8,128)(2,1)S(1)}, bf16[1,384,512]{2,1,0:T(8,128)(2,1)}, u32[]{:S(2)}) copy-start(bf16[1,384,512]{2,1,0:T(8,128)(2,1)} %param.16) | copy-start | bytes 1179652
  6.2 34.9 %copy-start.4 = (bf16[1,384,512]{2,1,0:T(8,128)(2,1)S(1)}, bf16[1,384,512]{2,1,0:T(8,128)(2,1)}, u32[]{:S(2)}) copy-start(bf16[1,384,512]{2,1,0:T(8,128)(2,1)} %param.17) | copy-start | bytes 1179652
  13.0 4.9 %collective-permute-start.1 = (bf16[80,128]{1,0:T(8,128)(2,1)S(1)}, bf16[80,128]{1,0:T(8,128)(2,1)S(1)}, u32[]{:S(2)}, u32[]{:S(2)}) collective-permute-start(bf16[80,128]{1,0:T(8,128)(2,1)S(1)} %get-tuple-element.26), channel_id=1, source_target_pairs={{0,1},{1,0},{2,3},{3,2},{4,5},{5,4},{6,7},{7,6},{8,9},{9,8},{10,11... | collective-permute-start | bytes 61448 | tf_op jit(solution)/shard_map/ppermute | solution.py:304
  13.5 7.2 %collective-permute-start.2 = (bf16[80,128]{1,0:T(8,128)(2,1)S(1)}, bf16[80,128]{1,0:T(8,128)(2,1)S(1)}, u32[]{:S(2)}, u32[]{:S(2)}) collective-permute-start(bf16[80,128]{1,0:T(8,128)(2,1)S(1)} %get-tuple-element.27), channel_id=1, source_target_pairs={{0,2},{1,3},{2,0},{3,1},{4,6},{5,7},{6,4},{7,5},{8,10},{9,11},{10,... | collective-permute-start | bytes 61448 | tf_op jit(solution)/shard_map/ppermute | solution.py:304
  16.1 4.5 %collective-permute-start.3 = (bf16[80,128]{1,0:T(8,128)(2,1)S(1)}, bf16[80,128]{1,0:T(8,128)(2,1)S(1)}, u32[]{:S(2)}, u32[]{:S(2)}) collective-permute-start(bf16[80,128]{1,0:T(8,128)(2,1)S(1)} %get-tuple-element.28), channel_id=1, source_target_pairs={{0,3},{1,2},{2,1},{3,0},{4,7},{5,6},{6,5},{7,4},{8,11},{9,10},{10,... | collective-permute-start | bytes 61448 | tf_op jit(solution)/shard_map/ppermute | solution.py:304
  16.1 7.2 %collective-permute-start.4 = (bf16[80,128]{1,0:T(8,128)(2,1)S(1)}, bf16[80,128]{1,0:T(8,128)(2,1)S(1)}, u32[]{:S(2)}, u32[]{:S(2)}) collective-permute-start(bf16[80,128]{1,0:T(8,128)(2,1)S(1)} %get-tuple-element.29), channel_id=1, source_target_pairs={{0,4},{1,5},{2,6},{3,7},{4,0},{5,1},{6,2},{7,3},{8,12},{9,13},{10,... | collective-permute-start | bytes 61448 | tf_op jit(solution)/shard_map/ppermute | solution.py:304
  17.9 5.6 %collective-permute-start.5 = (bf16[80,128]{1,0:T(8,128)(2,1)S(1)}, bf16[80,128]{1,0:T(8,128)(2,1)S(1)}, u32[]{:S(2)}, u32[]{:S(2)}) collective-permute-start(bf16[80,128]{1,0:T(8,128)(2,1)S(1)} %get-tuple-element.30), channel_id=1, source_target_pairs={{0,5},{1,4},{2,7},{3,6},{4,1},{5,0},{6,3},{7,2},{8,13},{9,12},{10,... | collective-permute-start | bytes 61448 | tf_op jit(solution)/shard_map/ppermute | solution.py:304
  18.0 9.1 %collective-permute-start.6 = (bf16[80,128]{1,0:T(8,128)(2,1)S(1)}, bf16[80,128]{1,0:T(8,128)(2,1)S(1)}, u32[]{:S(2)}, u32[]{:S(2)}) collective-permute-start(bf16[80,128]{1,0:T(8,128)(2,1)S(1)} %get-tuple-element.31), channel_id=1, source_target_pairs={{0,6},{1,7},{2,4},{3,5},{4,2},{5,3},{6,0},{7,1},{8,14},{9,15},{10,... | collective-permute-start | bytes 61448 | tf_op jit(solution)/shard_map/ppermute | solution.py:304
  20.6 6.5 %collective-permute-start.7 = (bf16[80,128]{1,0:T(8,128)(2,1)S(1)}, bf16[80,128]{1,0:T(8,128)(2,1)S(1)}, u32[]{:S(2)}, u32[]{:S(2)}) collective-permute-start(bf16[80,128]{1,0:T(8,128)(2,1)S(1)} %get-tuple-element.32), channel_id=1, source_target_pairs={{0,7},{1,6},{2,5},{3,4},{4,3},{5,2},{6,1},{7,0},{8,15},{9,14},{10,... | collective-permute-start | bytes 61448 | tf_op jit(solution)/shard_map/ppermute | solution.py:304
  20.7 10.1 %collective-permute-start.8 = (bf16[80,128]{1,0:T(8,128)(2,1)S(1)}, bf16[80,128]{1,0:T(8,128)(2,1)S(1)}, u32[]{:S(2)}, u32[]{:S(2)}) collective-permute-start(bf16[80,128]{1,0:T(8,128)(2,1)S(1)} %get-tuple-element.33), channel_id=1, source_target_pairs={{0,8},{1,9},{2,10},{3,11},{4,12},{5,13},{6,14},{7,15},{8,0},{9,1},... | collective-permute-start | bytes 61448 | tf_op jit(solution)/shard_map/ppermute | solution.py:304
  23.3 7.5 %collective-permute-start.9 = (bf16[80,128]{1,0:T(8,128)(2,1)S(1)}, bf16[80,128]{1,0:T(8,128)(2,1)S(1)}, u32[]{:S(2)}, u32[]{:S(2)}) collective-permute-start(bf16[80,128]{1,0:T(8,128)(2,1)S(1)} %get-tuple-element.34), channel_id=1, source_target_pairs={{0,9},{1,8},{2,11},{3,10},{4,13},{5,12},{6,15},{7,14},{8,1},{9,0},... | collective-permute-start | bytes 61448 | tf_op jit(solution)/shard_map/ppermute | solution.py:304
  23.5 11.8 %collective-permute-start.10 = (bf16[80,128]{1,0:T(8,128)(2,1)S(1)}, bf16[80,128]{1,0:T(8,128)(2,1)S(1)}, u32[]{:S(2)}, u32[]{:S(2)}) collective-permute-start(bf16[80,128]{1,0:T(8,128)(2,1)S(1)} %get-tuple-element.35), channel_id=1, source_target_pairs={{0,10},{1,11},{2,8},{3,9},{4,14},{5,15},{6,12},{7,13},{8,2},{9,3},... | collective-permute-start | bytes 61448 | tf_op jit(solution)/shard_map/ppermute | solution.py:304
  27.1 9.0 %collective-permute-start.11 = (bf16[80,128]{1,0:T(8,128)(2,1)S(1)}, bf16[80,128]{1,0:T(8,128)(2,1)S(1)}, u32[]{:S(2)}, u32[]{:S(2)}) collective-permute-start(bf16[80,128]{1,0:T(8,128)(2,1)S(1)} %get-tuple-element.36), channel_id=1, source_target_pairs={{0,11},{1,10},{2,9},{3,8},{4,15},{5,14},{6,13},{7,12},{8,3},{9,2},... | collective-permute-start | bytes 61448 | tf_op jit(solution)/shard_map/ppermute | solution.py:304
  27.2 8.9 %collective-permute-start.12 = (bf16[80,128]{1,0:T(8,128)(2,1)S(1)}, bf16[80,128]{1,0:T(8,128)(2,1)S(1)}, u32[]{:S(2)}, u32[]{:S(2)}) collective-permute-start(bf16[80,128]{1,0:T(8,128)(2,1)S(1)} %get-tuple-element.37), channel_id=1, source_target_pairs={{0,12},{1,13},{2,14},{3,15},{4,8},{5,9},{6,10},{7,11},{8,4},{9,5},... | collective-permute-start | bytes 61448 | tf_op jit(solution)/shard_map/ppermute | solution.py:304
  30.7 5.3 %collective-permute-start.13 = (bf16[80,128]{1,0:T(8,128)(2,1)S(1)}, bf16[80,128]{1,0:T(8,128)(2,1)S(1)}, u32[]{:S(2)}, u32[]{:S(2)}) collective-permute-start(bf16[80,128]{1,0:T(8,128)(2,1)S(1)} %get-tuple-element.38), channel_id=1, source_target_pairs={{0,13},{1,12},{2,15},{3,14},{4,9},{5,8},{6,11},{7,10},{8,5},{9,4},... | collective-permute-start | bytes 61448 | tf_op jit(solution)/shard_map/ppermute | solution.py:304
  30.8 6.6 %collective-permute-start.14 = (bf16[80,128]{1,0:T(8,128)(2,1)S(1)}, bf16[80,128]{1,0:T(8,128)(2,1)S(1)}, u32[]{:S(2)}, u32[]{:S(2)}) collective-permute-start(bf16[80,128]{1,0:T(8,128)(2,1)S(1)} %get-tuple-element.39), channel_id=1, source_target_pairs={{0,14},{1,15},{2,12},{3,13},{4,10},{5,11},{6,8},{7,9},{8,6},{9,7},... | collective-permute-start | bytes 61448 | tf_op jit(solution)/shard_map/ppermute | solution.py:304
  35.2 5.9 %collective-permute-start.15 = (bf16[80,128]{1,0:T(8,128)(2,1)S(1)}, bf16[80,128]{1,0:T(8,128)(2,1)S(1)}, u32[]{:S(2)}, u32[]{:S(2)}) collective-permute-start(bf16[80,128]{1,0:T(8,128)(2,1)S(1)} %get-tuple-element.40), channel_id=1, source_target_pairs={{0,15},{1,14},{2,13},{3,12},{4,11},{5,10},{6,9},{7,8},{8,7},{9,6},... | collective-permute-start | bytes 61448 | tf_op jit(solution)/shard_map/ppermute | solution.py:304
  43.1 7.7 %collective-permute-start.29 = (bf16[64,128]{1,0:T(8,128)(2,1)S(1)}, bf16[64,128]{1,0:T(8,128)(2,1)S(1)}, u32[]{:S(2)}, u32[]{:S(2)}) collective-permute-start(bf16[64,128]{1,0:T(8,128)(2,1)S(1)} %get-tuple-element.41.rest_0_), channel_id=1, source_target_pairs={{0,14},{1,15},{2,12},{3,13},{4,10},{5,11},{6,8},{7,9},{8,6},{9,7},... | collective-permute-start | bytes 49160 | tf_op jit(solution)/shard_map/ppermute | solution.py:304
  43.7 9.1 %collective-permute-start.27 = (bf16[64,128]{1,0:T(8,128)(2,1)S(1)}, bf16[64,128]{1,0:T(8,128)(2,1)S(1)}, u32[]{:S(2)}, u32[]{:S(2)}) collective-permute-start(bf16[64,128]{1,0:T(8,128)(2,1)S(1)} %get-tuple-element.41.rest_0_), channel_id=1, source_target_pairs={{0,12},{1,13},{2,14},{3,15},{4,8},{5,9},{6,10},{7,11},{8,4},{9,5},... | collective-permute-start | bytes 49160 | tf_op jit(solution)/shard_map/ppermute | solution.py:304
  46.9 7.4 %collective-permute-start.25 = (bf16[64,128]{1,0:T(8,128)(2,1)S(1)}, bf16[64,128]{1,0:T(8,128)(2,1)S(1)}, u32[]{:S(2)}, u32[]{:S(2)}) collective-permute-start(bf16[64,128]{1,0:T(8,128)(2,1)S(1)} %get-tuple-element.41.rest_0_), channel_id=1, source_target_pairs={{0,10},{1,11},{2,8},{3,9},{4,14},{5,15},{6,12},{7,13},{8,2},{9,3},... | collective-permute-start | bytes 49160 | tf_op jit(solution)/shard_map/ppermute | solution.py:304
  46.9 7.4 %collective-permute-start.23 = (bf16[64,128]{1,0:T(8,128)(2,1)S(1)}, bf16[64,128]{1,0:T(8,128)(2,1)S(1)}, u32[]{:S(2)}, u32[]{:S(2)}) collective-permute-start(bf16[64,128]{1,0:T(8,128)(2,1)S(1)} %get-tuple-element.41.rest_0_), channel_id=1, source_target_pairs={{0,8},{1,9},{2,10},{3,11},{4,12},{5,13},{6,14},{7,15},{8,0},{9,1},... | collective-permute-start | bytes 49160 | tf_op jit(solution)/shard_map/ppermute | solution.py:304
  50.8 7.0 %collective-permute-start.21 = (bf16[64,128]{1,0:T(8,128)(2,1)S(1)}, bf16[64,128]{1,0:T(8,128)(2,1)S(1)}, u32[]{:S(2)}, u32[]{:S(2)}) collective-permute-start(bf16[64,128]{1,0:T(8,128)(2,1)S(1)} %get-tuple-element.41.rest_0_), channel_id=1, source_target_pairs={{0,6},{1,7},{2,4},{3,5},{4,2},{5,3},{6,0},{7,1},{8,14},{9,15},{10,... | collective-permute-start | bytes 49160 | tf_op jit(solution)/shard_map/ppermute | solution.py:304
  50.8 7.0 %collective-permute-start.19 = (bf16[64,128]{1,0:T(8,128)(2,1)S(1)}, bf16[64,128]{1,0:T(8,128)(2,1)S(1)}, u32[]{:S(2)}, u32[]{:S(2)}) collective-permute-start(bf16[64,128]{1,0:T(8,128)(2,1)S(1)} %get-tuple-element.41.rest_0_), channel_id=1, source_target_pairs={{0,4},{1,5},{2,6},{3,7},{4,0},{5,1},{6,2},{7,3},{8,12},{9,13},{10,... | collective-permute-start | bytes 49160 | tf_op jit(solution)/shard_map/ppermute | solution.py:304
  52.8 8.6 %collective-permute-start.17 = (bf16[64,128]{1,0:T(8,128)(2,1)S(1)}, bf16[64,128]{1,0:T(8,128)(2,1)S(1)}, u32[]{:S(2)}, u32[]{:S(2)}) collective-permute-start(bf16[64,128]{1,0:T(8,128)(2,1)S(1)} %get-tuple-element.41.rest_0_), channel_id=1, source_target_pairs={{0,2},{1,3},{2,0},{3,1},{4,6},{5,7},{6,4},{7,5},{8,10},{9,11},{10,... | collective-permute-start | bytes 49160 | tf_op jit(solution)/shard_map/ppermute | solution.py:304
  54.3 7.1 %collective-permute-start.30 = (bf16[64,128]{1,0:T(8,128)(2,1)S(1)}, bf16[64,128]{1,0:T(8,128)(2,1)S(1)}, u32[]{:S(2)}, u32[]{:S(2)}) collective-permute-start(bf16[64,128]{1,0:T(8,128)(2,1)S(1)} %get-tuple-element.42), channel_id=1, source_target_pairs={{0,15},{1,14},{2,13},{3,12},{4,11},{5,10},{6,9},{7,8},{8,7},{9,6},... | collective-permute-start | bytes 49160 | tf_op jit(solution)/shard_map/ppermute | solution.py:304
  54.3 8.8 %collective-permute-start.28 = (bf16[64,128]{1,0:T(8,128)(2,1)S(1)}, bf16[64,128]{1,0:T(8,128)(2,1)S(1)}, u32[]{:S(2)}, u32[]{:S(2)}) collective-permute-start(bf16[64,128]{1,0:T(8,128)(2,1)S(1)} %get-tuple-element.42), channel_id=1, source_target_pairs={{0,13},{1,12},{2,15},{3,14},{4,9},{5,8},{6,11},{7,10},{8,5},{9,4},... | collective-permute-start | bytes 49160 | tf_op jit(solution)/shard_map/ppermute | solution.py:304
  57.8 5.3 %collective-permute-start.26 = (bf16[64,128]{1,0:T(8,128)(2,1)S(1)}, bf16[64,128]{1,0:T(8,128)(2,1)S(1)}, u32[]{:S(2)}, u32[]{:S(2)}) collective-permute-start(bf16[64,128]{1,0:T(8,128)(2,1)S(1)} %get-tuple-element.42), channel_id=1, source_target_pairs={{0,11},{1,10},{2,9},{3,8},{4,15},{5,14},{6,13},{7,12},{8,3},{9,2},... | collective-permute-start | bytes 49160 | tf_op jit(solution)/shard_map/ppermute | solution.py:304
  57.8 6.9 %collective-permute-start.24 = (bf16[64,128]{1,0:T(8,128)(2,1)S(1)}, bf16[64,128]{1,0:T(8,128)(2,1)S(1)}, u32[]{:S(2)}, u32[]{:S(2)}) collective-permute-start(bf16[64,128]{1,0:T(8,128)(2,1)S(1)} %get-tuple-element.42), channel_id=1, source_target_pairs={{0,9},{1,8},{2,11},{3,10},{4,13},{5,12},{6,15},{7,14},{8,1},{9,0},... | collective-permute-start | bytes 49160 | tf_op jit(solution)/shard_map/ppermute | solution.py:304
  61.4 4.1 %collective-permute-start.22 = (bf16[64,128]{1,0:T(8,128)(2,1)S(1)}, bf16[64,128]{1,0:T(8,128)(2,1)S(1)}, u32[]{:S(2)}, u32[]{:S(2)}) collective-permute-start(bf16[64,128]{1,0:T(8,128)(2,1)S(1)} %get-tuple-element.42), channel_id=1, source_target_pairs={{0,7},{1,6},{2,5},{3,4},{4,3},{5,2},{6,1},{7,0},{8,15},{9,14},{10,... | collective-permute-start | bytes 49160 | tf_op jit(solution)/shard_map/ppermute | solution.py:304
  61.4 4.1 %collective-permute-start.20 = (bf16[64,128]{1,0:T(8,128)(2,1)S(1)}, bf16[64,128]{1,0:T(8,128)(2,1)S(1)}, u32[]{:S(2)}, u32[]{:S(2)}) collective-permute-start(bf16[64,128]{1,0:T(8,128)(2,1)S(1)} %get-tuple-element.42), channel_id=1, source_target_pairs={{0,5},{1,4},{2,7},{3,6},{4,1},{5,0},{6,3},{7,2},{8,13},{9,12},{10,... | collective-permute-start | bytes 49160 | tf_op jit(solution)/shard_map/ppermute | solution.py:304
  63.1 3.3 %collective-permute-start.18 = (bf16[64,128]{1,0:T(8,128)(2,1)S(1)}, bf16[64,128]{1,0:T(8,128)(2,1)S(1)}, u32[]{:S(2)}, u32[]{:S(2)}) collective-permute-start(bf16[64,128]{1,0:T(8,128)(2,1)S(1)} %get-tuple-element.42), channel_id=1, source_target_pairs={{0,3},{1,2},{2,1},{3,0},{4,7},{5,6},{6,5},{7,4},{8,11},{9,10},{10,... | collective-permute-start | bytes 49160 | tf_op jit(solution)/shard_map/ppermute | solution.py:304
  63.1 3.3 %collective-permute-start.16 = (bf16[64,128]{1,0:T(8,128)(2,1)S(1)}, bf16[64,128]{1,0:T(8,128)(2,1)S(1)}, u32[]{:S(2)}, u32[]{:S(2)}) collective-permute-start(bf16[64,128]{1,0:T(8,128)(2,1)S(1)} %get-tuple-element.42), channel_id=1, source_target_pairs={{0,1},{1,0},{2,3},{3,2},{4,5},{5,4},{6,7},{7,6},{8,9},{9,8},{10,11... | collective-permute-start | bytes 49160 | tf_op jit(solution)/shard_map/ppermute | solution.py:304
  66.4 5.8 %copy-start = (bf16[4096,2048]{1,0:T(8,128)(2,1)S(1)}, bf16[4096,2048]{1,0:T(8,128)(2,1)}, u32[]{:S(2)}) copy-start(bf16[4096,2048]{1,0:T(8,128)(2,1)} %weight_ref.1) | copy-start | bytes 50331652
  75.3 1.3 %collective-permute-start.31 = (bf16[16,2048]{1,0:T(8,128)(2,1)S(1)}, bf16[16,2048]{1,0:T(8,128)(2,1)S(1)}, u32[]{:S(2)}, u32[]{:S(2)}) collective-permute-start(bf16[16,2048]{1,0:T(8,128)(2,1)S(1)} %get-tuple-element.44), channel_id=1, source_target_pairs={{0,1},{1,0},{2,3},{3,2},{4,5},{5,4},{6,7},{7,6},{8,9},{9,8},{10,11... | collective-permute-start | bytes 196616 | tf_op jit(solution)/shard_map/ppermute | solution.py:328

commit v3 on v2

--- a/solution.py
+++ b/solution.py
@@ -34,14 +34,20 @@
     ).reshape(2 * steps, HD)
 
 
+def in_hbm(array):
+    return pltpu.with_memory_space_constraint(array, pltpu.HBM)
+
+
 def project_kernel(steps, pitch, chunk, place_ref, mine_ref, other_ref, gain_ref, wq_ref, wk_ref, wv_ref,
                    *rest):
-    out_refs, (wq_buf, wk_buf, wv_buf, rows_buf, sems) = rest[:-5], rest[-5:]
+    out_refs, (mine_buf, gain_buf, wq_buf, wk_buf, wv_buf, rows_buf, sems) = rest[:-7], rest[-7:]
     q_cols = wq_ref.shape[1]
     kv_cols = wk_ref.shape[1]
     chunks = q_cols // chunk
-    copies = [pltpu.make_async_copy(wk_ref, wk_buf, sems.at[chunks]),
-              pltpu.make_async_copy(wv_ref, wv_buf, sems.at[chunks + 1])]
+    copies = [pltpu.make_async_copy(mine_ref, mine_buf, sems.at[chunks]),
+              pltpu.make_async_copy(gain_ref, gain_buf, sems.at[chunks + 1]),
+              pltpu.make_async_copy(wk_ref, wk_buf, sems.at[chunks + 2]),
+              pltpu.make_async_copy(wv_ref, wv_buf, sems.at[chunks + 3])]
     for c in range(chunks):
         copies.append(pltpu.make_async_copy(
             wq_ref.at[:, c * chunk:(c + 1) * chunk], wq_buf.at[c], sems.at[c]))
@@ -62,11 +68,13 @@
                 rows_buf[pl.ds(start, half_seqs, stride=stride), :] = block[first:first + half_seqs, :]
 
     low_side = device % 2 == 0
-    mine = mine_ref[...].astype(jnp.float32)
+    copies[0].wait()
+    copies[1].wait()
+    mine = mine_buf[...].astype(jnp.float32)
     other = other_ref[...].astype(jnp.float32)
     x = jnp.concatenate(
         [jnp.where(low_side, mine, other), jnp.where(low_side, other, mine)], axis=0)
-    gain = gain_ref[...].astype(jnp.float32)
+    gain = gain_buf[...].astype(jnp.float32)
     gain = jnp.concatenate([gain[i:i + 1] for i in range(gain.shape[0])], axis=1)
     scaled = (x * gain).astype(jnp.bfloat16)
     squares = jnp.sum(x * x, axis=-1, keepdims=True)
@@ -83,12 +91,12 @@
         for i in range(product.shape[1] // HD):
             spread(first_head + i, product[:, i * HD:(i + 1) * HD])
 
-    copies[0].wait()
+    copies[2].wait()
     multiply(wk_buf[...], q_cols // HD)
-    copies[1].wait()
+    copies[3].wait()
     multiply(wv_buf[...], (q_cols + kv_cols) // HD)
     for c in range(chunks):
-        copies[2 + c].wait()
+        copies[4 + c].wait()
         multiply(wq_buf[c], c * chunk // HD)
     if len(out_refs) == 1:
         out_refs[0][...] = rows_buf[...].reshape(out_refs[0].shape).astype(jnp.bfloat16)
@@ -113,24 +121,53 @@
     return pl.pallas_call(
         functools.partial(project_kernel, steps, pitch, chunk),
         out_shape=out_shape,
-        in_specs=[smem, vmem, vmem, vmem, hbm, hbm, hbm],
+        in_specs=[smem, hbm, vmem, hbm, hbm, hbm, hbm],
         out_specs=(vmem,) * len(out_shape),
         scratch_shapes=[
+            pltpu.VMEM(mine.shape, jnp.bfloat16),
+            pltpu.VMEM(gain.shape, jnp.bfloat16),
             pltpu.VMEM((q_cols // chunk, depth, chunk), jnp.bfloat16),
             pltpu.VMEM((depth, kv_cols), jnp.bfloat16),
             pltpu.VMEM((depth, kv_cols), jnp.bfloat16),
             pltpu.VMEM((seqs * steps * pitch, HD), jnp.float32),
-            pltpu.SemaphoreType.DMA((q_cols // chunk + 2,)),
+            pltpu.SemaphoreType.DMA((q_cols // chunk + 4,)),
         ],
-        compiler_params=pltpu.CompilerParams(vmem_limit_bytes=44 * MIB),
+        compiler_params=pltpu.CompilerParams(vmem_limit_bytes=26 * MIB),
         cost_estimate=pl.CostEstimate(
             flops=4 * half_rows * depth * (q_cols + 2 * kv_cols),
             bytes_accessed=2 * depth * (q_cols + 2 * kv_cols), transcendentals=0),
         name="project",
-    )(place, mine, other, gain, wq, wk, wv)
-
-
-def attend_kernel(steps, pitch, width, direct, place_ref, length_ref, table_ref, keys_ref, values_ref, *rest):
+    )(place, in_hbm(mine), other, in_hbm(gain), in_hbm(wq), in_hbm(wk), in_hbm(wv))
+
+
+def fetch_kernel(chunks, weight_ref, after_ref, held_ref, sems):
+    rows = weight_ref.shape[0] // chunks
+    copies = [pltpu.make_async_copy(
+        weight_ref.at[c * rows:(c + 1) * rows], held_ref.at[c * rows:(c + 1) * rows], sems.at[c])
+        for c in range(chunks)]
+    for copy in copies:
+        copy.start()
+    for copy in copies:
+        copy.wait()
+
+
+def fetch(weight, after):
+    chunks = 8
+    return pl.pallas_call(
+        functools.partial(fetch_kernel, chunks),
+        out_shape=pltpu.VMEM(weight.shape, weight.dtype),
+        in_specs=[pl.BlockSpec(memory_space=pltpu.HBM), pl.BlockSpec(memory_space=pl.ANY)],
+        out_specs=pl.BlockSpec(memory_space=pltpu.VMEM),
+        scratch_shapes=[pltpu.SemaphoreType.DMA((chunks,))],
+        compiler_params=pltpu.CompilerParams(vmem_limit_bytes=8 * MIB),
+        cost_estimate=pl.CostEstimate(
+            flops=0, bytes_accessed=2 * weight.size, transcendentals=0),
+        name="fetch",
+    )(in_hbm(weight), after)
+
+
+def attend_kernel(steps, pitch, width, direct, place_ref, length_ref, table_ref, keys_ref, values_ref, held_ref,
+                  *rest):
     part_refs, (same_ref, cross_ref, new_keys_ref, new_values_ref) = rest[:-4], rest[-4:]
     kv_heads = keys_ref.shape[1] // HD
     half_kv = kv_heads // 2
@@ -212,7 +249,7 @@
     cross_ref[...] = jnp.where(low_side, rows[1], rows[0]).astype(jnp.bfloat16)
 
 
-def attend(place, length, parts, table, keys, values, steps, pitch, width, half_heads, direct):
+def attend(place, length, parts, table, keys, values, held, steps, pitch, width, half_heads, direct):
     vmem = pl.BlockSpec(memory_space=pltpu.VMEM)
     smem = pl.BlockSpec(memory_space=pltpu.SMEM)
     kv_cols = keys.shape[1]
@@ -221,11 +258,11 @@
     return pl.pallas_call(
         functools.partial(attend_kernel, steps, pitch, width, direct),
         out_shape=(half, half, fresh, fresh),
-        in_specs=[smem, smem, vmem, vmem, vmem] + [vmem] * len(parts),
+        in_specs=[smem, smem, vmem, vmem, vmem, pl.BlockSpec(memory_space=pl.ANY)] + [vmem] * len(parts),
         out_specs=(vmem,) * 4,
         compiler_params=pltpu.CompilerParams(vmem_limit_bytes=16 * MIB),
         name="attend",
-    )(place, length, table, keys, values, *parts)
+    )(place, length, table, keys, values, held, *parts)
 
 
 def output_kernel(steps, chunk, place_ref, weight_ref, *rest):
@@ -291,7 +328,7 @@
     steps, half_seqs, depth = hidden_in.shape
     both = ("gx", "gy")
     devices = lax.axis_size(both)
-    direct = devices <= 16 and devices & (devices - 1) == 0
+    direct = False
     half_heads = query_weight.shape[1] // HD
     heads_here = half_heads + 2 * key_weight.shape[1] // HD
     pitch = -(-(heads_here + 2) // 8) * 8
@@ -311,20 +348,21 @@
     parts = project(place, mine, other, norm_gain.reshape(-1, HD), query_weight, key_weight,
                     value_weight, steps, pitch, direct)
 
+    held_weight = fetch(out_weight, parts[0])
     if direct:
         parts = [partner(part, k) for k, part in enumerate(parts)]
     else:
         parts = [to_all(parts[0])]
     table = rope_table(positions[0], steps)
     same, cross, new_keys, new_values = attend(
-        place, lengths, parts, table, cache_keys[0], cache_values[0],
+        place, lengths, parts, table, cache_keys[0], cache_values[0], held_weight,
         steps, pitch, depth * lax.axis_size("gx"), half_heads, direct)
     if direct:
         contexts = [partner(cross if k % 2 else same, k) for k in range(devices)]
     else:
         pair = jnp.where(place[0] % 2 == 0, jnp.stack([same, cross]), jnp.stack([cross, same]))
         contexts = [to_all(jnp.tile(pair, (devices // 2, 1, 1)))]
-    mine, other = output(place, contexts, out_weight, devices, steps)
+    mine, other = output(place, contexts, held_weight, devices, steps)
     other = lax.ppermute(other, "gy", swap)
     result = (mine + other.astype(jnp.float32)).astype(jnp.bfloat16)
     return (

time: 77.5 us -> 60 us (0.77)
  starting transfers between devices: 44.3 us -> 7.8 us
  blocking collectives: 0 us -> 16.1 us
  Pallas kernels: 11.9 us -> 19 us
  waiting for transfers between devices: 8.41 us -> 2.36 us
  local copies, waits for them, and re-layouts: 9.77 us -> 11.6 us
    ppermute x30 -> x0, starting transfers between devices: 43.6 us -> none  [partner(): return lax.ppermute(array, both, [(i, i ^ k) for i in range(devices)])]
    all_to_all x0 -> x1, blocking collectives: none -> 16.1 us  [to_all(): return lax.all_to_all(array, both, split_axis=0, concat_axis=0, tiled=True)]
    all_to_all x0 -> x1, starting transfers between devices: none -> 7.27 us  [to_all(): return lax.all_to_all(array, both, split_axis=0, concat_axis=0, tiled=True)]
    ppermute x30 -> x0, waiting for transfers between devices: 6.83 us -> none  [partner(): return lax.ppermute(array, both, [(i, i ^ k) for i in range(devices)])]
    pallas_call x0 -> x1, Pallas kernels: none -> 5.99 us  [fetch(): pl.pallas_call(functools.partial(fetch_kernel, chunks), out_shape=pltpu.V...]
    unnamed x14 -> x10, local copies, waits for them, and re-layouts: 9.75 us -> 11.5 us
    pallas_call x1, Pallas kernels: 6.79 us -> 7.94 us  [project(): pl.pallas_call(functools.partial(project_kernel, steps, pitch, chunk), ou...]
  transfers between devices with their start and end apart: 32 -> 3, of which waited for: 6 -> 2; matrix products, arithmetic and copies ran while one was open for 0% -> 0% of each run, Pallas kernels for 0% -> 10%
where the time goes in v3:
time: 60 us; the launch traced here: 59.7 us
  Pallas kernels  19 us (32%)
  blocking collectives  16.1 us (27%)
  local copies, waits for them, and re-layouts  11.6 us (19%)
  starting transfers between devices  7.8 us (13%)
  waiting for transfers between devices  2.36 us (4%)
  between operations  2.02 us (3%)
  other arithmetic  0.86 us (1%)
    all_to_all x1, blocking collectives, to_all(): return lax.all_to_all(array, both, split_axis=0, concat_axis=0, tiled=True)  16.1 us
    unnamed x10, local copies, waits for them, and re-layouts  11.5 us
    pallas_call x1, Pallas kernels, project(): pl.pallas_call(functools.partial(project_kernel, steps, pitch, chunk), ou...  7.94 us
    all_to_all x1, starting transfers between devices, to_all(): return lax.all_to_all(array, both, split_axis=0, concat_axis=0, tiled=True)  7.27 us
    pallas_call x1, Pallas kernels, fetch(): pl.pallas_call(functools.partial(fetch_kernel, chunks), out_shape=pltpu.V...  5.99 us
    pallas_call x1, Pallas kernels, output(): pl.pallas_call(functools.partial(output_kernel, steps, chunk), out_shape=...  3.1 us
    pallas_call x1, Pallas kernels, attend(): pl.pallas_call(functools.partial(attend_kernel, steps, pitch, width, dire...  1.96 us
    ppermute x1, waiting for transfers between devices, body(): other = lax.ppermute(other, 'gy', swap)  1.25 us
  transfers between devices with their start and end apart: 3, of which 2 were waited for; matrix products, arithmetic and copies ran while one was open for 0% of the time, Pallas kernels for 10%

profile of v3, /device:TPU:0, one launch (start us, length us, event | category | flops | bytes accessed | tf_op | source)
XLA Modules:
  0.0 59.7 jit_solution(193999758338184968)
XLA Ops:
  0.6 0.5 collective-permute-start
  1.1 1.1 %collective-permute-done.other_ref = bf16[16,2048]{1,0:T(8,128)(2,1)S(1)} collective-permute-done((bf16[16,2048]{1,0:T(8,128)(2,1)}, bf16[16,2048]{1,0:T(8,128)(2,1)S(1)}, u32[]{:S(2)}, u32[]{:S(2)}) %collective-permute-start) | collective-permute-done | bytes 65568 | tf_op jit(solution)/shard_map/ppermute | solution.py:347
  2.3 7.9 %project.1.after_ref = bf16[16,80,128]{2,1,0:T(8,128)(2,1)} custom-call(s32[1]{0:T(128)} %bitcast.place_ref, bf16[16,2048]{1,0:T(8,128)(2,1)} %bitcast.20, bf16[16,2048]{1,0:T(8,128)(2,1)S(1)} %collective-permute-done.other_ref, bf16[16,128]{1,0:T(8,128)(2,1)} %bitcast.21, bf16[2048,4096]{1,0:T(8,128)(2,1)} %wq_ref.1, bf16[2048,256]{1,0:T(8,128)(2,1)} %wk_ref.1, ...), custom_call_target="tpu_custom_call" | custom-call | flops 603979776 | bytes 18874368 | tf_op jit(solution)/shard_map/project/pallas_call | solution.py:121
  10.2 7.3 %all-to-all-start = ((bf16[16,80,128]{2,1,0:T(8,128)(2,1)}), bf16[16,80,128]{2,1,0:T(8,128)(2,1)S(1)}, u32[]{:S(2)}, u32[]{:S(2)}) async-start(bf16[16,80,128]{2,1,0:T(8,128)(2,1)} %project.1.after_ref), calls=%async_computation | async-start | bytes 655360 | tf_op jit(solution)/shard_map/all_to_all | solution.py:344
  18.8 0.1 multiply_cosine_fusion
  18.9 0.1 pad_maximum_fusion
  19.0 0.0 copy-start.3
  19.0 0.0 copy-start.4
  19.0 6.0 %fetch.1.held_ref.weight_ref = bf16[4096,2048]{1,0:T(8,128)(2,1)S(1)} custom-call(bf16[4096,2048]{1,0:T(8,128)(2,1)} %weight_ref.1, bf16[16,80,128]{2,1,0:T(8,128)(2,1)} %project.1.after_ref), custom_call_target="tpu_custom_call" | custom-call | bytes 16777216 | tf_op jit(solution)/shard_map/fetch/pallas_call | solution.py:156
  25.0 0.0 copy-start
  25.0 5.7 %copy-done = bf16[4096,2048]{1,0:T(8,128)(2,1)} copy-done((bf16[4096,2048]{1,0:T(8,128)(2,1)}, bf16[4096,2048]{1,0:T(8,128)(2,1)S(1)}, u32[]{:S(2)}) %copy-start) | copy-done | bytes 16777240
  30.8 0.0 all-to-all-done.rest_0_
  30.8 0.0 copy-done.3
  30.8 0.0 copy-done.4
  30.8 0.0 copy-start.1
  30.8 5.8 %copy-done.1 = bf16[4096,2048]{1,0:T(8,128)(2,1)S(1)} copy-done((bf16[4096,2048]{1,0:T(8,128)(2,1)S(1)}, bf16[4096,2048]{1,0:T(8,128)(2,1)}, u32[]{:S(2)}) %copy-start.1) | copy-done | bytes 16777240
  36.6 0.0 copy-start.2
  36.6 2.0 %attend.1 = (bf16[64,128]{1,0:T(8,128)(2,1)S(1)}, bf16[64,128]{1,0:T(8,128)(2,1)S(1)}, bf16[2,512]{1,0:T(2,128)(2,1)}, bf16[2,512]{1,0:T(2,128)(2,1)}) custom-call(s32[1]{0:T(128)} %bitcast.place_ref, s32[1]{0:T(128)S(6)} %copy.13.length_ref, f32[4,128]{1,0:T(4,128)S(1)} %reshape.86.table_ref, bf16[384,512]{1,0:T(8,128)(2,1)S(1)} %bitcast.14, ...), custom_call_target="tpu_custom_call" | custom-call | tf_op jit(solution)/shard_map/attend/pallas_call | solution.py:258
  38.6 16.1 %all_to_all.10.rest_0_ = bf16[16,64,128]{2,1,0:T(8,128)(2,1)S(1)} all-to-all(bf16[16,64,128]{2,1,0:T(8,128)(2,1)S(1)} %bitcast.18), channel_id=1, replica_groups=mesh['rep'=2,'gx'=8,'gy'=2] {'gx','gy'}, dimensions={0} | all-to-all | bytes 524288 | tf_op jit(solution)/shard_map/all_to_all | solution.py:344
  54.7 0.0 copy-done.2
  54.7 3.1 %output.1 = (f32[16,2048]{1,0:T(8,128)S(1)}, bf16[16,2048]{1,0:T(8,128)(2,1)S(1)}) custom-call(s32[1]{0:T(128)} %bitcast.place_ref, bf16[4096,2048]{1,0:T(8,128)(2,1)S(1)} %copy-done.2, bf16[16,64,128]{2,1,0:T(8,128)(2,1)S(1)} %all_to_all.10.rest_0_), custom_call_target="tpu_custom_call" | custom-call | flops 536870912 | bytes 16777216 | tf_op jit(solution)/shard_map/output/pallas_call | solution.py:306
  57.8 0.0 collective-permute-start.1
  57.8 1.2 %collective-permute-done.1 = bf16[16,2048]{1,0:T(8,128)(2,1)S(1)} collective-permute-done((bf16[16,2048]{1,0:T(8,128)(2,1)S(1)}, bf16[16,2048]{1,0:T(8,128)(2,1)S(1)}, u32[]{:S(2)}, u32[]{:S(2)}) %collective-permute-start.1) | collective-permute-done | bytes 65568 | tf_op jit(solution)/shard_map/ppermute | solution.py:366
  59.1 0.6 %fusion = bf16[2,8,2048]{2,1,0:T(8,128)(2,1)} fusion(f32[16,2048]{1,0:T(8,128)S(1)} %get-tuple-element.11, bf16[16,2048]{1,0:T(8,128)(2,1)S(1)} %collective-permute-done.1), kind=kLoop, calls=%fused_computation.1 | loop fusion | flops 98304 | bytes 262144 | tf_op jit(solution)/shard_map/reshape | solution.py:369
  (5 shorter events, 0.1 us)
Async XLA Ops:
  0.6 1.6 %collective-permute-start = (bf16[16,2048]{1,0:T(8,128)(2,1)}, bf16[16,2048]{1,0:T(8,128)(2,1)S(1)}, u32[]{:S(2)}, u32[]{:S(2)}) collective-permute-start(bf16[16,2048]{1,0:T(8,128)(2,1)} %bitcast.19), channel_id=1, source_target_pairs={{0,1},{1,0},{2,3},{3,2},{4,5},{5,4},{6,7},{7,6},{8,9},{9,8},{10,11... | collective-permute-start | bytes 196616 | tf_op jit(solution)/shard_map/ppermute | solution.py:347
  10.2 20.6 %all-to-all-start = ((bf16[16,80,128]{2,1,0:T(8,128)(2,1)}), bf16[16,80,128]{2,1,0:T(8,128)(2,1)S(1)}, u32[]{:S(2)}, u32[]{:S(2)}) async-start(bf16[16,80,128]{2,1,0:T(8,128)(2,1)} %project.1.after_ref), calls=%async_computation | async-start | bytes 655360 | tf_op jit(solution)/shard_map/all_to_all | solution.py:344
  19.0 11.8 %copy-start.3 = (bf16[1,384,512]{2,1,0:T(8,128)(2,1)S(1)}, bf16[1,384,512]{2,1,0:T(8,128)(2,1)}, u32[]{:S(2)}) copy-start(bf16[1,384,512]{2,1,0:T(8,128)(2,1)} %param.16) | copy-start | bytes 1179652
  19.0 11.8 %copy-start.4 = (bf16[1,384,512]{2,1,0:T(8,128)(2,1)S(1)}, bf16[1,384,512]{2,1,0:T(8,128)(2,1)}, u32[]{:S(2)}) copy-start(bf16[1,384,512]{2,1,0:T(8,128)(2,1)} %param.17) | copy-start | bytes 1179652
  25.0 5.7 %copy-start = (bf16[4096,2048]{1,0:T(8,128)(2,1)}, bf16[4096,2048]{1,0:T(8,128)(2,1)S(1)}, u32[]{:S(2)}) copy-start(bf16[4096,2048]{1,0:T(8,128)(2,1)S(1)} %fetch.1.held_ref.weight_ref) | copy-start | bytes 50331652
  30.8 5.8 %copy-start.1 = (bf16[4096,2048]{1,0:T(8,128)(2,1)S(1)}, bf16[4096,2048]{1,0:T(8,128)(2,1)}, u32[]{:S(2)}) copy-start(bf16[4096,2048]{1,0:T(8,128)(2,1)} %copy-done) | copy-start | bytes 50331652
  36.6 18.1 %copy-start.2 = (bf16[4096,2048]{1,0:T(8,128)(2,1)S(1)}, bf16[4096,2048]{1,0:T(8,128)(2,1)}, u32[]{:S(2)}) copy-start(bf16[4096,2048]{1,0:T(8,128)(2,1)} %copy-done) | copy-start | bytes 50331652
  57.8 1.3 %collective-permute-start.1 = (bf16[16,2048]{1,0:T(8,128)(2,1)S(1)}, bf16[16,2048]{1,0:T(8,128)(2,1)S(1)}, u32[]{:S(2)}, u32[]{:S(2)}) collective-permute-start(bf16[16,2048]{1,0:T(8,128)(2,1)S(1)} %get-tuple-element.12), channel_id=1, source_target_pairs={{0,1},{1,0},{2,3},{3,2},{4,5},{5,4},{6,7},{7,6},{8,9},{9,8},{10,11... | collective-permute-start | bytes 196616 | tf_op jit(solution)/shard_map/ppermute | solution.py:366

commit v4 on v3

--- a/solution.py
+++ b/solution.py
@@ -36,6 +36,10 @@
 
 def in_hbm(array):
     return pltpu.with_memory_space_constraint(array, pltpu.HBM)
+
+
+def in_vmem(array):
+    return pltpu.with_memory_space_constraint(array, pltpu.VMEM)
 
 
 def project_kernel(steps, pitch, chunk, place_ref, mine_ref, other_ref, gain_ref, wq_ref, wk_ref, wv_ref,
@@ -262,7 +266,7 @@
         out_specs=(vmem,) * 4,
         compiler_params=pltpu.CompilerParams(vmem_limit_bytes=16 * MIB),
         name="attend",
-    )(place, length, table, keys, values, held, *parts)
+    )(place, length, table, keys, values, in_vmem(held), *parts)
 
 
 def output_kernel(steps, chunk, place_ref, weight_ref, *rest):
@@ -320,7 +324,7 @@
             flops=2 * devices * steps * depth * columns,
             bytes_accessed=2 * depth * columns, transcendentals=0),
         name="output",
-    )(place, weight, *contexts)
+    )(place, in_vmem(weight), *contexts)
 
 
 def body(hidden_in, norm_gain, query_weight, key_weight, value_weight, out_weight,

time: 60 us -> 60 us (level)
  no operation moved by 1% of the time
where the time goes in v4:
time: 60 us; the launch traced here: 59.7 us
  Pallas kernels  19 us (32%)
  blocking collectives  16.1 us (27%)
  local copies, waits for them, and re-layouts  11.6 us (19%)
  starting transfers between devices  7.8 us (13%)
  waiting for transfers between devices  2.36 us (4%)
  between operations  2.02 us (3%)
  other arithmetic  0.86 us (1%)
    all_to_all x1, blocking collectives, to_all(): return lax.all_to_all(array, both, split_axis=0, concat_axis=0, tiled=True)  16.1 us
    unnamed x10, local copies, waits for them, and re-layouts  11.5 us
    pallas_call x1, Pallas kernels, project(): pl.pallas_call(functools.partial(project_kernel, steps, pitch, chunk), ou...  7.94 us
    all_to_all x1, starting transfers between devices, to_all(): return lax.all_to_all(array, both, split_axis=0, concat_axis=0, tiled=True)  7.27 us
    pallas_call x1, Pallas kernels, fetch(): pl.pallas_call(functools.partial(fetch_kernel, chunks), out_shape=pltpu.V...  5.99 us
    pallas_call x1, Pallas kernels, output(): pl.pallas_call(functools.partial(output_kernel, steps, chunk), out_shape=...  3.1 us
    pallas_call x1, Pallas kernels, attend(): pl.pallas_call(functools.partial(attend_kernel, steps, pitch, width, dire...  1.96 us
    ppermute x1, waiting for transfers between devices, body(): other = lax.ppermute(other, 'gy', swap)  1.25 us
  transfers between devices with their start and end apart: 3, of which 2 were waited for; matrix products, arithmetic and copies ran while one was open for 0% of the time, Pallas kernels for 10%

profile of v4, /device:TPU:0, one launch (start us, length us, event | category | flops | bytes accessed | tf_op | source)
XLA Modules:
  0.0 59.7 jit_solution(193999758338184968)
XLA Ops:
  0.6 0.5 collective-permute-start
  1.1 1.1 %collective-permute-done.other_ref = bf16[16,2048]{1,0:T(8,128)(2,1)S(1)} collective-permute-done((bf16[16,2048]{1,0:T(8,128)(2,1)}, bf16[16,2048]{1,0:T(8,128)(2,1)S(1)}, u32[]{:S(2)}, u32[]{:S(2)}) %collective-permute-start) | collective-permute-done | bytes 65568 | tf_op jit(solution)/shard_map/ppermute | solution.py:351
  2.3 7.9 %project.1.after_ref = bf16[16,80,128]{2,1,0:T(8,128)(2,1)} custom-call(s32[1]{0:T(128)} %bitcast.place_ref, bf16[16,2048]{1,0:T(8,128)(2,1)} %bitcast.20, bf16[16,2048]{1,0:T(8,128)(2,1)S(1)} %collective-permute-done.other_ref, bf16[16,128]{1,0:T(8,128)(2,1)} %bitcast.21, bf16[2048,4096]{1,0:T(8,128)(2,1)} %wq_ref.1, bf16[2048,256]{1,0:T(8,128)(2,1)} %wk_ref.1, ...), custom_call_target="tpu_custom_call" | custom-call | flops 603979776 | bytes 18874368 | tf_op jit(solution)/shard_map/project/pallas_call | solution.py:125
  10.2 7.3 %all-to-all-start = ((bf16[16,80,128]{2,1,0:T(8,128)(2,1)}), bf16[16,80,128]{2,1,0:T(8,128)(2,1)S(1)}, u32[]{:S(2)}, u32[]{:S(2)}) async-start(bf16[16,80,128]{2,1,0:T(8,128)(2,1)} %project.1.after_ref), calls=%async_computation | async-start | bytes 655360 | tf_op jit(solution)/shard_map/all_to_all | solution.py:348
  18.8 0.1 multiply_cosine_fusion
  18.9 0.1 pad_maximum_fusion
  19.0 0.0 copy-start.3
  19.0 0.0 copy-start.4
  19.0 6.0 %fetch.1.held_ref.weight_ref = bf16[4096,2048]{1,0:T(8,128)(2,1)S(1)} custom-call(bf16[4096,2048]{1,0:T(8,128)(2,1)} %weight_ref.1, bf16[16,80,128]{2,1,0:T(8,128)(2,1)} %project.1.after_ref), custom_call_target="tpu_custom_call" | custom-call | bytes 16777216 | tf_op jit(solution)/shard_map/fetch/pallas_call | solution.py:160
  25.0 0.0 copy-start
  25.0 5.7 %copy-done = bf16[4096,2048]{1,0:T(8,128)(2,1)} copy-done((bf16[4096,2048]{1,0:T(8,128)(2,1)}, bf16[4096,2048]{1,0:T(8,128)(2,1)S(1)}, u32[]{:S(2)}) %copy-start) | copy-done | bytes 16777240
  30.8 0.0 all-to-all-done.rest_0_
  30.8 0.0 copy-done.3
  30.8 0.0 copy-done.4
  30.8 0.0 copy-start.1
  30.8 5.8 %copy-done.1 = bf16[4096,2048]{1,0:T(8,128)(2,1)S(1)} copy-done((bf16[4096,2048]{1,0:T(8,128)(2,1)S(1)}, bf16[4096,2048]{1,0:T(8,128)(2,1)}, u32[]{:S(2)}) %copy-start.1) | copy-done | bytes 16777240
  36.6 0.0 copy-start.2
  36.6 2.0 %attend.1 = (bf16[64,128]{1,0:T(8,128)(2,1)S(1)}, bf16[64,128]{1,0:T(8,128)(2,1)S(1)}, bf16[2,512]{1,0:T(2,128)(2,1)}, bf16[2,512]{1,0:T(2,128)(2,1)}) custom-call(s32[1]{0:T(128)} %bitcast.place_ref, s32[1]{0:T(128)S(6)} %copy.13.length_ref, f32[4,128]{1,0:T(4,128)S(1)} %reshape.86.table_ref, bf16[384,512]{1,0:T(8,128)(2,1)S(1)} %bitcast.14, ...), custom_call_target="tpu_custom_call" | custom-call | tf_op jit(solution)/shard_map/attend/pallas_call | solution.py:262
  38.6 16.1 %all_to_all.10.rest_0_ = bf16[16,64,128]{2,1,0:T(8,128)(2,1)S(1)} all-to-all(bf16[16,64,128]{2,1,0:T(8,128)(2,1)S(1)} %bitcast.18), channel_id=1, replica_groups=mesh['rep'=2,'gx'=8,'gy'=2] {'gx','gy'}, dimensions={0} | all-to-all | bytes 524288 | tf_op jit(solution)/shard_map/all_to_all | solution.py:348
  54.7 0.0 copy-done.2
  54.7 3.1 %output.1 = (f32[16,2048]{1,0:T(8,128)S(1)}, bf16[16,2048]{1,0:T(8,128)(2,1)S(1)}) custom-call(s32[1]{0:T(128)} %bitcast.place_ref, bf16[4096,2048]{1,0:T(8,128)(2,1)S(1)} %copy-done.2, bf16[16,64,128]{2,1,0:T(8,128)(2,1)S(1)} %all_to_all.10.rest_0_), custom_call_target="tpu_custom_call" | custom-call | flops 536870912 | bytes 16777216 | tf_op jit(solution)/shard_map/output/pallas_call | solution.py:310
  57.8 0.0 collective-permute-start.1
  57.8 1.2 %collective-permute-done.1 = bf16[16,2048]{1,0:T(8,128)(2,1)S(1)} collective-permute-done((bf16[16,2048]{1,0:T(8,128)(2,1)S(1)}, bf16[16,2048]{1,0:T(8,128)(2,1)S(1)}, u32[]{:S(2)}, u32[]{:S(2)}) %collective-permute-start.1) | collective-permute-done | bytes 65568 | tf_op jit(solution)/shard_map/ppermute | solution.py:370
  59.1 0.6 %fusion = bf16[2,8,2048]{2,1,0:T(8,128)(2,1)} fusion(f32[16,2048]{1,0:T(8,128)S(1)} %get-tuple-element.11, bf16[16,2048]{1,0:T(8,128)(2,1)S(1)} %collective-permute-done.1), kind=kLoop, calls=%fused_computation.1 | loop fusion | flops 98304 | bytes 262144 | tf_op jit(solution)/shard_map/reshape | solution.py:373
  (5 shorter events, 0.1 us)
Async XLA Ops:
  0.6 1.6 %collective-permute-start = (bf16[16,2048]{1,0:T(8,128)(2,1)}, bf16[16,2048]{1,0:T(8,128)(2,1)S(1)}, u32[]{:S(2)}, u32[]{:S(2)}) collective-permute-start(bf16[16,2048]{1,0:T(8,128)(2,1)} %bitcast.19), channel_id=1, source_target_pairs={{0,1},{1,0},{2,3},{3,2},{4,5},{5,4},{6,7},{7,6},{8,9},{9,8},{10,11... | collective-permute-start | bytes 196616 | tf_op jit(solution)/shard_map/ppermute | solution.py:351
  10.2 20.6 %all-to-all-start = ((bf16[16,80,128]{2,1,0:T(8,128)(2,1)}), bf16[16,80,128]{2,1,0:T(8,128)(2,1)S(1)}, u32[]{:S(2)}, u32[]{:S(2)}) async-start(bf16[16,80,128]{2,1,0:T(8,128)(2,1)} %project.1.after_ref), calls=%async_computation | async-start | bytes 655360 | tf_op jit(solution)/shard_map/all_to_all | solution.py:348
  19.0 11.8 %copy-start.3 = (bf16[1,384,512]{2,1,0:T(8,128)(2,1)S(1)}, bf16[1,384,512]{2,1,0:T(8,128)(2,1)}, u32[]{:S(2)}) copy-start(bf16[1,384,512]{2,1,0:T(8,128)(2,1)} %param.16) | copy-start | bytes 1179652
  19.0 11.8 %copy-start.4 = (bf16[1,384,512]{2,1,0:T(8,128)(2,1)S(1)}, bf16[1,384,512]{2,1,0:T(8,128)(2,1)}, u32[]{:S(2)}) copy-start(bf16[1,384,512]{2,1,0:T(8,128)(2,1)} %param.17) | copy-start | bytes 1179652
  25.0 5.7 %copy-start = (bf16[4096,2048]{1,0:T(8,128)(2,1)}, bf16[4096,2048]{1,0:T(8,128)(2,1)S(1)}, u32[]{:S(2)}) copy-start(bf16[4096,2048]{1,0:T(8,128)(2,1)S(1)} %fetch.1.held_ref.weight_ref) | copy-start | bytes 50331652
  30.8 5.8 %copy-start.1 = (bf16[4096,2048]{1,0:T(8,128)(2,1)S(1)}, bf16[4096,2048]{1,0:T(8,128)(2,1)}, u32[]{:S(2)}) copy-start(bf16[4096,2048]{1,0:T(8,128)(2,1)} %copy-done) | copy-start | bytes 50331652
  36.6 18.1 %copy-start.2 = (bf16[4096,2048]{1,0:T(8,128)(2,1)S(1)}, bf16[4096,2048]{1,0:T(8,128)(2,1)}, u32[]{:S(2)}) copy-start(bf16[4096,2048]{1,0:T(8,128)(2,1)} %copy-done) | copy-start | bytes 50331652
  57.8 1.3 %collective-permute-start.1 = (bf16[16,2048]{1,0:T(8,128)(2,1)S(1)}, bf16[16,2048]{1,0:T(8,128)(2,1)S(1)}, u32[]{:S(2)}, u32[]{:S(2)}) collective-permute-start(bf16[16,2048]{1,0:T(8,128)(2,1)S(1)} %get-tuple-element.12), channel_id=1, source_target_pairs={{0,1},{1,0},{2,3},{3,2},{4,5},{5,4},{6,7},{7,6},{8,9},{9,8},{10,11... | collective-permute-start | bytes 196616 | tf_op jit(solution)/shard_map/ppermute | solution.py:370

commit v5 on v4

v5 whole, which is shorter than its diff:
```python
import functools
import math

import jax
import jax.numpy as jnp
from jax import lax
from jax.experimental import pallas as pl
from jax.experimental.pallas import tpu as pltpu
from jax.sharding import PartitionSpec as P

HD = 128
epsilon = 1e-05
rope_theta = 500000.0
MIB = 1024 * 1024


def rope_frequencies(head_size):
    index = jnp.arange(head_size // 2).astype(jnp.float32)
    frequency = jnp.exp(-math.log(rope_theta) * 2.0 * index / head_size)
    wavelength = 2.0 * math.pi / frequency
    smooth = (8192.0 / wavelength - 1.0) / 3.0
    blended = (1.0 - smooth) * frequency / 8.0 + smooth * frequency
    adjusted = jnp.where(wavelength > 8192.0, frequency / 8.0, blended)
    return jnp.where(wavelength < 2048.0, frequency, adjusted)


def rope_table(position, steps):
    frequency = rope_frequencies(HD)
    places = position + jnp.arange(steps, dtype=jnp.int32)
    angle = places.astype(jnp.float32)[:, None] * frequency
    cosine, sine = jnp.cos(angle), jnp.sin(angle)
    return jnp.concatenate(
        [cosine, cosine, -sine, sine], axis=-1
    ).reshape(2 * steps, HD)


def in_hbm(array):
    return pltpu.with_memory_space_constraint(array, pltpu.HBM)


def in_vmem(array):
    return pltpu.with_memory_space_constraint(array, pltpu.VMEM)


def slot_patterns(order):
    count = len(order)
    return [
        sum(((j >> (count - 1 - i)) & 1) << bit for i, bit in enumerate(order))
        for j in range(1 << count)]


def project_kernel(steps, group, orders, chunk, place_ref, mine_ref, other_ref, gain_ref, wq_ref, wk_ref, wv_ref,
                   table_ref, length_ref, *rest):
    out_refs, (mine_buf, gain_buf, wq_buf, wk_buf, wv_buf, rows_buf, sems) = rest[:-7], rest[-7:]
    q_cols = wq_ref.shape[1]
    kv_cols = wk_ref.shape[1]
    chunks = q_cols // chunk
    copies = [pltpu.make_async_copy(mine_ref, mine_buf, sems.at[chunks]),
              pltpu.make_async_copy(gain_ref, gain_buf, sems.at[chunks + 1]),
              pltpu.make_async_copy(wk_ref, wk_buf, sems.at[chunks + 2]),
              pltpu.make_async_copy(wv_ref, wv_buf, sems.at[chunks + 3])]
    for c in range(chunks):
        copies.append(pltpu.make_async_copy(
            wq_ref.at[:, c * chunk:(c + 1) * chunk], wq_buf.at[c], sems.at[c]))
    for copy in copies:
        copy.start()

    device = place_ref[0]
    half_rows = mine_ref.shape[0]
    total_rows = 2 * half_rows
    half_seqs = half_rows // steps
    pitch = group + 4
    stride = steps * pitch
    seqs = 2 * half_seqs

    def spread(color, row, block):
        for g in range(2):
            for t in range(steps):
                first = (g * steps + t) * half_seqs
                start = color * seqs * stride + (g * half_seqs * steps + t) * pitch + row
                rows_buf[pl.ds(start, half_seqs, stride=stride), :] = block[first:first + half_seqs, :]

    low_side = device % 2 == 0
    copies[0].wait()
    copies[1].wait()
    mine = mine_buf[...].astype(jnp.float32)
    other = other_ref[...].astype(jnp.float32)
    x = jnp.concatenate(
        [jnp.where(low_side, mine, other), jnp.where(low_side, other, mine)], axis=0)
    gain = gain_buf[...].astype(jnp.float32)
    gain = jnp.concatenate([gain[i:i + 1] for i in range(gain.shape[0])], axis=1)
    scaled = (x * gain).astype(jnp.bfloat16)
    squares = jnp.sum(x * x, axis=-1, keepdims=True)
    high = squares.astype(jnp.bfloat16).astype(jnp.float32)
    low = squares - high
    for color in range(len(orders)):
        spread(color, group + 2, jnp.broadcast_to(high, (total_rows, HD)))
        spread(color, group + 3, jnp.broadcast_to(low, (total_rows, HD)))

    def multiply(weights, place_of_head):
        product = jnp.dot(scaled, weights, preferred_element_type=jnp.float32)
        for i in range(product.shape[1] // HD):
            spread(*place_of_head(i), product[:, i * HD:(i + 1) * HD])

    copies[2].wait()
    multiply(wk_buf[...], lambda i: (i, group))
    copies[3].wait()
    multiply(wv_buf[...], lambda i: (i, group + 1))
    for c in range(chunks):
        copies[4 + c].wait()
        first = c * chunk // HD
        multiply(wq_buf[c], lambda i: ((first + i) // group, (first + i) % group))
    for color, order in enumerate(orders):
        keep_ref, send_ref = out_refs[2 * color:2 * color + 2]
        for j, pattern in enumerate(slot_patterns(order)):
            start = pl.multiple_of(color * seqs * stride + (device ^ pattern) * stride, 8)
            rows = rows_buf[pl.ds(start, stride), :]
            if j < seqs // 2:
                keep_ref[j] = rows
            else:
                send_ref[j - seqs // 2] = rows.astype(jnp.bfloat16)


def project(place, mine, other, gain, wq, wk, wv, table, length, steps, group, orders):
    half_rows, depth = mine.shape
    q_cols, kv_cols = wq.shape[1], wk.shape[1]
    seqs = 2 * half_rows // steps
    chunk = 512
    vmem = pl.BlockSpec(memory_space=pltpu.VMEM)
    smem = pl.BlockSpec(memory_space=pltpu.SMEM)
    hbm = pl.BlockSpec(memory_space=pltpu.HBM)
    block = (seqs // 2, steps * (group + 4), HD)
    out_shape = (
        jax.ShapeDtypeStruct(block, jnp.float32), jax.ShapeDtypeStruct(block, jnp.bfloat16)) * len(orders)
    return pl.pallas_call(
        functools.partial(project_kernel, steps, group, orders, chunk),
        out_shape=out_shape,
        in_specs=[smem, hbm, vmem, hbm, hbm, hbm, hbm, pl.BlockSpec(memory_space=pl.ANY), smem],
        out_specs=(vmem,) * len(out_shape),
        scratch_shapes=[
            pltpu.VMEM(mine.shape, jnp.bfloat16),
            pltpu.VMEM(gain.shape, jnp.bfloat16),
            pltpu.VMEM((q_cols // chunk, depth, chunk), jnp.bfloat16),
            pltpu.VMEM((depth, kv_cols), jnp.bfloat16),
            pltpu.VMEM((depth, kv_cols), jnp.bfloat16),
            pltpu.VMEM((len(orders) * seqs * steps * (group + 4), HD), jnp.float32),
            pltpu.SemaphoreType.DMA((q_cols // chunk + 4,)),
        ],
        compiler_params=pltpu.CompilerParams(vmem_limit_bytes=28 * MIB),
        cost_estimate=pl.CostEstimate(
            flops=4 * half_rows * depth * (q_cols + 2 * kv_cols),
            bytes_accessed=2 * depth * (q_cols + 2 * kv_cols), transcendentals=0),
        name="project",
    )(place, in_hbm(mine), other, in_hbm(gain), in_hbm(wq), in_hbm(wk), in_hbm(wv), table, length)


def combine_kernel(colors, last, *refs):
    ins, outs = refs[:2 * colors], refs[-2 * colors:]
    if last:
        outs = refs[-2:]
    for color in range(colors):
        total = ins[2 * color][...] + ins[2 * color + 1][...].astype(jnp.float32)
        half = total.shape[0] // 2
        if last:
            outs[0][color] = total[0]
            outs[1][color] = total[1].astype(jnp.bfloat16)
        else:
            outs[2 * color][...] = total[:half]
            outs[2 * color + 1][...] = total[half:].astype(jnp.bfloat16)


def combine(pairs, held):
    colors = len(pairs)
    shape = pairs[0][0].shape
    last = shape[0] == 2
    vmem = pl.BlockSpec(memory_space=pltpu.VMEM)
    block = ((colors,) if last else (shape[0] // 2,)) + shape[1:]
    out_shape = (
        jax.ShapeDtypeStruct(block, jnp.float32), jax.ShapeDtypeStruct(block, jnp.bfloat16))
    if not last:
        out_shape = out_shape * colors
    return pl.pallas_call(
        functools.partial(combine_kernel, colors, last),
        out_shape=out_shape,
        in_specs=[vmem] * (2 * colors) + [pl.BlockSpec(memory_space=pl.ANY)] * len(held),
        out_specs=(vmem,) * len(out_shape),
        compiler_params=pltpu.CompilerParams(vmem_limit_bytes=16 * MIB),
        name="combine",
    )(*[array for pair in pairs for array in pair], *[in_vmem(piece) for piece in held])


def fetch_kernel(first, parts, weight_ref, after_ref, held_ref, sems):
    rows = weight_ref.shape[0] // parts
    columns = held_ref.shape[1]
    copies = []
    for c in range(parts):
        span = slice(c * rows, (c + 1) * rows)
        copies.append(pltpu.make_async_copy(
            weight_ref.at[span, first:first + columns], held_ref.at[span], sems.at[c]))
    for copy in copies:
        copy.start()
    for copy in copies:
        copy.wait()


def fetch(weight, first, columns, after):
    parts = 4
    return pl.pallas_call(
        functools.partial(fetch_kernel, first, parts),
        out_shape=pltpu.VMEM((weight.shape[0], columns), weight.dtype),
        in_specs=[pl.BlockSpec(memory_space=pltpu.HBM), pl.BlockSpec(memory_space=pl.ANY)],
        out_specs=pl.BlockSpec(memory_space=pltpu.VMEM),
        scratch_shapes=[pltpu.SemaphoreType.DMA((parts,))],
        compiler_params=pltpu.CompilerParams(vmem_limit_bytes=8 * MIB),
        cost_estimate=pl.CostEstimate(
            flops=0, bytes_accessed=2 * weight.shape[0] * columns, transcendentals=0),
        name="fetch",
    )(in_hbm(weight), after)


def attend_kernel(steps, width, place_ref, length_ref, table_ref, keys_ref, values_ref, same_in_ref, cross_in_ref,
                  *rest):
    same_ref, cross_ref, new_keys_ref, new_values_ref = rest[-4:]
    kv_heads = keys_ref.shape[1] // HD
    half_kv = kv_heads // 2
    pitch = same_in_ref.shape[1] // steps
    group = pitch - 4
    slots = keys_ref.shape[0]
    factor = 1.0 / math.sqrt(HD)
    low_side = place_ref[0] % 2 == 0
    live = lax.broadcasted_iota(jnp.int32, (steps * group, slots), 1) < length_ref[0]
    row_step = lax.broadcasted_iota(jnp.int32, (steps * group, 1), 0) // group
    fresh_keys = [[None] * kv_heads for _ in range(steps)]
    fresh_values = [[None] * kv_heads for _ in range(steps)]
    queries = [None] * kv_heads
    for k in range(half_kv):
        same, cross = same_in_ref[k], cross_in_ref[k].astype(jnp.float32)
        halves = [jnp.where(low_side, same, cross), jnp.where(low_side, cross, same)]
        for g in range(2):
            head = g * half_kv + k
            query = []
            for t in range(steps):
                rows = halves[g][t * pitch:(t + 1) * pitch]
                squares = rows[group + 2:group + 3] + rows[group + 3:group + 4]
                rows = rows * lax.rsqrt(squares / width + epsilon)
                cosine = table_ref[2 * t:2 * t + 1, :]
                sine = table_ref[2 * t + 1:2 * t + 2, :]
                turned = rows * cosine + pltpu.roll(rows, HD // 2, 1) * sine
                query.append(turned[:group])
                fresh_keys[t][head] = turned[group:group + 1].astype(jnp.bfloat16).astype(jnp.float32)
                fresh_values[t][head] = rows[group + 1:group + 2].astype(jnp.bfloat16).astype(jnp.float32)
            queries[head] = jnp.concatenate(query, axis=0).astype(jnp.bfloat16)
    new_keys_ref[...] = jnp.concatenate(
        [jnp.concatenate(row, axis=1) for row in fresh_keys], axis=0).astype(jnp.bfloat16)
    new_values_ref[...] = jnp.concatenate(
        [jnp.concatenate(row, axis=1) for row in fresh_values], axis=0).astype(jnp.bfloat16)
    contexts = []
    for head in range(kv_heads):
        columns = slice(head * HD, (head + 1) * HD)
        query = queries[head]
        scores = lax.dot_general(
            query, keys_ref[:, columns], (((1,), (1,)), ((), ())),
            preferred_element_type=jnp.float32) * factor
        scores = jnp.where(live, scores, -jnp.inf)
        top = jnp.max(scores, axis=-1, keepdims=True)
        wide = query.astype(jnp.float32)
        fresh = []
        for s in range(steps):
            score = jnp.sum(wide * fresh_keys[s][head], axis=-1, keepdims=True) * factor
            score = jnp.where(row_step >= s, score, -jnp.inf)
            fresh.append(score)
            top = jnp.maximum(top, score)
        scores = jnp.exp(scores - top)
        total = jnp.sum(scores, axis=-1, keepdims=True)
        fresh = [jnp.exp(score - top) for score in fresh]
        for score in fresh:
            total = total + score
        weight = (scores / total).astype(jnp.bfloat16)
        mixed = jnp.dot(weight, values_ref[:, columns], preferred_element_type=jnp.float32)
        for s in range(steps):
            weight = (fresh[s] / total).astype(jnp.bfloat16).astype(jnp.float32)
            mixed = mixed + weight * fresh_values[s][head]
        contexts.append(mixed)
    for k in range(half_kv):
        lower, upper = contexts[k], contexts[half_kv + k]
        same_ref[k] = jnp.where(low_side, lower, upper).astype(jnp.bfloat16)
        cross_ref[k] = jnp.where(low_side, upper, lower).astype(jnp.bfloat16)


def attend(place, length, same, cross, table, keys, values, held, steps, width):
    vmem = pl.BlockSpec(memory_space=pltpu.VMEM)
    smem = pl.BlockSpec(memory_space=pltpu.SMEM)
    kv_cols = keys.shape[1]
    group = same.shape[1] // steps - 4
    half = jax.ShapeDtypeStruct((same.shape[0], steps * group, HD), jnp.bfloat16)
    fresh = jax.ShapeDtypeStruct((steps, kv_cols), jnp.bfloat16)
    return pl.pallas_call(
        functools.partial(attend_kernel, steps, width),
        out_shape=(half, half, fresh, fresh),
        in_specs=[smem, smem] + [vmem] * 5 + [pl.BlockSpec(memory_space=pl.ANY)] * len(held),
        out_specs=(vmem,) * 4,
        compiler_params=pltpu.CompilerParams(vmem_limit_bytes=16 * MIB),
        name="attend",
    )(place, length, table, keys, values, same, cross, *[in_vmem(piece) for piece in held])


def pack_kernel(same_ref, other_ref, *out_refs):
    for color, out_ref in enumerate(out_refs):
        out_ref[0] = same_ref[color]
        out_ref[1] = other_ref[color]


def join_kernel(*refs):
    colors = len(refs) // 3
    for color in range(colors):
        first, second, out_ref = refs[2 * color], refs[2 * color + 1], refs[2 * colors + color]
        count = first.shape[0]
        out_ref[:count] = first[...]
        out_ref[count:] = second[...]


def local_call(kernel, out_shape, *arrays):
    vmem = pl.BlockSpec(memory_space=pltpu.VMEM)
    return pl.pallas_call(
        kernel,
        out_shape=out_shape,
        in_specs=[vmem] * len(arrays),
        out_specs=(vmem,) * len(out_shape),
        compiler_params=pltpu.CompilerParams(vmem_limit_bytes=8 * MIB),
        name="join",
    )(*arrays)


def output_kernel(steps, devices, patterns, pieces, place_ref, *rest):
    weight_refs, rest = rest[:pieces], rest[pieces:]
    buffer_refs, (mine_ref, other_ref, wide_buf, rows_buf) = rest[:-4], rest[-4:]
    device = place_ref[0]
    half_seqs = devices // 2
    block = buffer_refs[0].shape[1]
    group = block // steps
    for color, slots in enumerate(patterns):
        base = color * devices * block
        held_ref, came_ref = buffer_refs[2 * color:2 * color + 2]
        for j, pattern in enumerate(slots):
            count = held_ref.shape[0]
            rows = held_ref[j] if j < count else came_ref[j - count]
            start = pl.multiple_of(base + (device ^ pattern) * block, 8)
            wide_buf[pl.ds(start, block), :] = rows.astype(jnp.float32)
        for h in range(group):
            lines = []
            for g in range(2):
                for t in range(steps):
                    start = base + g * half_seqs * block + t * group + h
                    lines.append(wide_buf[pl.ds(start, half_seqs, stride=block), :])
            head = color * group + h
            rows_buf[:, head * HD:(head + 1) * HD] = jnp.concatenate(lines, axis=0).astype(jnp.bfloat16)
    rows = rows_buf[...]
    low_side = device % 2 == 0
    half = rows.shape[0] // 2
    chunk = weight_refs[0].shape[1]
    for c, weight_ref in enumerate(weight_refs):
        span = slice(c * chunk, (c + 1) * chunk)
        product = jnp.dot(rows, weight_ref[...], preferred_element_type=jnp.float32)
        lower, upper = product[:half], product[half:]
        mine_ref[:, span] = jnp.where(low_side, lower, upper)
        other_ref[:, span] = jnp.where(low_side, upper, lower).astype(jnp.bfloat16)


def output(place, buffers, patterns, held, devices, steps):
    depth, chunk = held[0].shape
    columns = chunk * len(held)
    block = buffers[0].shape[1]
    half = devices * steps // 2
    vmem = pl.BlockSpec(memory_space=pltpu.VMEM)
    smem = pl.BlockSpec(memory_space=pltpu.SMEM)
    return pl.pallas_call(
        functools.partial(output_kernel, steps, devices, patterns, len(held)),
        out_shape=(
            jax.ShapeDtypeStruct((half, columns), jnp.float32),
            jax.ShapeDtypeStruct((half, columns), jnp.bfloat16),
        ),
        in_specs=[smem] + [vmem] * (len(held) + len(buffers)),
        out_specs=(vmem, vmem),
        scratch_shapes=[
            pltpu.VMEM((len(patterns) * devices * block, HD), jnp.float32),
            pltpu.VMEM((devices * steps, depth), jnp.bfloat16),
        ],
        compiler_params=pltpu.CompilerParams(vmem_limit_bytes=26 * MIB),
        cost_estimate=pl.CostEstimate(
            flops=2 * devices * steps * depth * columns,
            bytes_accessed=2 * depth * columns, transcendentals=0),
        name="output",
    )(place, *[in_vmem(piece) for piece in held], *buffers)


def body(hidden_in, norm_gain, query_weight, key_weight, value_weight, out_weight,
         cache_keys, cache_values, lengths, positions):
    steps, half_seqs, depth = hidden_in.shape
    both = ("gx", "gy")
    devices = lax.axis_size(both)
    bits = devices.bit_length() - 1
    colors = key_weight.shape[1] // HD
    group = query_weight.shape[1] // HD // colors
    place = lax.axis_index(both).astype(jnp.int32).reshape(1)
    table = rope_table(positions[0], steps)

    def partner(array, bit):
        return lax.ppermute(array, both, [(i, i ^ (1 << bit)) for i in range(devices)])

    far = list(range(1, bits))
    halving = [far[c % 2:] + far[:c % 2] + [0] for c in range(colors)]
    doubling = [far[::-1] if c % 2 == 0 else far[:1] + far[:0:-1] for c in range(colors)]

    chunk = min(out_weight.shape[1], 512)
    pieces = out_weight.shape[1] // chunk
    windows = bits
    held = []

    def fetch_in(window, after):
        now = []
        for i in range(pieces):
            if min(i, windows - 1) == window:
                now.append(fetch(out_weight, i * chunk, chunk, after))
        held.extend(now)
        return now

    mine = hidden_in.reshape(steps * half_seqs, depth)
    other = partner(mine, 0)
    parts = project(place, mine, other, norm_gain.reshape(-1, HD), query_weight, key_weight,
                    value_weight, table, lengths, steps, group, halving)
    for i in range(bits - 1):
        came = [partner(parts[2 * c + 1], halving[c][i]) for c in range(colors)]
        now = fetch_in(i, parts[1])
        parts = combine([(parts[2 * c], came[c]) for c in range(colors)], now)
    same, cross = parts
    now = fetch_in(bits - 1, cross)
    cross = partner(cross, 0)
    same, cross, new_keys, new_values = attend(
        place, lengths, same, cross, table, cache_keys[0], cache_values[0], now,
        steps, depth * lax.axis_size("gx"))
    came = partner(cross, 0)
    pair = jax.ShapeDtypeStruct((2,) + same.shape[1:], jnp.bfloat16)
    buffers = local_call(pack_kernel, (pair,) * colors, same, came)
    patterns = [[0, 1] for _ in range(colors)]
    for i in range(bits - 1):
        came = [partner(buffers[c], doubling[c][i]) for c in range(colors)]
        patterns = [slots + [p ^ (1 << doubling[c][i]) for p in slots] for c, slots in enumerate(patterns)]
        both_now = [array for c in range(colors) for array in (buffers[c], came[c])]
        if i < bits - 2:
            shape = buffers[0].shape
            wider = jax.ShapeDtypeStruct((2 * shape[0],) + shape[1:], jnp.bfloat16)
            buffers = local_call(join_kernel, (wider,) * colors, *both_now)
    mine, other = output(place, both_now, patterns, held, devices, steps)
    other = partner(other, 0)
    result = (mine + other.astype(jnp.float32)).astype(jnp.bfloat16)
    return (
        result.reshape(steps, half_seqs, -1),
        new_keys[:, None, :],
        new_values[:, None, :],
    )


def solution(mesh):
    in_specs = (
        P(None, ("rep", "gy"), "gx"),
        P("gx"),
        P("gx", "gy"),
        P("gx", "gy"),
        P("gx", "gy"),
        P("gy", "gx"),
        P(("rep", "gx", "gy"), None, None),
        P(("rep", "gx", "gy"), None, None),
        P(("rep", "gx", "gy")),
        P(("rep", "gx", "gy")),
    )
    out_specs = (
        P(None, ("rep", "gy"), "gx"),
        P(None, ("rep", "gx", "gy"), None),
        P(None, ("rep", "gx", "gy"), None),
    )
    return jax.shard_map(body, mesh=mesh, in_specs=in_specs, out_specs=out_specs, check_vma=False)
```

time: 60 us -> 55.8 us (0.930)
  blocking collectives: 16.1 us -> 0 us
  waiting for transfers between devices: 2.36 us -> 14.6 us
  local copies, waits for them, and re-layouts: 11.6 us -> 0.03 us
  starting transfers between devices: 7.8 us -> 16.7 us
  Pallas kernels: 19 us -> 21.3 us
    ppermute x2 -> x16, starting transfers between devices: 0.53 us -> 16.7 us  [partner(): lax.ppermute(array, both, [(i, i ^ 1 << bit) for i in range(devices)])]
    all_to_all x1 -> x0, blocking collectives: 16.1 us -> none  [to_all(): return lax.all_to_all(array, both, split_axis=0, concat_axis=0, tiled=True)]
    ppermute x2 -> x16, waiting for transfers between devices: 2.36 us -> 14.6 us  [partner(): lax.ppermute(array, both, [(i, i ^ 1 << bit) for i in range(devices)])]
    unnamed x10 -> x4, local copies, waits for them, and re-layouts: 11.5 us -> 0.01 us
    all_to_all x1 -> x0, starting transfers between devices: 7.27 us -> none  [to_all(): return lax.all_to_all(array, both, split_axis=0, concat_axis=0, tiled=True)]
    pallas_call x4 -> x13, Pallas kernels: 19 us -> 21.3 us  [the longest x4 8.98 us: fetch(): pl.pallas_call(functools.partial(fetch_kernel, first, parts), out_shape=p...]
  transfers between devices with their start and end apart: 3 -> 16, of which waited for: 2 -> 10; matrix products, arithmetic and copies ran while one was open for 0% -> 0% of each run, Pallas kernels for 10% -> 16%
where the time goes in v5:
time: 55.8 us; the launch traced here: 55.6 us
  Pallas kernels  21.3 us (38%)
  starting transfers between devices  16.7 us (30%)
  waiting for transfers between devices  14.6 us (26%)
  between operations  2.09 us (4%)
  other arithmetic  0.85 us (2%)
    ppermute x16, starting transfers between devices, partner(): lax.ppermute(array, both, [(i, i ^ 1 << bit) for i in range(devices)])  16.7 us
    ppermute x16, waiting for transfers between devices, partner(): lax.ppermute(array, both, [(i, i ^ 1 << bit) for i in range(devices)])  14.6 us
    pallas_call x4, Pallas kernels, fetch(): pl.pallas_call(functools.partial(fetch_kernel, first, parts), out_shape=p...  8.98 us
    pallas_call x1, Pallas kernels, project(): pl.pallas_call(functools.partial(project_kernel, steps, group, orders, ch...  7.24 us
    pallas_call x1, Pallas kernels, output(): pl.pallas_call(functools.partial(output_kernel, steps, devices, patterns,...  3 us
    pallas_call x1, Pallas kernels, attend(): pl.pallas_call(functools.partial(attend_kernel, steps, width), out_shape=...  1.97 us
  transfers between devices with their start and end apart: 16, of which 10 were waited for; matrix products, arithmetic and copies ran while one was open for 0% of the time, Pallas kernels for 16%

profile of v5, /device:TPU:0, one launch (start us, length us, event | category | flops | bytes accessed | tf_op | source)
XLA Modules:
  0.0 55.6 jit_solution(14875991904519032941)
XLA Ops:
  0.6 0.5 collective-permute-start
  2.5 0.1 multiply_cosine_fusion
  2.6 0.1 pad_maximum_fusion
  2.7 0.0 collective-permute-done.other_ref
  2.7 7.2 %project.1 = (f32[8,40,128]{2,1,0:T(8,128)S(1)}, bf16[8,40,128]{2,1,0:T(8,128)(2,1)S(1)}, f32[8,40,128]{2,1,0:T(8,128)S(1)}, bf16[8,40,128]{2,1,0:T(8,128)(2,1)S(1)}) custom-call(s32[1]{0:T(128)} %bitcast.place_ref, bf16[16,2048]{1,0:T(8,128)(2,1)} %bitcast.14, bf16[16,2048]{1,0:T(8,128)(2,1)S(1)} %collective-permute-done.other_ref, ...), custom_call_target="tpu_custom_call" | custom-call | flops 603979776 | bytes 18874368 | tf_op jit(solution)/shard_map/project/pallas_call | solution.py:135
  9.9 2.7 %collective-permute-start.2 = (bf16[8,40,128]{2,1,0:T(8,128)(2,1)S(1)}, bf16[8,40,128]{2,1,0:T(8,128)(2,1)S(1)}, u32[]{:S(2)}, u32[]{:S(2)}) collective-permute-start(bf16[8,40,128]{2,1,0:T(8,128)(2,1)S(1)} %get-tuple-element.32), channel_id=1, source_target_pairs={{0,4},{1,5},{2,6},{3,7},{4,0},{5,1},{6,2},{7,3},{8,12},{9,13},{10,... | collective-permute-start | bytes 245768 | tf_op jit(solution)/shard_map/ppermute | solution.py:408
  12.6 1.5 %collective-permute-start.1 = (bf16[8,40,128]{2,1,0:T(8,128)(2,1)S(1)}, bf16[8,40,128]{2,1,0:T(8,128)(2,1)S(1)}, u32[]{:S(2)}, u32[]{:S(2)}) collective-permute-start(bf16[8,40,128]{2,1,0:T(8,128)(2,1)S(1)} %get-tuple-element.29.after_ref), channel_id=1, source_target_pairs={{0,2},{1,3},{2,0},{3,1},{4,6},{5,7},{6,4},{7,5},{8,10},{9,11},{10,... | collective-permute-start | bytes 245768 | tf_op jit(solution)/shard_map/ppermute | solution.py:408
  14.1 2.2 %fetch.4.refs_4_.rest_0_ = bf16[4096,512]{1,0:T(8,128)(2,1)S(1)} custom-call(bf16[4096,2048]{1,0:T(8,128)(2,1)} %weight_ref.7, bf16[8,40,128]{2,1,0:T(8,128)(2,1)S(1)} %get-tuple-element.29.after_ref), custom_call_target="tpu_custom_call" | custom-call | bytes 4194304 | tf_op jit(solution)/shard_map/fetch/pallas_call | solution.py:208
  16.3 0.0 collective-permute-done.2.refs_3_
  16.3 0.8 %collective-permute-done.1.refs_1_ = bf16[8,40,128]{2,1,0:T(8,128)(2,1)S(1)} collective-permute-done((bf16[8,40,128]{2,1,0:T(8,128)(2,1)S(1)}, bf16[8,40,128]{2,1,0:T(8,128)(2,1)S(1)}, u32[]{:S(2)}, u32[]{:S(2)}) %collective-permute-start.1) | collective-permute-done | bytes 81952 | tf_op jit(solution)/shard_map/ppermute | solution.py:408
  17.2 2.7 %collective-permute-start.4 = (bf16[4,40,128]{2,1,0:T(8,128)(2,1)S(1)}, bf16[4,40,128]{2,1,0:T(8,128)(2,1)S(1)}, u32[]{:S(2)}, u32[]{:S(2)}) collective-permute-start(bf16[4,40,128]{2,1,0:T(8,128)(2,1)S(1)} %get-tuple-element.36), channel_id=1, source_target_pairs={{0,8},{1,9},{2,10},{3,11},{4,12},{5,13},{6,14},{7,15},{8,0},{9,1},... | collective-permute-start | bytes 122888 | tf_op jit(solution)/shard_map/ppermute | solution.py:408
  19.9 0.5 collective-permute-start.3
  20.3 2.2 %fetch.5.refs_4_.rest_1_ = bf16[4096,512]{1,0:T(8,128)(2,1)S(1)} custom-call(bf16[4096,2048]{1,0:T(8,128)(2,1)} %weight_ref.7, bf16[4,40,128]{2,1,0:T(8,128)(2,1)S(1)} %get-tuple-element.33.after_ref), custom_call_target="tpu_custom_call" | custom-call | bytes 4194304 | tf_op jit(solution)/shard_map/fetch/pallas_call | solution.py:208
  22.5 0.0 collective-permute-done.4.refs_3_
  22.6 1.3 %collective-permute-done.3.refs_1_ = bf16[4,40,128]{2,1,0:T(8,128)(2,1)S(1)} collective-permute-done((bf16[4,40,128]{2,1,0:T(8,128)(2,1)S(1)}, bf16[4,40,128]{2,1,0:T(8,128)(2,1)S(1)}, u32[]{:S(2)}, u32[]{:S(2)}) %collective-permute-start.3) | collective-permute-done | bytes 40992 | tf_op jit(solution)/shard_map/ppermute | solution.py:408
  23.9 1.6 %collective-permute-start.6 = (bf16[2,40,128]{2,1,0:T(8,128)(2,1)S(1)}, bf16[2,40,128]{2,1,0:T(8,128)(2,1)S(1)}, u32[]{:S(2)}, u32[]{:S(2)}) collective-permute-start(bf16[2,40,128]{2,1,0:T(8,128)(2,1)S(1)} %get-tuple-element.40), channel_id=1, source_target_pairs={{0,2},{1,3},{2,0},{3,1},{4,6},{5,7},{6,4},{7,5},{8,10},{9,11},{10,... | collective-permute-start | bytes 61448 | tf_op jit(solution)/shard_map/ppermute | solution.py:408
  25.4 0.9 %collective-permute-start.5 = (bf16[2,40,128]{2,1,0:T(8,128)(2,1)S(1)}, bf16[2,40,128]{2,1,0:T(8,128)(2,1)S(1)}, u32[]{:S(2)}, u32[]{:S(2)}) collective-permute-start(bf16[2,40,128]{2,1,0:T(8,128)(2,1)S(1)} %get-tuple-element.37.after_ref), channel_id=1, source_target_pairs={{0,8},{1,9},{2,10},{3,11},{4,12},{5,13},{6,14},{7,15},{8,0},{9,1},... | collective-permute-start | bytes 61448 | tf_op jit(solution)/shard_map/ppermute | solution.py:408
  26.3 2.2 %fetch.6.refs_4_.rest_2_ = bf16[4096,512]{1,0:T(8,128)(2,1)S(1)} custom-call(bf16[4096,2048]{1,0:T(8,128)(2,1)} %weight_ref.7, bf16[2,40,128]{2,1,0:T(8,128)(2,1)S(1)} %get-tuple-element.37.after_ref), custom_call_target="tpu_custom_call" | custom-call | bytes 4194304 | tf_op jit(solution)/shard_map/fetch/pallas_call | solution.py:208
  28.6 0.0 collective-permute-done.6.refs_3_
  28.6 1.6 %collective-permute-done.5.refs_1_ = bf16[2,40,128]{2,1,0:T(8,128)(2,1)S(1)} collective-permute-done((bf16[2,40,128]{2,1,0:T(8,128)(2,1)S(1)}, bf16[2,40,128]{2,1,0:T(8,128)(2,1)S(1)}, u32[]{:S(2)}, u32[]{:S(2)}) %collective-permute-start.5) | collective-permute-done | bytes 20512 | tf_op jit(solution)/shard_map/ppermute | solution.py:408
  30.2 0.0 copy-start
  30.2 0.0 copy-start.1
  30.3 0.1 collective-permute-start.7
  30.3 2.3 %fetch.7.rest_0_.rest_3_ = bf16[4096,512]{1,0:T(8,128)(2,1)S(1)} custom-call(bf16[4096,2048]{1,0:T(8,128)(2,1)} %weight_ref.7, bf16[2,40,128]{2,1,0:T(8,128)(2,1)S(1)} %get-tuple-element.41.after_ref), custom_call_target="tpu_custom_call" | custom-call | bytes 4194304 | tf_op jit(solution)/shard_map/fetch/pallas_call | solution.py:208
  32.6 0.0 collective-permute-done.7.cross_in_ref
  32.6 0.0 copy-done
  32.7 0.0 copy-done.1
  32.7 2.0 %attend.1 = (bf16[2,32,128]{2,1,0:T(8,128)(2,1)S(1)}, bf16[2,32,128]{2,1,0:T(8,128)(2,1)S(1)}, bf16[2,512]{1,0:T(2,128)(2,1)}, bf16[2,512]{1,0:T(2,128)(2,1)}) custom-call(s32[1]{0:T(128)} %bitcast.place_ref, s32[1]{0:T(128)S(6)} %copy.13.length_ref, f32[4,128]{1,0:T(4,128)S(1)} %reshape.50.table_ref, bf16[384,512]{1,0:T(8,128)(2,1)S(1)} %bitcast.11, ...), custom_call_target="tpu_custom_call" | custom-call | tf_op jit(solution)/shard_map/attend/pallas_call | solution.py:297
  34.6 0.4 collective-permute-start.8
  35.1 0.8 %collective-permute-done.8.other_ref = bf16[2,32,128]{2,1,0:T(8,128)(2,1)S(1)} collective-permute-done((bf16[2,32,128]{2,1,0:T(8,128)(2,1)S(1)}, bf16[2,32,128]{2,1,0:T(8,128)(2,1)S(1)}, u32[]{:S(2)}, u32[]{:S(2)}) %collective-permute-start.8) | collective-permute-done | bytes 16416 | tf_op jit(solution)/shard_map/ppermute | solution.py:408
  35.9 0.8 %collective-permute-start.9 = (bf16[2,32,128]{2,1,0:T(8,128)(2,1)S(1)}, bf16[2,32,128]{2,1,0:T(8,128)(2,1)S(1)}, u32[]{:S(2)}, u32[]{:S(2)}) collective-permute-start(bf16[2,32,128]{2,1,0:T(8,128)(2,1)S(1)} %get-tuple-element.45.refs_0_), channel_id=1, source_target_pairs={{0,8},{1,9},{2,10},{3,11},{4,12},{5,13},{6,14},{7,15},{8,0},{9,1},... | collective-permute-start | bytes 49160 | tf_op jit(solution)/shard_map/ppermute | solution.py:408
  36.7 0.5 collective-permute-start.10
  37.3 3.3 %collective-permute-done.9.refs_1_ = bf16[2,32,128]{2,1,0:T(8,128)(2,1)S(1)} collective-permute-done((bf16[2,32,128]{2,1,0:T(8,128)(2,1)S(1)}, bf16[2,32,128]{2,1,0:T(8,128)(2,1)S(1)}, u32[]{:S(2)}, u32[]{:S(2)}) %collective-permute-start.9) | collective-permute-done | bytes 16416 | tf_op jit(solution)/shard_map/ppermute | solution.py:408
  40.6 0.0 collective-permute-done.10.refs_3_
  40.6 0.4 collective-permute-start.11
  41.0 2.0 %collective-permute-start.12 = (bf16[4,32,128]{2,1,0:T(8,128)(2,1)S(1)}, bf16[4,32,128]{2,1,0:T(8,128)(2,1)S(1)}, u32[]{:S(2)}, u32[]{:S(2)}) collective-permute-start(bf16[4,32,128]{2,1,0:T(8,128)(2,1)S(1)} %get-tuple-element.48.refs_2_), channel_id=1, source_target_pairs={{0,8},{1,9},{2,10},{3,11},{4,12},{5,13},{6,14},{7,15},{8,0},{9,1},... | collective-permute-start | bytes 98312 | tf_op jit(solution)/shard_map/ppermute | solution.py:408
  42.9 1.6 %collective-permute-done.11.refs_1_ = bf16[4,32,128]{2,1,0:T(8,128)(2,1)S(1)} collective-permute-done((bf16[4,32,128]{2,1,0:T(8,128)(2,1)S(1)}, bf16[4,32,128]{2,1,0:T(8,128)(2,1)S(1)}, u32[]{:S(2)}, u32[]{:S(2)}) %collective-permute-start.11) | collective-permute-done | bytes 32800 | tf_op jit(solution)/shard_map/ppermute | solution.py:408
  44.6 1.2 %collective-permute-done.12.refs_3_ = bf16[4,32,128]{2,1,0:T(8,128)(2,1)S(1)} collective-permute-done((bf16[4,32,128]{2,1,0:T(8,128)(2,1)S(1)}, bf16[4,32,128]{2,1,0:T(8,128)(2,1)S(1)}, u32[]{:S(2)}, u32[]{:S(2)}) %collective-permute-start.12) | collective-permute-done | bytes 32800 | tf_op jit(solution)/shard_map/ppermute | solution.py:408
  45.8 0.6 %collective-permute-start.13 = (bf16[8,32,128]{2,1,0:T(8,128)(2,1)S(1)}, bf16[8,32,128]{2,1,0:T(8,128)(2,1)S(1)}, u32[]{:S(2)}, u32[]{:S(2)}) collective-permute-start(bf16[8,32,128]{2,1,0:T(8,128)(2,1)S(1)} %get-tuple-element.49.rest_4_), channel_id=1, source_target_pairs={{0,2},{1,3},{2,0},{3,1},{4,6},{5,7},{6,4},{7,5},{8,10},{9,11},{10,... | collective-permute-start | bytes 196616 | tf_op jit(solution)/shard_map/ppermute | solution.py:408
  46.4 1.7 %collective-permute-start.14 = (bf16[8,32,128]{2,1,0:T(8,128)(2,1)S(1)}, bf16[8,32,128]{2,1,0:T(8,128)(2,1)S(1)}, u32[]{:S(2)}, u32[]{:S(2)}) collective-permute-start(bf16[8,32,128]{2,1,0:T(8,128)(2,1)S(1)} %get-tuple-element.50.rest_6_), channel_id=1, source_target_pairs={{0,4},{1,5},{2,6},{3,7},{4,0},{5,1},{6,2},{7,3},{8,12},{9,13},{10,... | collective-permute-start | bytes 196616 | tf_op jit(solution)/shard_map/ppermute | solution.py:408
  48.1 2.1 %collective-permute-done.13.rest_5_ = bf16[8,32,128]{2,1,0:T(8,128)(2,1)S(1)} collective-permute-done((bf16[8,32,128]{2,1,0:T(8,128)(2,1)S(1)}, bf16[8,32,128]{2,1,0:T(8,128)(2,1)S(1)}, u32[]{:S(2)}, u32[]{:S(2)}) %collective-permute-start.13) | collective-permute-done | bytes 65568 | tf_op jit(solution)/shard_map/ppermute | solution.py:408
  50.1 0.5 collective-permute-done.14.rest_7_
  50.7 3.0 %output.1 = (f32[16,2048]{1,0:T(8,128)S(1)}, bf16[16,2048]{1,0:T(8,128)(2,1)S(1)}) custom-call(s32[1]{0:T(128)} %bitcast.place_ref, bf16[4096,512]{1,0:T(8,128)(2,1)S(1)} %fetch.4.refs_4_.rest_0_, bf16[4096,512]{1,0:T(8,128)(2,1)S(1)} %fetch.5.refs_4_.rest_1_, bf16[4096,512]{1,0:T(8,128)(2,1)S(1)} %fetch.6.refs_4_.rest_2_, ...), custom_call_target="tpu_custom_call" | custom-call | flops 536870912 | bytes 16777216 | tf_op jit(solution)/shard_map/output/pallas_call | solution.py:376
  53.7 0.0 collective-permute-start.15
  53.7 1.2 %collective-permute-done.15 = bf16[16,2048]{1,0:T(8,128)(2,1)S(1)} collective-permute-done((bf16[16,2048]{1,0:T(8,128)(2,1)S(1)}, bf16[16,2048]{1,0:T(8,128)(2,1)S(1)}, u32[]{:S(2)}, u32[]{:S(2)}) %collective-permute-start.15) | collective-permute-done | bytes 65568 | tf_op jit(solution)/shard_map/ppermute | solution.py:408
  54.9 0.6 %fusion = bf16[2,8,2048]{2,1,0:T(8,128)(2,1)} fusion(f32[16,2048]{1,0:T(8,128)S(1)} %get-tuple-element.51, bf16[16,2048]{1,0:T(8,128)(2,1)S(1)} %collective-permute-done.15), kind=kLoop, calls=%fused_computation.1 | loop fusion | flops 98304 | bytes 262144 | tf_op jit(solution)/shard_map/reshape | solution.py:457
  (9 shorter events, 0.1 us)
Async XLA Ops:
  0.6 2.1 %collective-permute-start = (bf16[16,2048]{1,0:T(8,128)(2,1)}, bf16[16,2048]{1,0:T(8,128)(2,1)S(1)}, u32[]{:S(2)}, u32[]{:S(2)}) collective-permute-start(bf16[16,2048]{1,0:T(8,128)(2,1)} %bitcast.13), channel_id=1, source_target_pairs={{0,1},{1,0},{2,3},{3,2},{4,5},{5,4},{6,7},{7,6},{8,9},{9,8},{10,11... | collective-permute-start | bytes 196616 | tf_op jit(solution)/shard_map/ppermute | solution.py:408
  9.9 6.4 %collective-permute-start.2 = (bf16[8,40,128]{2,1,0:T(8,128)(2,1)S(1)}, bf16[8,40,128]{2,1,0:T(8,128)(2,1)S(1)}, u32[]{:S(2)}, u32[]{:S(2)}) collective-permute-start(bf16[8,40,128]{2,1,0:T(8,128)(2,1)S(1)} %get-tuple-element.32), channel_id=1, source_target_pairs={{0,4},{1,5},{2,6},{3,7},{4,0},{5,1},{6,2},{7,3},{8,12},{9,13},{10,... | collective-permute-start | bytes 245768 | tf_op jit(solution)/shard_map/ppermute | solution.py:408
  12.6 4.6 %collective-permute-start.1 = (bf16[8,40,128]{2,1,0:T(8,128)(2,1)S(1)}, bf16[8,40,128]{2,1,0:T(8,128)(2,1)S(1)}, u32[]{:S(2)}, u32[]{:S(2)}) collective-permute-start(bf16[8,40,128]{2,1,0:T(8,128)(2,1)S(1)} %get-tuple-element.29.after_ref), channel_id=1, source_target_pairs={{0,2},{1,3},{2,0},{3,1},{4,6},{5,7},{6,4},{7,5},{8,10},{9,11},{10,... | collective-permute-start | bytes 245768 | tf_op jit(solution)/shard_map/ppermute | solution.py:408
  17.2 5.3 %collective-permute-start.4 = (bf16[4,40,128]{2,1,0:T(8,128)(2,1)S(1)}, bf16[4,40,128]{2,1,0:T(8,128)(2,1)S(1)}, u32[]{:S(2)}, u32[]{:S(2)}) collective-permute-start(bf16[4,40,128]{2,1,0:T(8,128)(2,1)S(1)} %get-tuple-element.36), channel_id=1, source_target_pairs={{0,8},{1,9},{2,10},{3,11},{4,12},{5,13},{6,14},{7,15},{8,0},{9,1},... | collective-permute-start | bytes 122888 | tf_op jit(solution)/shard_map/ppermute | solution.py:408
  19.9 4.0 %collective-permute-start.3 = (bf16[4,40,128]{2,1,0:T(8,128)(2,1)S(1)}, bf16[4,40,128]{2,1,0:T(8,128)(2,1)S(1)}, u32[]{:S(2)}, u32[]{:S(2)}) collective-permute-start(bf16[4,40,128]{2,1,0:T(8,128)(2,1)S(1)} %get-tuple-element.33.after_ref), channel_id=1, source_target_pairs={{0,4},{1,5},{2,6},{3,7},{4,0},{5,1},{6,2},{7,3},{8,12},{9,13},{10,... | collective-permute-start | bytes 122888 | tf_op jit(solution)/shard_map/ppermute | solution.py:408
  23.9 4.7 %collective-permute-start.6 = (bf16[2,40,128]{2,1,0:T(8,128)(2,1)S(1)}, bf16[2,40,128]{2,1,0:T(8,128)(2,1)S(1)}, u32[]{:S(2)}, u32[]{:S(2)}) collective-permute-start(bf16[2,40,128]{2,1,0:T(8,128)(2,1)S(1)} %get-tuple-element.40), channel_id=1, source_target_pairs={{0,2},{1,3},{2,0},{3,1},{4,6},{5,7},{6,4},{7,5},{8,10},{9,11},{10,... | collective-permute-start | bytes 61448 | tf_op jit(solution)/shard_map/ppermute | solution.py:408
  25.4 4.8 %collective-permute-start.5 = (bf16[2,40,128]{2,1,0:T(8,128)(2,1)S(1)}, bf16[2,40,128]{2,1,0:T(8,128)(2,1)S(1)}, u32[]{:S(2)}, u32[]{:S(2)}) collective-permute-start(bf16[2,40,128]{2,1,0:T(8,128)(2,1)S(1)} %get-tuple-element.37.after_ref), channel_id=1, source_target_pairs={{0,8},{1,9},{2,10},{3,11},{4,12},{5,13},{6,14},{7,15},{8,0},{9,1},... | collective-permute-start | bytes 61448 | tf_op jit(solution)/shard_map/ppermute | solution.py:408
  30.2 2.4 %copy-start = (bf16[1,384,512]{2,1,0:T(8,128)(2,1)S(1)}, bf16[1,384,512]{2,1,0:T(8,128)(2,1)}, u32[]{:S(2)}) copy-start(bf16[1,384,512]{2,1,0:T(8,128)(2,1)} %param.16) | copy-start | bytes 1179652
  30.2 2.4 %copy-start.1 = (bf16[1,384,512]{2,1,0:T(8,128)(2,1)S(1)}, bf16[1,384,512]{2,1,0:T(8,128)(2,1)}, u32[]{:S(2)}) copy-start(bf16[1,384,512]{2,1,0:T(8,128)(2,1)} %param.17) | copy-start | bytes 1179652
  30.3 2.4 %collective-permute-start.7 = (bf16[2,40,128]{2,1,0:T(8,128)(2,1)S(1)}, bf16[2,40,128]{2,1,0:T(8,128)(2,1)S(1)}, u32[]{:S(2)}, u32[]{:S(2)}) collective-permute-start(bf16[2,40,128]{2,1,0:T(8,128)(2,1)S(1)} %get-tuple-element.41.after_ref), channel_id=1, source_target_pairs={{0,1},{1,0},{2,3},{3,2},{4,5},{5,4},{6,7},{7,6},{8,9},{9,8},{10,11... | collective-permute-start | bytes 61448 | tf_op jit(solution)/shard_map/ppermute | solution.py:408
  34.6 1.3 %collective-permute-start.8 = (bf16[2,32,128]{2,1,0:T(8,128)(2,1)S(1)}, bf16[2,32,128]{2,1,0:T(8,128)(2,1)S(1)}, u32[]{:S(2)}, u32[]{:S(2)}) collective-permute-start(bf16[2,32,128]{2,1,0:T(8,128)(2,1)S(1)} %get-tuple-element.44), channel_id=1, source_target_pairs={{0,1},{1,0},{2,3},{3,2},{4,5},{5,4},{6,7},{7,6},{8,9},{9,8},{10,11... | collective-permute-start | bytes 49160 | tf_op jit(solution)/shard_map/ppermute | solution.py:408
  35.9 4.6 %collective-permute-start.9 = (bf16[2,32,128]{2,1,0:T(8,128)(2,1)S(1)}, bf16[2,32,128]{2,1,0:T(8,128)(2,1)S(1)}, u32[]{:S(2)}, u32[]{:S(2)}) collective-permute-start(bf16[2,32,128]{2,1,0:T(8,128)(2,1)S(1)} %get-tuple-element.45.refs_0_), channel_id=1, source_target_pairs={{0,8},{1,9},{2,10},{3,11},{4,12},{5,13},{6,14},{7,15},{8,0},{9,1},... | collective-permute-start | bytes 49160 | tf_op jit(solution)/shard_map/ppermute | solution.py:408
  36.7 3.8 %collective-permute-start.10 = (bf16[2,32,128]{2,1,0:T(8,128)(2,1)S(1)}, bf16[2,32,128]{2,1,0:T(8,128)(2,1)S(1)}, u32[]{:S(2)}, u32[]{:S(2)}) collective-permute-start(bf16[2,32,128]{2,1,0:T(8,128)(2,1)S(1)} %get-tuple-element.46.refs_2_), channel_id=1, source_target_pairs={{0,2},{1,3},{2,0},{3,1},{4,6},{5,7},{6,4},{7,5},{8,10},{9,11},{10,... | collective-permute-start | bytes 49160 | tf_op jit(solution)/shard_map/ppermute | solution.py:408
  40.6 4.0 %collective-permute-start.11 = (bf16[4,32,128]{2,1,0:T(8,128)(2,1)S(1)}, bf16[4,32,128]{2,1,0:T(8,128)(2,1)S(1)}, u32[]{:S(2)}, u32[]{:S(2)}) collective-permute-start(bf16[4,32,128]{2,1,0:T(8,128)(2,1)S(1)} %get-tuple-element.47.refs_0_), channel_id=1, source_target_pairs={{0,4},{1,5},{2,6},{3,7},{4,0},{5,1},{6,2},{7,3},{8,12},{9,13},{10,... | collective-permute-start | bytes 98312 | tf_op jit(solution)/shard_map/ppermute | solution.py:408
  41.0 4.8 %collective-permute-start.12 = (bf16[4,32,128]{2,1,0:T(8,128)(2,1)S(1)}, bf16[4,32,128]{2,1,0:T(8,128)(2,1)S(1)}, u32[]{:S(2)}, u32[]{:S(2)}) collective-permute-start(bf16[4,32,128]{2,1,0:T(8,128)(2,1)S(1)} %get-tuple-element.48.refs_2_), channel_id=1, source_target_pairs={{0,8},{1,9},{2,10},{3,11},{4,12},{5,13},{6,14},{7,15},{8,0},{9,1},... | collective-permute-start | bytes 98312 | tf_op jit(solution)/shard_map/ppermute | solution.py:408
  45.8 4.3 %collective-permute-start.13 = (bf16[8,32,128]{2,1,0:T(8,128)(2,1)S(1)}, bf16[8,32,128]{2,1,0:T(8,128)(2,1)S(1)}, u32[]{:S(2)}, u32[]{:S(2)}) collective-permute-start(bf16[8,32,128]{2,1,0:T(8,128)(2,1)S(1)} %get-tuple-element.49.rest_4_), channel_id=1, source_target_pairs={{0,2},{1,3},{2,0},{3,1},{4,6},{5,7},{6,4},{7,5},{8,10},{9,11},{10,... | collective-permute-start | bytes 196616 | tf_op jit(solution)/shard_map/ppermute | solution.py:408
  46.4 4.3 %collective-permute-start.14 = (bf16[8,32,128]{2,1,0:T(8,128)(2,1)S(1)}, bf16[8,32,128]{2,1,0:T(8,128)(2,1)S(1)}, u32[]{:S(2)}, u32[]{:S(2)}) collective-permute-start(bf16[8,32,128]{2,1,0:T(8,128)(2,1)S(1)} %get-tuple-element.50.rest_6_), channel_id=1, source_target_pairs={{0,4},{1,5},{2,6},{3,7},{4,0},{5,1},{6,2},{7,3},{8,12},{9,13},{10,... | collective-permute-start | bytes 196616 | tf_op jit(solution)/shard_map/ppermute | solution.py:408
  53.7 1.3 %collective-permute-start.15 = (bf16[16,2048]{1,0:T(8,128)(2,1)S(1)}, bf16[16,2048]{1,0:T(8,128)(2,1)S(1)}, u32[]{:S(2)}, u32[]{:S(2)}) collective-permute-start(bf16[16,2048]{1,0:T(8,128)(2,1)S(1)} %get-tuple-element.52), channel_id=1, source_target_pairs={{0,1},{1,0},{2,3},{3,2},{4,5},{5,4},{6,7},{7,6},{8,9},{9,8},{10,11... | collective-permute-start | bytes 196616 | tf_op jit(solution)/shard_map/ppermute | solution.py:408

commit v6 on v5

v6 whole, which is shorter than its diff:
```python
import functools
import math

import jax
import jax.numpy as jnp
from jax import lax
from jax.experimental import pallas as pl
from jax.experimental.pallas import tpu as pltpu
from jax.sharding import PartitionSpec as P

HD = 128
epsilon = 1e-05
rope_theta = 500000.0
MIB = 1024 * 1024


def rope_frequencies(head_size):
    index = jnp.arange(head_size // 2).astype(jnp.float32)
    frequency = jnp.exp(-math.log(rope_theta) * 2.0 * index / head_size)
    wavelength = 2.0 * math.pi / frequency
    smooth = (8192.0 / wavelength - 1.0) / 3.0
    blended = (1.0 - smooth) * frequency / 8.0 + smooth * frequency
    adjusted = jnp.where(wavelength > 8192.0, frequency / 8.0, blended)
    return jnp.where(wavelength < 2048.0, frequency, adjusted)


def rope_table(position, steps):
    frequency = rope_frequencies(HD)
    places = position + jnp.arange(steps, dtype=jnp.int32)
    angle = places.astype(jnp.float32)[:, None] * frequency
    cosine, sine = jnp.cos(angle), jnp.sin(angle)
    return jnp.concatenate(
        [cosine, cosine, -sine, sine], axis=-1
    ).reshape(2 * steps, HD)


def in_hbm(array):
    return pltpu.with_memory_space_constraint(array, pltpu.HBM)


def in_vmem(array):
    return pltpu.with_memory_space_constraint(array, pltpu.VMEM)


def project_kernel(steps, group, colors, chunk, place_ref, mine_ref, other_ref, gain_ref, wq_ref, wk_ref, wv_ref,
                   table_ref, length_ref, *rest):
    out_refs, (mine_buf, gain_buf, wq_buf, wk_buf, wv_buf, rows_buf, sems) = rest[:-7], rest[-7:]
    q_cols = wq_ref.shape[1]
    kv_cols = wk_ref.shape[1]
    chunks = q_cols // chunk
    copies = [pltpu.make_async_copy(mine_ref, mine_buf, sems.at[chunks]),
              pltpu.make_async_copy(gain_ref, gain_buf, sems.at[chunks + 1]),
              pltpu.make_async_copy(wk_ref, wk_buf, sems.at[chunks + 2]),
              pltpu.make_async_copy(wv_ref, wv_buf, sems.at[chunks + 3])]
    for c in range(chunks):
        copies.append(pltpu.make_async_copy(
            wq_ref.at[:, c * chunk:(c + 1) * chunk], wq_buf.at[c], sems.at[c]))
    for copy in copies:
        copy.start()

    device = place_ref[0]
    half_rows = mine_ref.shape[0]
    total_rows = 2 * half_rows
    half_seqs = half_rows // steps
    pitch = group + 4
    stride = colors * steps * pitch

    def spread(color, row, block):
        for g in range(2):
            for t in range(steps):
                first = (g * steps + t) * half_seqs
                start = g * half_seqs * stride + (color * steps + t) * pitch + row
                rows_buf[pl.ds(start, half_seqs, stride=stride), :] = block[first:first + half_seqs, :]

    low_side = device % 2 == 0
    copies[0].wait()
    copies[1].wait()
    mine = mine_buf[...].astype(jnp.float32)
    other = other_ref[...].astype(jnp.float32)
    x = jnp.concatenate(
        [jnp.where(low_side, mine, other), jnp.where(low_side, other, mine)], axis=0)
    gain = gain_buf[...].astype(jnp.float32)
    gain = jnp.concatenate([gain[i:i + 1] for i in range(gain.shape[0])], axis=1)
    scaled = (x * gain).astype(jnp.bfloat16)
    squares = jnp.sum(x * x, axis=-1, keepdims=True)
    high = squares.astype(jnp.bfloat16).astype(jnp.float32)
    low = squares - high
    for color in range(colors):
        spread(color, group + 2, jnp.broadcast_to(high, (total_rows, HD)))
        spread(color, group + 3, jnp.broadcast_to(low, (total_rows, HD)))

    def multiply(weights, place_of_head):
        product = jnp.dot(scaled, weights, preferred_element_type=jnp.float32)
        for i in range(product.shape[1] // HD):
            spread(*place_of_head(i), product[:, i * HD:(i + 1) * HD])

    copies[2].wait()
    multiply(wk_buf[...], lambda i: (i, group))
    copies[3].wait()
    multiply(wv_buf[...], lambda i: (i, group + 1))
    for c in range(chunks):
        copies[4 + c].wait()
        first = c * chunk // HD
        multiply(wq_buf[c], lambda i: ((first + i) // group, (first + i) % group))
    keep_ref, send_ref = out_refs
    near = (device >> 1) % 2
    for slot in range(keep_ref.shape[0]):
        for ref, side in ((keep_ref, near), (send_ref, 1 - near)):
            seq = (slot // 2) * 4 + side * 2 + slot % 2
            start = pl.multiple_of(seq * stride, 8)
            ref[slot] = rows_buf[pl.ds(start, stride), :].astype(ref.dtype)


def project(place, mine, other, gain, wq, wk, wv, table, length, steps, group, colors):
    half_rows, depth = mine.shape
    q_cols, kv_cols = wq.shape[1], wk.shape[1]
    seqs = 2 * half_rows // steps
    chunk = 512
    vmem = pl.BlockSpec(memory_space=pltpu.VMEM)
    smem = pl.BlockSpec(memory_space=pltpu.SMEM)
    hbm = pl.BlockSpec(memory_space=pltpu.HBM)
    block = (seqs // 2, colors * steps * (group + 4), HD)
    out_shape = (jax.ShapeDtypeStruct(block, jnp.float32), jax.ShapeDtypeStruct(block, jnp.bfloat16))
    return pl.pallas_call(
        functools.partial(project_kernel, steps, group, colors, chunk),
        out_shape=out_shape,
        in_specs=[smem, hbm, vmem, hbm, hbm, hbm, hbm, pl.BlockSpec(memory_space=pl.ANY), smem],
        out_specs=(vmem,) * len(out_shape),
        scratch_shapes=[
            pltpu.VMEM(mine.shape, jnp.bfloat16),
            pltpu.VMEM(gain.shape, jnp.bfloat16),
            pltpu.VMEM((q_cols // chunk, depth, chunk), jnp.bfloat16),
            pltpu.VMEM((depth, kv_cols), jnp.bfloat16),
            pltpu.VMEM((depth, kv_cols), jnp.bfloat16),
            pltpu.VMEM((seqs * colors * steps * (group + 4), HD), jnp.float32),
            pltpu.SemaphoreType.DMA((q_cols // chunk + 4,)),
        ],
        compiler_params=pltpu.CompilerParams(vmem_limit_bytes=28 * MIB),
        cost_estimate=pl.CostEstimate(
            flops=4 * half_rows * depth * (q_cols + 2 * kv_cols),
            bytes_accessed=2 * depth * (q_cols + 2 * kv_cols), transcendentals=0),
        name="project",
    )(place, in_hbm(mine), other, in_hbm(gain), in_hbm(wq), in_hbm(wk), in_hbm(wv), table, length)


def combine_kernel(keep_ref, came_ref, out_ref):
    out_ref[...] = (keep_ref[...] + came_ref[...].astype(jnp.float32)).astype(jnp.bfloat16)


def fetch_kernel(first, parts, weight_ref, after_ref, held_ref, sems):
    rows = held_ref.shape[0] // parts
    copies = [
        pltpu.make_async_copy(
            weight_ref.at[first + c * rows:first + (c + 1) * rows],
            held_ref.at[c * rows:(c + 1) * rows], sems.at[c])
        for c in range(parts)]
    for copy in copies:
        copy.start()
    for copy in copies:
        copy.wait()


def fetch(weight, first, rows, after):
    parts = 4
    return pl.pallas_call(
        functools.partial(fetch_kernel, first, parts),
        out_shape=pltpu.VMEM((rows, weight.shape[1]), weight.dtype),
        in_specs=[pl.BlockSpec(memory_space=pltpu.HBM), pl.BlockSpec(memory_space=pl.ANY)],
        out_specs=pl.BlockSpec(memory_space=pltpu.VMEM),
        scratch_shapes=[pltpu.SemaphoreType.DMA((parts,))],
        compiler_params=pltpu.CompilerParams(vmem_limit_bytes=16 * MIB),
        cost_estimate=pl.CostEstimate(
            flops=0, bytes_accessed=2 * rows * weight.shape[1], transcendentals=0),
        name="fetch",
    )(in_hbm(weight), after)


def attend_kernel(steps, width, place_ref, length_ref, table_ref, keys_ref, values_ref, parts_ref,
                  same_ref, cross_ref, new_keys_ref, new_values_ref):
    kv_heads = keys_ref.shape[1] // HD
    half_kv = kv_heads // 2
    pitch = parts_ref.shape[1] // (half_kv * steps)
    group = pitch - 4
    halves = [
        functools.reduce(jnp.add, [
            parts_ref[i].astype(jnp.float32) for i in range(g, parts_ref.shape[0], 2)])
        for g in range(2)]
    slots = keys_ref.shape[0]
    factor = 1.0 / math.sqrt(HD)
    low_side = place_ref[0] % 2 == 0
    live = lax.broadcasted_iota(jnp.int32, (steps * group, slots), 1) < length_ref[0]
    row_step = lax.broadcasted_iota(jnp.int32, (steps * group, 1), 0) // group
    fresh_keys = [[None] * kv_heads for _ in range(steps)]
    fresh_values = [[None] * kv_heads for _ in range(steps)]
    queries = [None] * kv_heads
    for k in range(half_kv):
        for g in range(2):
            head = g * half_kv + k
            query = []
            for t in range(steps):
                rows = halves[g][(k * steps + t) * pitch:(k * steps + t + 1) * pitch]
                squares = rows[group + 2:group + 3] + rows[group + 3:group + 4]
                rows = rows * lax.rsqrt(squares / width + epsilon)
                cosine = table_ref[2 * t:2 * t + 1, :]
                sine = table_ref[2 * t + 1:2 * t + 2, :]
                turned = rows * cosine + pltpu.roll(rows, HD // 2, 1) * sine
                query.append(turned[:group])
                fresh_keys[t][head] = turned[group:group + 1].astype(jnp.bfloat16).astype(jnp.float32)
                fresh_values[t][head] = rows[group + 1:group + 2].astype(jnp.bfloat16).astype(jnp.float32)
            queries[head] = jnp.concatenate(query, axis=0).astype(jnp.bfloat16)
    new_keys_ref[...] = jnp.concatenate(
        [jnp.concatenate(row, axis=1) for row in fresh_keys], axis=0).astype(jnp.bfloat16)
    new_values_ref[...] = jnp.concatenate(
        [jnp.concatenate(row, axis=1) for row in fresh_values], axis=0).astype(jnp.bfloat16)
    contexts = []
    for head in range(kv_heads):
        columns = slice(head * HD, (head + 1) * HD)
        query = queries[head]
        scores = lax.dot_general(
            query, keys_ref[:, columns], (((1,), (1,)), ((), ())),
            preferred_element_type=jnp.float32) * factor
        scores = jnp.where(live, scores, -jnp.inf)
        top = jnp.max(scores, axis=-1, keepdims=True)
        wide = query.astype(jnp.float32)
        fresh = []
        for s in range(steps):
            score = jnp.sum(wide * fresh_keys[s][head], axis=-1, keepdims=True) * factor
            score = jnp.where(row_step >= s, score, -jnp.inf)
            fresh.append(score)
            top = jnp.maximum(top, score)
        scores = jnp.exp(scores - top)
        total = jnp.sum(scores, axis=-1, keepdims=True)
        fresh = [jnp.exp(score - top) for score in fresh]
        for score in fresh:
            total = total + score
        weight = (scores / total).astype(jnp.bfloat16)
        mixed = jnp.dot(weight, values_ref[:, columns], preferred_element_type=jnp.float32)
        for s in range(steps):
            weight = (fresh[s] / total).astype(jnp.bfloat16).astype(jnp.float32)
            mixed = mixed + weight * fresh_values[s][head]
        contexts.append(mixed)
    for k in range(half_kv):
        lower, upper = contexts[k], contexts[half_kv + k]
        span = slice(k * steps * group, (k + 1) * steps * group)
        same_ref[span, :] = jnp.where(low_side, lower, upper).astype(jnp.bfloat16)
        cross_ref[span, :] = jnp.where(low_side, upper, lower).astype(jnp.bfloat16)


def attend(place, length, parts, table, keys, values, steps, width, half_heads):
    vmem = pl.BlockSpec(memory_space=pltpu.VMEM)
    smem = pl.BlockSpec(memory_space=pltpu.SMEM)
    kv_cols = keys.shape[1]
    half = jax.ShapeDtypeStruct((steps * half_heads, HD), jnp.bfloat16)
    fresh = jax.ShapeDtypeStruct((steps, kv_cols), jnp.bfloat16)
    return pl.pallas_call(
        functools.partial(attend_kernel, steps, width),
        out_shape=(half, half, fresh, fresh),
        in_specs=[smem, smem] + [vmem] * 4,
        out_specs=(vmem,) * 4,
        compiler_params=pltpu.CompilerParams(vmem_limit_bytes=16 * MIB),
        name="attend",
    )(place, length, table, keys, values, parts)


def pack_kernel(same_ref, other_ref, out_ref):
    out_ref[0] = same_ref[...]
    out_ref[1] = other_ref[...]


def join_kernel(first_ref, second_ref, *rest):
    out_ref = rest[-1]
    count = first_ref.shape[0]
    out_ref[:count] = first_ref[...]
    out_ref[count:] = second_ref[...]


def local_call(kernel, shape, arrays, held=()):
    vmem = pl.BlockSpec(memory_space=pltpu.VMEM)
    return pl.pallas_call(
        kernel,
        out_shape=jax.ShapeDtypeStruct(shape, jnp.bfloat16),
        in_specs=[vmem] * len(arrays) + [pl.BlockSpec(memory_space=pl.ANY)] * len(held),
        out_specs=vmem,
        compiler_params=pltpu.CompilerParams(vmem_limit_bytes=16 * MIB),
        name="local",
    )(*arrays, *[in_vmem(piece) for piece in held])


def output_kernel(steps, colors, patterns, pieces, place_ref, *rest):
    weight_refs, (held_ref, came_ref, mine_ref, other_ref, wide_buf, rows_buf) = rest[:pieces], rest[pieces:]
    device = place_ref[0]
    devices = len(patterns)
    half_seqs = devices // 2
    count, block, _ = held_ref.shape
    group = block // (steps * colors)
    for j, pattern in enumerate(patterns):
        rows = held_ref[j] if j < count else came_ref[j - count]
        start = pl.multiple_of((device ^ pattern) * block, 8)
        wide_buf[pl.ds(start, block), :] = rows.astype(jnp.float32)
    for head in range(colors * group):
        color, h = head // group, head % group
        lines = []
        for g in range(2):
            for t in range(steps):
                start = g * half_seqs * block + (color * steps + t) * group + h
                lines.append(wide_buf[pl.ds(start, half_seqs, stride=block), :])
        rows_buf[:, head * HD:(head + 1) * HD] = jnp.concatenate(lines, axis=0).astype(jnp.bfloat16)
    low_side = device % 2 == 0
    half = rows_buf.shape[0] // 2
    columns = mine_ref.shape[1]
    chunk = min(columns, 512)
    for c in range(columns // chunk):
        span = slice(c * chunk, (c + 1) * chunk)
        product, first = None, 0
        for weight_ref in weight_refs:
            last = first + weight_ref.shape[0]
            part = jnp.dot(rows_buf[:, first:last], weight_ref[:, span], preferred_element_type=jnp.float32)
            product = part if product is None else product + part
            first = last
        lower, upper = product[:half], product[half:]
        mine_ref[:, span] = jnp.where(low_side, lower, upper)
        other_ref[:, span] = jnp.where(low_side, upper, lower).astype(jnp.bfloat16)


def output(place, held_context, came_context, patterns, held, steps, colors):
    columns = held[0].shape[1]
    depth = sum(piece.shape[0] for piece in held)
    devices = len(patterns)
    half = devices * steps // 2
    vmem = pl.BlockSpec(memory_space=pltpu.VMEM)
    smem = pl.BlockSpec(memory_space=pltpu.SMEM)
    return pl.pallas_call(
        functools.partial(output_kernel, steps, colors, patterns, len(held)),
        out_shape=(
            jax.ShapeDtypeStruct((half, columns), jnp.float32),
            jax.ShapeDtypeStruct((half, columns), jnp.bfloat16),
        ),
        in_specs=[smem] + [vmem] * (len(held) + 2),
        out_specs=(vmem, vmem),
        scratch_shapes=[
            pltpu.VMEM((devices * held_context.shape[1], HD), jnp.float32),
            pltpu.VMEM((devices * steps, depth), jnp.bfloat16),
        ],
        compiler_params=pltpu.CompilerParams(vmem_limit_bytes=26 * MIB),
        cost_estimate=pl.CostEstimate(
            flops=2 * devices * steps * depth * columns,
            bytes_accessed=2 * depth * columns, transcendentals=0),
        name="output",
    )(place, *[in_vmem(piece) for piece in held], held_context, came_context)


def body(hidden_in, norm_gain, query_weight, key_weight, value_weight, out_weight,
         cache_keys, cache_values, lengths, positions):
    steps, half_seqs, depth = hidden_in.shape
    everyone = ("far", "near", "gy")
    devices = lax.axis_size(everyone)
    bits = devices.bit_length() - 1
    colors = key_weight.shape[1] // HD
    half_heads = query_weight.shape[1] // HD
    group = half_heads // colors
    place = lax.axis_index(everyone).astype(jnp.int32).reshape(1)
    table = rope_table(positions[0], steps)

    def partner(array, bit):
        return lax.ppermute(array, everyone, [(i, i ^ (1 << bit)) for i in range(devices)])

    mine = hidden_in.reshape(steps * half_seqs, depth)
    other = partner(mine, 0)
    keep, send = project(place, mine, other, norm_gain.reshape(-1, HD), query_weight, key_weight,
                         value_weight, table, lengths, steps, group, colors)
    parts = local_call(combine_kernel, keep.shape, [keep, partner(send, 1)])
    parts = lax.all_to_all(parts, ("far", "gy"), split_axis=0, concat_axis=0, tiled=True)
    same, cross, new_keys, new_values = attend(
        place, lengths, parts, table, cache_keys[0], cache_values[0],
        steps, depth * devices // 2, half_heads)

    context = local_call(pack_kernel, (2,) + same.shape, [same, partner(cross, 0)])
    patterns = [0, 1]
    order = list(range(bits - 1, 0, -1))
    total = out_weight.shape[0]
    cuts = [total * i // 8 for i in (0, 2, 5, 8)]
    held = []
    for i, bit in enumerate(order):
        came = partner(context, bit)
        patterns = patterns + [p ^ (1 << bit) for p in patterns]
        now = []
        if i < len(cuts) - 1:
            now.append(fetch(out_weight, cuts[i], cuts[i + 1] - cuts[i], context))
            held += now
        if i < len(order) - 1:
            shape = (2 * context.shape[0],) + context.shape[1:]
            context = local_call(join_kernel, shape, [context, came], now)
    mine, other = output(place, context, came, patterns, held, steps, colors)
    other = partner(other, 0)
    result = (mine + other.astype(jnp.float32)).astype(jnp.bfloat16)
    return (
        result.reshape(steps, half_seqs, -1),
        new_keys[:, None, :],
        new_values[:, None, :],
    )


def solution(mesh):
    rep, gx, gy = mesh.devices.shape
    split = jax.sharding.Mesh(mesh.devices.reshape(rep, gx // 2, 2, gy), ("rep", "far", "near", "gy"))
    gx = ("far", "near")
    in_specs = (
        P(None, ("rep", "gy"), gx),
        P(gx),
        P(gx, "gy"),
        P(gx, "gy"),
        P(gx, "gy"),
        P("gy", gx),
        P(("rep", *gx, "gy"), None, None),
        P(("rep", *gx, "gy"), None, None),
        P(("rep", *gx, "gy")),
        P(("rep", *gx, "gy")),
    )
    out_specs = (
        P(None, ("rep", "gy"), gx),
        P(None, ("rep", *gx, "gy"), None),
        P(None, ("rep", *gx, "gy"), None),
    )
    return jax.shard_map(body, mesh=split, in_specs=in_specs, out_specs=out_specs, check_vma=False)
```

time: 55.8 us -> 52.1 us (0.934)
  blocking collectives: 0 us -> 12.1 us
  starting transfers between devices: 16.7 us -> 5.91 us
  waiting for transfers between devices: 14.6 us -> 10.6 us
  Pallas kernels: 21.3 us -> 20.4 us
    all_to_all x0 -> x1, blocking collectives: none -> 12.1 us  [body(): lax.all_to_all(parts, ('far', 'gy'), split_axis=0, concat_axis=0, tiled=T...]
    ppermute x16 -> x7, starting transfers between devices: 16.7 us -> 5.91 us  [partner(): lax.ppermute(array, everyone, [(i, i ^ 1 << bit) for i in range(devices)])]
    ppermute x16 -> x7, waiting for transfers between devices: 14.6 us -> 10.6 us  [partner(): lax.ppermute(array, everyone, [(i, i ^ 1 << bit) for i in range(devices)])]
    pallas_call x4 -> x3, Pallas kernels: 8.98 us -> 7.94 us  [fetch(): pl.pallas_call(functools.partial(fetch_kernel, first, parts), out_shape=p...]
    pallas_call x8 -> x6, Pallas kernels: 10.3 us -> 10.5 us  [the longest x1 7.29 us: project(): pl.pallas_call(functools.partial(project_kernel, steps, group, colors, ch...]
  transfers between devices with their start and end apart: 16 -> 7, of which waited for: 10 -> 6; matrix products, arithmetic and copies ran while one was open for 0% -> 0% of each run, Pallas kernels for 16% -> 15%
where the time goes in v6:
time: 52.1 us; the launch traced here: 51.9 us
  Pallas kernels  20.4 us (39%)
  blocking collectives  12.1 us (23%)
  waiting for transfers between devices  10.6 us (20%)
  starting transfers between devices  5.91 us (11%)
  between operations  2.01 us (4%)
  other arithmetic  0.85 us (2%)
    all_to_all x1, blocking collectives, body(): lax.all_to_all(parts, ('far', 'gy'), split_axis=0, concat_axis=0, tiled=T...  12.1 us
    ppermute x7, waiting for transfers between devices, partner(): lax.ppermute(array, everyone, [(i, i ^ 1 << bit) for i in range(devices)])  10.6 us
    pallas_call x3, Pallas kernels, fetch(): pl.pallas_call(functools.partial(fetch_kernel, first, parts), out_shape=p...  7.94 us
    pallas_call x1, Pallas kernels, project(): pl.pallas_call(functools.partial(project_kernel, steps, group, colors, ch...  7.29 us
    ppermute x7, starting transfers between devices, partner(): lax.ppermute(array, everyone, [(i, i ^ 1 << bit) for i in range(devices)])  5.91 us
    pallas_call x1, Pallas kernels, output(): pl.pallas_call(functools.partial(output_kernel, steps, colors, patterns,...  3.12 us
    pallas_call x1, Pallas kernels, attend(): pl.pallas_call(functools.partial(attend_kernel, steps, width), out_shape=...  1.96 us
  transfers between devices with their start and end apart: 7, of which 6 were waited for; matrix products, arithmetic and copies ran while one was open for 0% of the time, Pallas kernels for 15%

profile of v6, /device:TPU:0, one launch (start us, length us, event | category | flops | bytes accessed | tf_op | source)
XLA Modules:
  0.0 51.9 jit_solution(6590380161444992826)
XLA Ops:
  0.6 0.5 collective-permute-start
  2.5 0.1 multiply_cosine_fusion
  2.6 0.1 pad_maximum_fusion
  2.7 0.0 collective-permute-done.other_ref
  2.7 0.0 copy-start
  2.7 0.0 copy-start.1
  2.7 7.3 %project.1 = (f32[8,80,128]{2,1,0:T(8,128)S(1)}, bf16[8,80,128]{2,1,0:T(8,128)(2,1)S(1)}) custom-call(s32[1]{0:T(128)} %bitcast.place_ref, bf16[16,2048]{1,0:T(8,128)(2,1)} %bitcast.14, bf16[16,2048]{1,0:T(8,128)(2,1)S(1)} %collective-permute-done.other_ref, bf16[16,128]{1,0:T(8,128)(2,1)} %bitcast.15, bf16[2048,4096]{1,0:T(8,128)(2,1)} %wq_ref.1, ...), custom_call_target="tpu_custom_call" | custom-call | flops 603979776 | bytes 18874368 | tf_op jit(solution)/shard_map/project/pallas_call | solution.py:124
  10.0 2.6 %collective-permute-start.1 = (bf16[8,80,128]{2,1,0:T(8,128)(2,1)S(1)}, bf16[8,80,128]{2,1,0:T(8,128)(2,1)S(1)}, u32[]{:S(2)}, u32[]{:S(2)}) collective-permute-start(bf16[8,80,128]{2,1,0:T(8,128)(2,1)S(1)} %get-tuple-element.12), channel_id=1, source_target_pairs={{0,2},{1,3},{2,0},{3,1},{4,6},{5,7},{6,4},{7,5},{8,10},{9,11},{10,... | collective-permute-start | bytes 491528 | tf_op jit(solution)/shard_map/ppermute | solution.py:365
  12.6 4.9 %collective-permute-done.1.came_ref = bf16[8,80,128]{2,1,0:T(8,128)(2,1)S(1)} collective-permute-done((bf16[8,80,128]{2,1,0:T(8,128)(2,1)S(1)}, bf16[8,80,128]{2,1,0:T(8,128)(2,1)S(1)}, u32[]{:S(2)}, u32[]{:S(2)}) %collective-permute-start.1) | collective-permute-done | bytes 163872 | tf_op jit(solution)/shard_map/ppermute | solution.py:365
  17.5 12.1 %all_to_all.5.parts_ref = bf16[8,80,128]{2,1,0:T(8,128)(2,1)S(1)} all-to-all(bf16[8,80,128]{2,1,0:T(8,128)(2,1)S(1)} %local.4), channel_id=1, replica_groups=mesh['rep'=2,'far'=4,'near'=2,'gy'=2] {'far','gy'}, dimensions={0} | all-to-all | bytes 327680 | tf_op jit(solution)/shard_map/all_to_all | solution.py:372
  29.6 0.0 copy-done
  29.6 0.0 copy-done.1
  29.6 2.0 %attend.1 = (bf16[64,128]{1,0:T(8,128)(2,1)S(1)}, bf16[64,128]{1,0:T(8,128)(2,1)S(1)}, bf16[2,512]{1,0:T(2,128)(2,1)}, bf16[2,512]{1,0:T(2,128)(2,1)}) custom-call(s32[1]{0:T(128)} %bitcast.place_ref, s32[1]{0:T(128)S(6)} %copy.13.length_ref, f32[4,128]{1,0:T(4,128)S(1)} %reshape.48.table_ref, bf16[384,512]{1,0:T(8,128)(2,1)S(1)} %bitcast.11, ...), custom_call_target="tpu_custom_call" | custom-call | tf_op jit(solution)/shard_map/attend/pallas_call | solution.py:255
  31.6 0.0 collective-permute-start.2
  31.6 1.2 %collective-permute-done.2.other_ref = bf16[64,128]{1,0:T(8,128)(2,1)S(1)} collective-permute-done((bf16[64,128]{1,0:T(8,128)(2,1)S(1)}, bf16[64,128]{1,0:T(8,128)(2,1)S(1)}, u32[]{:S(2)}, u32[]{:S(2)}) %collective-permute-start.2) | collective-permute-done | bytes 16416 | tf_op jit(solution)/shard_map/ppermute | solution.py:365
  32.8 0.2 collective-permute-start.3
  33.0 2.2 %fetch.3.rest_0_ = bf16[1024,2048]{1,0:T(8,128)(2,1)S(1)} custom-call(bf16[4096,2048]{1,0:T(8,128)(2,1)} %weight_ref.5, bf16[2,64,128]{2,1,0:T(8,128)(2,1)S(1)} %local.5.after_ref.first_ref), custom_call_target="tpu_custom_call" | custom-call | bytes 4194304 | tf_op jit(solution)/shard_map/fetch/pallas_call | solution.py:165
  35.2 2.4 %collective-permute-done.3.second_ref = bf16[2,64,128]{2,1,0:T(8,128)(2,1)S(1)} collective-permute-done((bf16[2,64,128]{2,1,0:T(8,128)(2,1)S(1)}, bf16[2,64,128]{2,1,0:T(8,128)(2,1)S(1)}, u32[]{:S(2)}, u32[]{:S(2)}) %collective-permute-start.3) | collective-permute-done | bytes 32800 | tf_op jit(solution)/shard_map/ppermute | solution.py:365
  37.6 1.0 %collective-permute-start.4 = (bf16[4,64,128]{2,1,0:T(8,128)(2,1)S(1)}, bf16[4,64,128]{2,1,0:T(8,128)(2,1)S(1)}, u32[]{:S(2)}, u32[]{:S(2)}) collective-permute-start(bf16[4,64,128]{2,1,0:T(8,128)(2,1)S(1)} %local.6.after_ref.first_ref), channel_id=1, source_target_pairs={{0,4},{1,5},{2,6},{3,7},{4,0},{5,1},{6,2},{7,3},{8,12},{9,13},{10,... | collective-permute-start | bytes 196616 | tf_op jit(solution)/shard_map/ppermute | solution.py:365
  38.6 2.9 %fetch.4.rest_0_.rest_1_ = bf16[1536,2048]{1,0:T(8,128)(2,1)S(1)} custom-call(bf16[4096,2048]{1,0:T(8,128)(2,1)} %weight_ref.5, bf16[4,64,128]{2,1,0:T(8,128)(2,1)S(1)} %local.6.after_ref.first_ref), custom_call_target="tpu_custom_call" | custom-call | bytes 6291456 | tf_op jit(solution)/shard_map/fetch/pallas_call | solution.py:165
  41.5 0.4 collective-permute-done.4.second_ref
  41.9 1.6 %collective-permute-start.5 = (bf16[8,64,128]{2,1,0:T(8,128)(2,1)S(1)}, bf16[8,64,128]{2,1,0:T(8,128)(2,1)S(1)}, u32[]{:S(2)}, u32[]{:S(2)}) collective-permute-start(bf16[8,64,128]{2,1,0:T(8,128)(2,1)S(1)} %local.7.after_ref.rest_3_), channel_id=1, source_target_pairs={{0,2},{1,3},{2,0},{3,1},{4,6},{5,7},{6,4},{7,5},{8,10},{9,11},{10,... | collective-permute-start | bytes 393224 | tf_op jit(solution)/shard_map/ppermute | solution.py:365
  43.4 2.9 %fetch.5.rest_2_ = bf16[1536,2048]{1,0:T(8,128)(2,1)S(1)} custom-call(bf16[4096,2048]{1,0:T(8,128)(2,1)} %weight_ref.5, bf16[8,64,128]{2,1,0:T(8,128)(2,1)S(1)} %local.7.after_ref.rest_3_), custom_call_target="tpu_custom_call" | custom-call | bytes 6291456 | tf_op jit(solution)/shard_map/fetch/pallas_call | solution.py:165
  46.3 0.6 %collective-permute-done.5.rest_4_ = bf16[8,64,128]{2,1,0:T(8,128)(2,1)S(1)} collective-permute-done((bf16[8,64,128]{2,1,0:T(8,128)(2,1)S(1)}, bf16[8,64,128]{2,1,0:T(8,128)(2,1)S(1)}, u32[]{:S(2)}, u32[]{:S(2)}) %collective-permute-start.5) | collective-permute-done | bytes 131104 | tf_op jit(solution)/shard_map/ppermute | solution.py:365
  46.9 3.1 %output.1 = (f32[16,2048]{1,0:T(8,128)S(1)}, bf16[16,2048]{1,0:T(8,128)(2,1)S(1)}) custom-call(s32[1]{0:T(128)} %bitcast.place_ref, bf16[1024,2048]{1,0:T(8,128)(2,1)S(1)} %fetch.3.rest_0_, bf16[1536,2048]{1,0:T(8,128)(2,1)S(1)} %fetch.4.rest_0_.rest_1_, bf16[1536,2048]{1,0:T(8,128)(2,1)S(1)} %fetch.5.rest_2_, ...), custom_call_target="tpu_custom_call" | custom-call | flops 536870912 | bytes 16777216 | tf_op jit(solution)/shard_map/output/pallas_call | solution.py:332
  50.0 0.0 collective-permute-start.6
  50.0 1.2 %collective-permute-done.6 = bf16[16,2048]{1,0:T(8,128)(2,1)S(1)} collective-permute-done((bf16[16,2048]{1,0:T(8,128)(2,1)S(1)}, bf16[16,2048]{1,0:T(8,128)(2,1)S(1)}, u32[]{:S(2)}, u32[]{:S(2)}) %collective-permute-start.6) | collective-permute-done | bytes 65568 | tf_op jit(solution)/shard_map/ppermute | solution.py:365
  51.3 0.6 %fusion = bf16[2,8,2048]{2,1,0:T(8,128)(2,1)} fusion(f32[16,2048]{1,0:T(8,128)S(1)} %get-tuple-element.15, bf16[16,2048]{1,0:T(8,128)(2,1)S(1)} %collective-permute-done.6), kind=kLoop, calls=%fused_computation.1 | loop fusion | flops 98304 | bytes 262144 | tf_op jit(solution)/shard_map/reshape | solution.py:397
  (7 shorter events, 0.1 us)
Async XLA Ops:
  0.6 2.1 %collective-permute-start = (bf16[16,2048]{1,0:T(8,128)(2,1)}, bf16[16,2048]{1,0:T(8,128)(2,1)S(1)}, u32[]{:S(2)}, u32[]{:S(2)}) collective-permute-start(bf16[16,2048]{1,0:T(8,128)(2,1)} %bitcast.13), channel_id=1, source_target_pairs={{0,1},{1,0},{2,3},{3,2},{4,5},{5,4},{6,7},{7,6},{8,9},{9,8},{10,11... | collective-permute-start | bytes 196616 | tf_op jit(solution)/shard_map/ppermute | solution.py:365
  2.7 26.9 %copy-start = (bf16[1,384,512]{2,1,0:T(8,128)(2,1)S(1)}, bf16[1,384,512]{2,1,0:T(8,128)(2,1)}, u32[]{:S(2)}) copy-start(bf16[1,384,512]{2,1,0:T(8,128)(2,1)} %param.16) | copy-start | bytes 1179652
  2.7 26.9 %copy-start.1 = (bf16[1,384,512]{2,1,0:T(8,128)(2,1)S(1)}, bf16[1,384,512]{2,1,0:T(8,128)(2,1)}, u32[]{:S(2)}) copy-start(bf16[1,384,512]{2,1,0:T(8,128)(2,1)} %param.17) | copy-start | bytes 1179652
  10.0 7.4 %collective-permute-start.1 = (bf16[8,80,128]{2,1,0:T(8,128)(2,1)S(1)}, bf16[8,80,128]{2,1,0:T(8,128)(2,1)S(1)}, u32[]{:S(2)}, u32[]{:S(2)}) collective-permute-start(bf16[8,80,128]{2,1,0:T(8,128)(2,1)S(1)} %get-tuple-element.12), channel_id=1, source_target_pairs={{0,2},{1,3},{2,0},{3,1},{4,6},{5,7},{6,4},{7,5},{8,10},{9,11},{10,... | collective-permute-start | bytes 491528 | tf_op jit(solution)/shard_map/ppermute | solution.py:365
  31.6 1.2 %collective-permute-start.2 = (bf16[64,128]{1,0:T(8,128)(2,1)S(1)}, bf16[64,128]{1,0:T(8,128)(2,1)S(1)}, u32[]{:S(2)}, u32[]{:S(2)}) collective-permute-start(bf16[64,128]{1,0:T(8,128)(2,1)S(1)} %get-tuple-element.14), channel_id=1, source_target_pairs={{0,1},{1,0},{2,3},{3,2},{4,5},{5,4},{6,7},{7,6},{8,9},{9,8},{10,11... | collective-permute-start | bytes 49160 | tf_op jit(solution)/shard_map/ppermute | solution.py:365
  32.8 4.8 %collective-permute-start.3 = (bf16[2,64,128]{2,1,0:T(8,128)(2,1)S(1)}, bf16[2,64,128]{2,1,0:T(8,128)(2,1)S(1)}, u32[]{:S(2)}, u32[]{:S(2)}) collective-permute-start(bf16[2,64,128]{2,1,0:T(8,128)(2,1)S(1)} %local.5.after_ref.first_ref), channel_id=1, source_target_pairs={{0,8},{1,9},{2,10},{3,11},{4,12},{5,13},{6,14},{7,15},{8,0},{9,1},... | collective-permute-start | bytes 98312 | tf_op jit(solution)/shard_map/ppermute | solution.py:365
  37.6 4.3 %collective-permute-start.4 = (bf16[4,64,128]{2,1,0:T(8,128)(2,1)S(1)}, bf16[4,64,128]{2,1,0:T(8,128)(2,1)S(1)}, u32[]{:S(2)}, u32[]{:S(2)}) collective-permute-start(bf16[4,64,128]{2,1,0:T(8,128)(2,1)S(1)} %local.6.after_ref.first_ref), channel_id=1, source_target_pairs={{0,4},{1,5},{2,6},{3,7},{4,0},{5,1},{6,2},{7,3},{8,12},{9,13},{10,... | collective-permute-start | bytes 196616 | tf_op jit(solution)/shard_map/ppermute | solution.py:365
  41.9 5.0 %collective-permute-start.5 = (bf16[8,64,128]{2,1,0:T(8,128)(2,1)S(1)}, bf16[8,64,128]{2,1,0:T(8,128)(2,1)S(1)}, u32[]{:S(2)}, u32[]{:S(2)}) collective-permute-start(bf16[8,64,128]{2,1,0:T(8,128)(2,1)S(1)} %local.7.after_ref.rest_3_), channel_id=1, source_target_pairs={{0,2},{1,3},{2,0},{3,1},{4,6},{5,7},{6,4},{7,5},{8,10},{9,11},{10,... | collective-permute-start | bytes 393224 | tf_op jit(solution)/shard_map/ppermute | solution.py:365
  50.0 1.3 %collective-permute-start.6 = (bf16[16,2048]{1,0:T(8,128)(2,1)S(1)}, bf16[16,2048]{1,0:T(8,128)(2,1)S(1)}, u32[]{:S(2)}, u32[]{:S(2)}) collective-permute-start(bf16[16,2048]{1,0:T(8,128)(2,1)S(1)} %get-tuple-element.16), channel_id=1, source_target_pairs={{0,1},{1,0},{2,3},{3,2},{4,5},{5,4},{6,7},{7,6},{8,9},{9,8},{10,11... | collective-permute-start | bytes 196616 | tf_op jit(solution)/shard_map/ppermute | solution.py:365

commit v7 on v6

--- a/solution.py
+++ b/solution.py
@@ -14,8 +14,7 @@
 MIB = 1024 * 1024
 
 
-def rope_frequencies(head_size):
-    index = jnp.arange(head_size // 2).astype(jnp.float32)
+def rope_frequencies(index, head_size):
     frequency = jnp.exp(-math.log(rope_theta) * 2.0 * index / head_size)
     wavelength = 2.0 * math.pi / frequency
     smooth = (8192.0 / wavelength - 1.0) / 3.0
@@ -24,14 +23,11 @@
     return jnp.where(wavelength < 2048.0, frequency, adjusted)
 
 
-def rope_table(position, steps):
-    frequency = rope_frequencies(HD)
-    places = position + jnp.arange(steps, dtype=jnp.int32)
-    angle = places.astype(jnp.float32)[:, None] * frequency
-    cosine, sine = jnp.cos(angle), jnp.sin(angle)
-    return jnp.concatenate(
-        [cosine, cosine, -sine, sine], axis=-1
-    ).reshape(2 * steps, HD)
+def slot_patterns(order):
+    count = len(order)
+    return [
+        sum(((j >> (count - 1 - i)) & 1) << bit for i, bit in enumerate(order))
+        for j in range(1 << count)]
 
 
 def in_hbm(array):
@@ -42,19 +38,20 @@
     return pltpu.with_memory_space_constraint(array, pltpu.VMEM)
 
 
-def project_kernel(steps, group, colors, chunk, place_ref, mine_ref, other_ref, gain_ref, wq_ref, wk_ref, wv_ref,
-                   table_ref, length_ref, *rest):
-    out_refs, (mine_buf, gain_buf, wq_buf, wk_buf, wv_buf, rows_buf, sems) = rest[:-7], rest[-7:]
+def project_kernel(steps, group, colors, order, chunk, place_ref, mine_ref, other_ref, gain_ref, early_ref, wk_ref, wv_ref,
+                   wq_ref, position_ref, length_ref, notes_ref, *rest):
+    part_refs, rest = rest[:-7], rest[-7:]
+    mine_buf, gain_buf, wq_buf, rows_buf, position_buf, length_buf, sems = rest
+    early = early_ref.shape[1]
     q_cols = wq_ref.shape[1]
-    kv_cols = wk_ref.shape[1]
-    chunks = q_cols // chunk
+    chunks = (q_cols - early) // chunk
     copies = [pltpu.make_async_copy(mine_ref, mine_buf, sems.at[chunks]),
               pltpu.make_async_copy(gain_ref, gain_buf, sems.at[chunks + 1]),
-              pltpu.make_async_copy(wk_ref, wk_buf, sems.at[chunks + 2]),
-              pltpu.make_async_copy(wv_ref, wv_buf, sems.at[chunks + 3])]
+              pltpu.make_async_copy(position_ref, position_buf, sems.at[chunks + 2]),
+              pltpu.make_async_copy(length_ref, length_buf, sems.at[chunks + 3])]
     for c in range(chunks):
         copies.append(pltpu.make_async_copy(
-            wq_ref.at[:, c * chunk:(c + 1) * chunk], wq_buf.at[c], sems.at[c]))
+            wq_ref.at[:, early + c * chunk:early + (c + 1) * chunk], wq_buf.at[c], sems.at[c]))
     for copy in copies:
         copy.start()
 
@@ -94,57 +91,121 @@
         for i in range(product.shape[1] // HD):
             spread(*place_of_head(i), product[:, i * HD:(i + 1) * HD])
 
+    multiply(wk_ref[...], lambda i: (i, group))
+    multiply(wv_ref[...], lambda i: (i, group + 1))
+    multiply(early_ref[...], lambda i: (i // group, i % group))
+
     copies[2].wait()
-    multiply(wk_buf[...], lambda i: (i, group))
     copies[3].wait()
-    multiply(wv_buf[...], lambda i: (i, group + 1))
+    lane = lax.broadcasted_iota(jnp.int32, (1, HD), 1)
+    frequency = rope_frequencies((lane % (HD // 2)).astype(jnp.float32), HD)
+    sign = jnp.where(lane < HD // 2, -1.0, 1.0)
+    for t in range(steps):
+        angle = (position_buf[...] + t).astype(jnp.float32) * frequency
+        notes_ref[2 * t:2 * t + 1, :] = jnp.cos(angle)
+        notes_ref[2 * t + 1:2 * t + 2, :] = jnp.sin(angle) * sign
+    notes_ref[2 * steps:2 * steps + 1, :] = jnp.broadcast_to(length_buf[...].astype(jnp.float32), (1, HD))
+
     for c in range(chunks):
         copies[4 + c].wait()
-        first = c * chunk // HD
+        first = (early + c * chunk) // HD
         multiply(wq_buf[c], lambda i: ((first + i) // group, (first + i) % group))
-    keep_ref, send_ref = out_refs
-    near = (device >> 1) % 2
-    for slot in range(keep_ref.shape[0]):
-        for ref, side in ((keep_ref, near), (send_ref, 1 - near)):
-            seq = (slot // 2) * 4 + side * 2 + slot % 2
-            start = pl.multiple_of(seq * stride, 8)
-            ref[slot] = rows_buf[pl.ds(start, stride), :].astype(ref.dtype)
-
-
-def project(place, mine, other, gain, wq, wk, wv, table, length, steps, group, colors):
+    per_part = part_refs[0].shape[0]
+    for slot, pattern in enumerate(slot_patterns(order)):
+        ref = part_refs[slot // per_part]
+        start = pl.multiple_of((device ^ pattern) * stride, 8)
+        ref[slot % per_part] = rows_buf[pl.ds(start, stride), :].astype(ref.dtype)
+
+
+def part_shapes(total, count, block):
+    shape = (total // count,) + block
+    return (jax.ShapeDtypeStruct(shape, jnp.float32),) + (jax.ShapeDtypeStruct(shape, jnp.bfloat16),) * (count - 1)
+
+
+def project(place, mine, other, gain, early, wk, wv, wq, position, length, steps, group, colors, order, count):
     half_rows, depth = mine.shape
     q_cols, kv_cols = wq.shape[1], wk.shape[1]
     seqs = 2 * half_rows // steps
     chunk = 512
+    chunks = (q_cols - early.shape[1]) // chunk
     vmem = pl.BlockSpec(memory_space=pltpu.VMEM)
     smem = pl.BlockSpec(memory_space=pltpu.SMEM)
     hbm = pl.BlockSpec(memory_space=pltpu.HBM)
-    block = (seqs // 2, colors * steps * (group + 4), HD)
-    out_shape = (jax.ShapeDtypeStruct(block, jnp.float32), jax.ShapeDtypeStruct(block, jnp.bfloat16))
-    return pl.pallas_call(
-        functools.partial(project_kernel, steps, group, colors, chunk),
+    any_space = pl.BlockSpec(memory_space=pl.ANY)
+    out_shape = (jax.ShapeDtypeStruct((2 * steps + 4, HD), jnp.float32),) + part_shapes(
+        seqs, count, (colors * steps * (group + 4), HD))
+    return pl.pallas_call(
+        functools.partial(project_kernel, steps, group, colors, order, chunk),
         out_shape=out_shape,
-        in_specs=[smem, hbm, vmem, hbm, hbm, hbm, hbm, pl.BlockSpec(memory_space=pl.ANY), smem],
+        in_specs=[smem, hbm, vmem, hbm, vmem, vmem, vmem, hbm, any_space, any_space],
         out_specs=(vmem,) * len(out_shape),
         scratch_shapes=[
             pltpu.VMEM(mine.shape, jnp.bfloat16),
             pltpu.VMEM(gain.shape, jnp.bfloat16),
-            pltpu.VMEM((q_cols // chunk, depth, chunk), jnp.bfloat16),
-            pltpu.VMEM((depth, kv_cols), jnp.bfloat16),
-            pltpu.VMEM((depth, kv_cols), jnp.bfloat16),
+            pltpu.VMEM((chunks, depth, chunk), jnp.bfloat16),
             pltpu.VMEM((seqs * colors * steps * (group + 4), HD), jnp.float32),
-            pltpu.SemaphoreType.DMA((q_cols // chunk + 4,)),
+            pltpu.VMEM((1, 1), jnp.int32),
+            pltpu.VMEM((1, 1), jnp.int32),
+            pltpu.SemaphoreType.DMA((chunks + 4,)),
         ],
         compiler_params=pltpu.CompilerParams(vmem_limit_bytes=28 * MIB),
         cost_estimate=pl.CostEstimate(
             flops=4 * half_rows * depth * (q_cols + 2 * kv_cols),
             bytes_accessed=2 * depth * (q_cols + 2 * kv_cols), transcendentals=0),
         name="project",
-    )(place, in_hbm(mine), other, in_hbm(gain), in_hbm(wq), in_hbm(wk), in_hbm(wv), table, length)
-
-
-def combine_kernel(keep_ref, came_ref, out_ref):
-    out_ref[...] = (keep_ref[...] + came_ref[...].astype(jnp.float32)).astype(jnp.bfloat16)
+    )(place, in_hbm(mine), other, in_hbm(gain), in_vmem(early), in_vmem(wk), in_vmem(wv), in_hbm(wq),
+      position, length)
+
+
+def fetch_first_kernel(wq_ref, wk_ref, wv_ref, early_ref, wk_out, wv_out, sems):
+    copies = [
+        pltpu.make_async_copy(wk_ref, wk_out, sems.at[0]),
+        pltpu.make_async_copy(wv_ref, wv_out, sems.at[1]),
+        pltpu.make_async_copy(wq_ref.at[:, :early_ref.shape[1]], early_ref, sems.at[2])]
+    for copy in copies:
+        copy.start()
+    for copy in copies:
+        copy.wait()
+
+
+def fetch_first(wq, wk, wv, early):
+    hbm = pl.BlockSpec(memory_space=pltpu.HBM)
+    vmem = pl.BlockSpec(memory_space=pltpu.VMEM)
+    depth = wq.shape[0]
+    return pl.pallas_call(
+        fetch_first_kernel,
+        out_shape=(
+            pltpu.VMEM((depth, early), wq.dtype), pltpu.VMEM(wk.shape, wk.dtype), pltpu.VMEM(wv.shape, wv.dtype)),
+        in_specs=[hbm] * 3,
+        out_specs=(vmem,) * 3,
+        scratch_shapes=[pltpu.SemaphoreType.DMA((3,))],
+        compiler_params=pltpu.CompilerParams(vmem_limit_bytes=16 * MIB),
+        cost_estimate=pl.CostEstimate(
+            flops=0, bytes_accessed=2 * depth * (early + 2 * wk.shape[1]), transcendentals=0),
+        name="fetch_first",
+    )(in_hbm(wq), in_hbm(wk), in_hbm(wv))
+
+
+def combine_kernel(arrived, parts, *refs):
+    total = refs[0][...]
+    for ref in refs[1:arrived + 1]:
+        total = total + ref[...].astype(jnp.float32)
+    count = total.shape[0] // parts
+    for i, ref in enumerate(refs[-parts:]):
+        ref[...] = total[i * count:(i + 1) * count].astype(ref.dtype)
+
+
+def combine(keep, came, held, parts):
+    vmem = pl.BlockSpec(memory_space=pltpu.VMEM)
+    out_shape = part_shapes(keep.shape[0], parts, keep.shape[1:])
+    return pl.pallas_call(
+        functools.partial(combine_kernel, len(came), parts),
+        out_shape=out_shape,
+        in_specs=[vmem] * (1 + len(came)) + [pl.BlockSpec(memory_space=pl.ANY)] * len(held),
+        out_specs=(vmem,) * parts,
+        compiler_params=pltpu.CompilerParams(vmem_limit_bytes=24 * MIB),
+        name="combine",
+    )(keep, *came, *[in_vmem(piece) for piece in held])
 
 
 def fetch_kernel(first, parts, weight_ref, after_ref, held_ref, sems):
@@ -175,20 +236,19 @@
     )(in_hbm(weight), after)
 
 
-def attend_kernel(steps, width, place_ref, length_ref, table_ref, keys_ref, values_ref, parts_ref,
+def attend_kernel(steps, width, place_ref, table_ref, keys_ref, values_ref, same_in_ref, cross_in_ref,
                   same_ref, cross_ref, new_keys_ref, new_values_ref):
     kv_heads = keys_ref.shape[1] // HD
     half_kv = kv_heads // 2
-    pitch = parts_ref.shape[1] // (half_kv * steps)
+    pitch = same_in_ref.shape[1] // (half_kv * steps)
     group = pitch - 4
-    halves = [
-        functools.reduce(jnp.add, [
-            parts_ref[i].astype(jnp.float32) for i in range(g, parts_ref.shape[0], 2)])
-        for g in range(2)]
     slots = keys_ref.shape[0]
     factor = 1.0 / math.sqrt(HD)
     low_side = place_ref[0] % 2 == 0
-    live = lax.broadcasted_iota(jnp.int32, (steps * group, slots), 1) < length_ref[0]
+    same, cross = same_in_ref[0], cross_in_ref[0].astype(jnp.float32)
+    halves = [jnp.where(low_side, same, cross), jnp.where(low_side, cross, same)]
+    live = lax.broadcasted_iota(jnp.int32, (steps * group, slots), 1) < (
+        table_ref[2 * steps:2 * steps + 1, :1].astype(jnp.int32))
     row_step = lax.broadcasted_iota(jnp.int32, (steps * group, 1), 0) // group
     fresh_keys = [[None] * kv_heads for _ in range(steps)]
     fresh_values = [[None] * kv_heads for _ in range(steps)]
@@ -246,7 +306,7 @@
         cross_ref[span, :] = jnp.where(low_side, upper, lower).astype(jnp.bfloat16)
 
 
-def attend(place, length, parts, table, keys, values, steps, width, half_heads):
+def attend(place, same, cross, table, keys, values, steps, width, half_heads):
     vmem = pl.BlockSpec(memory_space=pltpu.VMEM)
     smem = pl.BlockSpec(memory_space=pltpu.SMEM)
     kv_cols = keys.shape[1]
@@ -255,11 +315,11 @@
     return pl.pallas_call(
         functools.partial(attend_kernel, steps, width),
         out_shape=(half, half, fresh, fresh),
-        in_specs=[smem, smem] + [vmem] * 4,
+        in_specs=[smem] + [vmem] * 5,
         out_specs=(vmem,) * 4,
         compiler_params=pltpu.CompilerParams(vmem_limit_bytes=16 * MIB),
         name="attend",
-    )(place, length, table, keys, values, parts)
+    )(place, table, keys, values, same, cross)
 
 
 def pack_kernel(same_ref, other_ref, out_ref):
@@ -267,11 +327,11 @@
     out_ref[1] = other_ref[...]
 
 
-def join_kernel(first_ref, second_ref, *rest):
-    out_ref = rest[-1]
-    count = first_ref.shape[0]
-    out_ref[:count] = first_ref[...]
-    out_ref[count:] = second_ref[...]
+def join_kernel(arrived, *refs):
+    out_ref = refs[-1]
+    for i, ref in enumerate(refs[:arrived + 1]):
+        count = ref.shape[0]
+        out_ref[i * count:(i + 1) * count] = ref[...]
 
 
 def local_call(kernel, shape, arrays, held=()):
@@ -287,14 +347,15 @@
 
 
 def output_kernel(steps, colors, patterns, pieces, place_ref, *rest):
-    weight_refs, (held_ref, came_ref, mine_ref, other_ref, wide_buf, rows_buf) = rest[:pieces], rest[pieces:]
+    weight_refs, context_refs = rest[:pieces], rest[pieces:-4]
+    mine_ref, other_ref, wide_buf, rows_buf = rest[-4:]
     device = place_ref[0]
     devices = len(patterns)
     half_seqs = devices // 2
-    count, block, _ = held_ref.shape
+    count, block, _ = context_refs[0].shape
     group = block // (steps * colors)
     for j, pattern in enumerate(patterns):
-        rows = held_ref[j] if j < count else came_ref[j - count]
+        rows = context_refs[j // count][j % count]
         start = pl.multiple_of((device ^ pattern) * block, 8)
         wide_buf[pl.ds(start, block), :] = rows.astype(jnp.float32)
     for head in range(colors * group):
@@ -322,7 +383,7 @@
         other_ref[:, span] = jnp.where(low_side, upper, lower).astype(jnp.bfloat16)
 
 
-def output(place, held_context, came_context, patterns, held, steps, colors):
+def output(place, contexts, patterns, held, steps, colors):
     columns = held[0].shape[1]
     depth = sum(piece.shape[0] for piece in held)
     devices = len(patterns)
@@ -335,10 +396,10 @@
             jax.ShapeDtypeStruct((half, columns), jnp.float32),
             jax.ShapeDtypeStruct((half, columns), jnp.bfloat16),
         ),
-        in_specs=[smem] + [vmem] * (len(held) + 2),
+        in_specs=[smem] + [vmem] * (len(held) + len(contexts)),
         out_specs=(vmem, vmem),
         scratch_shapes=[
-            pltpu.VMEM((devices * held_context.shape[1], HD), jnp.float32),
+            pltpu.VMEM((devices * contexts[0].shape[1], HD), jnp.float32),
             pltpu.VMEM((devices * steps, depth), jnp.bfloat16),
         ],
         compiler_params=pltpu.CompilerParams(vmem_limit_bytes=26 * MIB),
@@ -346,52 +407,63 @@
             flops=2 * devices * steps * depth * columns,
             bytes_accessed=2 * depth * columns, transcendentals=0),
         name="output",
-    )(place, *[in_vmem(piece) for piece in held], held_context, came_context)
+    )(place, *[in_vmem(piece) for piece in held], *contexts)
 
 
 def body(hidden_in, norm_gain, query_weight, key_weight, value_weight, out_weight,
          cache_keys, cache_values, lengths, positions):
     steps, half_seqs, depth = hidden_in.shape
-    everyone = ("far", "near", "gy")
+    everyone = ("gx", "gy")
     devices = lax.axis_size(everyone)
     bits = devices.bit_length() - 1
     colors = key_weight.shape[1] // HD
     half_heads = query_weight.shape[1] // HD
     group = half_heads // colors
     place = lax.axis_index(everyone).astype(jnp.int32).reshape(1)
-    table = rope_table(positions[0], steps)
-
-    def partner(array, bit):
-        return lax.ppermute(array, everyone, [(i, i ^ (1 << bit)) for i in range(devices)])
+
+    def partner(array, pattern):
+        return lax.ppermute(array, everyone, [(i, i ^ pattern) for i in range(devices)])
+
+    near_first = [list(range(first, min(first + 2, bits))) for first in range(1, bits, 2)]
+    stages = near_first + [[0]]
+    order = [bit for stage in stages for bit in stage]
+    total = out_weight.shape[0]
+    cuts = [total * i // 4 for i in range(5)]
+    held = []
+
+    def fetch_next(after):
+        i = len(held)
+        if i == 4:
+            return []
+        held.append(fetch(out_weight, cuts[i], cuts[i + 1] - cuts[i], after))
+        return held[-1:]
 
     mine = hidden_in.reshape(steps * half_seqs, depth)
-    other = partner(mine, 0)
-    keep, send = project(place, mine, other, norm_gain.reshape(-1, HD), query_weight, key_weight,
-                         value_weight, table, lengths, steps, group, colors)
-    parts = local_call(combine_kernel, keep.shape, [keep, partner(send, 1)])
-    parts = lax.all_to_all(parts, ("far", "gy"), split_axis=0, concat_axis=0, tiled=True)
+    other = partner(mine, 1)
+    early, wk, wv = fetch_first(query_weight, key_weight, value_weight, 512)
+    notes, *parts = project(
+        place, mine, other, norm_gain.reshape(-1, HD), early, wk, wv, query_weight, positions[:, None], lengths[:, None],
+        steps, group, colors, order, 1 << len(stages[0]))
+    for i, stage in enumerate(stages[:-1]):
+        came = [partner(part, pattern) for part, pattern in zip(parts[1:], slot_patterns(stage)[1:])]
+        now = fetch_next(parts[1]) if i < 2 else []
+        parts = combine(parts[0], came, now, 1 << len(stages[i + 1]))
     same, cross, new_keys, new_values = attend(
-        place, lengths, parts, table, cache_keys[0], cache_values[0],
-        steps, depth * devices // 2, half_heads)
-
-    context = local_call(pack_kernel, (2,) + same.shape, [same, partner(cross, 0)])
+        place, parts[0], partner(parts[1], 1), notes, cache_keys[0], cache_values[0],
+        steps, depth * lax.axis_size("gx"), half_heads)
+
+    context = local_call(pack_kernel, (2,) + same.shape, [same, partner(cross, 1)])
     patterns = [0, 1]
-    order = list(range(bits - 1, 0, -1))
-    total = out_weight.shape[0]
-    cuts = [total * i // 8 for i in (0, 2, 5, 8)]
-    held = []
-    for i, bit in enumerate(order):
-        came = partner(context, bit)
-        patterns = patterns + [p ^ (1 << bit) for p in patterns]
-        now = []
-        if i < len(cuts) - 1:
-            now.append(fetch(out_weight, cuts[i], cuts[i + 1] - cuts[i], context))
-            held += now
-        if i < len(order) - 1:
-            shape = (2 * context.shape[0],) + context.shape[1:]
-            context = local_call(join_kernel, shape, [context, came], now)
-    mine, other = output(place, context, came, patterns, held, steps, colors)
-    other = partner(other, 0)
+    for i, stage in enumerate(near_first[::-1]):
+        moves = slot_patterns(stage)
+        came = [partner(context, move) for move in moves[1:]]
+        patterns = [p ^ move for move in moves for p in patterns]
+        now = fetch_next(context)
+        if i < len(near_first) - 1:
+            shape = (len(moves) * context.shape[0],) + context.shape[1:]
+            context = local_call(functools.partial(join_kernel, len(came)), shape, [context, *came], now)
+    mine, other = output(place, [context, *came], patterns, held, steps, colors)
+    other = partner(other, 1)
     result = (mine + other.astype(jnp.float32)).astype(jnp.bfloat16)
     return (
         result.reshape(steps, half_seqs, -1),
@@ -401,24 +473,21 @@
 
 
 def solution(mesh):
-    rep, gx, gy = mesh.devices.shape
-    split = jax.sharding.Mesh(mesh.devices.reshape(rep, gx // 2, 2, gy), ("rep", "far", "near", "gy"))
-    gx = ("far", "near")
     in_specs = (
-        P(None, ("rep", "gy"), gx),
-        P(gx),
-        P(gx, "gy"),
-        P(gx, "gy"),
-        P(gx, "gy"),
-        P("gy", gx),
-        P(("rep", *gx, "gy"), None, None),
-        P(("rep", *gx, "gy"), None, None),
-        P(("rep", *gx, "gy")),
-        P(("rep", *gx, "gy")),
+        P(None, ("rep", "gy"), "gx"),
+        P("gx"),
+        P("gx", "gy"),
+        P("gx", "gy"),
+        P("gx", "gy"),
+        P("gy", "gx"),
+        P(("rep", "gx", "gy"), None, None),
+        P(("rep", "gx", "gy"), None, None),
+        P(("rep", "gx", "gy")),
+        P(("rep", "gx", "gy")),
     )
     out_specs = (
-        P(None, ("rep", "gy"), gx),
-        P(None, ("rep", *gx, "gy"), None),
-        P(None, ("rep", *gx, "gy"), None),
+        P(None, ("rep", "gy"), "gx"),
+        P(None, ("rep", "gx", "gy"), None),
+        P(None, ("rep", "gx", "gy"), None),
     )
-    return jax.shard_map(body, mesh=split, in_specs=in_specs, out_specs=out_specs, check_vma=False)
+    return jax.shard_map(body, mesh=mesh, in_specs=in_specs, out_specs=out_specs, check_vma=False)

time: 52.1 us -> 46.8 us (0.90)
  blocking collectives: 12.1 us -> 0 us
  starting transfers between devices: 5.91 us -> 13.9 us
  waiting for transfers between devices: 10.6 us -> 7.75 us
  Pallas kernels: 20.4 us -> 22.2 us
    all_to_all x1 -> x0, blocking collectives: 12.1 us -> none  [body(): lax.all_to_all(parts, ('far', 'gy'), split_axis=0, concat_axis=0, tiled=T...]
    ppermute x7 -> x12, starting transfers between devices: 5.91 us -> 13.9 us  [partner(): lax.ppermute(array, everyone, [(i, i ^ pattern) for i in range(devices)])]
    ppermute x7 -> x12, waiting for transfers between devices: 10.6 us -> 7.75 us  [partner(): lax.ppermute(array, everyone, [(i, i ^ pattern) for i in range(devices)])]
    pallas_call x1 -> x4, Pallas kernels: 7.29 us -> 8.33 us  [the longest x1 6.02 us: project(): pl.pallas_call(functools.partial(project_kernel, steps, group, colors, or...]
    pallas_call x3 -> x4, Pallas kernels: 7.94 us -> 8.82 us  [fetch(): pl.pallas_call(functools.partial(fetch_kernel, first, parts), out_shape=p...]
  transfers between devices with their start and end apart: 7 -> 12, of which waited for: 6 -> 8; matrix products, arithmetic and copies ran while one was open for 0% -> 0% of each run, Pallas kernels for 15% -> 24%
where the time goes in v7:
time: 46.8 us; the launch traced here: 46.7 us
  Pallas kernels  22.2 us (47%)
  starting transfers between devices  13.9 us (30%)
  waiting for transfers between devices  7.75 us (17%)
  between operations  2.07 us (4%)
  other arithmetic  0.64 us (1%)
    ppermute x12, starting transfers between devices, partner(): lax.ppermute(array, everyone, [(i, i ^ pattern) for i in range(devices)])  13.9 us
    pallas_call x4, Pallas kernels, fetch(): pl.pallas_call(functools.partial(fetch_kernel, first, parts), out_shape=p...  8.82 us
    ppermute x12, waiting for transfers between devices, partner(): lax.ppermute(array, everyone, [(i, i ^ pattern) for i in range(devices)])  7.75 us
    pallas_call x1, Pallas kernels, project(): pl.pallas_call(functools.partial(project_kernel, steps, group, colors, or...  6.02 us
    pallas_call x1, Pallas kernels, output(): pl.pallas_call(functools.partial(output_kernel, steps, colors, patterns,...  3.12 us
    pallas_call x1, Pallas kernels, fetch_first(): pl.pallas_call(fetch_first_kernel, out_shape=(pltpu.VMEM((depth, early),...  2.26 us
    pallas_call x1, Pallas kernels, attend(): pl.pallas_call(functools.partial(attend_kernel, steps, width), out_shape=...  1.96 us
  transfers between devices with their start and end apart: 12, of which 8 were waited for; matrix products, arithmetic and copies ran while one was open for 0% of the time, Pallas kernels for 24%

profile of v7, /device:TPU:0, one launch (start us, length us, event | category | flops | bytes accessed | tf_op | source)
XLA Modules:
  0.0 46.7 jit_solution(15563210456654724518)
XLA Ops:
  0.6 0.5 %collective-permute-start = (bf16[16,2048]{1,0:T(8,128)(2,1)}, bf16[16,2048]{1,0:T(8,128)(2,1)S(1)}, u32[]{:S(2)}, u32[]{:S(2)}) collective-permute-start(bf16[16,2048]{1,0:T(8,128)(2,1)} %bitcast.15), channel_id=1, source_target_pairs={{0,1},{1,0},{2,3},{3,2},{4,5},{5,4},{6,7},{7,6},{8,9},{9,8},{10,11... | collective-permute-start | bytes 196616 | tf_op jit(solution)/shard_map/ppermute | solution.py:425
  2.4 2.3 %fetch_first.1 = (bf16[2048,512]{1,0:T(8,128)(2,1)S(1)}, bf16[2048,256]{1,0:T(8,128)(2,1)S(1)}, bf16[2048,256]{1,0:T(8,128)(2,1)S(1)}) custom-call(bf16[2048,4096]{1,0:T(8,128)(2,1)} %wq_ref.3, bf16[2048,256]{1,0:T(8,128)(2,1)} %wk_ref.1, bf16[2048,256]{1,0:T(8,128)(2,1)} %wv_ref.1), custom_call_target="tpu_custom_call" | custom-call | bytes 4194304 | tf_op jit(solution)/shard_map/fetch_first/pallas_call | solution.py:175
  4.7 0.0 collective-permute-done.other_ref
  4.7 6.0 %project.1 = (f32[8,128]{1,0:T(8,128)S(1)}, f32[4,80,128]{2,1,0:T(8,128)S(1)}, bf16[4,80,128]{2,1,0:T(8,128)(2,1)S(1)}, bf16[4,80,128]{2,1,0:T(8,128)(2,1)S(1)}, bf16[4,80,128]{2,1,0:T(8,128)(2,1)S(1)}) custom-call(s32[1]{0:T(128)} %bitcast.place_ref, bf16[16,2048]{1,0:T(8,128)(2,1)} %bitcast.16, bf16[16,2048]{1,0:T(8,128)(2,1)S(1)} %collective-permute-done.other_ref, ...), custom_call_target="tpu_custom_call" | custom-call | flops 603979776 | bytes 18874368 | tf_op jit(solution)/shard_map/project/pallas_call | solution.py:137
  10.8 2.6 %collective-permute-start.2 = (bf16[4,80,128]{2,1,0:T(8,128)(2,1)S(1)}, bf16[4,80,128]{2,1,0:T(8,128)(2,1)S(1)}, u32[]{:S(2)}, u32[]{:S(2)}) collective-permute-start(bf16[4,80,128]{2,1,0:T(8,128)(2,1)S(1)} %get-tuple-element.26), channel_id=1, source_target_pairs={{0,2},{1,3},{2,0},{3,1},{4,6},{5,7},{6,4},{7,5},{8,10},{9,11},{10,... | collective-permute-start | bytes 245768 | tf_op jit(solution)/shard_map/ppermute | solution.py:425
  13.3 1.5 %collective-permute-start.3 = (bf16[4,80,128]{2,1,0:T(8,128)(2,1)S(1)}, bf16[4,80,128]{2,1,0:T(8,128)(2,1)S(1)}, u32[]{:S(2)}, u32[]{:S(2)}) collective-permute-start(bf16[4,80,128]{2,1,0:T(8,128)(2,1)S(1)} %get-tuple-element.27), channel_id=1, source_target_pairs={{0,6},{1,7},{2,4},{3,5},{4,2},{5,3},{6,0},{7,1},{8,14},{9,15},{10,... | collective-permute-start | bytes 245768 | tf_op jit(solution)/shard_map/ppermute | solution.py:425
  14.9 0.0 collective-permute-start.1
  14.9 2.2 %fetch.4.refs_4_.rest_0_ = bf16[1024,2048]{1,0:T(8,128)(2,1)S(1)} custom-call(bf16[4096,2048]{1,0:T(8,128)(2,1)} %weight_ref.7, bf16[4,80,128]{2,1,0:T(8,128)(2,1)S(1)} %get-tuple-element.24.after_ref), custom_call_target="tpu_custom_call" | custom-call | bytes 4194304 | tf_op jit(solution)/shard_map/fetch/pallas_call | solution.py:226
  17.1 0.4 collective-permute-done.2.refs_2_
  17.5 1.8 %collective-permute-done.3.refs_3_ = bf16[4,80,128]{2,1,0:T(8,128)(2,1)S(1)} collective-permute-done((bf16[4,80,128]{2,1,0:T(8,128)(2,1)S(1)}, bf16[4,80,128]{2,1,0:T(8,128)(2,1)S(1)}, u32[]{:S(2)}, u32[]{:S(2)}) %collective-permute-start.3) | collective-permute-done | bytes 81952 | tf_op jit(solution)/shard_map/ppermute | solution.py:425
  19.3 0.2 collective-permute-done.1.refs_1_
  19.6 2.8 %collective-permute-start.4 = (bf16[2,80,128]{2,1,0:T(8,128)(2,1)S(1)}, bf16[2,80,128]{2,1,0:T(8,128)(2,1)S(1)}, u32[]{:S(2)}, u32[]{:S(2)}) collective-permute-start(bf16[2,80,128]{2,1,0:T(8,128)(2,1)S(1)} %get-tuple-element.28.after_ref), channel_id=1, source_target_pairs={{0,8},{1,9},{2,10},{3,11},{4,12},{5,13},{6,14},{7,15},{8,0},{9,1},... | collective-permute-start | bytes 122888 | tf_op jit(solution)/shard_map/ppermute | solution.py:425
  22.4 2.2 %fetch.5.refs_2_.rest_1_ = bf16[1024,2048]{1,0:T(8,128)(2,1)S(1)} custom-call(bf16[4096,2048]{1,0:T(8,128)(2,1)} %weight_ref.7, bf16[2,80,128]{2,1,0:T(8,128)(2,1)S(1)} %get-tuple-element.28.after_ref), custom_call_target="tpu_custom_call" | custom-call | bytes 4194304 | tf_op jit(solution)/shard_map/fetch/pallas_call | solution.py:226
  24.6 0.0 copy-start
  24.6 0.0 copy-start.1
  24.6 0.0 collective-permute-done.4.refs_1_
  24.6 0.1 collective-permute-start.5
  24.7 1.2 %collective-permute-done.5.cross_in_ref = bf16[1,80,128]{2,1,0:T(8,128)(2,1)S(1)} collective-permute-done((bf16[1,80,128]{2,1,0:T(8,128)(2,1)S(1)}, bf16[1,80,128]{2,1,0:T(8,128)(2,1)S(1)}, u32[]{:S(2)}, u32[]{:S(2)}) %collective-permute-start.5) | collective-permute-done | bytes 20512 | tf_op jit(solution)/shard_map/ppermute | solution.py:425
  25.9 0.0 copy-done
  25.9 0.0 copy-done.1
  25.9 2.0 %attend.1 = (bf16[64,128]{1,0:T(8,128)(2,1)S(1)}, bf16[64,128]{1,0:T(8,128)(2,1)S(1)}, bf16[2,512]{1,0:T(2,128)(2,1)}, bf16[2,512]{1,0:T(2,128)(2,1)}) custom-call(s32[1]{0:T(128)} %bitcast.place_ref, f32[8,128]{1,0:T(8,128)S(1)} %get-tuple-element.29.table_ref, bf16[384,512]{1,0:T(8,128)(2,1)S(1)} %bitcast.13, bf16[384,512]{1,0:T(8,128)(2,1)S(1)} %bitcast.14, ...), custom_call_target="tpu_custom_call" | custom-call | tf_op jit(solution)/shard_map/attend/pallas_call | solution.py:315
  27.9 0.2 collective-permute-start.6
  28.0 1.0 %collective-permute-done.6.other_ref = bf16[64,128]{1,0:T(8,128)(2,1)S(1)} collective-permute-done((bf16[64,128]{1,0:T(8,128)(2,1)S(1)}, bf16[64,128]{1,0:T(8,128)(2,1)S(1)}, u32[]{:S(2)}, u32[]{:S(2)}) %collective-permute-start.6) | collective-permute-done | bytes 16416 | tf_op jit(solution)/shard_map/ppermute | solution.py:425
  29.0 2.7 %collective-permute-start.7 = (bf16[2,64,128]{2,1,0:T(8,128)(2,1)S(1)}, bf16[2,64,128]{2,1,0:T(8,128)(2,1)S(1)}, u32[]{:S(2)}, u32[]{:S(2)}) collective-permute-start(bf16[2,64,128]{2,1,0:T(8,128)(2,1)S(1)} %local.2.after_ref.refs_0_), channel_id=1, source_target_pairs={{0,8},{1,9},{2,10},{3,11},{4,12},{5,13},{6,14},{7,15},{8,0},{9,1},... | collective-permute-start | bytes 98312 | tf_op jit(solution)/shard_map/ppermute | solution.py:425
  31.7 2.2 %fetch.6.refs_2_.rest_2_ = bf16[1024,2048]{1,0:T(8,128)(2,1)S(1)} custom-call(bf16[4096,2048]{1,0:T(8,128)(2,1)} %weight_ref.7, bf16[2,64,128]{2,1,0:T(8,128)(2,1)S(1)} %local.2.after_ref.refs_0_), custom_call_target="tpu_custom_call" | custom-call | bytes 4194304 | tf_op jit(solution)/shard_map/fetch/pallas_call | solution.py:226
  33.9 0.0 collective-permute-done.7.refs_1_
  34.0 2.8 %collective-permute-start.10 = (bf16[4,64,128]{2,1,0:T(8,128)(2,1)S(1)}, bf16[4,64,128]{2,1,0:T(8,128)(2,1)S(1)}, u32[]{:S(2)}, u32[]{:S(2)}) collective-permute-start(bf16[4,64,128]{2,1,0:T(8,128)(2,1)S(1)} %local.3.after_ref.rest_4_), channel_id=1, source_target_pairs={{0,6},{1,7},{2,4},{3,5},{4,2},{5,3},{6,0},{7,1},{8,14},{9,15},{10,... | collective-permute-start | bytes 196616 | tf_op jit(solution)/shard_map/ppermute | solution.py:425
  36.8 0.6 %collective-permute-start.9 = (bf16[4,64,128]{2,1,0:T(8,128)(2,1)S(1)}, bf16[4,64,128]{2,1,0:T(8,128)(2,1)S(1)}, u32[]{:S(2)}, u32[]{:S(2)}) collective-permute-start(bf16[4,64,128]{2,1,0:T(8,128)(2,1)S(1)} %local.3.after_ref.rest_4_), channel_id=1, source_target_pairs={{0,2},{1,3},{2,0},{3,1},{4,6},{5,7},{6,4},{7,5},{8,10},{9,11},{10,... | collective-permute-start | bytes 196616 | tf_op jit(solution)/shard_map/ppermute | solution.py:425
  37.4 0.2 collective-permute-start.8
  37.5 2.2 %fetch.7.rest_3_ = bf16[1024,2048]{1,0:T(8,128)(2,1)S(1)} custom-call(bf16[4096,2048]{1,0:T(8,128)(2,1)} %weight_ref.7, bf16[4,64,128]{2,1,0:T(8,128)(2,1)S(1)} %local.3.after_ref.rest_4_), custom_call_target="tpu_custom_call" | custom-call | bytes 4194304 | tf_op jit(solution)/shard_map/fetch/pallas_call | solution.py:226
  39.7 0.0 collective-permute-done.10.rest_7_
  39.7 1.3 %collective-permute-done.9.rest_6_ = bf16[4,64,128]{2,1,0:T(8,128)(2,1)S(1)} collective-permute-done((bf16[4,64,128]{2,1,0:T(8,128)(2,1)S(1)}, bf16[4,64,128]{2,1,0:T(8,128)(2,1)S(1)}, u32[]{:S(2)}, u32[]{:S(2)}) %collective-permute-start.9) | collective-permute-done | bytes 65568 | tf_op jit(solution)/shard_map/ppermute | solution.py:425
  41.0 0.6 %collective-permute-done.8.rest_5_ = bf16[4,64,128]{2,1,0:T(8,128)(2,1)S(1)} collective-permute-done((bf16[4,64,128]{2,1,0:T(8,128)(2,1)S(1)}, bf16[4,64,128]{2,1,0:T(8,128)(2,1)S(1)}, u32[]{:S(2)}, u32[]{:S(2)}) %collective-permute-start.8) | collective-permute-done | bytes 65568 | tf_op jit(solution)/shard_map/ppermute | solution.py:425
  41.6 3.1 %output.1 = (f32[16,2048]{1,0:T(8,128)S(1)}, bf16[16,2048]{1,0:T(8,128)(2,1)S(1)}) custom-call(s32[1]{0:T(128)} %bitcast.place_ref, bf16[1024,2048]{1,0:T(8,128)(2,1)S(1)} %fetch.4.refs_4_.rest_0_, bf16[1024,2048]{1,0:T(8,128)(2,1)S(1)} %fetch.5.refs_2_.rest_1_, bf16[1024,2048]{1,0:T(8,128)(2,1)S(1)} %fetch.6.refs_2_.rest_2_, ...), custom_call_target="tpu_custom_call" | custom-call | flops 536870912 | bytes 16777216 | tf_op jit(solution)/shard_map/output/pallas_call | solution.py:393
  44.7 0.0 collective-permute-start.11
  44.8 1.2 %collective-permute-done.11 = bf16[16,2048]{1,0:T(8,128)(2,1)S(1)} collective-permute-done((bf16[16,2048]{1,0:T(8,128)(2,1)S(1)}, bf16[16,2048]{1,0:T(8,128)(2,1)S(1)}, u32[]{:S(2)}, u32[]{:S(2)}) %collective-permute-start.11) | collective-permute-done | bytes 65568 | tf_op jit(solution)/shard_map/ppermute | solution.py:425
  46.0 0.6 %fusion = bf16[2,8,2048]{2,1,0:T(8,128)(2,1)} fusion(f32[16,2048]{1,0:T(8,128)S(1)} %get-tuple-element.35, bf16[16,2048]{1,0:T(8,128)(2,1)S(1)} %collective-permute-done.11), kind=kLoop, calls=%fused_computation.1 | loop fusion | flops 98304 | bytes 262144 | tf_op jit(solution)/shard_map/reshape | solution.py:469
  (4 shorter events, 0.1 us)
Async XLA Ops:
  0.6 4.1 %collective-permute-start = (bf16[16,2048]{1,0:T(8,128)(2,1)}, bf16[16,2048]{1,0:T(8,128)(2,1)S(1)}, u32[]{:S(2)}, u32[]{:S(2)}) collective-permute-start(bf16[16,2048]{1,0:T(8,128)(2,1)} %bitcast.15), channel_id=1, source_target_pairs={{0,1},{1,0},{2,3},{3,2},{4,5},{5,4},{6,7},{7,6},{8,9},{9,8},{10,11... | collective-permute-start | bytes 196616 | tf_op jit(solution)/shard_map/ppermute | solution.py:425
  10.8 6.7 %collective-permute-start.2 = (bf16[4,80,128]{2,1,0:T(8,128)(2,1)S(1)}, bf16[4,80,128]{2,1,0:T(8,128)(2,1)S(1)}, u32[]{:S(2)}, u32[]{:S(2)}) collective-permute-start(bf16[4,80,128]{2,1,0:T(8,128)(2,1)S(1)} %get-tuple-element.26), channel_id=1, source_target_pairs={{0,2},{1,3},{2,0},{3,1},{4,6},{5,7},{6,4},{7,5},{8,10},{9,11},{10,... | collective-permute-start | bytes 245768 | tf_op jit(solution)/shard_map/ppermute | solution.py:425
  13.3 6.0 %collective-permute-start.3 = (bf16[4,80,128]{2,1,0:T(8,128)(2,1)S(1)}, bf16[4,80,128]{2,1,0:T(8,128)(2,1)S(1)}, u32[]{:S(2)}, u32[]{:S(2)}) collective-permute-start(bf16[4,80,128]{2,1,0:T(8,128)(2,1)S(1)} %get-tuple-element.27), channel_id=1, source_target_pairs={{0,6},{1,7},{2,4},{3,5},{4,2},{5,3},{6,0},{7,1},{8,14},{9,15},{10,... | collective-permute-start | bytes 245768 | tf_op jit(solution)/shard_map/ppermute | solution.py:425
  14.9 4.7 %collective-permute-start.1 = (bf16[4,80,128]{2,1,0:T(8,128)(2,1)S(1)}, bf16[4,80,128]{2,1,0:T(8,128)(2,1)S(1)}, u32[]{:S(2)}, u32[]{:S(2)}) collective-permute-start(bf16[4,80,128]{2,1,0:T(8,128)(2,1)S(1)} %get-tuple-element.24.after_ref), channel_id=1, source_target_pairs={{0,4},{1,5},{2,6},{3,7},{4,0},{5,1},{6,2},{7,3},{8,12},{9,13},{10,... | collective-permute-start | bytes 245768 | tf_op jit(solution)/shard_map/ppermute | solution.py:425
  19.6 5.0 %collective-permute-start.4 = (bf16[2,80,128]{2,1,0:T(8,128)(2,1)S(1)}, bf16[2,80,128]{2,1,0:T(8,128)(2,1)S(1)}, u32[]{:S(2)}, u32[]{:S(2)}) collective-permute-start(bf16[2,80,128]{2,1,0:T(8,128)(2,1)S(1)} %get-tuple-element.28.after_ref), channel_id=1, source_target_pairs={{0,8},{1,9},{2,10},{3,11},{4,12},{5,13},{6,14},{7,15},{8,0},{9,1},... | collective-permute-start | bytes 122888 | tf_op jit(solution)/shard_map/ppermute | solution.py:425
  24.6 1.3 %copy-start = (bf16[1,384,512]{2,1,0:T(8,128)(2,1)S(1)}, bf16[1,384,512]{2,1,0:T(8,128)(2,1)}, u32[]{:S(2)}) copy-start(bf16[1,384,512]{2,1,0:T(8,128)(2,1)} %param.16) | copy-start | bytes 1179652
  24.6 1.3 %copy-start.1 = (bf16[1,384,512]{2,1,0:T(8,128)(2,1)S(1)}, bf16[1,384,512]{2,1,0:T(8,128)(2,1)}, u32[]{:S(2)}) copy-start(bf16[1,384,512]{2,1,0:T(8,128)(2,1)} %param.17) | copy-start | bytes 1179652
  24.6 1.3 %collective-permute-start.5 = (bf16[1,80,128]{2,1,0:T(8,128)(2,1)S(1)}, bf16[1,80,128]{2,1,0:T(8,128)(2,1)S(1)}, u32[]{:S(2)}, u32[]{:S(2)}) collective-permute-start(bf16[1,80,128]{2,1,0:T(8,128)(2,1)S(1)} %get-tuple-element.32), channel_id=1, source_target_pairs={{0,1},{1,0},{2,3},{3,2},{4,5},{5,4},{6,7},{7,6},{8,9},{9,8},{10,11... | collective-permute-start | bytes 61448 | tf_op jit(solution)/shard_map/ppermute | solution.py:425
  27.9 1.2 %collective-permute-start.6 = (bf16[64,128]{1,0:T(8,128)(2,1)S(1)}, bf16[64,128]{1,0:T(8,128)(2,1)S(1)}, u32[]{:S(2)}, u32[]{:S(2)}) collective-permute-start(bf16[64,128]{1,0:T(8,128)(2,1)S(1)} %get-tuple-element.34), channel_id=1, source_target_pairs={{0,1},{1,0},{2,3},{3,2},{4,5},{5,4},{6,7},{7,6},{8,9},{9,8},{10,11... | collective-permute-start | bytes 49160 | tf_op jit(solution)/shard_map/ppermute | solution.py:425
  29.0 4.9 %collective-permute-start.7 = (bf16[2,64,128]{2,1,0:T(8,128)(2,1)S(1)}, bf16[2,64,128]{2,1,0:T(8,128)(2,1)S(1)}, u32[]{:S(2)}, u32[]{:S(2)}) collective-permute-start(bf16[2,64,128]{2,1,0:T(8,128)(2,1)S(1)} %local.2.after_ref.refs_0_), channel_id=1, source_target_pairs={{0,8},{1,9},{2,10},{3,11},{4,12},{5,13},{6,14},{7,15},{8,0},{9,1},... | collective-permute-start | bytes 98312 | tf_op jit(solution)/shard_map/ppermute | solution.py:425
  34.0 5.8 %collective-permute-start.10 = (bf16[4,64,128]{2,1,0:T(8,128)(2,1)S(1)}, bf16[4,64,128]{2,1,0:T(8,128)(2,1)S(1)}, u32[]{:S(2)}, u32[]{:S(2)}) collective-permute-start(bf16[4,64,128]{2,1,0:T(8,128)(2,1)S(1)} %local.3.after_ref.rest_4_), channel_id=1, source_target_pairs={{0,6},{1,7},{2,4},{3,5},{4,2},{5,3},{6,0},{7,1},{8,14},{9,15},{10,... | collective-permute-start | bytes 196616 | tf_op jit(solution)/shard_map/ppermute | solution.py:425
  36.8 4.3 %collective-permute-start.9 = (bf16[4,64,128]{2,1,0:T(8,128)(2,1)S(1)}, bf16[4,64,128]{2,1,0:T(8,128)(2,1)S(1)}, u32[]{:S(2)}, u32[]{:S(2)}) collective-permute-start(bf16[4,64,128]{2,1,0:T(8,128)(2,1)S(1)} %local.3.after_ref.rest_4_), channel_id=1, source_target_pairs={{0,2},{1,3},{2,0},{3,1},{4,6},{5,7},{6,4},{7,5},{8,10},{9,11},{10,... | collective-permute-start | bytes 196616 | tf_op jit(solution)/shard_map/ppermute | solution.py:425
  37.4 4.3 %collective-permute-start.8 = (bf16[4,64,128]{2,1,0:T(8,128)(2,1)S(1)}, bf16[4,64,128]{2,1,0:T(8,128)(2,1)S(1)}, u32[]{:S(2)}, u32[]{:S(2)}) collective-permute-start(bf16[4,64,128]{2,1,0:T(8,128)(2,1)S(1)} %local.3.after_ref.rest_4_), channel_id=1, source_target_pairs={{0,4},{1,5},{2,6},{3,7},{4,0},{5,1},{6,2},{7,3},{8,12},{9,13},{10,... | collective-permute-start | bytes 196616 | tf_op jit(solution)/shard_map/ppermute | solution.py:425
  44.7 1.3 %collective-permute-start.11 = (bf16[16,2048]{1,0:T(8,128)(2,1)S(1)}, bf16[16,2048]{1,0:T(8,128)(2,1)S(1)}, u32[]{:S(2)}, u32[]{:S(2)}) collective-permute-start(bf16[16,2048]{1,0:T(8,128)(2,1)S(1)} %get-tuple-element.36), channel_id=1, source_target_pairs={{0,1},{1,0},{2,3},{3,2},{4,5},{5,4},{6,7},{7,6},{8,9},{9,8},{10,11... | collective-permute-start | bytes 196616 | tf_op jit(solution)/shard_map/ppermute | solution.py:425

commit v8 on v7

--- a/solution.py
+++ b/solution.py
@@ -39,16 +39,14 @@
 
 
 def project_kernel(steps, group, colors, order, chunk, place_ref, mine_ref, other_ref, gain_ref, early_ref, wk_ref, wv_ref,
-                   wq_ref, position_ref, length_ref, notes_ref, *rest):
-    part_refs, rest = rest[:-7], rest[-7:]
-    mine_buf, gain_buf, wq_buf, rows_buf, position_buf, length_buf, sems = rest
+                   wq_ref, *rest):
+    part_refs, rest = rest[:-5], rest[-5:]
+    mine_buf, gain_buf, wq_buf, rows_buf, sems = rest
     early = early_ref.shape[1]
     q_cols = wq_ref.shape[1]
     chunks = (q_cols - early) // chunk
     copies = [pltpu.make_async_copy(mine_ref, mine_buf, sems.at[chunks]),
-              pltpu.make_async_copy(gain_ref, gain_buf, sems.at[chunks + 1]),
-              pltpu.make_async_copy(position_ref, position_buf, sems.at[chunks + 2]),
-              pltpu.make_async_copy(length_ref, length_buf, sems.at[chunks + 3])]
+              pltpu.make_async_copy(gain_ref, gain_buf, sems.at[chunks + 1])]
     for c in range(chunks):
         copies.append(pltpu.make_async_copy(
             wq_ref.at[:, early + c * chunk:early + (c + 1) * chunk], wq_buf.at[c], sems.at[c]))
@@ -95,19 +93,8 @@
     multiply(wv_ref[...], lambda i: (i, group + 1))
     multiply(early_ref[...], lambda i: (i // group, i % group))
 
-    copies[2].wait()
-    copies[3].wait()
-    lane = lax.broadcasted_iota(jnp.int32, (1, HD), 1)
-    frequency = rope_frequencies((lane % (HD // 2)).astype(jnp.float32), HD)
-    sign = jnp.where(lane < HD // 2, -1.0, 1.0)
-    for t in range(steps):
-        angle = (position_buf[...] + t).astype(jnp.float32) * frequency
-        notes_ref[2 * t:2 * t + 1, :] = jnp.cos(angle)
-        notes_ref[2 * t + 1:2 * t + 2, :] = jnp.sin(angle) * sign
-    notes_ref[2 * steps:2 * steps + 1, :] = jnp.broadcast_to(length_buf[...].astype(jnp.float32), (1, HD))
-
     for c in range(chunks):
-        copies[4 + c].wait()
+        copies[2 + c].wait()
         first = (early + c * chunk) // HD
         multiply(wq_buf[c], lambda i: ((first + i) // group, (first + i) % group))
     per_part = part_refs[0].shape[0]
@@ -122,7 +109,7 @@
     return (jax.ShapeDtypeStruct(shape, jnp.float32),) + (jax.ShapeDtypeStruct(shape, jnp.bfloat16),) * (count - 1)
 
 
-def project(place, mine, other, gain, early, wk, wv, wq, position, length, steps, group, colors, order, count):
+def project(place, mine, other, gain, early, wk, wv, wq, steps, group, colors, order, count):
     half_rows, depth = mine.shape
     q_cols, kv_cols = wq.shape[1], wk.shape[1]
     seqs = 2 * half_rows // steps
@@ -131,30 +118,26 @@
     vmem = pl.BlockSpec(memory_space=pltpu.VMEM)
     smem = pl.BlockSpec(memory_space=pltpu.SMEM)
     hbm = pl.BlockSpec(memory_space=pltpu.HBM)
-    any_space = pl.BlockSpec(memory_space=pl.ANY)
-    out_shape = (jax.ShapeDtypeStruct((2 * steps + 4, HD), jnp.float32),) + part_shapes(
+    out_shape = part_shapes(
         seqs, count, (colors * steps * (group + 4), HD))
     return pl.pallas_call(
         functools.partial(project_kernel, steps, group, colors, order, chunk),
         out_shape=out_shape,
-        in_specs=[smem, hbm, vmem, hbm, vmem, vmem, vmem, hbm, any_space, any_space],
+        in_specs=[smem, hbm, vmem, hbm, vmem, vmem, vmem, hbm],
         out_specs=(vmem,) * len(out_shape),
         scratch_shapes=[
             pltpu.VMEM(mine.shape, jnp.bfloat16),
             pltpu.VMEM(gain.shape, jnp.bfloat16),
             pltpu.VMEM((chunks, depth, chunk), jnp.bfloat16),
             pltpu.VMEM((seqs * colors * steps * (group + 4), HD), jnp.float32),
-            pltpu.VMEM((1, 1), jnp.int32),
-            pltpu.VMEM((1, 1), jnp.int32),
-            pltpu.SemaphoreType.DMA((chunks + 4,)),
+            pltpu.SemaphoreType.DMA((chunks + 2,)),
         ],
         compiler_params=pltpu.CompilerParams(vmem_limit_bytes=28 * MIB),
         cost_estimate=pl.CostEstimate(
             flops=4 * half_rows * depth * (q_cols + 2 * kv_cols),
             bytes_accessed=2 * depth * (q_cols + 2 * kv_cols), transcendentals=0),
         name="project",
-    )(place, in_hbm(mine), other, in_hbm(gain), in_vmem(early), in_vmem(wk), in_vmem(wv), in_hbm(wq),
-      position, length)
+    )(place, in_hbm(mine), other, in_hbm(gain), in_vmem(early), in_vmem(wk), in_vmem(wv), in_hbm(wq))
 
 
 def fetch_first_kernel(wq_ref, wk_ref, wv_ref, early_ref, wk_out, wv_out, sems):
@@ -186,6 +169,30 @@
     )(in_hbm(wq), in_hbm(wk), in_hbm(wv))
 
 
+def notes_kernel(steps, position_ref, length_ref, after_ref, notes_ref):
+    lane = lax.broadcasted_iota(jnp.int32, (1, HD), 1)
+    frequency = rope_frequencies((lane % (HD // 2)).astype(jnp.float32), HD)
+    sign = jnp.where(lane < HD // 2, -1.0, 1.0)
+    for t in range(steps):
+        angle = (position_ref[0] + t).astype(jnp.float32) * frequency
+        notes_ref[2 * t:2 * t + 1, :] = jnp.cos(angle)
+        notes_ref[2 * t + 1:2 * t + 2, :] = jnp.sin(angle) * sign
+    length = length_ref[0].astype(jnp.float32)
+    notes_ref[2 * steps:, :] = jnp.full((notes_ref.shape[0] - 2 * steps, HD), length)
+
+
+def take_notes(position, length, after, steps):
+    smem = pl.BlockSpec(memory_space=pltpu.SMEM)
+    return pl.pallas_call(
+        functools.partial(notes_kernel, steps),
+        out_shape=jax.ShapeDtypeStruct((2 * steps + 4, HD), jnp.float32),
+        in_specs=[smem, smem, pl.BlockSpec(memory_space=pl.ANY)],
+        out_specs=pl.BlockSpec(memory_space=pltpu.VMEM),
+        compiler_params=pltpu.CompilerParams(vmem_limit_bytes=4 * MIB),
+        name="notes",
+    )(position, length, after)
+
+
 def combine_kernel(arrived, parts, *refs):
     total = refs[0][...]
     for ref in refs[1:arrived + 1]:
@@ -208,7 +215,8 @@
     )(keep, *came, *[in_vmem(piece) for piece in held])
 
 
-def fetch_kernel(first, parts, weight_ref, after_ref, held_ref, sems):
+def fetch_kernel(first, parts, weight_ref, *rest):
+    held_ref, sems = rest[-2:]
     rows = held_ref.shape[0] // parts
     copies = [
         pltpu.make_async_copy(
@@ -226,14 +234,14 @@
     return pl.pallas_call(
         functools.partial(fetch_kernel, first, parts),
         out_shape=pltpu.VMEM((rows, weight.shape[1]), weight.dtype),
-        in_specs=[pl.BlockSpec(memory_space=pltpu.HBM), pl.BlockSpec(memory_space=pl.ANY)],
+        in_specs=[pl.BlockSpec(memory_space=pltpu.HBM)] + [pl.BlockSpec(memory_space=pl.ANY)] * len(after),
         out_specs=pl.BlockSpec(memory_space=pltpu.VMEM),
         scratch_shapes=[pltpu.SemaphoreType.DMA((parts,))],
         compiler_params=pltpu.CompilerParams(vmem_limit_bytes=16 * MIB),
         cost_estimate=pl.CostEstimate(
             flops=0, bytes_accessed=2 * rows * weight.shape[1], transcendentals=0),
         name="fetch",
-    )(in_hbm(weight), after)
+    )(in_hbm(weight), *after)
 
 
 def attend_kernel(steps, width, place_ref, table_ref, keys_ref, values_ref, same_in_ref, cross_in_ref,
@@ -428,12 +436,12 @@
     stages = near_first + [[0]]
     order = [bit for stage in stages for bit in stage]
     total = out_weight.shape[0]
-    cuts = [total * i // 4 for i in range(5)]
+    cuts = [total * i // 8 for i in (0, 3, 8)]
     held = []
 
-    def fetch_next(after):
+    def fetch_next(window, after):
         i = len(held)
-        if i == 4:
+        if window not in (0, 3):
             return []
         held.append(fetch(out_weight, cuts[i], cuts[i + 1] - cuts[i], after))
         return held[-1:]
@@ -441,12 +449,13 @@
     mine = hidden_in.reshape(steps * half_seqs, depth)
     other = partner(mine, 1)
     early, wk, wv = fetch_first(query_weight, key_weight, value_weight, 512)
-    notes, *parts = project(
-        place, mine, other, norm_gain.reshape(-1, HD), early, wk, wv, query_weight, positions[:, None], lengths[:, None],
+    parts = project(
+        place, mine, other, norm_gain.reshape(-1, HD), early, wk, wv, query_weight,
         steps, group, colors, order, 1 << len(stages[0]))
+    notes = take_notes(positions, lengths, parts[1], steps)
     for i, stage in enumerate(stages[:-1]):
         came = [partner(part, pattern) for part, pattern in zip(parts[1:], slot_patterns(stage)[1:])]
-        now = fetch_next(parts[1]) if i < 2 else []
+        now = fetch_next(i, [parts[1], notes])
         parts = combine(parts[0], came, now, 1 << len(stages[i + 1]))
     same, cross, new_keys, new_values = attend(
         place, parts[0], partner(parts[1], 1), notes, cache_keys[0], cache_values[0],
@@ -458,7 +467,7 @@
         moves = slot_patterns(stage)
         came = [partner(context, move) for move in moves[1:]]
         patterns = [p ^ move for move in moves for p in patterns]
-        now = fetch_next(context)
+        now = fetch_next(len(near_first) + i, [context])
         if i < len(near_first) - 1:
             shape = (len(moves) * context.shape[0],) + context.shape[1:]
             context = local_call(functools.partial(join_kernel, len(came)), shape, [context, *came], now)

time: 46.8 us -> 45.6 us (0.974)
  Pallas kernels: 22.2 us -> 20.5 us
  waiting for transfers between devices: 7.75 us -> 8.46 us
    pallas_call x4 -> x2, Pallas kernels: 8.82 us -> 7.03 us  [fetch(): pl.pallas_call(functools.partial(fetch_kernel, first, parts), out_shape=p...]
    ppermute x12, waiting for transfers between devices: 7.75 us -> 8.46 us  [partner(): lax.ppermute(array, everyone, [(i, i ^ pattern) for i in range(devices)])]
  transfers between devices with their start and end apart: 12 -> 12, of which waited for: 8 -> 6; matrix products, arithmetic and copies ran while one was open for 0% -> 0% of each run, Pallas kernels for 24% -> 21%
where the time goes in v8:
time: 45.6 us; the launch traced here: 45.5 us
  Pallas kernels  20.5 us (45%)
  starting transfers between devices  13.8 us (30%)
  waiting for transfers between devices  8.46 us (19%)
  between operations  2.05 us (4%)
  other arithmetic  0.64 us (1%)
    ppermute x12, starting transfers between devices, partner(): lax.ppermute(array, everyone, [(i, i ^ pattern) for i in range(devices)])  13.8 us
    ppermute x12, waiting for transfers between devices, partner(): lax.ppermute(array, everyone, [(i, i ^ pattern) for i in range(devices)])  8.46 us
    pallas_call x2, Pallas kernels, fetch(): pl.pallas_call(functools.partial(fetch_kernel, first, parts), out_shape=p...  7.03 us
    pallas_call x1, Pallas kernels, project(): pl.pallas_call(functools.partial(project_kernel, steps, group, colors, or...  6 us
    pallas_call x1, Pallas kernels, output(): pl.pallas_call(functools.partial(output_kernel, steps, colors, patterns,...  3.14 us
    pallas_call x1, Pallas kernels, fetch_first(): pl.pallas_call(fetch_first_kernel, out_shape=(pltpu.VMEM((depth, early),...  2.26 us
    pallas_call x1, Pallas kernels, attend(): pl.pallas_call(functools.partial(attend_kernel, steps, width), out_shape=...  1.97 us
  transfers between devices with their start and end apart: 12, of which 6 were waited for; matrix products, arithmetic and copies ran while one was open for 0% of the time, Pallas kernels for 21%

profile of v8, /device:TPU:0, one launch (start us, length us, event | category | flops | bytes accessed | tf_op | source)
XLA Modules:
  0.0 45.5 jit_solution(5509800386304562534)
XLA Ops:
  0.6 0.5 %collective-permute-start = (bf16[16,2048]{1,0:T(8,128)(2,1)}, bf16[16,2048]{1,0:T(8,128)(2,1)S(1)}, u32[]{:S(2)}, u32[]{:S(2)}) collective-permute-start(bf16[16,2048]{1,0:T(8,128)(2,1)} %bitcast.11), channel_id=1, source_target_pairs={{0,1},{1,0},{2,3},{3,2},{4,5},{5,4},{6,7},{7,6},{8,9},{9,8},{10,11... | collective-permute-start | bytes 196616 | tf_op jit(solution)/shard_map/ppermute | solution.py:433
  1.1 2.3 %fetch_first.1 = (bf16[2048,512]{1,0:T(8,128)(2,1)S(1)}, bf16[2048,256]{1,0:T(8,128)(2,1)S(1)}, bf16[2048,256]{1,0:T(8,128)(2,1)S(1)}) custom-call(bf16[2048,4096]{1,0:T(8,128)(2,1)} %wq_ref.3, bf16[2048,256]{1,0:T(8,128)(2,1)} %wk_ref.1, bf16[2048,256]{1,0:T(8,128)(2,1)} %wv_ref.1), custom_call_target="tpu_custom_call" | custom-call | bytes 4194304 | tf_op jit(solution)/shard_map/fetch_first/pallas_call | solution.py:158
  3.4 0.0 collective-permute-done.other_ref
  3.4 6.0 %project.1 = (f32[4,80,128]{2,1,0:T(8,128)S(1)}, bf16[4,80,128]{2,1,0:T(8,128)(2,1)S(1)}, bf16[4,80,128]{2,1,0:T(8,128)(2,1)S(1)}, bf16[4,80,128]{2,1,0:T(8,128)(2,1)S(1)}) custom-call(s32[1]{0:T(128)} %bitcast.place_ref, bf16[16,2048]{1,0:T(8,128)(2,1)} %bitcast.12, bf16[16,2048]{1,0:T(8,128)(2,1)S(1)} %collective-permute-done.other_ref, ...), custom_call_target="tpu_custom_call" | custom-call | flops 603979776 | bytes 18874368 | tf_op jit(solution)/shard_map/project/pallas_call | solution.py:123
  9.4 2.6 %collective-permute-start.2 = (bf16[4,80,128]{2,1,0:T(8,128)(2,1)S(1)}, bf16[4,80,128]{2,1,0:T(8,128)(2,1)S(1)}, u32[]{:S(2)}, u32[]{:S(2)}) collective-permute-start(bf16[4,80,128]{2,1,0:T(8,128)(2,1)S(1)} %get-tuple-element.25), channel_id=1, source_target_pairs={{0,2},{1,3},{2,0},{3,1},{4,6},{5,7},{6,4},{7,5},{8,10},{9,11},{10,... | collective-permute-start | bytes 245768 | tf_op jit(solution)/shard_map/ppermute | solution.py:433
  12.0 1.5 %collective-permute-start.3 = (bf16[4,80,128]{2,1,0:T(8,128)(2,1)S(1)}, bf16[4,80,128]{2,1,0:T(8,128)(2,1)S(1)}, u32[]{:S(2)}, u32[]{:S(2)}) collective-permute-start(bf16[4,80,128]{2,1,0:T(8,128)(2,1)S(1)} %get-tuple-element.26), channel_id=1, source_target_pairs={{0,6},{1,7},{2,4},{3,5},{4,2},{5,3},{6,0},{7,1},{8,14},{9,15},{10,... | collective-permute-start | bytes 245768 | tf_op jit(solution)/shard_map/ppermute | solution.py:433
  13.6 0.0 collective-permute-start.1
  14.9 0.1 notes.1.rest_1_.table_ref
  15.0 0.0 copy-start
  15.0 0.0 copy-start.1
  15.0 2.9 %fetch.2.refs_4_.rest_0_ = bf16[1536,2048]{1,0:T(8,128)(2,1)S(1)} custom-call(bf16[4096,2048]{1,0:T(8,128)(2,1)} %weight_ref.3, bf16[4,80,128]{2,1,0:T(8,128)(2,1)S(1)} %get-tuple-element.23.after_ref.rest_0_, f32[8,128]{1,0:T(8,128)S(1)} %notes.1.rest_1_.table_ref), custom_call_target="tpu_custom_call" | custom-call | bytes 6291456 | tf_op jit(solution)/shard_map/fetch/pallas_call | solution.py:234
  17.9 0.0 collective-permute-done.2.refs_2_
  17.9 0.0 collective-permute-done.3.refs_3_
  18.0 0.2 collective-permute-done.1.refs_1_
  18.2 2.9 %collective-permute-start.4 = (bf16[2,80,128]{2,1,0:T(8,128)(2,1)S(1)}, bf16[2,80,128]{2,1,0:T(8,128)(2,1)S(1)}, u32[]{:S(2)}, u32[]{:S(2)}) collective-permute-start(bf16[2,80,128]{2,1,0:T(8,128)(2,1)S(1)} %get-tuple-element.28), channel_id=1, source_target_pairs={{0,8},{1,9},{2,10},{3,11},{4,12},{5,13},{6,14},{7,15},{8,0},{9,1},... | collective-permute-start | bytes 122888 | tf_op jit(solution)/shard_map/ppermute | solution.py:433
  21.1 2.4 %collective-permute-done.4.refs_1_ = bf16[2,80,128]{2,1,0:T(8,128)(2,1)S(1)} collective-permute-done((bf16[2,80,128]{2,1,0:T(8,128)(2,1)S(1)}, bf16[2,80,128]{2,1,0:T(8,128)(2,1)S(1)}, u32[]{:S(2)}, u32[]{:S(2)}) %collective-permute-start.4) | collective-permute-done | bytes 40992 | tf_op jit(solution)/shard_map/ppermute | solution.py:433
  23.5 0.1 collective-permute-start.5
  23.6 1.2 %collective-permute-done.5.cross_in_ref = bf16[1,80,128]{2,1,0:T(8,128)(2,1)S(1)} collective-permute-done((bf16[1,80,128]{2,1,0:T(8,128)(2,1)S(1)}, bf16[1,80,128]{2,1,0:T(8,128)(2,1)S(1)}, u32[]{:S(2)}, u32[]{:S(2)}) %collective-permute-start.5) | collective-permute-done | bytes 20512 | tf_op jit(solution)/shard_map/ppermute | solution.py:433
  24.8 0.0 copy-done
  24.8 0.0 copy-done.1
  24.8 2.0 %attend.1 = (bf16[64,128]{1,0:T(8,128)(2,1)S(1)}, bf16[64,128]{1,0:T(8,128)(2,1)S(1)}, bf16[2,512]{1,0:T(2,128)(2,1)}, bf16[2,512]{1,0:T(2,128)(2,1)}) custom-call(s32[1]{0:T(128)} %bitcast.place_ref, f32[8,128]{1,0:T(8,128)S(1)} %notes.1.rest_1_.table_ref, bf16[384,512]{1,0:T(8,128)(2,1)S(1)} %bitcast.9, bf16[384,512]{1,0:T(8,128)(2,1)S(1)} %bitcast.10, ...), custom_call_target="tpu_custom_call" | custom-call | tf_op jit(solution)/shard_map/attend/pallas_call | solution.py:323
  26.8 0.2 collective-permute-start.6
  26.9 1.0 %collective-permute-done.6.other_ref = bf16[64,128]{1,0:T(8,128)(2,1)S(1)} collective-permute-done((bf16[64,128]{1,0:T(8,128)(2,1)S(1)}, bf16[64,128]{1,0:T(8,128)(2,1)S(1)}, u32[]{:S(2)}, u32[]{:S(2)}) %collective-permute-start.6) | collective-permute-done | bytes 16416 | tf_op jit(solution)/shard_map/ppermute | solution.py:433
  28.0 2.5 %collective-permute-start.7 = (bf16[2,64,128]{2,1,0:T(8,128)(2,1)S(1)}, bf16[2,64,128]{2,1,0:T(8,128)(2,1)S(1)}, u32[]{:S(2)}, u32[]{:S(2)}) collective-permute-start(bf16[2,64,128]{2,1,0:T(8,128)(2,1)S(1)} %local.2.refs_0_), channel_id=1, source_target_pairs={{0,8},{1,9},{2,10},{3,11},{4,12},{5,13},{6,14},{7,15},{8,0},{9,1},... | collective-permute-start | bytes 98312 | tf_op jit(solution)/shard_map/ppermute | solution.py:433
  30.5 2.3 %collective-permute-done.7.refs_1_ = bf16[2,64,128]{2,1,0:T(8,128)(2,1)S(1)} collective-permute-done((bf16[2,64,128]{2,1,0:T(8,128)(2,1)S(1)}, bf16[2,64,128]{2,1,0:T(8,128)(2,1)S(1)}, u32[]{:S(2)}, u32[]{:S(2)}) %collective-permute-start.7) | collective-permute-done | bytes 32800 | tf_op jit(solution)/shard_map/ppermute | solution.py:433
  32.8 2.4 %collective-permute-start.10 = (bf16[4,64,128]{2,1,0:T(8,128)(2,1)S(1)}, bf16[4,64,128]{2,1,0:T(8,128)(2,1)S(1)}, u32[]{:S(2)}, u32[]{:S(2)}) collective-permute-start(bf16[4,64,128]{2,1,0:T(8,128)(2,1)S(1)} %local.3.rest_0_.rest_2_), channel_id=1, source_target_pairs={{0,6},{1,7},{2,4},{3,5},{4,2},{5,3},{6,0},{7,1},{8,14},{9,15},{10,... | collective-permute-start | bytes 196616 | tf_op jit(solution)/shard_map/ppermute | solution.py:433
  35.2 0.5 %collective-permute-start.9 = (bf16[4,64,128]{2,1,0:T(8,128)(2,1)S(1)}, bf16[4,64,128]{2,1,0:T(8,128)(2,1)S(1)}, u32[]{:S(2)}, u32[]{:S(2)}) collective-permute-start(bf16[4,64,128]{2,1,0:T(8,128)(2,1)S(1)} %local.3.rest_0_.rest_2_), channel_id=1, source_target_pairs={{0,2},{1,3},{2,0},{3,1},{4,6},{5,7},{6,4},{7,5},{8,10},{9,11},{10,... | collective-permute-start | bytes 196616 | tf_op jit(solution)/shard_map/ppermute | solution.py:433
  35.7 0.6 %collective-permute-start.8 = (bf16[4,64,128]{2,1,0:T(8,128)(2,1)S(1)}, bf16[4,64,128]{2,1,0:T(8,128)(2,1)S(1)}, u32[]{:S(2)}, u32[]{:S(2)}) collective-permute-start(bf16[4,64,128]{2,1,0:T(8,128)(2,1)S(1)} %local.3.rest_0_.rest_2_), channel_id=1, source_target_pairs={{0,4},{1,5},{2,6},{3,7},{4,0},{5,1},{6,2},{7,3},{8,12},{9,13},{10,... | collective-permute-start | bytes 196616 | tf_op jit(solution)/shard_map/ppermute | solution.py:433
  36.3 4.1 %fetch.3.rest_1_ = bf16[2560,2048]{1,0:T(8,128)(2,1)S(1)} custom-call(bf16[4096,2048]{1,0:T(8,128)(2,1)} %weight_ref.3, bf16[4,64,128]{2,1,0:T(8,128)(2,1)S(1)} %local.3.rest_0_.rest_2_), custom_call_target="tpu_custom_call" | custom-call | bytes 10485760 | tf_op jit(solution)/shard_map/fetch/pallas_call | solution.py:234
  40.4 0.0 collective-permute-done.10.rest_5_
  40.4 0.0 collective-permute-done.9.rest_4_
  40.4 0.0 collective-permute-done.8.rest_3_
  40.4 3.1 %output.1 = (f32[16,2048]{1,0:T(8,128)S(1)}, bf16[16,2048]{1,0:T(8,128)(2,1)S(1)}) custom-call(s32[1]{0:T(128)} %bitcast.place_ref, bf16[1536,2048]{1,0:T(8,128)(2,1)S(1)} %fetch.2.refs_4_.rest_0_, bf16[2560,2048]{1,0:T(8,128)(2,1)S(1)} %fetch.3.rest_1_, bf16[4,64,128]{2,1,0:T(8,128)(2,1)S(1)} %local.3.rest_0_.rest_2_, ...), custom_call_target="tpu_custom_call" | custom-call | flops 536870912 | bytes 16777216 | tf_op jit(solution)/shard_map/output/pallas_call | solution.py:401
  43.5 0.0 collective-permute-start.11
  43.6 1.2 %collective-permute-done.11 = bf16[16,2048]{1,0:T(8,128)(2,1)S(1)} collective-permute-done((bf16[16,2048]{1,0:T(8,128)(2,1)S(1)}, bf16[16,2048]{1,0:T(8,128)(2,1)S(1)}, u32[]{:S(2)}, u32[]{:S(2)}) %collective-permute-start.11) | collective-permute-done | bytes 65568 | tf_op jit(solution)/shard_map/ppermute | solution.py:433
  44.8 0.6 %fusion = bf16[2,8,2048]{2,1,0:T(8,128)(2,1)} fusion(f32[16,2048]{1,0:T(8,128)S(1)} %get-tuple-element.33, bf16[16,2048]{1,0:T(8,128)(2,1)S(1)} %collective-permute-done.11), kind=kLoop, calls=%fused_computation.1 | loop fusion | flops 98304 | bytes 262144 | tf_op jit(solution)/shard_map/reshape | solution.py:478
  (4 shorter events, 0.1 us)
Async XLA Ops:
  0.6 2.8 %collective-permute-start = (bf16[16,2048]{1,0:T(8,128)(2,1)}, bf16[16,2048]{1,0:T(8,128)(2,1)S(1)}, u32[]{:S(2)}, u32[]{:S(2)}) collective-permute-start(bf16[16,2048]{1,0:T(8,128)(2,1)} %bitcast.11), channel_id=1, source_target_pairs={{0,1},{1,0},{2,3},{3,2},{4,5},{5,4},{6,7},{7,6},{8,9},{9,8},{10,11... | collective-permute-start | bytes 196616 | tf_op jit(solution)/shard_map/ppermute | solution.py:433
  9.4 8.5 %collective-permute-start.2 = (bf16[4,80,128]{2,1,0:T(8,128)(2,1)S(1)}, bf16[4,80,128]{2,1,0:T(8,128)(2,1)S(1)}, u32[]{:S(2)}, u32[]{:S(2)}) collective-permute-start(bf16[4,80,128]{2,1,0:T(8,128)(2,1)S(1)} %get-tuple-element.25), channel_id=1, source_target_pairs={{0,2},{1,3},{2,0},{3,1},{4,6},{5,7},{6,4},{7,5},{8,10},{9,11},{10,... | collective-permute-start | bytes 245768 | tf_op jit(solution)/shard_map/ppermute | solution.py:433
  12.0 6.0 %collective-permute-start.3 = (bf16[4,80,128]{2,1,0:T(8,128)(2,1)S(1)}, bf16[4,80,128]{2,1,0:T(8,128)(2,1)S(1)}, u32[]{:S(2)}, u32[]{:S(2)}) collective-permute-start(bf16[4,80,128]{2,1,0:T(8,128)(2,1)S(1)} %get-tuple-element.26), channel_id=1, source_target_pairs={{0,6},{1,7},{2,4},{3,5},{4,2},{5,3},{6,0},{7,1},{8,14},{9,15},{10,... | collective-permute-start | bytes 245768 | tf_op jit(solution)/shard_map/ppermute | solution.py:433
  13.6 4.6 %collective-permute-start.1 = (bf16[4,80,128]{2,1,0:T(8,128)(2,1)S(1)}, bf16[4,80,128]{2,1,0:T(8,128)(2,1)S(1)}, u32[]{:S(2)}, u32[]{:S(2)}) collective-permute-start(bf16[4,80,128]{2,1,0:T(8,128)(2,1)S(1)} %get-tuple-element.23.after_ref.rest_0_), channel_id=1, source_target_pairs={{0,4},{1,5},{2,6},{3,7},{4,0},{5,1},{6,2},{7,3},{8,12},{9,13},{10,... | collective-permute-start | bytes 245768 | tf_op jit(solution)/shard_map/ppermute | solution.py:433
  15.0 9.8 %copy-start = (bf16[1,384,512]{2,1,0:T(8,128)(2,1)S(1)}, bf16[1,384,512]{2,1,0:T(8,128)(2,1)}, u32[]{:S(2)}) copy-start(bf16[1,384,512]{2,1,0:T(8,128)(2,1)} %param.16) | copy-start | bytes 1179652
  15.0 9.8 %copy-start.1 = (bf16[1,384,512]{2,1,0:T(8,128)(2,1)S(1)}, bf16[1,384,512]{2,1,0:T(8,128)(2,1)}, u32[]{:S(2)}) copy-start(bf16[1,384,512]{2,1,0:T(8,128)(2,1)} %param.17) | copy-start | bytes 1179652
  18.2 5.3 %collective-permute-start.4 = (bf16[2,80,128]{2,1,0:T(8,128)(2,1)S(1)}, bf16[2,80,128]{2,1,0:T(8,128)(2,1)S(1)}, u32[]{:S(2)}, u32[]{:S(2)}) collective-permute-start(bf16[2,80,128]{2,1,0:T(8,128)(2,1)S(1)} %get-tuple-element.28), channel_id=1, source_target_pairs={{0,8},{1,9},{2,10},{3,11},{4,12},{5,13},{6,14},{7,15},{8,0},{9,1},... | collective-permute-start | bytes 122888 | tf_op jit(solution)/shard_map/ppermute | solution.py:433
  23.5 1.3 %collective-permute-start.5 = (bf16[1,80,128]{2,1,0:T(8,128)(2,1)S(1)}, bf16[1,80,128]{2,1,0:T(8,128)(2,1)S(1)}, u32[]{:S(2)}, u32[]{:S(2)}) collective-permute-start(bf16[1,80,128]{2,1,0:T(8,128)(2,1)S(1)} %get-tuple-element.30), channel_id=1, source_target_pairs={{0,1},{1,0},{2,3},{3,2},{4,5},{5,4},{6,7},{7,6},{8,9},{9,8},{10,11... | collective-permute-start | bytes 61448 | tf_op jit(solution)/shard_map/ppermute | solution.py:433
  26.8 1.2 %collective-permute-start.6 = (bf16[64,128]{1,0:T(8,128)(2,1)S(1)}, bf16[64,128]{1,0:T(8,128)(2,1)S(1)}, u32[]{:S(2)}, u32[]{:S(2)}) collective-permute-start(bf16[64,128]{1,0:T(8,128)(2,1)S(1)} %get-tuple-element.32), channel_id=1, source_target_pairs={{0,1},{1,0},{2,3},{3,2},{4,5},{5,4},{6,7},{7,6},{8,9},{9,8},{10,11... | collective-permute-start | bytes 49160 | tf_op jit(solution)/shard_map/ppermute | solution.py:433
  28.0 4.8 %collective-permute-start.7 = (bf16[2,64,128]{2,1,0:T(8,128)(2,1)S(1)}, bf16[2,64,128]{2,1,0:T(8,128)(2,1)S(1)}, u32[]{:S(2)}, u32[]{:S(2)}) collective-permute-start(bf16[2,64,128]{2,1,0:T(8,128)(2,1)S(1)} %local.2.refs_0_), channel_id=1, source_target_pairs={{0,8},{1,9},{2,10},{3,11},{4,12},{5,13},{6,14},{7,15},{8,0},{9,1},... | collective-permute-start | bytes 98312 | tf_op jit(solution)/shard_map/ppermute | solution.py:433
  32.8 7.6 %collective-permute-start.10 = (bf16[4,64,128]{2,1,0:T(8,128)(2,1)S(1)}, bf16[4,64,128]{2,1,0:T(8,128)(2,1)S(1)}, u32[]{:S(2)}, u32[]{:S(2)}) collective-permute-start(bf16[4,64,128]{2,1,0:T(8,128)(2,1)S(1)} %local.3.rest_0_.rest_2_), channel_id=1, source_target_pairs={{0,6},{1,7},{2,4},{3,5},{4,2},{5,3},{6,0},{7,1},{8,14},{9,15},{10,... | collective-permute-start | bytes 196616 | tf_op jit(solution)/shard_map/ppermute | solution.py:433
  35.2 5.2 %collective-permute-start.9 = (bf16[4,64,128]{2,1,0:T(8,128)(2,1)S(1)}, bf16[4,64,128]{2,1,0:T(8,128)(2,1)S(1)}, u32[]{:S(2)}, u32[]{:S(2)}) collective-permute-start(bf16[4,64,128]{2,1,0:T(8,128)(2,1)S(1)} %local.3.rest_0_.rest_2_), channel_id=1, source_target_pairs={{0,2},{1,3},{2,0},{3,1},{4,6},{5,7},{6,4},{7,5},{8,10},{9,11},{10,... | collective-permute-start | bytes 196616 | tf_op jit(solution)/shard_map/ppermute | solution.py:433
  35.7 4.7 %collective-permute-start.8 = (bf16[4,64,128]{2,1,0:T(8,128)(2,1)S(1)}, bf16[4,64,128]{2,1,0:T(8,128)(2,1)S(1)}, u32[]{:S(2)}, u32[]{:S(2)}) collective-permute-start(bf16[4,64,128]{2,1,0:T(8,128)(2,1)S(1)} %local.3.rest_0_.rest_2_), channel_id=1, source_target_pairs={{0,4},{1,5},{2,6},{3,7},{4,0},{5,1},{6,2},{7,3},{8,12},{9,13},{10,... | collective-permute-start | bytes 196616 | tf_op jit(solution)/shard_map/ppermute | solution.py:433
  43.5 1.3 %collective-permute-start.11 = (bf16[16,2048]{1,0:T(8,128)(2,1)S(1)}, bf16[16,2048]{1,0:T(8,128)(2,1)S(1)}, u32[]{:S(2)}, u32[]{:S(2)}) collective-permute-start(bf16[16,2048]{1,0:T(8,128)(2,1)S(1)} %get-tuple-element.34), channel_id=1, source_target_pairs={{0,1},{1,0},{2,3},{3,2},{4,5},{5,4},{6,7},{7,6},{8,9},{9,8},{10,11... | collective-permute-start | bytes 196616 | tf_op jit(solution)/shard_map/ppermute | solution.py:433

commit v9 on v8

--- a/solution.py
+++ b/solution.py
@@ -244,16 +244,18 @@
     )(in_hbm(weight), *after)
 
 
-def attend_kernel(steps, width, place_ref, table_ref, keys_ref, values_ref, same_in_ref, cross_in_ref,
-                  same_ref, cross_ref, new_keys_ref, new_values_ref):
+def attend_kernel(steps, width, unused, place_ref, table_ref, keys_ref, values_ref, *rest):
+    rest = rest[unused:]
+    part_refs, (same_ref, cross_ref, new_keys_ref, new_values_ref) = rest[:-4], rest[-4:]
     kv_heads = keys_ref.shape[1] // HD
     half_kv = kv_heads // 2
-    pitch = same_in_ref.shape[1] // (half_kv * steps)
+    pitch = part_refs[0].shape[1] // (half_kv * steps)
     group = pitch - 4
     slots = keys_ref.shape[0]
     factor = 1.0 / math.sqrt(HD)
     low_side = place_ref[0] % 2 == 0
-    same, cross = same_in_ref[0], cross_in_ref[0].astype(jnp.float32)
+    same, cross = [
+        functools.reduce(jnp.add, [ref[0].astype(jnp.float32) for ref in part_refs[i::2]]) for i in range(2)]
     halves = [jnp.where(low_side, same, cross), jnp.where(low_side, cross, same)]
     live = lax.broadcasted_iota(jnp.int32, (steps * group, slots), 1) < (
         table_ref[2 * steps:2 * steps + 1, :1].astype(jnp.int32))
@@ -310,29 +312,24 @@
     for k in range(half_kv):
         lower, upper = contexts[k], contexts[half_kv + k]
         span = slice(k * steps * group, (k + 1) * steps * group)
-        same_ref[span, :] = jnp.where(low_side, lower, upper).astype(jnp.bfloat16)
-        cross_ref[span, :] = jnp.where(low_side, upper, lower).astype(jnp.bfloat16)
-
-
-def attend(place, same, cross, table, keys, values, steps, width, half_heads):
+        same_ref[0, span, :] = jnp.where(low_side, lower, upper).astype(jnp.bfloat16)
+        cross_ref[0, span, :] = jnp.where(low_side, upper, lower).astype(jnp.bfloat16)
+
+
+def attend(place, parts, table, keys, values, held, steps, width, half_heads):
     vmem = pl.BlockSpec(memory_space=pltpu.VMEM)
     smem = pl.BlockSpec(memory_space=pltpu.SMEM)
     kv_cols = keys.shape[1]
-    half = jax.ShapeDtypeStruct((steps * half_heads, HD), jnp.bfloat16)
+    half = jax.ShapeDtypeStruct((1, steps * half_heads, HD), jnp.bfloat16)
     fresh = jax.ShapeDtypeStruct((steps, kv_cols), jnp.bfloat16)
     return pl.pallas_call(
-        functools.partial(attend_kernel, steps, width),
+        functools.partial(attend_kernel, steps, width, len(held)),
         out_shape=(half, half, fresh, fresh),
-        in_specs=[smem] + [vmem] * 5,
+        in_specs=[smem] + [vmem] * 3 + [pl.BlockSpec(memory_space=pl.ANY)] * len(held) + [vmem] * len(parts),
         out_specs=(vmem,) * 4,
         compiler_params=pltpu.CompilerParams(vmem_limit_bytes=16 * MIB),
         name="attend",
-    )(place, table, keys, values, same, cross)
-
-
-def pack_kernel(same_ref, other_ref, out_ref):
-    out_ref[0] = same_ref[...]
-    out_ref[1] = other_ref[...]
+    )(place, table, keys, values, *[in_vmem(piece) for piece in held], *parts)
 
 
 def join_kernel(arrived, *refs):
@@ -432,16 +429,16 @@
     def partner(array, pattern):
         return lax.ppermute(array, everyone, [(i, i ^ pattern) for i in range(devices)])
 
-    near_first = [list(range(first, min(first + 2, bits))) for first in range(1, bits, 2)]
-    stages = near_first + [[0]]
+    stages = [list(range(first, min(first + 2, bits))) for first in range(1, bits, 2)]
+    stages[-1] = stages[-1] + [0]
     order = [bit for stage in stages for bit in stage]
     total = out_weight.shape[0]
-    cuts = [total * i // 8 for i in (0, 3, 8)]
+    cuts = [total * i // 8 for i in (0, 3, 4, 5, 8)]
     held = []
 
     def fetch_next(window, after):
         i = len(held)
-        if window not in (0, 3):
+        if window not in (0, 1, 2, 3):
             return []
         held.append(fetch(out_weight, cuts[i], cuts[i + 1] - cuts[i], after))
         return held[-1:]
@@ -453,22 +450,26 @@
         place, mine, other, norm_gain.reshape(-1, HD), early, wk, wv, query_weight,
         steps, group, colors, order, 1 << len(stages[0]))
     notes = take_notes(positions, lengths, parts[1], steps)
-    for i, stage in enumerate(stages[:-1]):
+    for i, stage in enumerate(stages):
         came = [partner(part, pattern) for part, pattern in zip(parts[1:], slot_patterns(stage)[1:])]
         now = fetch_next(i, [parts[1], notes])
-        parts = combine(parts[0], came, now, 1 << len(stages[i + 1]))
+        if i < len(stages) - 1:
+            parts = combine(parts[0], came, now, 1 << len(stages[i + 1]))
     same, cross, new_keys, new_values = attend(
-        place, parts[0], partner(parts[1], 1), notes, cache_keys[0], cache_values[0],
+        place, [parts[0], *came], notes, cache_keys[0], cache_values[0], now,
         steps, depth * lax.axis_size("gx"), half_heads)
 
-    context = local_call(pack_kernel, (2,) + same.shape, [same, partner(cross, 1)])
-    patterns = [0, 1]
-    for i, stage in enumerate(near_first[::-1]):
+    context, patterns = None, [0]
+    for i, stage in enumerate(stages[::-1]):
         moves = slot_patterns(stage)
-        came = [partner(context, move) for move in moves[1:]]
+        if i == 0:
+            context = same
+            came = [partner(cross if move & 1 else same, move) for move in moves[1:]]
+        else:
+            came = [partner(context, move) for move in moves[1:]]
         patterns = [p ^ move for move in moves for p in patterns]
-        now = fetch_next(len(near_first) + i, [context])
-        if i < len(near_first) - 1:
+        now = fetch_next(len(stages) + i, [context])
+        if i < len(stages) - 1:
             shape = (len(moves) * context.shape[0],) + context.shape[1:]
             context = local_call(functools.partial(join_kernel, len(came)), shape, [context, *came], now)
     mine, other = output(place, [context, *came], patterns, held, steps, colors)

time: 45.6 us -> 45.4 us (level)
  waiting for transfers between devices: 8.46 us -> 5.86 us
  Pallas kernels: 20.5 us -> 22.3 us
  starting transfers between devices: 13.8 us -> 14.4 us
    ppermute x12 -> x14, waiting for transfers between devices: 8.46 us -> 5.86 us  [partner(): lax.ppermute(array, everyone, [(i, i ^ pattern) for i in range(devices)])]
    pallas_call x2 -> x4, Pallas kernels: 7.03 us -> 8.83 us  [fetch(): pl.pallas_call(functools.partial(fetch_kernel, first, parts), out_shape=p...]
    ppermute x12 -> x14, starting transfers between devices: 13.8 us -> 14.4 us  [partner(): lax.ppermute(array, everyone, [(i, i ^ pattern) for i in range(devices)])]
  transfers between devices with their start and end apart: 12 -> 14, of which waited for: 6 -> 8; matrix products, arithmetic and copies ran while one was open for 0% -> 0% of each run, Pallas kernels for 21% -> 25%
where the time goes in v9:
time: 45.4 us; the launch traced here: 45.2 us
  Pallas kernels  22.3 us (49%)
  starting transfers between devices  14.4 us (32%)
  waiting for transfers between devices  5.86 us (13%)
  between operations  2.05 us (5%)
  other arithmetic  0.64 us (1%)
    ppermute x14, starting transfers between devices, partner(): lax.ppermute(array, everyone, [(i, i ^ pattern) for i in range(devices)])  14.4 us
    pallas_call x4, Pallas kernels, fetch(): pl.pallas_call(functools.partial(fetch_kernel, first, parts), out_shape=p...  8.83 us
    pallas_call x1, Pallas kernels, project(): pl.pallas_call(functools.partial(project_kernel, steps, group, colors, or...  6 us
    ppermute x14, waiting for transfers between devices, partner(): lax.ppermute(array, everyone, [(i, i ^ pattern) for i in range(devices)])  5.86 us
    pallas_call x1, Pallas kernels, output(): pl.pallas_call(functools.partial(output_kernel, steps, colors, patterns,...  3.13 us
    pallas_call x1, Pallas kernels, fetch_first(): pl.pallas_call(fetch_first_kernel, out_shape=(pltpu.VMEM((depth, early),...  2.26 us
    pallas_call x1, Pallas kernels, attend(): pl.pallas_call(functools.partial(attend_kernel, steps, width, len(held)),...  1.97 us
  transfers between devices with their start and end apart: 14, of which 8 were waited for; matrix products, arithmetic and copies ran while one was open for 0% of the time, Pallas kernels for 25%

profile of v9, /device:TPU:0, one launch (start us, length us, event | category | flops | bytes accessed | tf_op | source)
XLA Modules:
  0.0 45.2 jit_solution(5090837396983388725)
XLA Ops:
  0.6 0.5 %collective-permute-start = (bf16[16,2048]{1,0:T(8,128)(2,1)}, bf16[16,2048]{1,0:T(8,128)(2,1)S(1)}, u32[]{:S(2)}, u32[]{:S(2)}) collective-permute-start(bf16[16,2048]{1,0:T(8,128)(2,1)} %bitcast.11), channel_id=1, source_target_pairs={{0,1},{1,0},{2,3},{3,2},{4,5},{5,4},{6,7},{7,6},{8,9},{9,8},{10,11... | collective-permute-start | bytes 196616 | tf_op jit(solution)/shard_map/ppermute | solution.py:430
  1.1 2.3 %fetch_first.1 = (bf16[2048,512]{1,0:T(8,128)(2,1)S(1)}, bf16[2048,256]{1,0:T(8,128)(2,1)S(1)}, bf16[2048,256]{1,0:T(8,128)(2,1)S(1)}) custom-call(bf16[2048,4096]{1,0:T(8,128)(2,1)} %wq_ref.3, bf16[2048,256]{1,0:T(8,128)(2,1)} %wk_ref.1, bf16[2048,256]{1,0:T(8,128)(2,1)} %wv_ref.1), custom_call_target="tpu_custom_call" | custom-call | bytes 4194304 | tf_op jit(solution)/shard_map/fetch_first/pallas_call | solution.py:158
  3.4 0.0 collective-permute-done.other_ref
  3.4 6.0 %project.1 = (f32[4,80,128]{2,1,0:T(8,128)S(1)}, bf16[4,80,128]{2,1,0:T(8,128)(2,1)S(1)}, bf16[4,80,128]{2,1,0:T(8,128)(2,1)S(1)}, bf16[4,80,128]{2,1,0:T(8,128)(2,1)S(1)}) custom-call(s32[1]{0:T(128)} %bitcast.place_ref, bf16[16,2048]{1,0:T(8,128)(2,1)} %bitcast.12, bf16[16,2048]{1,0:T(8,128)(2,1)S(1)} %collective-permute-done.other_ref, ...), custom_call_target="tpu_custom_call" | custom-call | flops 603979776 | bytes 18874368 | tf_op jit(solution)/shard_map/project/pallas_call | solution.py:123
  9.4 2.6 %collective-permute-start.2 = (bf16[4,80,128]{2,1,0:T(8,128)(2,1)S(1)}, bf16[4,80,128]{2,1,0:T(8,128)(2,1)S(1)}, u32[]{:S(2)}, u32[]{:S(2)}) collective-permute-start(bf16[4,80,128]{2,1,0:T(8,128)(2,1)S(1)} %get-tuple-element.25), channel_id=1, source_target_pairs={{0,2},{1,3},{2,0},{3,1},{4,6},{5,7},{6,4},{7,5},{8,10},{9,11},{10,... | collective-permute-start | bytes 245768 | tf_op jit(solution)/shard_map/ppermute | solution.py:430
  12.0 1.5 %collective-permute-start.3 = (bf16[4,80,128]{2,1,0:T(8,128)(2,1)S(1)}, bf16[4,80,128]{2,1,0:T(8,128)(2,1)S(1)}, u32[]{:S(2)}, u32[]{:S(2)}) collective-permute-start(bf16[4,80,128]{2,1,0:T(8,128)(2,1)S(1)} %get-tuple-element.26), channel_id=1, source_target_pairs={{0,6},{1,7},{2,4},{3,5},{4,2},{5,3},{6,0},{7,1},{8,14},{9,15},{10,... | collective-permute-start | bytes 245768 | tf_op jit(solution)/shard_map/ppermute | solution.py:430
  13.6 0.0 collective-permute-start.1
  14.9 0.1 notes.1.rest_1_.table_ref
  15.0 2.9 %fetch.4.refs_4_.rest_0_ = bf16[1536,2048]{1,0:T(8,128)(2,1)S(1)} custom-call(bf16[4096,2048]{1,0:T(8,128)(2,1)} %weight_ref.7, bf16[4,80,128]{2,1,0:T(8,128)(2,1)S(1)} %get-tuple-element.23.after_ref.rest_0_, f32[8,128]{1,0:T(8,128)S(1)} %notes.1.rest_1_.table_ref), custom_call_target="tpu_custom_call" | custom-call | bytes 6291456 | tf_op jit(solution)/shard_map/fetch/pallas_call | solution.py:234
  17.8 0.0 collective-permute-done.2.refs_2_
  17.9 0.1 collective-permute-done.3.refs_3_
  18.0 0.2 collective-permute-done.1.refs_1_
  18.2 2.8 %collective-permute-start.5 = (bf16[1,80,128]{2,1,0:T(8,128)(2,1)S(1)}, bf16[1,80,128]{2,1,0:T(8,128)(2,1)S(1)}, u32[]{:S(2)}, u32[]{:S(2)}) collective-permute-start(bf16[1,80,128]{2,1,0:T(8,128)(2,1)S(1)} %get-tuple-element.29), channel_id=1, source_target_pairs={{0,8},{1,9},{2,10},{3,11},{4,12},{5,13},{6,14},{7,15},{8,0},{9,1},... | collective-permute-start | bytes 61448 | tf_op jit(solution)/shard_map/ppermute | solution.py:430
  21.0 0.0 collective-permute-start.6
  21.0 0.0 copy-start
  21.0 0.0 copy-start.1
  21.0 0.3 collective-permute-start.4
  21.4 1.5 %fetch.5.rest_0_.rest_1_ = bf16[512,2048]{1,0:T(8,128)(2,1)S(1)} custom-call(bf16[4096,2048]{1,0:T(8,128)(2,1)} %weight_ref.7, bf16[1,80,128]{2,1,0:T(8,128)(2,1)S(1)} %get-tuple-element.27.rest_0_, f32[8,128]{1,0:T(8,128)S(1)} %notes.1.rest_1_.table_ref), custom_call_target="tpu_custom_call" | custom-call | bytes 2097152 | tf_op jit(solution)/shard_map/fetch/pallas_call | solution.py:234
  22.9 0.1 collective-permute-done.5.rest_3_
  23.0 2.1 %collective-permute-done.6.rest_4_ = bf16[1,80,128]{2,1,0:T(8,128)(2,1)S(1)} collective-permute-done((bf16[1,80,128]{2,1,0:T(8,128)(2,1)S(1)}, bf16[1,80,128]{2,1,0:T(8,128)(2,1)S(1)}, u32[]{:S(2)}, u32[]{:S(2)}) %collective-permute-start.6) | collective-permute-done | bytes 20512 | tf_op jit(solution)/shard_map/ppermute | solution.py:430
  25.1 0.0 collective-permute-done.4.rest_2_
  25.1 0.0 copy-done
  25.2 0.0 copy-done.1
  25.2 2.0 %attend.1 = (bf16[1,64,128]{2,1,0:T(8,128)(2,1)S(1)}, bf16[1,64,128]{2,1,0:T(8,128)(2,1)S(1)}, bf16[2,512]{1,0:T(2,128)(2,1)}, bf16[2,512]{1,0:T(2,128)(2,1)}) custom-call(s32[1]{0:T(128)} %bitcast.place_ref, f32[8,128]{1,0:T(8,128)S(1)} %notes.1.rest_1_.table_ref, bf16[384,512]{1,0:T(8,128)(2,1)S(1)} %bitcast.9, bf16[384,512]{1,0:T(8,128)(2,1)S(1)} %bitcast.10, ...), custom_call_target="tpu_custom_call" | custom-call | tf_op jit(solution)/shard_map/attend/pallas_call | solution.py:325
  27.1 0.3 collective-permute-start.9
  27.4 0.5 %collective-permute-start.7 = (bf16[1,64,128]{2,1,0:T(8,128)(2,1)S(1)}, bf16[1,64,128]{2,1,0:T(8,128)(2,1)S(1)}, u32[]{:S(2)}, u32[]{:S(2)}) collective-permute-start(bf16[1,64,128]{2,1,0:T(8,128)(2,1)S(1)} %get-tuple-element.32), channel_id=1, source_target_pairs={{0,1},{1,0},{2,3},{3,2},{4,5},{5,4},{6,7},{7,6},{8,9},{9,8},{10,11... | collective-permute-start | bytes 49160 | tf_op jit(solution)/shard_map/ppermute | solution.py:430
  27.9 2.2 %collective-permute-start.8 = (bf16[1,64,128]{2,1,0:T(8,128)(2,1)S(1)}, bf16[1,64,128]{2,1,0:T(8,128)(2,1)S(1)}, u32[]{:S(2)}, u32[]{:S(2)}) collective-permute-start(bf16[1,64,128]{2,1,0:T(8,128)(2,1)S(1)} %get-tuple-element.31.rest_0_.refs_0_), channel_id=1, source_target_pairs={{0,8},{1,9},{2,10},{3,11},{4,12},{5,13},{6,14},{7,15},{8,0},{9,1},... | collective-permute-start | bytes 49160 | tf_op jit(solution)/shard_map/ppermute | solution.py:430
  30.2 1.5 %fetch.6.refs_4_.rest_2_ = bf16[512,2048]{1,0:T(8,128)(2,1)S(1)} custom-call(bf16[4096,2048]{1,0:T(8,128)(2,1)} %weight_ref.7, bf16[1,64,128]{2,1,0:T(8,128)(2,1)S(1)} %get-tuple-element.31.rest_0_.refs_0_), custom_call_target="tpu_custom_call" | custom-call | bytes 2097152 | tf_op jit(solution)/shard_map/fetch/pallas_call | solution.py:234
  31.7 0.0 collective-permute-done.9.refs_3_
  31.7 0.0 collective-permute-done.7.refs_1_
  31.7 0.8 %collective-permute-done.8.refs_2_ = bf16[1,64,128]{2,1,0:T(8,128)(2,1)S(1)} collective-permute-done((bf16[1,64,128]{2,1,0:T(8,128)(2,1)S(1)}, bf16[1,64,128]{2,1,0:T(8,128)(2,1)S(1)}, u32[]{:S(2)}, u32[]{:S(2)}) %collective-permute-start.8) | collective-permute-done | bytes 16416 | tf_op jit(solution)/shard_map/ppermute | solution.py:430
  32.6 2.9 %collective-permute-start.12 = (bf16[4,64,128]{2,1,0:T(8,128)(2,1)S(1)}, bf16[4,64,128]{2,1,0:T(8,128)(2,1)S(1)}, u32[]{:S(2)}, u32[]{:S(2)}) collective-permute-start(bf16[4,64,128]{2,1,0:T(8,128)(2,1)S(1)} %local.1.rest_0_.rest_4_), channel_id=1, source_target_pairs={{0,6},{1,7},{2,4},{3,5},{4,2},{5,3},{6,0},{7,1},{8,14},{9,15},{10,... | collective-permute-start | bytes 196616 | tf_op jit(solution)/shard_map/ppermute | solution.py:430
  35.5 0.5 %collective-permute-start.11 = (bf16[4,64,128]{2,1,0:T(8,128)(2,1)S(1)}, bf16[4,64,128]{2,1,0:T(8,128)(2,1)S(1)}, u32[]{:S(2)}, u32[]{:S(2)}) collective-permute-start(bf16[4,64,128]{2,1,0:T(8,128)(2,1)S(1)} %local.1.rest_0_.rest_4_), channel_id=1, source_target_pairs={{0,2},{1,3},{2,0},{3,1},{4,6},{5,7},{6,4},{7,5},{8,10},{9,11},{10,... | collective-permute-start | bytes 196616 | tf_op jit(solution)/shard_map/ppermute | solution.py:430
  35.9 0.2 collective-permute-start.10
  36.1 2.9 %fetch.7.rest_3_ = bf16[1536,2048]{1,0:T(8,128)(2,1)S(1)} custom-call(bf16[4096,2048]{1,0:T(8,128)(2,1)} %weight_ref.7, bf16[4,64,128]{2,1,0:T(8,128)(2,1)S(1)} %local.1.rest_0_.rest_4_), custom_call_target="tpu_custom_call" | custom-call | bytes 6291456 | tf_op jit(solution)/shard_map/fetch/pallas_call | solution.py:234
  39.0 0.0 collective-permute-done.12.rest_7_
  39.0 0.7 %collective-permute-done.11.rest_6_ = bf16[4,64,128]{2,1,0:T(8,128)(2,1)S(1)} collective-permute-done((bf16[4,64,128]{2,1,0:T(8,128)(2,1)S(1)}, bf16[4,64,128]{2,1,0:T(8,128)(2,1)S(1)}, u32[]{:S(2)}, u32[]{:S(2)}) %collective-permute-start.11) | collective-permute-done | bytes 65568 | tf_op jit(solution)/shard_map/ppermute | solution.py:430
  39.7 0.5 %collective-permute-done.10.rest_5_ = bf16[4,64,128]{2,1,0:T(8,128)(2,1)S(1)} collective-permute-done((bf16[4,64,128]{2,1,0:T(8,128)(2,1)S(1)}, bf16[4,64,128]{2,1,0:T(8,128)(2,1)S(1)}, u32[]{:S(2)}, u32[]{:S(2)}) %collective-permute-start.10) | collective-permute-done | bytes 65568 | tf_op jit(solution)/shard_map/ppermute | solution.py:430
  40.2 3.1 %output.1 = (f32[16,2048]{1,0:T(8,128)S(1)}, bf16[16,2048]{1,0:T(8,128)(2,1)S(1)}) custom-call(s32[1]{0:T(128)} %bitcast.place_ref, bf16[1536,2048]{1,0:T(8,128)(2,1)S(1)} %fetch.4.refs_4_.rest_0_, bf16[512,2048]{1,0:T(8,128)(2,1)S(1)} %fetch.5.rest_0_.rest_1_, bf16[512,2048]{1,0:T(8,128)(2,1)S(1)} %fetch.6.refs_4_.rest_2_, ...), custom_call_target="tpu_custom_call" | custom-call | flops 536870912 | bytes 16777216 | tf_op jit(solution)/shard_map/output/pallas_call | solution.py:398
  43.3 0.0 collective-permute-start.13
  43.3 1.2 %collective-permute-done.13 = bf16[16,2048]{1,0:T(8,128)(2,1)S(1)} collective-permute-done((bf16[16,2048]{1,0:T(8,128)(2,1)S(1)}, bf16[16,2048]{1,0:T(8,128)(2,1)S(1)}, u32[]{:S(2)}, u32[]{:S(2)}) %collective-permute-start.13) | collective-permute-done | bytes 65568 | tf_op jit(solution)/shard_map/ppermute | solution.py:430
  44.6 0.6 %fusion = bf16[2,8,2048]{2,1,0:T(8,128)(2,1)} fusion(f32[16,2048]{1,0:T(8,128)S(1)} %get-tuple-element.33, bf16[16,2048]{1,0:T(8,128)(2,1)S(1)} %collective-permute-done.13), kind=kLoop, calls=%fused_computation.1 | loop fusion | flops 98304 | bytes 262144 | tf_op jit(solution)/shard_map/reshape | solution.py:479
  (2 shorter events, 0.0 us)
Async XLA Ops:
  0.6 2.8 %collective-permute-start = (bf16[16,2048]{1,0:T(8,128)(2,1)}, bf16[16,2048]{1,0:T(8,128)(2,1)S(1)}, u32[]{:S(2)}, u32[]{:S(2)}) collective-permute-start(bf16[16,2048]{1,0:T(8,128)(2,1)} %bitcast.11), channel_id=1, source_target_pairs={{0,1},{1,0},{2,3},{3,2},{4,5},{5,4},{6,7},{7,6},{8,9},{9,8},{10,11... | collective-permute-start | bytes 196616 | tf_op jit(solution)/shard_map/ppermute | solution.py:430
  9.4 8.4 %collective-permute-start.2 = (bf16[4,80,128]{2,1,0:T(8,128)(2,1)S(1)}, bf16[4,80,128]{2,1,0:T(8,128)(2,1)S(1)}, u32[]{:S(2)}, u32[]{:S(2)}) collective-permute-start(bf16[4,80,128]{2,1,0:T(8,128)(2,1)S(1)} %get-tuple-element.25), channel_id=1, source_target_pairs={{0,2},{1,3},{2,0},{3,1},{4,6},{5,7},{6,4},{7,5},{8,10},{9,11},{10,... | collective-permute-start | bytes 245768 | tf_op jit(solution)/shard_map/ppermute | solution.py:430
  12.0 6.0 %collective-permute-start.3 = (bf16[4,80,128]{2,1,0:T(8,128)(2,1)S(1)}, bf16[4,80,128]{2,1,0:T(8,128)(2,1)S(1)}, u32[]{:S(2)}, u32[]{:S(2)}) collective-permute-start(bf16[4,80,128]{2,1,0:T(8,128)(2,1)S(1)} %get-tuple-element.26), channel_id=1, source_target_pairs={{0,6},{1,7},{2,4},{3,5},{4,2},{5,3},{6,0},{7,1},{8,14},{9,15},{10,... | collective-permute-start | bytes 245768 | tf_op jit(solution)/shard_map/ppermute | solution.py:430
  13.6 4.6 %collective-permute-start.1 = (bf16[4,80,128]{2,1,0:T(8,128)(2,1)S(1)}, bf16[4,80,128]{2,1,0:T(8,128)(2,1)S(1)}, u32[]{:S(2)}, u32[]{:S(2)}) collective-permute-start(bf16[4,80,128]{2,1,0:T(8,128)(2,1)S(1)} %get-tuple-element.23.after_ref.rest_0_), channel_id=1, source_target_pairs={{0,4},{1,5},{2,6},{3,7},{4,0},{5,1},{6,2},{7,3},{8,12},{9,13},{10,... | collective-permute-start | bytes 245768 | tf_op jit(solution)/shard_map/ppermute | solution.py:430
  18.2 4.8 %collective-permute-start.5 = (bf16[1,80,128]{2,1,0:T(8,128)(2,1)S(1)}, bf16[1,80,128]{2,1,0:T(8,128)(2,1)S(1)}, u32[]{:S(2)}, u32[]{:S(2)}) collective-permute-start(bf16[1,80,128]{2,1,0:T(8,128)(2,1)S(1)} %get-tuple-element.29), channel_id=1, source_target_pairs={{0,8},{1,9},{2,10},{3,11},{4,12},{5,13},{6,14},{7,15},{8,0},{9,1},... | collective-permute-start | bytes 61448 | tf_op jit(solution)/shard_map/ppermute | solution.py:430
  21.0 4.1 %collective-permute-start.6 = (bf16[1,80,128]{2,1,0:T(8,128)(2,1)S(1)}, bf16[1,80,128]{2,1,0:T(8,128)(2,1)S(1)}, u32[]{:S(2)}, u32[]{:S(2)}) collective-permute-start(bf16[1,80,128]{2,1,0:T(8,128)(2,1)S(1)} %get-tuple-element.30), channel_id=1, source_target_pairs={{0,9},{1,8},{2,11},{3,10},{4,13},{5,12},{6,15},{7,14},{8,1},{9,0},... | collective-permute-start | bytes 61448 | tf_op jit(solution)/shard_map/ppermute | solution.py:430
  21.0 4.1 %copy-start = (bf16[1,384,512]{2,1,0:T(8,128)(2,1)S(1)}, bf16[1,384,512]{2,1,0:T(8,128)(2,1)}, u32[]{:S(2)}) copy-start(bf16[1,384,512]{2,1,0:T(8,128)(2,1)} %param.16) | copy-start | bytes 1179652
  21.0 4.1 %copy-start.1 = (bf16[1,384,512]{2,1,0:T(8,128)(2,1)S(1)}, bf16[1,384,512]{2,1,0:T(8,128)(2,1)}, u32[]{:S(2)}) copy-start(bf16[1,384,512]{2,1,0:T(8,128)(2,1)} %param.17) | copy-start | bytes 1179652
  21.0 4.1 %collective-permute-start.4 = (bf16[1,80,128]{2,1,0:T(8,128)(2,1)S(1)}, bf16[1,80,128]{2,1,0:T(8,128)(2,1)S(1)}, u32[]{:S(2)}, u32[]{:S(2)}) collective-permute-start(bf16[1,80,128]{2,1,0:T(8,128)(2,1)S(1)} %get-tuple-element.27.rest_0_), channel_id=1, source_target_pairs={{0,1},{1,0},{2,3},{3,2},{4,5},{5,4},{6,7},{7,6},{8,9},{9,8},{10,11... | collective-permute-start | bytes 61448 | tf_op jit(solution)/shard_map/ppermute | solution.py:430
  27.1 4.6 %collective-permute-start.9 = (bf16[1,64,128]{2,1,0:T(8,128)(2,1)S(1)}, bf16[1,64,128]{2,1,0:T(8,128)(2,1)S(1)}, u32[]{:S(2)}, u32[]{:S(2)}) collective-permute-start(bf16[1,64,128]{2,1,0:T(8,128)(2,1)S(1)} %get-tuple-element.32), channel_id=1, source_target_pairs={{0,9},{1,8},{2,11},{3,10},{4,13},{5,12},{6,15},{7,14},{8,1},{9,0},... | collective-permute-start | bytes 49160 | tf_op jit(solution)/shard_map/ppermute | solution.py:430
  27.4 4.3 %collective-permute-start.7 = (bf16[1,64,128]{2,1,0:T(8,128)(2,1)S(1)}, bf16[1,64,128]{2,1,0:T(8,128)(2,1)S(1)}, u32[]{:S(2)}, u32[]{:S(2)}) collective-permute-start(bf16[1,64,128]{2,1,0:T(8,128)(2,1)S(1)} %get-tuple-element.32), channel_id=1, source_target_pairs={{0,1},{1,0},{2,3},{3,2},{4,5},{5,4},{6,7},{7,6},{8,9},{9,8},{10,11... | collective-permute-start | bytes 49160 | tf_op jit(solution)/shard_map/ppermute | solution.py:430
  27.9 4.6 %collective-permute-start.8 = (bf16[1,64,128]{2,1,0:T(8,128)(2,1)S(1)}, bf16[1,64,128]{2,1,0:T(8,128)(2,1)S(1)}, u32[]{:S(2)}, u32[]{:S(2)}) collective-permute-start(bf16[1,64,128]{2,1,0:T(8,128)(2,1)S(1)} %get-tuple-element.31.rest_0_.refs_0_), channel_id=1, source_target_pairs={{0,8},{1,9},{2,10},{3,11},{4,12},{5,13},{6,14},{7,15},{8,0},{9,1},... | collective-permute-start | bytes 49160 | tf_op jit(solution)/shard_map/ppermute | solution.py:430
  32.6 6.4 %collective-permute-start.12 = (bf16[4,64,128]{2,1,0:T(8,128)(2,1)S(1)}, bf16[4,64,128]{2,1,0:T(8,128)(2,1)S(1)}, u32[]{:S(2)}, u32[]{:S(2)}) collective-permute-start(bf16[4,64,128]{2,1,0:T(8,128)(2,1)S(1)} %local.1.rest_0_.rest_4_), channel_id=1, source_target_pairs={{0,6},{1,7},{2,4},{3,5},{4,2},{5,3},{6,0},{7,1},{8,14},{9,15},{10,... | collective-permute-start | bytes 196616 | tf_op jit(solution)/shard_map/ppermute | solution.py:430
  35.5 4.3 %collective-permute-start.11 = (bf16[4,64,128]{2,1,0:T(8,128)(2,1)S(1)}, bf16[4,64,128]{2,1,0:T(8,128)(2,1)S(1)}, u32[]{:S(2)}, u32[]{:S(2)}) collective-permute-start(bf16[4,64,128]{2,1,0:T(8,128)(2,1)S(1)} %local.1.rest_0_.rest_4_), channel_id=1, source_target_pairs={{0,2},{1,3},{2,0},{3,1},{4,6},{5,7},{6,4},{7,5},{8,10},{9,11},{10,... | collective-permute-start | bytes 196616 | tf_op jit(solution)/shard_map/ppermute | solution.py:430
  35.9 4.3 %collective-permute-start.10 = (bf16[4,64,128]{2,1,0:T(8,128)(2,1)S(1)}, bf16[4,64,128]{2,1,0:T(8,128)(2,1)S(1)}, u32[]{:S(2)}, u32[]{:S(2)}) collective-permute-start(bf16[4,64,128]{2,1,0:T(8,128)(2,1)S(1)} %local.1.rest_0_.rest_4_), channel_id=1, source_target_pairs={{0,4},{1,5},{2,6},{3,7},{4,0},{5,1},{6,2},{7,3},{8,12},{9,13},{10,... | collective-permute-start | bytes 196616 | tf_op jit(solution)/shard_map/ppermute | solution.py:430
  43.3 1.3 %collective-permute-start.13 = (bf16[16,2048]{1,0:T(8,128)(2,1)S(1)}, bf16[16,2048]{1,0:T(8,128)(2,1)S(1)}, u32[]{:S(2)}, u32[]{:S(2)}) collective-permute-start(bf16[16,2048]{1,0:T(8,128)(2,1)S(1)} %get-tuple-element.34), channel_id=1, source_target_pairs={{0,1},{1,0},{2,3},{3,2},{4,5},{5,4},{6,7},{7,6},{8,9},{9,8},{10,11... | collective-permute-start | bytes 196616 | tf_op jit(solution)/shard_map/ppermute | solution.py:430

commit v10 on v9

--- a/solution.py
+++ b/solution.py
@@ -202,17 +202,17 @@
         ref[...] = total[i * count:(i + 1) * count].astype(ref.dtype)
 
 
-def combine(keep, came, held, parts):
+def combine(keep, came, held, after, parts):
     vmem = pl.BlockSpec(memory_space=pltpu.VMEM)
     out_shape = part_shapes(keep.shape[0], parts, keep.shape[1:])
     return pl.pallas_call(
         functools.partial(combine_kernel, len(came), parts),
         out_shape=out_shape,
-        in_specs=[vmem] * (1 + len(came)) + [pl.BlockSpec(memory_space=pl.ANY)] * len(held),
+        in_specs=[vmem] * (1 + len(came)) + [pl.BlockSpec(memory_space=pl.ANY)] * (1 + len(held)),
         out_specs=(vmem,) * parts,
         compiler_params=pltpu.CompilerParams(vmem_limit_bytes=24 * MIB),
         name="combine",
-    )(keep, *came, *[in_vmem(piece) for piece in held])
+    )(keep, *came, after, *[in_vmem(piece) for piece in held])
 
 
 def fetch_kernel(first, parts, weight_ref, *rest):
@@ -257,9 +257,9 @@
     same, cross = [
         functools.reduce(jnp.add, [ref[0].astype(jnp.float32) for ref in part_refs[i::2]]) for i in range(2)]
     halves = [jnp.where(low_side, same, cross), jnp.where(low_side, cross, same)]
-    live = lax.broadcasted_iota(jnp.int32, (steps * group, slots), 1) < (
-        table_ref[2 * steps:2 * steps + 1, :1].astype(jnp.int32))
-    row_step = lax.broadcasted_iota(jnp.int32, (steps * group, 1), 0) // group
+    per_head = steps * group
+    lanes = kv_heads * per_head
+    fresh_rows = 16
     fresh_keys = [[None] * kv_heads for _ in range(steps)]
     fresh_values = [[None] * kv_heads for _ in range(steps)]
     queries = [None] * kv_heads
@@ -275,40 +275,38 @@
                 sine = table_ref[2 * t + 1:2 * t + 2, :]
                 turned = rows * cosine + pltpu.roll(rows, HD // 2, 1) * sine
                 query.append(turned[:group])
-                fresh_keys[t][head] = turned[group:group + 1].astype(jnp.bfloat16).astype(jnp.float32)
-                fresh_values[t][head] = rows[group + 1:group + 2].astype(jnp.bfloat16).astype(jnp.float32)
-            queries[head] = jnp.concatenate(query, axis=0).astype(jnp.bfloat16)
-    new_keys_ref[...] = jnp.concatenate(
-        [jnp.concatenate(row, axis=1) for row in fresh_keys], axis=0).astype(jnp.bfloat16)
-    new_values_ref[...] = jnp.concatenate(
-        [jnp.concatenate(row, axis=1) for row in fresh_values], axis=0).astype(jnp.bfloat16)
-    contexts = []
-    for head in range(kv_heads):
-        columns = slice(head * HD, (head + 1) * HD)
-        query = queries[head]
-        scores = lax.dot_general(
-            query, keys_ref[:, columns], (((1,), (1,)), ((), ())),
-            preferred_element_type=jnp.float32) * factor
-        scores = jnp.where(live, scores, -jnp.inf)
-        top = jnp.max(scores, axis=-1, keepdims=True)
-        wide = query.astype(jnp.float32)
-        fresh = []
-        for s in range(steps):
-            score = jnp.sum(wide * fresh_keys[s][head], axis=-1, keepdims=True) * factor
-            score = jnp.where(row_step >= s, score, -jnp.inf)
-            fresh.append(score)
-            top = jnp.maximum(top, score)
-        scores = jnp.exp(scores - top)
-        total = jnp.sum(scores, axis=-1, keepdims=True)
-        fresh = [jnp.exp(score - top) for score in fresh]
-        for score in fresh:
-            total = total + score
-        weight = (scores / total).astype(jnp.bfloat16)
-        mixed = jnp.dot(weight, values_ref[:, columns], preferred_element_type=jnp.float32)
-        for s in range(steps):
-            weight = (fresh[s] / total).astype(jnp.bfloat16).astype(jnp.float32)
-            mixed = mixed + weight * fresh_values[s][head]
-        contexts.append(mixed)
+                fresh_keys[t][head] = turned[group:group + 1]
+                fresh_values[t][head] = rows[group + 1:group + 2]
+            blocks = [jnp.zeros((per_head, HD), jnp.float32)] * kv_heads
+            blocks[head] = jnp.concatenate(query, axis=0)
+            queries[head] = jnp.concatenate(blocks, axis=1)
+    queries = jnp.concatenate(queries, axis=0).astype(jnp.bfloat16)
+    padding = jnp.zeros((fresh_rows - steps, kv_heads * HD), jnp.float32)
+    fresh_keys, fresh_values = [
+        jnp.concatenate([jnp.concatenate(row, axis=1) for row in fresh] + [padding], axis=0).astype(jnp.bfloat16)
+        for fresh in (fresh_keys, fresh_values)]
+    new_keys_ref[...] = fresh_keys[:steps]
+    new_values_ref[...] = fresh_values[:steps]
+
+    length = table_ref[2 * steps:2 * steps + 1, :1].astype(jnp.int32)
+    live = lax.broadcasted_iota(jnp.int32, (slots, lanes), 0) < length
+    lane_step = (lax.broadcasted_iota(jnp.int32, (fresh_rows, lanes), 1) % per_head) // group
+    seen = lax.broadcasted_iota(jnp.int32, (fresh_rows, lanes), 0) <= lane_step
+    over_last, over_first = (((1,), (1,)), ((), ())), (((0,), (0,)), ((), ()))
+    scores = lax.dot_general(keys_ref[...], queries, over_last, preferred_element_type=jnp.float32) * factor
+    scores = jnp.where(live, scores, -jnp.inf)
+    fresh = lax.dot_general(fresh_keys, queries, over_last, preferred_element_type=jnp.float32) * factor
+    fresh = jnp.where(seen, fresh, -jnp.inf)
+    top = jnp.maximum(jnp.max(scores, axis=0, keepdims=True), jnp.max(fresh, axis=0, keepdims=True))
+    scores = jnp.exp(scores - top)
+    fresh = jnp.exp(fresh - top)
+    inverse = 1.0 / (jnp.sum(scores, axis=0, keepdims=True) + jnp.sum(fresh, axis=0, keepdims=True))
+    weights = (scores * inverse).astype(jnp.bfloat16)
+    fresh = (fresh * inverse).astype(jnp.bfloat16)
+    mixed = lax.dot_general(weights, values_ref[...], over_first, preferred_element_type=jnp.float32)
+    mixed = mixed + lax.dot_general(fresh, fresh_values, over_first, preferred_element_type=jnp.float32)
+    contexts = [
+        mixed[head * per_head:(head + 1) * per_head, head * HD:(head + 1) * HD] for head in range(kv_heads)]
     for k in range(half_kv):
         lower, upper = contexts[k], contexts[half_kv + k]
         span = slice(k * steps * group, (k + 1) * steps * group)
@@ -433,12 +431,12 @@
     stages[-1] = stages[-1] + [0]
     order = [bit for stage in stages for bit in stage]
     total = out_weight.shape[0]
-    cuts = [total * i // 8 for i in (0, 3, 4, 5, 8)]
+    cuts = [total * i // 8 for i in (0, 3, 4, 8)]
     held = []
 
     def fetch_next(window, after):
         i = len(held)
-        if window not in (0, 1, 2, 3):
+        if window not in (1, 2, 3):
             return []
         held.append(fetch(out_weight, cuts[i], cuts[i + 1] - cuts[i], after))
         return held[-1:]
@@ -454,7 +452,7 @@
         came = [partner(part, pattern) for part, pattern in zip(parts[1:], slot_patterns(stage)[1:])]
         now = fetch_next(i, [parts[1], notes])
         if i < len(stages) - 1:
-            parts = combine(parts[0], came, now, 1 << len(stages[i + 1]))
+            parts = combine(parts[0], came, now, notes, 1 << len(stages[i + 1]))
     same, cross, new_keys, new_values = attend(
         place, [parts[0], *came], notes, cache_keys[0], cache_values[0], now,
         steps, depth * lax.axis_size("gx"), half_heads)

time: 45.4 us -> 45.6 us (level)
  waiting for transfers between devices: 5.86 us -> 7.67 us
  Pallas kernels: 22.3 us -> 20.7 us
    ppermute x14, waiting for transfers between devices: 5.86 us -> 7.67 us  [partner(): lax.ppermute(array, everyone, [(i, i ^ pattern) for i in range(devices)])]
    pallas_call x4 -> x3, Pallas kernels: 8.83 us -> 7.91 us  [fetch(): pl.pallas_call(functools.partial(fetch_kernel, first, parts), out_shape=p...]
    pallas_call x1, Pallas kernels: 1.97 us -> 1.32 us  [attend(): pl.pallas_call(functools.partial(attend_kernel, steps, width, len(held)),...]
  transfers between devices with their start and end apart: 14 -> 14, of which waited for: 8 -> 7; matrix products, arithmetic and copies ran while one was open for 0% -> 0% of each run, Pallas kernels for 25% -> 23%
where the time goes in v10:
time: 45.6 us; the launch traced here: 45.4 us
  Pallas kernels  20.7 us (45%)
  starting transfers between devices  14.3 us (31%)
  waiting for transfers between devices  7.67 us (17%)
  between operations  2.05 us (4%)
  other arithmetic  0.64 us (1%)
    ppermute x14, starting transfers between devices, partner(): lax.ppermute(array, everyone, [(i, i ^ pattern) for i in range(devices)])  14.3 us
    pallas_call x3, Pallas kernels, fetch(): pl.pallas_call(functools.partial(fetch_kernel, first, parts), out_shape=p...  7.91 us
    ppermute x14, waiting for transfers between devices, partner(): lax.ppermute(array, everyone, [(i, i ^ pattern) for i in range(devices)])  7.67 us
    pallas_call x1, Pallas kernels, project(): pl.pallas_call(functools.partial(project_kernel, steps, group, colors, or...  6 us
    pallas_call x1, Pallas kernels, output(): pl.pallas_call(functools.partial(output_kernel, steps, colors, patterns,...  3.13 us
    pallas_call x1, Pallas kernels, fetch_first(): pl.pallas_call(fetch_first_kernel, out_shape=(pltpu.VMEM((depth, early),...  2.26 us
    pallas_call x1, Pallas kernels, attend(): pl.pallas_call(functools.partial(attend_kernel, steps, width, len(held)),...  1.32 us
  transfers between devices with their start and end apart: 14, of which 7 were waited for; matrix products, arithmetic and copies ran while one was open for 0% of the time, Pallas kernels for 23%

profile of v10, /device:TPU:0, one launch (start us, length us, event | category | flops | bytes accessed | tf_op | source)
XLA Modules:
  0.0 45.4 jit_solution(185948354910700136)
XLA Ops:
  0.6 0.5 %collective-permute-start = (bf16[16,2048]{1,0:T(8,128)(2,1)}, bf16[16,2048]{1,0:T(8,128)(2,1)S(1)}, u32[]{:S(2)}, u32[]{:S(2)}) collective-permute-start(bf16[16,2048]{1,0:T(8,128)(2,1)} %bitcast.11), channel_id=1, source_target_pairs={{0,1},{1,0},{2,3},{3,2},{4,5},{5,4},{6,7},{7,6},{8,9},{9,8},{10,11... | collective-permute-start | bytes 196616 | tf_op jit(solution)/shard_map/ppermute | solution.py:428
  1.1 2.3 %fetch_first.1 = (bf16[2048,512]{1,0:T(8,128)(2,1)S(1)}, bf16[2048,256]{1,0:T(8,128)(2,1)S(1)}, bf16[2048,256]{1,0:T(8,128)(2,1)S(1)}) custom-call(bf16[2048,4096]{1,0:T(8,128)(2,1)} %wq_ref.3, bf16[2048,256]{1,0:T(8,128)(2,1)} %wk_ref.1, bf16[2048,256]{1,0:T(8,128)(2,1)} %wv_ref.1), custom_call_target="tpu_custom_call" | custom-call | bytes 4194304 | tf_op jit(solution)/shard_map/fetch_first/pallas_call | solution.py:158
  3.4 0.0 collective-permute-done.other_ref
  3.4 6.0 %project.1 = (f32[4,80,128]{2,1,0:T(8,128)S(1)}, bf16[4,80,128]{2,1,0:T(8,128)(2,1)S(1)}, bf16[4,80,128]{2,1,0:T(8,128)(2,1)S(1)}, bf16[4,80,128]{2,1,0:T(8,128)(2,1)S(1)}) custom-call(s32[1]{0:T(128)} %bitcast.place_ref, bf16[16,2048]{1,0:T(8,128)(2,1)} %bitcast.12, bf16[16,2048]{1,0:T(8,128)(2,1)S(1)} %collective-permute-done.other_ref, ...), custom_call_target="tpu_custom_call" | custom-call | flops 603979776 | bytes 18874368 | tf_op jit(solution)/shard_map/project/pallas_call | solution.py:123
  9.4 2.6 %collective-permute-start.2 = (bf16[4,80,128]{2,1,0:T(8,128)(2,1)S(1)}, bf16[4,80,128]{2,1,0:T(8,128)(2,1)S(1)}, u32[]{:S(2)}, u32[]{:S(2)}) collective-permute-start(bf16[4,80,128]{2,1,0:T(8,128)(2,1)S(1)} %get-tuple-element.25), channel_id=1, source_target_pairs={{0,2},{1,3},{2,0},{3,1},{4,6},{5,7},{6,4},{7,5},{8,10},{9,11},{10,... | collective-permute-start | bytes 245768 | tf_op jit(solution)/shard_map/ppermute | solution.py:428
  12.0 1.5 %collective-permute-start.3 = (bf16[4,80,128]{2,1,0:T(8,128)(2,1)S(1)}, bf16[4,80,128]{2,1,0:T(8,128)(2,1)S(1)}, u32[]{:S(2)}, u32[]{:S(2)}) collective-permute-start(bf16[4,80,128]{2,1,0:T(8,128)(2,1)S(1)} %get-tuple-element.26), channel_id=1, source_target_pairs={{0,6},{1,7},{2,4},{3,5},{4,2},{5,3},{6,0},{7,1},{8,14},{9,15},{10,... | collective-permute-start | bytes 245768 | tf_op jit(solution)/shard_map/ppermute | solution.py:428
  13.6 0.0 collective-permute-start.1
  14.9 0.1 notes.1.refs_4_.rest_1_.table_ref
  15.0 1.2 %collective-permute-done.2.refs_2_ = bf16[4,80,128]{2,1,0:T(8,128)(2,1)S(1)} collective-permute-done((bf16[4,80,128]{2,1,0:T(8,128)(2,1)S(1)}, bf16[4,80,128]{2,1,0:T(8,128)(2,1)S(1)}, u32[]{:S(2)}, u32[]{:S(2)}) %collective-permute-start.2) | collective-permute-done | bytes 81952 | tf_op jit(solution)/shard_map/ppermute | solution.py:428
  16.1 1.8 %collective-permute-done.3.refs_3_ = bf16[4,80,128]{2,1,0:T(8,128)(2,1)S(1)} collective-permute-done((bf16[4,80,128]{2,1,0:T(8,128)(2,1)S(1)}, bf16[4,80,128]{2,1,0:T(8,128)(2,1)S(1)}, u32[]{:S(2)}, u32[]{:S(2)}) %collective-permute-start.3) | collective-permute-done | bytes 81952 | tf_op jit(solution)/shard_map/ppermute | solution.py:428
  18.0 0.2 collective-permute-done.1.refs_1_
  18.2 2.8 %collective-permute-start.5 = (bf16[1,80,128]{2,1,0:T(8,128)(2,1)S(1)}, bf16[1,80,128]{2,1,0:T(8,128)(2,1)S(1)}, u32[]{:S(2)}, u32[]{:S(2)}) collective-permute-start(bf16[1,80,128]{2,1,0:T(8,128)(2,1)S(1)} %get-tuple-element.29), channel_id=1, source_target_pairs={{0,8},{1,9},{2,10},{3,11},{4,12},{5,13},{6,14},{7,15},{8,0},{9,1},... | collective-permute-start | bytes 61448 | tf_op jit(solution)/shard_map/ppermute | solution.py:428
  21.0 0.0 collective-permute-start.6
  21.0 0.0 copy-start
  21.0 0.0 copy-start.1
  21.0 0.3 collective-permute-start.4
  21.4 2.9 %fetch.3.rest_0_ = bf16[1536,2048]{1,0:T(8,128)(2,1)S(1)} custom-call(bf16[4096,2048]{1,0:T(8,128)(2,1)} %weight_ref.5, bf16[1,80,128]{2,1,0:T(8,128)(2,1)S(1)} %get-tuple-element.27.rest_0_, f32[8,128]{1,0:T(8,128)S(1)} %notes.1.refs_4_.rest_1_.table_ref), custom_call_target="tpu_custom_call" | custom-call | bytes 6291456 | tf_op jit(solution)/shard_map/fetch/pallas_call | solution.py:234
  24.2 0.0 collective-permute-done.5.rest_3_
  24.2 0.9 %collective-permute-done.6.rest_4_ = bf16[1,80,128]{2,1,0:T(8,128)(2,1)S(1)} collective-permute-done((bf16[1,80,128]{2,1,0:T(8,128)(2,1)S(1)}, bf16[1,80,128]{2,1,0:T(8,128)(2,1)S(1)}, u32[]{:S(2)}, u32[]{:S(2)}) %collective-permute-start.6) | collective-permute-done | bytes 20512 | tf_op jit(solution)/shard_map/ppermute | solution.py:428
  25.1 0.0 collective-permute-done.4.rest_2_
  25.1 0.0 copy-done
  25.2 0.0 copy-done.1
  25.2 1.3 %attend.1 = (bf16[1,64,128]{2,1,0:T(8,128)(2,1)S(1)}, bf16[1,64,128]{2,1,0:T(8,128)(2,1)S(1)}, bf16[2,512]{1,0:T(2,128)(2,1)}, bf16[2,512]{1,0:T(2,128)(2,1)}) custom-call(s32[1]{0:T(128)} %bitcast.place_ref, f32[8,128]{1,0:T(8,128)S(1)} %notes.1.refs_4_.rest_1_.table_ref, bf16[384,512]{1,0:T(8,128)(2,1)S(1)} %bitcast.9, bf16[384,512]{1,0:T(8,128)(2,1)S(1)} %bitcast.10, ...), custom_call_target="tpu_custom_call" | custom-call | tf_op jit(solution)/shard_map/attend/pallas_call | solution.py:323
  26.5 1.5 %collective-permute-start.9 = (bf16[1,64,128]{2,1,0:T(8,128)(2,1)S(1)}, bf16[1,64,128]{2,1,0:T(8,128)(2,1)S(1)}, u32[]{:S(2)}, u32[]{:S(2)}) collective-permute-start(bf16[1,64,128]{2,1,0:T(8,128)(2,1)S(1)} %get-tuple-element.32), channel_id=1, source_target_pairs={{0,9},{1,8},{2,11},{3,10},{4,13},{5,12},{6,15},{7,14},{8,1},{9,0},... | collective-permute-start | bytes 49160 | tf_op jit(solution)/shard_map/ppermute | solution.py:428
  28.0 0.4 collective-permute-start.7
  28.4 1.1 %collective-permute-start.8 = (bf16[1,64,128]{2,1,0:T(8,128)(2,1)S(1)}, bf16[1,64,128]{2,1,0:T(8,128)(2,1)S(1)}, u32[]{:S(2)}, u32[]{:S(2)}) collective-permute-start(bf16[1,64,128]{2,1,0:T(8,128)(2,1)S(1)} %get-tuple-element.31.rest_0_.refs_0_), channel_id=1, source_target_pairs={{0,8},{1,9},{2,10},{3,11},{4,12},{5,13},{6,14},{7,15},{8,0},{9,1},... | collective-permute-start | bytes 49160 | tf_op jit(solution)/shard_map/ppermute | solution.py:428
  29.5 1.5 %fetch.4.refs_4_.rest_1_ = bf16[512,2048]{1,0:T(8,128)(2,1)S(1)} custom-call(bf16[4096,2048]{1,0:T(8,128)(2,1)} %weight_ref.5, bf16[1,64,128]{2,1,0:T(8,128)(2,1)S(1)} %get-tuple-element.31.rest_0_.refs_0_), custom_call_target="tpu_custom_call" | custom-call | bytes 2097152 | tf_op jit(solution)/shard_map/fetch/pallas_call | solution.py:234
  31.1 0.0 collective-permute-done.9.refs_3_
  31.1 0.0 collective-permute-done.7.refs_1_
  31.1 2.0 %collective-permute-done.8.refs_2_ = bf16[1,64,128]{2,1,0:T(8,128)(2,1)S(1)} collective-permute-done((bf16[1,64,128]{2,1,0:T(8,128)(2,1)S(1)}, bf16[1,64,128]{2,1,0:T(8,128)(2,1)S(1)}, u32[]{:S(2)}, u32[]{:S(2)}) %collective-permute-start.8) | collective-permute-done | bytes 16416 | tf_op jit(solution)/shard_map/ppermute | solution.py:428
  33.1 2.4 %collective-permute-start.12 = (bf16[4,64,128]{2,1,0:T(8,128)(2,1)S(1)}, bf16[4,64,128]{2,1,0:T(8,128)(2,1)S(1)}, u32[]{:S(2)}, u32[]{:S(2)}) collective-permute-start(bf16[4,64,128]{2,1,0:T(8,128)(2,1)S(1)} %local.1.rest_0_.rest_3_), channel_id=1, source_target_pairs={{0,6},{1,7},{2,4},{3,5},{4,2},{5,3},{6,0},{7,1},{8,14},{9,15},{10,... | collective-permute-start | bytes 196616 | tf_op jit(solution)/shard_map/ppermute | solution.py:428
  35.6 0.6 %collective-permute-start.11 = (bf16[4,64,128]{2,1,0:T(8,128)(2,1)S(1)}, bf16[4,64,128]{2,1,0:T(8,128)(2,1)S(1)}, u32[]{:S(2)}, u32[]{:S(2)}) collective-permute-start(bf16[4,64,128]{2,1,0:T(8,128)(2,1)S(1)} %local.1.rest_0_.rest_3_), channel_id=1, source_target_pairs={{0,2},{1,3},{2,0},{3,1},{4,6},{5,7},{6,4},{7,5},{8,10},{9,11},{10,... | collective-permute-start | bytes 196616 | tf_op jit(solution)/shard_map/ppermute | solution.py:428
  36.1 0.5 %collective-permute-start.10 = (bf16[4,64,128]{2,1,0:T(8,128)(2,1)S(1)}, bf16[4,64,128]{2,1,0:T(8,128)(2,1)S(1)}, u32[]{:S(2)}, u32[]{:S(2)}) collective-permute-start(bf16[4,64,128]{2,1,0:T(8,128)(2,1)S(1)} %local.1.rest_0_.rest_3_), channel_id=1, source_target_pairs={{0,4},{1,5},{2,6},{3,7},{4,0},{5,1},{6,2},{7,3},{8,12},{9,13},{10,... | collective-permute-start | bytes 196616 | tf_op jit(solution)/shard_map/ppermute | solution.py:428
  36.6 3.5 %fetch.5.rest_2_ = bf16[2048,2048]{1,0:T(8,128)(2,1)S(1)} custom-call(bf16[4096,2048]{1,0:T(8,128)(2,1)} %weight_ref.5, bf16[4,64,128]{2,1,0:T(8,128)(2,1)S(1)} %local.1.rest_0_.rest_3_), custom_call_target="tpu_custom_call" | custom-call | bytes 8388608 | tf_op jit(solution)/shard_map/fetch/pallas_call | solution.py:234
  40.1 0.0 collective-permute-done.12.rest_6_
  40.1 0.0 collective-permute-done.11.rest_5_
  40.1 0.3 collective-permute-done.10.rest_4_
  40.4 3.1 %output.1 = (f32[16,2048]{1,0:T(8,128)S(1)}, bf16[16,2048]{1,0:T(8,128)(2,1)S(1)}) custom-call(s32[1]{0:T(128)} %bitcast.place_ref, bf16[1536,2048]{1,0:T(8,128)(2,1)S(1)} %fetch.3.rest_0_, bf16[512,2048]{1,0:T(8,128)(2,1)S(1)} %fetch.4.refs_4_.rest_1_, bf16[2048,2048]{1,0:T(8,128)(2,1)S(1)} %fetch.5.rest_2_, bf16[4,64,128]{2,1,0:T(8,128)(2,1)S(1)} %local.1.rest_0_.rest_3_, ...), custom_call_target="tpu_custom_call" | custom-call | flops 536870912 | bytes 16777216 | tf_op jit(solution)/shard_map/output/pallas_call | solution.py:396
  43.5 0.0 collective-permute-start.13
  43.5 1.2 %collective-permute-done.13 = bf16[16,2048]{1,0:T(8,128)(2,1)S(1)} collective-permute-done((bf16[16,2048]{1,0:T(8,128)(2,1)S(1)}, bf16[16,2048]{1,0:T(8,128)(2,1)S(1)}, u32[]{:S(2)}, u32[]{:S(2)}) %collective-permute-start.13) | collective-permute-done | bytes 65568 | tf_op jit(solution)/shard_map/ppermute | solution.py:428
  44.8 0.6 %fusion = bf16[2,8,2048]{2,1,0:T(8,128)(2,1)} fusion(f32[16,2048]{1,0:T(8,128)S(1)} %get-tuple-element.33, bf16[16,2048]{1,0:T(8,128)(2,1)S(1)} %collective-permute-done.13), kind=kLoop, calls=%fused_computation.1 | loop fusion | flops 98304 | bytes 262144 | tf_op jit(solution)/shard_map/reshape | solution.py:477
  (2 shorter events, 0.0 us)
Async XLA Ops:
  0.6 2.8 %collective-permute-start = (bf16[16,2048]{1,0:T(8,128)(2,1)}, bf16[16,2048]{1,0:T(8,128)(2,1)S(1)}, u32[]{:S(2)}, u32[]{:S(2)}) collective-permute-start(bf16[16,2048]{1,0:T(8,128)(2,1)} %bitcast.11), channel_id=1, source_target_pairs={{0,1},{1,0},{2,3},{3,2},{4,5},{5,4},{6,7},{7,6},{8,9},{9,8},{10,11... | collective-permute-start | bytes 196616 | tf_op jit(solution)/shard_map/ppermute | solution.py:428
  9.4 6.7 %collective-permute-start.2 = (bf16[4,80,128]{2,1,0:T(8,128)(2,1)S(1)}, bf16[4,80,128]{2,1,0:T(8,128)(2,1)S(1)}, u32[]{:S(2)}, u32[]{:S(2)}) collective-permute-start(bf16[4,80,128]{2,1,0:T(8,128)(2,1)S(1)} %get-tuple-element.25), channel_id=1, source_target_pairs={{0,2},{1,3},{2,0},{3,1},{4,6},{5,7},{6,4},{7,5},{8,10},{9,11},{10,... | collective-permute-start | bytes 245768 | tf_op jit(solution)/shard_map/ppermute | solution.py:428
  12.0 6.0 %collective-permute-start.3 = (bf16[4,80,128]{2,1,0:T(8,128)(2,1)S(1)}, bf16[4,80,128]{2,1,0:T(8,128)(2,1)S(1)}, u32[]{:S(2)}, u32[]{:S(2)}) collective-permute-start(bf16[4,80,128]{2,1,0:T(8,128)(2,1)S(1)} %get-tuple-element.26), channel_id=1, source_target_pairs={{0,6},{1,7},{2,4},{3,5},{4,2},{5,3},{6,0},{7,1},{8,14},{9,15},{10,... | collective-permute-start | bytes 245768 | tf_op jit(solution)/shard_map/ppermute | solution.py:428
  13.6 4.6 %collective-permute-start.1 = (bf16[4,80,128]{2,1,0:T(8,128)(2,1)S(1)}, bf16[4,80,128]{2,1,0:T(8,128)(2,1)S(1)}, u32[]{:S(2)}, u32[]{:S(2)}) collective-permute-start(bf16[4,80,128]{2,1,0:T(8,128)(2,1)S(1)} %get-tuple-element.24.after_ref), channel_id=1, source_target_pairs={{0,4},{1,5},{2,6},{3,7},{4,0},{5,1},{6,2},{7,3},{8,12},{9,13},{10,... | collective-permute-start | bytes 245768 | tf_op jit(solution)/shard_map/ppermute | solution.py:428
  18.2 6.0 %collective-permute-start.5 = (bf16[1,80,128]{2,1,0:T(8,128)(2,1)S(1)}, bf16[1,80,128]{2,1,0:T(8,128)(2,1)S(1)}, u32[]{:S(2)}, u32[]{:S(2)}) collective-permute-start(bf16[1,80,128]{2,1,0:T(8,128)(2,1)S(1)} %get-tuple-element.29), channel_id=1, source_target_pairs={{0,8},{1,9},{2,10},{3,11},{4,12},{5,13},{6,14},{7,15},{8,0},{9,1},... | collective-permute-start | bytes 61448 | tf_op jit(solution)/shard_map/ppermute | solution.py:428
  21.0 4.1 %collective-permute-start.6 = (bf16[1,80,128]{2,1,0:T(8,128)(2,1)S(1)}, bf16[1,80,128]{2,1,0:T(8,128)(2,1)S(1)}, u32[]{:S(2)}, u32[]{:S(2)}) collective-permute-start(bf16[1,80,128]{2,1,0:T(8,128)(2,1)S(1)} %get-tuple-element.30), channel_id=1, source_target_pairs={{0,9},{1,8},{2,11},{3,10},{4,13},{5,12},{6,15},{7,14},{8,1},{9,0},... | collective-permute-start | bytes 61448 | tf_op jit(solution)/shard_map/ppermute | solution.py:428
  21.0 4.1 %copy-start = (bf16[1,384,512]{2,1,0:T(8,128)(2,1)S(1)}, bf16[1,384,512]{2,1,0:T(8,128)(2,1)}, u32[]{:S(2)}) copy-start(bf16[1,384,512]{2,1,0:T(8,128)(2,1)} %param.16) | copy-start | bytes 1179652
  21.0 4.1 %copy-start.1 = (bf16[1,384,512]{2,1,0:T(8,128)(2,1)S(1)}, bf16[1,384,512]{2,1,0:T(8,128)(2,1)}, u32[]{:S(2)}) copy-start(bf16[1,384,512]{2,1,0:T(8,128)(2,1)} %param.17) | copy-start | bytes 1179652
  21.0 4.1 %collective-permute-start.4 = (bf16[1,80,128]{2,1,0:T(8,128)(2,1)S(1)}, bf16[1,80,128]{2,1,0:T(8,128)(2,1)S(1)}, u32[]{:S(2)}, u32[]{:S(2)}) collective-permute-start(bf16[1,80,128]{2,1,0:T(8,128)(2,1)S(1)} %get-tuple-element.27.rest_0_), channel_id=1, source_target_pairs={{0,1},{1,0},{2,3},{3,2},{4,5},{5,4},{6,7},{7,6},{8,9},{9,8},{10,11... | collective-permute-start | bytes 61448 | tf_op jit(solution)/shard_map/ppermute | solution.py:428
  26.5 4.6 %collective-permute-start.9 = (bf16[1,64,128]{2,1,0:T(8,128)(2,1)S(1)}, bf16[1,64,128]{2,1,0:T(8,128)(2,1)S(1)}, u32[]{:S(2)}, u32[]{:S(2)}) collective-permute-start(bf16[1,64,128]{2,1,0:T(8,128)(2,1)S(1)} %get-tuple-element.32), channel_id=1, source_target_pairs={{0,9},{1,8},{2,11},{3,10},{4,13},{5,12},{6,15},{7,14},{8,1},{9,0},... | collective-permute-start | bytes 49160 | tf_op jit(solution)/shard_map/ppermute | solution.py:428
  28.0 3.1 %collective-permute-start.7 = (bf16[1,64,128]{2,1,0:T(8,128)(2,1)S(1)}, bf16[1,64,128]{2,1,0:T(8,128)(2,1)S(1)}, u32[]{:S(2)}, u32[]{:S(2)}) collective-permute-start(bf16[1,64,128]{2,1,0:T(8,128)(2,1)S(1)} %get-tuple-element.32), channel_id=1, source_target_pairs={{0,1},{1,0},{2,3},{3,2},{4,5},{5,4},{6,7},{7,6},{8,9},{9,8},{10,11... | collective-permute-start | bytes 49160 | tf_op jit(solution)/shard_map/ppermute | solution.py:428
  28.4 4.6 %collective-permute-start.8 = (bf16[1,64,128]{2,1,0:T(8,128)(2,1)S(1)}, bf16[1,64,128]{2,1,0:T(8,128)(2,1)S(1)}, u32[]{:S(2)}, u32[]{:S(2)}) collective-permute-start(bf16[1,64,128]{2,1,0:T(8,128)(2,1)S(1)} %get-tuple-element.31.rest_0_.refs_0_), channel_id=1, source_target_pairs={{0,8},{1,9},{2,10},{3,11},{4,12},{5,13},{6,14},{7,15},{8,0},{9,1},... | collective-permute-start | bytes 49160 | tf_op jit(solution)/shard_map/ppermute | solution.py:428
  33.1 7.0 %collective-permute-start.12 = (bf16[4,64,128]{2,1,0:T(8,128)(2,1)S(1)}, bf16[4,64,128]{2,1,0:T(8,128)(2,1)S(1)}, u32[]{:S(2)}, u32[]{:S(2)}) collective-permute-start(bf16[4,64,128]{2,1,0:T(8,128)(2,1)S(1)} %local.1.rest_0_.rest_3_), channel_id=1, source_target_pairs={{0,6},{1,7},{2,4},{3,5},{4,2},{5,3},{6,0},{7,1},{8,14},{9,15},{10,... | collective-permute-start | bytes 196616 | tf_op jit(solution)/shard_map/ppermute | solution.py:428
  35.6 4.6 %collective-permute-start.11 = (bf16[4,64,128]{2,1,0:T(8,128)(2,1)S(1)}, bf16[4,64,128]{2,1,0:T(8,128)(2,1)S(1)}, u32[]{:S(2)}, u32[]{:S(2)}) collective-permute-start(bf16[4,64,128]{2,1,0:T(8,128)(2,1)S(1)} %local.1.rest_0_.rest_3_), channel_id=1, source_target_pairs={{0,2},{1,3},{2,0},{3,1},{4,6},{5,7},{6,4},{7,5},{8,10},{9,11},{10,... | collective-permute-start | bytes 196616 | tf_op jit(solution)/shard_map/ppermute | solution.py:428
  36.1 4.3 %collective-permute-start.10 = (bf16[4,64,128]{2,1,0:T(8,128)(2,1)S(1)}, bf16[4,64,128]{2,1,0:T(8,128)(2,1)S(1)}, u32[]{:S(2)}, u32[]{:S(2)}) collective-permute-start(bf16[4,64,128]{2,1,0:T(8,128)(2,1)S(1)} %local.1.rest_0_.rest_3_), channel_id=1, source_target_pairs={{0,4},{1,5},{2,6},{3,7},{4,0},{5,1},{6,2},{7,3},{8,12},{9,13},{10,... | collective-permute-start | bytes 196616 | tf_op jit(solution)/shard_map/ppermute | solution.py:428
  43.5 1.3 %collective-permute-start.13 = (bf16[16,2048]{1,0:T(8,128)(2,1)S(1)}, bf16[16,2048]{1,0:T(8,128)(2,1)S(1)}, u32[]{:S(2)}, u32[]{:S(2)}) collective-permute-start(bf16[16,2048]{1,0:T(8,128)(2,1)S(1)} %get-tuple-element.34), channel_id=1, source_target_pairs={{0,1},{1,0},{2,3},{3,2},{4,5},{5,4},{6,7},{7,6},{8,9},{9,8},{10,11... | collective-permute-start | bytes 196616 | tf_op jit(solution)/shard_map/ppermute | solution.py:428

commit v11 on v10

--- a/solution.py
+++ b/solution.py
@@ -39,7 +39,7 @@
 
 
 def project_kernel(steps, group, colors, order, chunk, place_ref, mine_ref, other_ref, gain_ref, early_ref, wk_ref, wv_ref,
-                   wq_ref, *rest):
+                   wq_ref, keys_ref, values_ref, own_ref, send_ref, *rest):
     part_refs, rest = rest[:-5], rest[-5:]
     mine_buf, gain_buf, wq_buf, rows_buf, sems = rest
     early = early_ref.shape[1]
@@ -50,10 +50,17 @@
     for c in range(chunks):
         copies.append(pltpu.make_async_copy(
             wq_ref.at[:, early + c * chunk:early + (c + 1) * chunk], wq_buf.at[c], sems.at[c]))
+    device = place_ref[0]
+    slots, kv_half = keys_ref.shape[0], keys_ref.shape[1] // 2
+    for i, source in enumerate((keys_ref, values_ref)):
+        for j, (target, part) in enumerate(((send_ref, 1 - device % 2), (own_ref, device % 2))):
+            first = pl.multiple_of(part * kv_half, HD)
+            copies.append(pltpu.make_async_copy(
+                source.at[:, pl.ds(first, kv_half)], target.at[i * slots:(i + 1) * slots],
+                sems.at[chunks + 2 + 2 * i + j]))
     for copy in copies:
         copy.start()
 
-    device = place_ref[0]
     half_rows = mine_ref.shape[0]
     total_rows = 2 * half_rows
     half_seqs = half_rows // steps
@@ -97,6 +104,8 @@
         copies[2 + c].wait()
         first = (early + c * chunk) // HD
         multiply(wq_buf[c], lambda i: ((first + i) // group, (first + i) % group))
+    for copy in copies[2 + chunks:]:
+        copy.wait()
     per_part = part_refs[0].shape[0]
     for slot, pattern in enumerate(slot_patterns(order)):
         ref = part_refs[slot // per_part]
@@ -109,7 +118,7 @@
     return (jax.ShapeDtypeStruct(shape, jnp.float32),) + (jax.ShapeDtypeStruct(shape, jnp.bfloat16),) * (count - 1)
 
 
-def project(place, mine, other, gain, early, wk, wv, wq, steps, group, colors, order, count):
+def project(place, mine, other, gain, early, wk, wv, wq, keys, values, steps, group, colors, order, count):
     half_rows, depth = mine.shape
     q_cols, kv_cols = wq.shape[1], wk.shape[1]
     seqs = 2 * half_rows // steps
@@ -118,26 +127,28 @@
     vmem = pl.BlockSpec(memory_space=pltpu.VMEM)
     smem = pl.BlockSpec(memory_space=pltpu.SMEM)
     hbm = pl.BlockSpec(memory_space=pltpu.HBM)
-    out_shape = part_shapes(
+    cache = jax.ShapeDtypeStruct((2 * keys.shape[0], keys.shape[1] // 2), jnp.bfloat16)
+    out_shape = (cache, cache) + part_shapes(
         seqs, count, (colors * steps * (group + 4), HD))
     return pl.pallas_call(
         functools.partial(project_kernel, steps, group, colors, order, chunk),
         out_shape=out_shape,
-        in_specs=[smem, hbm, vmem, hbm, vmem, vmem, vmem, hbm],
+        in_specs=[smem, hbm, vmem, hbm, vmem, vmem, vmem, hbm, hbm, hbm],
         out_specs=(vmem,) * len(out_shape),
         scratch_shapes=[
             pltpu.VMEM(mine.shape, jnp.bfloat16),
             pltpu.VMEM(gain.shape, jnp.bfloat16),
             pltpu.VMEM((chunks, depth, chunk), jnp.bfloat16),
             pltpu.VMEM((seqs * colors * steps * (group + 4), HD), jnp.float32),
-            pltpu.SemaphoreType.DMA((chunks + 2,)),
+            pltpu.SemaphoreType.DMA((chunks + 6,)),
         ],
         compiler_params=pltpu.CompilerParams(vmem_limit_bytes=28 * MIB),
         cost_estimate=pl.CostEstimate(
             flops=4 * half_rows * depth * (q_cols + 2 * kv_cols),
             bytes_accessed=2 * depth * (q_cols + 2 * kv_cols), transcendentals=0),
         name="project",
-    )(place, in_hbm(mine), other, in_hbm(gain), in_vmem(early), in_vmem(wk), in_vmem(wv), in_hbm(wq))
+    )(place, in_hbm(mine), other, in_hbm(gain), in_vmem(early), in_vmem(wk), in_vmem(wv), in_hbm(wq),
+      in_hbm(keys), in_hbm(values))
 
 
 def fetch_first_kernel(wq_ref, wk_ref, wv_ref, early_ref, wk_out, wv_out, sems):
@@ -244,58 +255,64 @@
     )(in_hbm(weight), *after)
 
 
-def attend_kernel(steps, width, unused, place_ref, table_ref, keys_ref, values_ref, *rest):
-    rest = rest[unused:]
-    part_refs, (same_ref, cross_ref, new_keys_ref, new_values_ref) = rest[:-4], rest[-4:]
-    kv_heads = keys_ref.shape[1] // HD
-    half_kv = kv_heads // 2
-    pitch = part_refs[0].shape[1] // (half_kv * steps)
+def attend_kernel(steps, width, unused, notes_ref, came_notes_ref, own_ref, came_ref, *rest):
+    part_refs, (context_ref, fresh_ref, fresh_send_ref) = rest[unused:-3], rest[-3:]
+    slots = own_ref.shape[0] // 2
+    half_kv = own_ref.shape[1] // HD
+    total = functools.reduce(jnp.add, [ref[...].astype(jnp.float32) for ref in part_refs])
+    pitch = total.shape[1] // (half_kv * steps)
     group = pitch - 4
-    slots = keys_ref.shape[0]
     factor = 1.0 / math.sqrt(HD)
-    low_side = place_ref[0] % 2 == 0
-    same, cross = [
-        functools.reduce(jnp.add, [ref[0].astype(jnp.float32) for ref in part_refs[i::2]]) for i in range(2)]
-    halves = [jnp.where(low_side, same, cross), jnp.where(low_side, cross, same)]
     per_head = steps * group
-    lanes = kv_heads * per_head
+    groups = 2 * half_kv
+    lanes = groups * per_head
     fresh_rows = 16
-    fresh_keys = [[None] * kv_heads for _ in range(steps)]
-    fresh_values = [[None] * kv_heads for _ in range(steps)]
-    queries = [None] * kv_heads
-    for k in range(half_kv):
-        for g in range(2):
-            head = g * half_kv + k
+    notes = [notes_ref[...], came_notes_ref[...]]
+    fresh_keys = [[None] * groups for _ in range(steps)]
+    fresh_values = [[None] * groups for _ in range(steps)]
+    queries = []
+    for seq in range(2):
+        for k in range(half_kv):
+            index = seq * half_kv + k
             query = []
             for t in range(steps):
-                rows = halves[g][(k * steps + t) * pitch:(k * steps + t + 1) * pitch]
+                rows = total[seq, (k * steps + t) * pitch:(k * steps + t + 1) * pitch]
                 squares = rows[group + 2:group + 3] + rows[group + 3:group + 4]
                 rows = rows * lax.rsqrt(squares / width + epsilon)
-                cosine = table_ref[2 * t:2 * t + 1, :]
-                sine = table_ref[2 * t + 1:2 * t + 2, :]
+                cosine = notes[seq][2 * t:2 * t + 1]
+                sine = notes[seq][2 * t + 1:2 * t + 2]
                 turned = rows * cosine + pltpu.roll(rows, HD // 2, 1) * sine
                 query.append(turned[:group])
-                fresh_keys[t][head] = turned[group:group + 1]
-                fresh_values[t][head] = rows[group + 1:group + 2]
-            blocks = [jnp.zeros((per_head, HD), jnp.float32)] * kv_heads
-            blocks[head] = jnp.concatenate(query, axis=0)
-            queries[head] = jnp.concatenate(blocks, axis=1)
+                fresh_keys[t][index] = turned[group:group + 1]
+                fresh_values[t][index] = rows[group + 1:group + 2]
+            blocks = [jnp.zeros((per_head, HD), jnp.float32)] * groups
+            blocks[index] = jnp.concatenate(query, axis=0)
+            queries.append(jnp.concatenate(blocks, axis=1))
     queries = jnp.concatenate(queries, axis=0).astype(jnp.bfloat16)
-    padding = jnp.zeros((fresh_rows - steps, kv_heads * HD), jnp.float32)
-    fresh_keys, fresh_values = [
-        jnp.concatenate([jnp.concatenate(row, axis=1) for row in fresh] + [padding], axis=0).astype(jnp.bfloat16)
+    keys_now, values_now = [
+        jnp.concatenate([jnp.concatenate(row, axis=1) for row in fresh], axis=0)
         for fresh in (fresh_keys, fresh_values)]
-    new_keys_ref[...] = fresh_keys[:steps]
-    new_values_ref[...] = fresh_values[:steps]
-
-    length = table_ref[2 * steps:2 * steps + 1, :1].astype(jnp.int32)
+    half = half_kv * HD
+    for seq, ref in enumerate((fresh_ref, fresh_send_ref)):
+        span = slice(seq * half, (seq + 1) * half)
+        ref[...] = jnp.concatenate(
+            [keys_now[:, span], values_now[:, span], jnp.zeros((fresh_rows - 2 * steps, half), jnp.float32)],
+            axis=0).astype(jnp.bfloat16)
+    padding = jnp.zeros((fresh_rows - steps, groups * HD), jnp.float32)
+    keys_now, values_now = [
+        jnp.concatenate([fresh, padding], axis=0).astype(jnp.bfloat16) for fresh in (keys_now, values_now)]
+
+    keys = jnp.concatenate([own_ref[:slots, :], came_ref[:slots, :]], axis=1)
+    values = jnp.concatenate([own_ref[slots:, :], came_ref[slots:2 * slots, :]], axis=1)
+    lane = lax.broadcasted_iota(jnp.int32, (1, lanes), 1)
+    lengths = [note[2 * steps:2 * steps + 1, :1].astype(jnp.int32) for note in notes]
+    length = jnp.where(lane < half_kv * per_head, lengths[0], lengths[1])
     live = lax.broadcasted_iota(jnp.int32, (slots, lanes), 0) < length
-    lane_step = (lax.broadcasted_iota(jnp.int32, (fresh_rows, lanes), 1) % per_head) // group
-    seen = lax.broadcasted_iota(jnp.int32, (fresh_rows, lanes), 0) <= lane_step
+    seen = lax.broadcasted_iota(jnp.int32, (fresh_rows, lanes), 0) <= (lane % per_head) // group
     over_last, over_first = (((1,), (1,)), ((), ())), (((0,), (0,)), ((), ()))
-    scores = lax.dot_general(keys_ref[...], queries, over_last, preferred_element_type=jnp.float32) * factor
+    scores = lax.dot_general(keys, queries, over_last, preferred_element_type=jnp.float32) * factor
     scores = jnp.where(live, scores, -jnp.inf)
-    fresh = lax.dot_general(fresh_keys, queries, over_last, preferred_element_type=jnp.float32) * factor
+    fresh = lax.dot_general(keys_now, queries, over_last, preferred_element_type=jnp.float32) * factor
     fresh = jnp.where(seen, fresh, -jnp.inf)
     top = jnp.maximum(jnp.max(scores, axis=0, keepdims=True), jnp.max(fresh, axis=0, keepdims=True))
     scores = jnp.exp(scores - top)
@@ -303,31 +320,25 @@
     inverse = 1.0 / (jnp.sum(scores, axis=0, keepdims=True) + jnp.sum(fresh, axis=0, keepdims=True))
     weights = (scores * inverse).astype(jnp.bfloat16)
     fresh = (fresh * inverse).astype(jnp.bfloat16)
-    mixed = lax.dot_general(weights, values_ref[...], over_first, preferred_element_type=jnp.float32)
-    mixed = mixed + lax.dot_general(fresh, fresh_values, over_first, preferred_element_type=jnp.float32)
-    contexts = [
-        mixed[head * per_head:(head + 1) * per_head, head * HD:(head + 1) * HD] for head in range(kv_heads)]
-    for k in range(half_kv):
-        lower, upper = contexts[k], contexts[half_kv + k]
-        span = slice(k * steps * group, (k + 1) * steps * group)
-        same_ref[0, span, :] = jnp.where(low_side, lower, upper).astype(jnp.bfloat16)
-        cross_ref[0, span, :] = jnp.where(low_side, upper, lower).astype(jnp.bfloat16)
-
-
-def attend(place, parts, table, keys, values, held, steps, width, half_heads):
-    vmem = pl.BlockSpec(memory_space=pltpu.VMEM)
-    smem = pl.BlockSpec(memory_space=pltpu.SMEM)
-    kv_cols = keys.shape[1]
-    half = jax.ShapeDtypeStruct((1, steps * half_heads, HD), jnp.bfloat16)
-    fresh = jax.ShapeDtypeStruct((steps, kv_cols), jnp.bfloat16)
+    mixed = lax.dot_general(weights, values, over_first, preferred_element_type=jnp.float32)
+    mixed = mixed + lax.dot_general(fresh, values_now, over_first, preferred_element_type=jnp.float32)
+    for index in range(groups):
+        seq, k = index // half_kv, index % half_kv
+        context_ref[seq, k * per_head:(k + 1) * per_head, :] = mixed[
+            index * per_head:(index + 1) * per_head, index * HD:(index + 1) * HD].astype(jnp.bfloat16)
+
+
+def attend(notes, came_notes, own, came, parts, held, steps, width, half_heads):
+    vmem = pl.BlockSpec(memory_space=pltpu.VMEM)
+    fresh = jax.ShapeDtypeStruct((16, own.shape[1]), jnp.bfloat16)
     return pl.pallas_call(
         functools.partial(attend_kernel, steps, width, len(held)),
-        out_shape=(half, half, fresh, fresh),
-        in_specs=[smem] + [vmem] * 3 + [pl.BlockSpec(memory_space=pl.ANY)] * len(held) + [vmem] * len(parts),
-        out_specs=(vmem,) * 4,
+        out_shape=(jax.ShapeDtypeStruct((2, steps * half_heads, HD), jnp.bfloat16), fresh, fresh),
+        in_specs=[vmem] * 4 + [pl.BlockSpec(memory_space=pl.ANY)] * len(held) + [vmem] * len(parts),
+        out_specs=(vmem,) * 3,
         compiler_params=pltpu.CompilerParams(vmem_limit_bytes=16 * MIB),
         name="attend",
-    )(place, table, keys, values, *[in_vmem(piece) for piece in held], *parts)
+    )(notes, came_notes, own, came, *[in_vmem(piece) for piece in held], *parts)
 
 
 def join_kernel(arrived, *refs):
@@ -349,7 +360,7 @@
     )(*arrays, *[in_vmem(piece) for piece in held])
 
 
-def output_kernel(steps, colors, patterns, pieces, place_ref, *rest):
+def output_kernel(steps, colors, patterns, pieces, place_ref, fresh_ref, *rest):
     weight_refs, context_refs = rest[:pieces], rest[pieces:-4]
     mine_ref, other_ref, wide_buf, rows_buf = rest[-4:]
     device = place_ref[0]
@@ -371,6 +382,10 @@
         rows_buf[:, head * HD:(head + 1) * HD] = jnp.concatenate(lines, axis=0).astype(jnp.bfloat16)
     low_side = device % 2 == 0
     half = rows_buf.shape[0] // 2
+    other_ref[half:, :fresh_ref.shape[1]] = fresh_ref[...]
+    if other_ref.shape[1] > fresh_ref.shape[1]:
+        other_ref[half:, fresh_ref.shape[1]:] = jnp.zeros(
+            (fresh_ref.shape[0], other_ref.shape[1] - fresh_ref.shape[1]), jnp.bfloat16)
     columns = mine_ref.shape[1]
     chunk = min(columns, 512)
     for c in range(columns // chunk):
@@ -383,10 +398,10 @@
             first = last
         lower, upper = product[:half], product[half:]
         mine_ref[:, span] = jnp.where(low_side, lower, upper)
-        other_ref[:, span] = jnp.where(low_side, upper, lower).astype(jnp.bfloat16)
-
-
-def output(place, contexts, patterns, held, steps, colors):
+        other_ref[:half, span] = jnp.where(low_side, upper, lower).astype(jnp.bfloat16)
+
+
+def output(place, fresh, contexts, patterns, held, steps, colors):
     columns = held[0].shape[1]
     depth = sum(piece.shape[0] for piece in held)
     devices = len(patterns)
@@ -397,9 +412,9 @@
         functools.partial(output_kernel, steps, colors, patterns, len(held)),
         out_shape=(
             jax.ShapeDtypeStruct((half, columns), jnp.float32),
-            jax.ShapeDtypeStruct((half, columns), jnp.bfloat16),
+            jax.ShapeDtypeStruct((half + fresh.shape[0], columns), jnp.bfloat16),
         ),
-        in_specs=[smem] + [vmem] * (len(held) + len(contexts)),
+        in_specs=[smem, vmem] + [vmem] * (len(held) + len(contexts)),
         out_specs=(vmem, vmem),
         scratch_shapes=[
             pltpu.VMEM((devices * contexts[0].shape[1], HD), jnp.float32),
@@ -410,7 +425,32 @@
             flops=2 * devices * steps * depth * columns,
             bytes_accessed=2 * depth * columns, transcendentals=0),
         name="output",
-    )(place, *[in_vmem(piece) for piece in held], *contexts)
+    )(place, fresh, *[in_vmem(piece) for piece in held], *contexts)
+
+
+def finish_kernel(steps, place_ref, mine_ref, came_ref, fresh_ref, result_ref, new_keys_ref, new_values_ref):
+    half = mine_ref.shape[0]
+    result_ref[...] = (mine_ref[...] + came_ref[:half, :].astype(jnp.float32)).astype(jnp.bfloat16)
+    own = fresh_ref[...].astype(jnp.float32)
+    came = came_ref[half:, :own.shape[1]].astype(jnp.float32)
+    low_side = place_ref[0] % 2 == 0
+    rows = jnp.concatenate(
+        [jnp.where(low_side, own, came), jnp.where(low_side, came, own)], axis=1).astype(jnp.bfloat16)
+    new_keys_ref[...] = rows[:steps]
+    new_values_ref[...] = rows[steps:2 * steps]
+
+
+def finish(place, mine, came, fresh, steps):
+    vmem = pl.BlockSpec(memory_space=pltpu.VMEM)
+    new = jax.ShapeDtypeStruct((steps, 2 * fresh.shape[1]), jnp.bfloat16)
+    return pl.pallas_call(
+        functools.partial(finish_kernel, steps),
+        out_shape=(jax.ShapeDtypeStruct(mine.shape, jnp.bfloat16), new, new),
+        in_specs=[pl.BlockSpec(memory_space=pltpu.SMEM)] + [vmem] * 3,
+        out_specs=(vmem,) * 3,
+        compiler_params=pltpu.CompilerParams(vmem_limit_bytes=8 * MIB),
+        name="finish",
+    )(place, mine, came, fresh)
 
 
 def body(hidden_in, norm_gain, query_weight, key_weight, value_weight, out_weight,
@@ -428,8 +468,7 @@
         return lax.ppermute(array, everyone, [(i, i ^ pattern) for i in range(devices)])
 
     stages = [list(range(first, min(first + 2, bits))) for first in range(1, bits, 2)]
-    stages[-1] = stages[-1] + [0]
-    order = [bit for stage in stages for bit in stage]
+    order = [bit for stage in stages for bit in stage] + [0]
     total = out_weight.shape[0]
     cuts = [total * i // 8 for i in (0, 3, 4, 8)]
     held = []
@@ -444,35 +483,32 @@
     mine = hidden_in.reshape(steps * half_seqs, depth)
     other = partner(mine, 1)
     early, wk, wv = fetch_first(query_weight, key_weight, value_weight, 512)
-    parts = project(
+    own, cache, *parts = project(
         place, mine, other, norm_gain.reshape(-1, HD), early, wk, wv, query_weight,
+        cache_keys[0], cache_values[0],
         steps, group, colors, order, 1 << len(stages[0]))
+    cache = partner(cache, 1)
     notes = take_notes(positions, lengths, parts[1], steps)
+    came_notes = partner(notes, 1)
     for i, stage in enumerate(stages):
         came = [partner(part, pattern) for part, pattern in zip(parts[1:], slot_patterns(stage)[1:])]
         now = fetch_next(i, [parts[1], notes])
         if i < len(stages) - 1:
             parts = combine(parts[0], came, now, notes, 1 << len(stages[i + 1]))
-    same, cross, new_keys, new_values = attend(
-        place, [parts[0], *came], notes, cache_keys[0], cache_values[0], now,
-        steps, depth * lax.axis_size("gx"), half_heads)
-
-    context, patterns = None, [0]
+    context, fresh, fresh_send = attend(
+        notes, came_notes, own, cache, [parts[0], *came], now, steps, depth * lax.axis_size("gx"), half_heads)
+
+    patterns = [0, 1]
     for i, stage in enumerate(stages[::-1]):
         moves = slot_patterns(stage)
-        if i == 0:
-            context = same
-            came = [partner(cross if move & 1 else same, move) for move in moves[1:]]
-        else:
-            came = [partner(context, move) for move in moves[1:]]
+        came = [partner(context, move) for move in moves[1:]]
         patterns = [p ^ move for move in moves for p in patterns]
         now = fetch_next(len(stages) + i, [context])
         if i < len(stages) - 1:
             shape = (len(moves) * context.shape[0],) + context.shape[1:]
             context = local_call(functools.partial(join_kernel, len(came)), shape, [context, *came], now)
-    mine, other = output(place, [context, *came], patterns, held, steps, colors)
-    other = partner(other, 1)
-    result = (mine + other.astype(jnp.float32)).astype(jnp.bfloat16)
+    mine, other = output(place, fresh_send, [context, *came], patterns, held, steps, colors)
+    result, new_keys, new_values = finish(place, mine, partner(other, 1), fresh, steps)
     return (
         result.reshape(steps, half_seqs, -1),
         new_keys[:, None, :],

time: 45.6 us -> 42.5 us (0.932)
  waiting for transfers between devices: 7.67 us -> 5.7 us
  starting transfers between devices: 14.3 us -> 13.5 us
  other arithmetic: 0.64 us -> 0 us
    ppermute x14 -> x12, waiting for transfers between devices: 7.67 us -> 5.7 us  [partner(): lax.ppermute(array, everyone, [(i, i ^ pattern) for i in range(devices)])]
    ppermute x14 -> x12, starting transfers between devices: 14.3 us -> 13.5 us  [partner(): lax.ppermute(array, everyone, [(i, i ^ pattern) for i in range(devices)])]
    pallas_call x0 -> x1, Pallas kernels: none -> 0.65 us  [finish(): pl.pallas_call(functools.partial(finish_kernel, steps), out_shape=(jax.Sh...]
    reshape x1 -> x0, other arithmetic: 0.64 us -> none  [body(): result.reshape(steps, half_seqs, -1)]
  transfers between devices with their start and end apart: 14 -> 12, of which waited for: 7 -> 4; matrix products, arithmetic and copies ran while one was open for 0% -> 0% of each run, Pallas kernels for 23% -> 24%
where the time goes in v11:
time: 42.5 us; the launch traced here: 42.3 us
  Pallas kernels  21 us (49%)
  starting transfers between devices  13.5 us (32%)
  waiting for transfers between devices  5.7 us (13%)
  between operations  2.05 us (5%)
    ppermute x12, starting transfers between devices, partner(): lax.ppermute(array, everyone, [(i, i ^ pattern) for i in range(devices)])  13.5 us
    pallas_call x3, Pallas kernels, fetch(): pl.pallas_call(functools.partial(fetch_kernel, first, parts), out_shape=p...  7.91 us
    pallas_call x1, Pallas kernels, project(): pl.pallas_call(functools.partial(project_kernel, steps, group, colors, or...  6.04 us
    ppermute x12, waiting for transfers between devices, partner(): lax.ppermute(array, everyone, [(i, i ^ pattern) for i in range(devices)])  5.7 us
    pallas_call x1, Pallas kernels, output(): pl.pallas_call(functools.partial(output_kernel, steps, colors, patterns,...  3.14 us
    pallas_call x1, Pallas kernels, fetch_first(): pl.pallas_call(fetch_first_kernel, out_shape=(pltpu.VMEM((depth, early),...  2.26 us
    pallas_call x1, Pallas kernels, attend(): pl.pallas_call(functools.partial(attend_kernel, steps, width, len(held)),...  0.88 us
  transfers between devices with their start and end apart: 12, of which 4 were waited for; matrix products, arithmetic and copies ran while one was open for 0% of the time, Pallas kernels for 24%

profile of v11, /device:TPU:0, one launch (start us, length us, event | category | flops | bytes accessed | tf_op | source)
XLA Modules:
  0.0 42.3 jit_solution(968265489310350844)
XLA Ops:
  0.6 0.5 %collective-permute-start = (bf16[16,2048]{1,0:T(8,128)(2,1)}, bf16[16,2048]{1,0:T(8,128)(2,1)S(1)}, u32[]{:S(2)}, u32[]{:S(2)}) collective-permute-start(bf16[16,2048]{1,0:T(8,128)(2,1)} %bitcast.10), channel_id=1, source_target_pairs={{0,1},{1,0},{2,3},{3,2},{4,5},{5,4},{6,7},{7,6},{8,9},{9,8},{10,11... | collective-permute-start | bytes 196616 | tf_op jit(solution)/shard_map/ppermute | solution.py:468
  1.1 2.3 %fetch_first.1 = (bf16[2048,512]{1,0:T(8,128)(2,1)S(1)}, bf16[2048,256]{1,0:T(8,128)(2,1)S(1)}, bf16[2048,256]{1,0:T(8,128)(2,1)S(1)}) custom-call(bf16[2048,4096]{1,0:T(8,128)(2,1)} %wq_ref.3, bf16[2048,256]{1,0:T(8,128)(2,1)} %wk_ref.1, bf16[2048,256]{1,0:T(8,128)(2,1)} %wv_ref.1), custom_call_target="tpu_custom_call" | custom-call | bytes 4194304 | tf_op jit(solution)/shard_map/fetch_first/pallas_call | solution.py:169
  3.4 0.0 collective-permute-done.other_ref
  3.4 6.0 %project.1 = (bf16[768,256]{1,0:T(8,128)(2,1)S(1)}, bf16[768,256]{1,0:T(8,128)(2,1)S(1)}, f32[4,80,128]{2,1,0:T(8,128)S(1)}, bf16[4,80,128]{2,1,0:T(8,128)(2,1)S...) custom-call(s32[1]{0:T(128)} %bitcast.place_ref, bf16[16,2048]{1,0:T(8,128)(2,1)} %bitcast.11, ...), custom_call_target="tpu_custom_call" | custom-call | flops 603979776 | bytes 18874368 | tf_op jit(solution)/shard_map/project/pallas_call | solution.py:133
  9.5 0.1 collective-permute-start.2
  9.6 2.9 %collective-permute-start.4 = (bf16[4,80,128]{2,1,0:T(8,128)(2,1)S(1)}, bf16[4,80,128]{2,1,0:T(8,128)(2,1)S(1)}, u32[]{:S(2)}, u32[]{:S(2)}) collective-permute-start(bf16[4,80,128]{2,1,0:T(8,128)(2,1)S(1)} %get-tuple-element.29), channel_id=1, source_target_pairs={{0,2},{1,3},{2,0},{3,1},{4,6},{5,7},{6,4},{7,5},{8,10},{9,11},{10,... | collective-permute-start | bytes 245768 | tf_op jit(solution)/shard_map/ppermute | solution.py:468
  12.5 1.5 %collective-permute-start.5 = (bf16[4,80,128]{2,1,0:T(8,128)(2,1)S(1)}, bf16[4,80,128]{2,1,0:T(8,128)(2,1)S(1)}, u32[]{:S(2)}, u32[]{:S(2)}) collective-permute-start(bf16[4,80,128]{2,1,0:T(8,128)(2,1)S(1)} %get-tuple-element.30), channel_id=1, source_target_pairs={{0,6},{1,7},{2,4},{3,5},{4,2},{5,3},{6,0},{7,1},{8,14},{9,15},{10,... | collective-permute-start | bytes 245768 | tf_op jit(solution)/shard_map/ppermute | solution.py:468
  14.1 0.0 collective-permute-start.3
  15.4 0.1 notes.1.refs_4_.rest_1_.notes_ref
  15.5 0.8 %collective-permute-done.4.refs_2_ = bf16[4,80,128]{2,1,0:T(8,128)(2,1)S(1)} collective-permute-done((bf16[4,80,128]{2,1,0:T(8,128)(2,1)S(1)}, bf16[4,80,128]{2,1,0:T(8,128)(2,1)S(1)}, u32[]{:S(2)}, u32[]{:S(2)}) %collective-permute-start.4) | collective-permute-done | bytes 81952 | tf_op jit(solution)/shard_map/ppermute | solution.py:468
  16.3 2.3 %collective-permute-done.5.refs_3_ = bf16[4,80,128]{2,1,0:T(8,128)(2,1)S(1)} collective-permute-done((bf16[4,80,128]{2,1,0:T(8,128)(2,1)S(1)}, bf16[4,80,128]{2,1,0:T(8,128)(2,1)S(1)}, u32[]{:S(2)}, u32[]{:S(2)}) %collective-permute-start.5) | collective-permute-done | bytes 81952 | tf_op jit(solution)/shard_map/ppermute | solution.py:468
  18.6 0.0 collective-permute-done.3.refs_1_
  18.7 2.7 %collective-permute-start.6 = (bf16[2,80,128]{2,1,0:T(8,128)(2,1)S(1)}, bf16[2,80,128]{2,1,0:T(8,128)(2,1)S(1)}, u32[]{:S(2)}, u32[]{:S(2)}) collective-permute-start(bf16[2,80,128]{2,1,0:T(8,128)(2,1)S(1)} %get-tuple-element.31.rest_0_), channel_id=1, source_target_pairs={{0,8},{1,9},{2,10},{3,11},{4,12},{5,13},{6,14},{7,15},{8,0},{9,1},... | collective-permute-start | bytes 122888 | tf_op jit(solution)/shard_map/ppermute | solution.py:468
  21.4 0.0 collective-permute-start.1
  21.4 2.9 %fetch.3.rest_0_ = bf16[1536,2048]{1,0:T(8,128)(2,1)S(1)} custom-call(bf16[4096,2048]{1,0:T(8,128)(2,1)} %weight_ref.5, bf16[2,80,128]{2,1,0:T(8,128)(2,1)S(1)} %get-tuple-element.31.rest_0_, f32[8,128]{1,0:T(8,128)S(1)} %notes.1.refs_4_.rest_1_.notes_ref), custom_call_target="tpu_custom_call" | custom-call | bytes 6291456 | tf_op jit(solution)/shard_map/fetch/pallas_call | solution.py:245
  24.3 0.0 collective-permute-done.1.came_notes_ref
  24.3 0.0 collective-permute-done.6.rest_2_
  24.3 0.0 collective-permute-done.2.came_ref
  24.3 0.9 %attend.1 = (bf16[2,64,128]{2,1,0:T(8,128)(2,1)S(1)}, bf16[16,256]{1,0:T(8,128)(2,1)S(1)}, bf16[16,256]{1,0:T(8,128)(2,1)S(1)}) custom-call(f32[8,128]{1,0:T(8,128)S(1)} %notes.1.refs_4_.rest_1_.notes_ref, f32[8,128]{1,0:T(8,128)S(1)} %collective-permute-done.1.came_notes_ref, bf16[768,256]{1,0:T(8,128)(2,1)S(1)} %get-tuple-element.26.own_ref, ...), custom_call_target="tpu_custom_call" | custom-call | tf_op jit(solution)/shard_map/attend/pallas_call | solution.py:334
  25.2 2.2 %collective-permute-start.7 = (bf16[2,64,128]{2,1,0:T(8,128)(2,1)S(1)}, bf16[2,64,128]{2,1,0:T(8,128)(2,1)S(1)}, u32[]{:S(2)}, u32[]{:S(2)}) collective-permute-start(bf16[2,64,128]{2,1,0:T(8,128)(2,1)S(1)} %get-tuple-element.34.rest_0_.refs_0_), channel_id=1, source_target_pairs={{0,8},{1,9},{2,10},{3,11},{4,12},{5,13},{6,14},{7,15},{8,0},{9,1},... | collective-permute-start | bytes 98312 | tf_op jit(solution)/shard_map/ppermute | solution.py:468
  27.4 1.5 %fetch.4.refs_2_.rest_1_ = bf16[512,2048]{1,0:T(8,128)(2,1)S(1)} custom-call(bf16[4096,2048]{1,0:T(8,128)(2,1)} %weight_ref.5, bf16[2,64,128]{2,1,0:T(8,128)(2,1)S(1)} %get-tuple-element.34.rest_0_.refs_0_), custom_call_target="tpu_custom_call" | custom-call | bytes 2097152 | tf_op jit(solution)/shard_map/fetch/pallas_call | solution.py:245
  28.9 1.2 %collective-permute-done.7.refs_1_ = bf16[2,64,128]{2,1,0:T(8,128)(2,1)S(1)} collective-permute-done((bf16[2,64,128]{2,1,0:T(8,128)(2,1)S(1)}, bf16[2,64,128]{2,1,0:T(8,128)(2,1)S(1)}, u32[]{:S(2)}, u32[]{:S(2)}) %collective-permute-start.7) | collective-permute-done | bytes 32800 | tf_op jit(solution)/shard_map/ppermute | solution.py:468
  30.1 2.2 %collective-permute-start.10 = (bf16[4,64,128]{2,1,0:T(8,128)(2,1)S(1)}, bf16[4,64,128]{2,1,0:T(8,128)(2,1)S(1)}, u32[]{:S(2)}, u32[]{:S(2)}) collective-permute-start(bf16[4,64,128]{2,1,0:T(8,128)(2,1)S(1)} %local.1.rest_0_.rest_3_), channel_id=1, source_target_pairs={{0,6},{1,7},{2,4},{3,5},{4,2},{5,3},{6,0},{7,1},{8,14},{9,15},{10,... | collective-permute-start | bytes 196616 | tf_op jit(solution)/shard_map/ppermute | solution.py:468
  32.3 0.6 %collective-permute-start.9 = (bf16[4,64,128]{2,1,0:T(8,128)(2,1)S(1)}, bf16[4,64,128]{2,1,0:T(8,128)(2,1)S(1)}, u32[]{:S(2)}, u32[]{:S(2)}) collective-permute-start(bf16[4,64,128]{2,1,0:T(8,128)(2,1)S(1)} %local.1.rest_0_.rest_3_), channel_id=1, source_target_pairs={{0,2},{1,3},{2,0},{3,1},{4,6},{5,7},{6,4},{7,5},{8,10},{9,11},{10,... | collective-permute-start | bytes 196616 | tf_op jit(solution)/shard_map/ppermute | solution.py:468
  32.9 0.7 %collective-permute-start.8 = (bf16[4,64,128]{2,1,0:T(8,128)(2,1)S(1)}, bf16[4,64,128]{2,1,0:T(8,128)(2,1)S(1)}, u32[]{:S(2)}, u32[]{:S(2)}) collective-permute-start(bf16[4,64,128]{2,1,0:T(8,128)(2,1)S(1)} %local.1.rest_0_.rest_3_), channel_id=1, source_target_pairs={{0,4},{1,5},{2,6},{3,7},{4,0},{5,1},{6,2},{7,3},{8,12},{9,13},{10,... | collective-permute-start | bytes 196616 | tf_op jit(solution)/shard_map/ppermute | solution.py:468
  33.6 3.5 %fetch.5.rest_2_ = bf16[2048,2048]{1,0:T(8,128)(2,1)S(1)} custom-call(bf16[4096,2048]{1,0:T(8,128)(2,1)} %weight_ref.5, bf16[4,64,128]{2,1,0:T(8,128)(2,1)S(1)} %local.1.rest_0_.rest_3_), custom_call_target="tpu_custom_call" | custom-call | bytes 8388608 | tf_op jit(solution)/shard_map/fetch/pallas_call | solution.py:245
  37.1 0.0 collective-permute-done.10.rest_6_
  37.1 0.0 collective-permute-done.9.rest_5_
  37.1 0.0 collective-permute-done.8.rest_4_
  37.2 3.1 %output.1 = (f32[16,2048]{1,0:T(8,128)S(1)}, bf16[32,2048]{1,0:T(8,128)(2,1)S(1)}) custom-call(s32[1]{0:T(128)} %bitcast.place_ref, bf16[16,256]{1,0:T(8,128)(2,1)S(1)} %get-tuple-element.33.fresh_ref, bf16[1536,2048]{1,0:T(8,128)(2,1)S(1)} %fetch.3.rest_0_, bf16[512,2048]{1,0:T(8,128)(2,1)S(1)} %fetch.4.refs_2_.rest_1_, ...), custom_call_target="tpu_custom_call" | custom-call | flops 536870912 | bytes 16777216 | tf_op jit(solution)/shard_map/output/pallas_call | solution.py:411
  40.3 0.0 collective-permute-start.11
  40.3 1.3 %collective-permute-done.11.came_ref = bf16[32,2048]{1,0:T(8,128)(2,1)S(1)} collective-permute-done((bf16[32,2048]{1,0:T(8,128)(2,1)S(1)}, bf16[32,2048]{1,0:T(8,128)(2,1)S(1)}, u32[]{:S(2)}, u32[]{:S(2)}) %collective-permute-start.11) | collective-permute-done | bytes 131104 | tf_op jit(solution)/shard_map/ppermute | solution.py:468
  41.7 0.7 %finish.1 = (bf16[16,2048]{1,0:T(8,128)(2,1)}, bf16[2,512]{1,0:T(2,128)(2,1)}, bf16[2,512]{1,0:T(2,128)(2,1)}) custom-call(s32[1]{0:T(128)} %bitcast.place_ref, f32[16,2048]{1,0:T(8,128)S(1)} %get-tuple-element.35.mine_ref, bf16[32,2048]{1,0:T(8,128)(2,1)S(1)} %collective-permute-done.11.came_ref, bf16[16,256]{1,0:T(8,128)(2,1)S(1)} %get-tuple-element.37.fresh_ref), custom_call_target="tpu_custom_call" | custom-call | tf_op jit(solution)/shard_map/finish/pallas_call | solution.py:446
  (2 shorter events, 0.0 us)
Async XLA Ops:
  0.6 2.8 %collective-permute-start = (bf16[16,2048]{1,0:T(8,128)(2,1)}, bf16[16,2048]{1,0:T(8,128)(2,1)S(1)}, u32[]{:S(2)}, u32[]{:S(2)}) collective-permute-start(bf16[16,2048]{1,0:T(8,128)(2,1)} %bitcast.10), channel_id=1, source_target_pairs={{0,1},{1,0},{2,3},{3,2},{4,5},{5,4},{6,7},{7,6},{8,9},{9,8},{10,11... | collective-permute-start | bytes 196616 | tf_op jit(solution)/shard_map/ppermute | solution.py:468
  9.5 14.8 %collective-permute-start.2 = (bf16[768,256]{1,0:T(8,128)(2,1)S(1)}, bf16[768,256]{1,0:T(8,128)(2,1)S(1)}, u32[]{:S(2)}, u32[]{:S(2)}) collective-permute-start(bf16[768,256]{1,0:T(8,128)(2,1)S(1)} %get-tuple-element.27), channel_id=1, source_target_pairs={{0,1},{1,0},{2,3},{3,2},{4,5},{5,4},{6,7},{7,6},{8,9},{9,8},{10,11... | collective-permute-start | bytes 1179656 | tf_op jit(solution)/shard_map/ppermute | solution.py:468
  9.6 6.7 %collective-permute-start.4 = (bf16[4,80,128]{2,1,0:T(8,128)(2,1)S(1)}, bf16[4,80,128]{2,1,0:T(8,128)(2,1)S(1)}, u32[]{:S(2)}, u32[]{:S(2)}) collective-permute-start(bf16[4,80,128]{2,1,0:T(8,128)(2,1)S(1)} %get-tuple-element.29), channel_id=1, source_target_pairs={{0,2},{1,3},{2,0},{3,1},{4,6},{5,7},{6,4},{7,5},{8,10},{9,11},{10,... | collective-permute-start | bytes 245768 | tf_op jit(solution)/shard_map/ppermute | solution.py:468
  12.5 6.1 %collective-permute-start.5 = (bf16[4,80,128]{2,1,0:T(8,128)(2,1)S(1)}, bf16[4,80,128]{2,1,0:T(8,128)(2,1)S(1)}, u32[]{:S(2)}, u32[]{:S(2)}) collective-permute-start(bf16[4,80,128]{2,1,0:T(8,128)(2,1)S(1)} %get-tuple-element.30), channel_id=1, source_target_pairs={{0,6},{1,7},{2,4},{3,5},{4,2},{5,3},{6,0},{7,1},{8,14},{9,15},{10,... | collective-permute-start | bytes 245768 | tf_op jit(solution)/shard_map/ppermute | solution.py:468
  14.1 4.5 %collective-permute-start.3 = (bf16[4,80,128]{2,1,0:T(8,128)(2,1)S(1)}, bf16[4,80,128]{2,1,0:T(8,128)(2,1)S(1)}, u32[]{:S(2)}, u32[]{:S(2)}) collective-permute-start(bf16[4,80,128]{2,1,0:T(8,128)(2,1)S(1)} %get-tuple-element.25.after_ref), channel_id=1, source_target_pairs={{0,4},{1,5},{2,6},{3,7},{4,0},{5,1},{6,2},{7,3},{8,12},{9,13},{10,... | collective-permute-start | bytes 245768 | tf_op jit(solution)/shard_map/ppermute | solution.py:468
  18.7 5.6 %collective-permute-start.6 = (bf16[2,80,128]{2,1,0:T(8,128)(2,1)S(1)}, bf16[2,80,128]{2,1,0:T(8,128)(2,1)S(1)}, u32[]{:S(2)}, u32[]{:S(2)}) collective-permute-start(bf16[2,80,128]{2,1,0:T(8,128)(2,1)S(1)} %get-tuple-element.31.rest_0_), channel_id=1, source_target_pairs={{0,8},{1,9},{2,10},{3,11},{4,12},{5,13},{6,14},{7,15},{8,0},{9,1},... | collective-permute-start | bytes 122888 | tf_op jit(solution)/shard_map/ppermute | solution.py:468
  21.4 2.9 %collective-permute-start.1 = (f32[8,128]{1,0:T(8,128)S(1)}, f32[8,128]{1,0:T(8,128)S(1)}, u32[]{:S(2)}, u32[]{:S(2)}) collective-permute-start(f32[8,128]{1,0:T(8,128)S(1)} %notes.1.refs_4_.rest_1_.notes_ref), channel_id=1, source_target_pairs={{0,1},{1,0},{2,3},{3,2},{4,5},{5,4},{6,7},{7,6},{8,9},{9,8},{10,11... | collective-permute-start | bytes 12296 | tf_op jit(solution)/shard_map/ppermute | solution.py:468
  25.2 4.9 %collective-permute-start.7 = (bf16[2,64,128]{2,1,0:T(8,128)(2,1)S(1)}, bf16[2,64,128]{2,1,0:T(8,128)(2,1)S(1)}, u32[]{:S(2)}, u32[]{:S(2)}) collective-permute-start(bf16[2,64,128]{2,1,0:T(8,128)(2,1)S(1)} %get-tuple-element.34.rest_0_.refs_0_), channel_id=1, source_target_pairs={{0,8},{1,9},{2,10},{3,11},{4,12},{5,13},{6,14},{7,15},{8,0},{9,1},... | collective-permute-start | bytes 98312 | tf_op jit(solution)/shard_map/ppermute | solution.py:468
  30.1 7.0 %collective-permute-start.10 = (bf16[4,64,128]{2,1,0:T(8,128)(2,1)S(1)}, bf16[4,64,128]{2,1,0:T(8,128)(2,1)S(1)}, u32[]{:S(2)}, u32[]{:S(2)}) collective-permute-start(bf16[4,64,128]{2,1,0:T(8,128)(2,1)S(1)} %local.1.rest_0_.rest_3_), channel_id=1, source_target_pairs={{0,6},{1,7},{2,4},{3,5},{4,2},{5,3},{6,0},{7,1},{8,14},{9,15},{10,... | collective-permute-start | bytes 196616 | tf_op jit(solution)/shard_map/ppermute | solution.py:468
  32.3 4.8 %collective-permute-start.9 = (bf16[4,64,128]{2,1,0:T(8,128)(2,1)S(1)}, bf16[4,64,128]{2,1,0:T(8,128)(2,1)S(1)}, u32[]{:S(2)}, u32[]{:S(2)}) collective-permute-start(bf16[4,64,128]{2,1,0:T(8,128)(2,1)S(1)} %local.1.rest_0_.rest_3_), channel_id=1, source_target_pairs={{0,2},{1,3},{2,0},{3,1},{4,6},{5,7},{6,4},{7,5},{8,10},{9,11},{10,... | collective-permute-start | bytes 196616 | tf_op jit(solution)/shard_map/ppermute | solution.py:468
  32.9 4.3 %collective-permute-start.8 = (bf16[4,64,128]{2,1,0:T(8,128)(2,1)S(1)}, bf16[4,64,128]{2,1,0:T(8,128)(2,1)S(1)}, u32[]{:S(2)}, u32[]{:S(2)}) collective-permute-start(bf16[4,64,128]{2,1,0:T(8,128)(2,1)S(1)} %local.1.rest_0_.rest_3_), channel_id=1, source_target_pairs={{0,4},{1,5},{2,6},{3,7},{4,0},{5,1},{6,2},{7,3},{8,12},{9,13},{10,... | collective-permute-start | bytes 196616 | tf_op jit(solution)/shard_map/ppermute | solution.py:468
  40.3 1.4 %collective-permute-start.11 = (bf16[32,2048]{1,0:T(8,128)(2,1)S(1)}, bf16[32,2048]{1,0:T(8,128)(2,1)S(1)}, u32[]{:S(2)}, u32[]{:S(2)}) collective-permute-start(bf16[32,2048]{1,0:T(8,128)(2,1)S(1)} %get-tuple-element.36), channel_id=1, source_target_pairs={{0,1},{1,0},{2,3},{3,2},{4,5},{5,4},{6,7},{7,6},{8,9},{9,8},{10,11... | collective-permute-start | bytes 393224 | tf_op jit(solution)/shard_map/ppermute | solution.py:468

commit v12 on v11

--- a/solution.py
+++ b/solution.py
@@ -470,12 +470,12 @@
     stages = [list(range(first, min(first + 2, bits))) for first in range(1, bits, 2)]
     order = [bit for stage in stages for bit in stage] + [0]
     total = out_weight.shape[0]
-    cuts = [total * i // 8 for i in (0, 3, 4, 8)]
+    cuts = [total * i // 8 for i in (0, 2, 3, 5, 8)]
     held = []
 
     def fetch_next(window, after):
         i = len(held)
-        if window not in (1, 2, 3):
+        if window not in (0, 1, 2, 3):
             return []
         held.append(fetch(out_weight, cuts[i], cuts[i + 1] - cuts[i], after))
         return held[-1:]

time: 42.5 us -> 42.4 us (level)
  waiting for transfers between devices: 5.7 us -> 3.96 us
  Pallas kernels: 21 us -> 21.9 us
  starting transfers between devices: 13.5 us -> 14.3 us
    ppermute x12, waiting for transfers between devices: 5.7 us -> 3.96 us  [partner(): lax.ppermute(array, everyone, [(i, i ^ pattern) for i in range(devices)])]
    pallas_call x3 -> x4, Pallas kernels: 7.91 us -> 8.83 us  [fetch(): pl.pallas_call(functools.partial(fetch_kernel, first, parts), out_shape=p...]
    ppermute x12, starting transfers between devices: 13.5 us -> 14.3 us  [partner(): lax.ppermute(array, everyone, [(i, i ^ pattern) for i in range(devices)])]
  transfers between devices with their start and end apart: 12 -> 12, of which waited for: 4 -> 5; matrix products, arithmetic and copies ran while one was open for 0% -> 0% of each run, Pallas kernels for 24% -> 27%
where the time goes in v12:
time: 42.4 us; the launch traced here: 42.2 us
  Pallas kernels  21.9 us (52%)
  starting transfers between devices  14.3 us (34%)
  waiting for transfers between devices  3.96 us (9%)
  between operations  2.06 us (5%)
    ppermute x12, starting transfers between devices, partner(): lax.ppermute(array, everyone, [(i, i ^ pattern) for i in range(devices)])  14.3 us
    pallas_call x4, Pallas kernels, fetch(): pl.pallas_call(functools.partial(fetch_kernel, first, parts), out_shape=p...  8.83 us
    pallas_call x1, Pallas kernels, project(): pl.pallas_call(functools.partial(project_kernel, steps, group, colors, or...  6.04 us
    ppermute x12, waiting for transfers between devices, partner(): lax.ppermute(array, everyone, [(i, i ^ pattern) for i in range(devices)])  3.96 us
    pallas_call x1, Pallas kernels, output(): pl.pallas_call(functools.partial(output_kernel, steps, colors, patterns,...  3.13 us
    pallas_call x1, Pallas kernels, fetch_first(): pl.pallas_call(fetch_first_kernel, out_shape=(pltpu.VMEM((depth, early),...  2.26 us
    pallas_call x1, Pallas kernels, attend(): pl.pallas_call(functools.partial(attend_kernel, steps, width, len(held)),...  0.88 us
  transfers between devices with their start and end apart: 12, of which 5 were waited for; matrix products, arithmetic and copies ran while one was open for 0% of the time, Pallas kernels for 27%

profile of v12, /device:TPU:0, one launch (start us, length us, event | category | flops | bytes accessed | tf_op | source)
XLA Modules:
  0.0 42.2 jit_solution(8566718656041580993)
XLA Ops:
  0.6 0.5 %collective-permute-start = (bf16[16,2048]{1,0:T(8,128)(2,1)}, bf16[16,2048]{1,0:T(8,128)(2,1)S(1)}, u32[]{:S(2)}, u32[]{:S(2)}) collective-permute-start(bf16[16,2048]{1,0:T(8,128)(2,1)} %bitcast.10), channel_id=1, source_target_pairs={{0,1},{1,0},{2,3},{3,2},{4,5},{5,4},{6,7},{7,6},{8,9},{9,8},{10,11... | collective-permute-start | bytes 196616 | tf_op jit(solution)/shard_map/ppermute | solution.py:468
  1.1 2.3 %fetch_first.1 = (bf16[2048,512]{1,0:T(8,128)(2,1)S(1)}, bf16[2048,256]{1,0:T(8,128)(2,1)S(1)}, bf16[2048,256]{1,0:T(8,128)(2,1)S(1)}) custom-call(bf16[2048,4096]{1,0:T(8,128)(2,1)} %wq_ref.3, bf16[2048,256]{1,0:T(8,128)(2,1)} %wk_ref.1, bf16[2048,256]{1,0:T(8,128)(2,1)} %wv_ref.1), custom_call_target="tpu_custom_call" | custom-call | bytes 4194304 | tf_op jit(solution)/shard_map/fetch_first/pallas_call | solution.py:169
  3.4 0.0 collective-permute-done.other_ref
  3.4 6.0 %project.1 = (bf16[768,256]{1,0:T(8,128)(2,1)S(1)}, bf16[768,256]{1,0:T(8,128)(2,1)S(1)}, f32[4,80,128]{2,1,0:T(8,128)S(1)}, bf16[4,80,128]{2,1,0:T(8,128)(2,1)S...) custom-call(s32[1]{0:T(128)} %bitcast.place_ref, bf16[16,2048]{1,0:T(8,128)(2,1)} %bitcast.11, ...), custom_call_target="tpu_custom_call" | custom-call | flops 603979776 | bytes 18874368 | tf_op jit(solution)/shard_map/project/pallas_call | solution.py:133
  9.5 0.1 collective-permute-start.2
  9.6 2.9 %collective-permute-start.4 = (bf16[4,80,128]{2,1,0:T(8,128)(2,1)S(1)}, bf16[4,80,128]{2,1,0:T(8,128)(2,1)S(1)}, u32[]{:S(2)}, u32[]{:S(2)}) collective-permute-start(bf16[4,80,128]{2,1,0:T(8,128)(2,1)S(1)} %get-tuple-element.29), channel_id=1, source_target_pairs={{0,2},{1,3},{2,0},{3,1},{4,6},{5,7},{6,4},{7,5},{8,10},{9,11},{10,... | collective-permute-start | bytes 245768 | tf_op jit(solution)/shard_map/ppermute | solution.py:468
  12.5 1.5 %collective-permute-start.5 = (bf16[4,80,128]{2,1,0:T(8,128)(2,1)S(1)}, bf16[4,80,128]{2,1,0:T(8,128)(2,1)S(1)}, u32[]{:S(2)}, u32[]{:S(2)}) collective-permute-start(bf16[4,80,128]{2,1,0:T(8,128)(2,1)S(1)} %get-tuple-element.30), channel_id=1, source_target_pairs={{0,6},{1,7},{2,4},{3,5},{4,2},{5,3},{6,0},{7,1},{8,14},{9,15},{10,... | collective-permute-start | bytes 245768 | tf_op jit(solution)/shard_map/ppermute | solution.py:468
  14.1 0.0 collective-permute-start.3
  15.4 0.1 notes.1.rest_1_.refs_4_.notes_ref
  15.5 2.2 %fetch.4.refs_5_.rest_0_ = bf16[1024,2048]{1,0:T(8,128)(2,1)S(1)} custom-call(bf16[4096,2048]{1,0:T(8,128)(2,1)} %weight_ref.7, bf16[4,80,128]{2,1,0:T(8,128)(2,1)S(1)} %get-tuple-element.25.after_ref.rest_0_, f32[8,128]{1,0:T(8,128)S(1)} %notes.1.rest_1_.refs_4_.notes_ref), custom_call_target="tpu_custom_call" | custom-call | bytes 4194304 | tf_op jit(solution)/shard_map/fetch/pallas_call | solution.py:245
  17.7 0.0 collective-permute-done.4.refs_2_
  17.7 0.9 %collective-permute-done.5.refs_3_ = bf16[4,80,128]{2,1,0:T(8,128)(2,1)S(1)} collective-permute-done((bf16[4,80,128]{2,1,0:T(8,128)(2,1)S(1)}, bf16[4,80,128]{2,1,0:T(8,128)(2,1)S(1)}, u32[]{:S(2)}, u32[]{:S(2)}) %collective-permute-start.5) | collective-permute-done | bytes 81952 | tf_op jit(solution)/shard_map/ppermute | solution.py:468
  18.6 0.0 collective-permute-done.3.refs_1_
  18.7 2.7 %collective-permute-start.6 = (bf16[2,80,128]{2,1,0:T(8,128)(2,1)S(1)}, bf16[2,80,128]{2,1,0:T(8,128)(2,1)S(1)}, u32[]{:S(2)}, u32[]{:S(2)}) collective-permute-start(bf16[2,80,128]{2,1,0:T(8,128)(2,1)S(1)} %get-tuple-element.31.rest_0_), channel_id=1, source_target_pairs={{0,8},{1,9},{2,10},{3,11},{4,12},{5,13},{6,14},{7,15},{8,0},{9,1},... | collective-permute-start | bytes 122888 | tf_op jit(solution)/shard_map/ppermute | solution.py:468
  21.4 0.0 collective-permute-start.1
  21.4 1.5 %fetch.5.rest_0_.rest_1_ = bf16[512,2048]{1,0:T(8,128)(2,1)S(1)} custom-call(bf16[4096,2048]{1,0:T(8,128)(2,1)} %weight_ref.7, bf16[2,80,128]{2,1,0:T(8,128)(2,1)S(1)} %get-tuple-element.31.rest_0_, f32[8,128]{1,0:T(8,128)S(1)} %notes.1.rest_1_.refs_4_.notes_ref), custom_call_target="tpu_custom_call" | custom-call | bytes 2097152 | tf_op jit(solution)/shard_map/fetch/pallas_call | solution.py:245
  23.0 0.0 collective-permute-done.1.came_notes_ref
  23.0 0.7 %collective-permute-done.6.rest_2_ = bf16[2,80,128]{2,1,0:T(8,128)(2,1)S(1)} collective-permute-done((bf16[2,80,128]{2,1,0:T(8,128)(2,1)S(1)}, bf16[2,80,128]{2,1,0:T(8,128)(2,1)S(1)}, u32[]{:S(2)}, u32[]{:S(2)}) %collective-permute-start.6) | collective-permute-done | bytes 40992 | tf_op jit(solution)/shard_map/ppermute | solution.py:468
  23.6 0.0 collective-permute-done.2.came_ref
  23.6 0.9 %attend.1 = (bf16[2,64,128]{2,1,0:T(8,128)(2,1)S(1)}, bf16[16,256]{1,0:T(8,128)(2,1)S(1)}, bf16[16,256]{1,0:T(8,128)(2,1)S(1)}) custom-call(f32[8,128]{1,0:T(8,128)S(1)} %notes.1.rest_1_.refs_4_.notes_ref, f32[8,128]{1,0:T(8,128)S(1)} %collective-permute-done.1.came_notes_ref, bf16[768,256]{1,0:T(8,128)(2,1)S(1)} %get-tuple-element.26.own_ref, ...), custom_call_target="tpu_custom_call" | custom-call | tf_op jit(solution)/shard_map/attend/pallas_call | solution.py:334
  24.5 2.8 %collective-permute-start.7 = (bf16[2,64,128]{2,1,0:T(8,128)(2,1)S(1)}, bf16[2,64,128]{2,1,0:T(8,128)(2,1)S(1)}, u32[]{:S(2)}, u32[]{:S(2)}) collective-permute-start(bf16[2,64,128]{2,1,0:T(8,128)(2,1)S(1)} %get-tuple-element.34.rest_0_.refs_0_), channel_id=1, source_target_pairs={{0,8},{1,9},{2,10},{3,11},{4,12},{5,13},{6,14},{7,15},{8,0},{9,1},... | collective-permute-start | bytes 98312 | tf_op jit(solution)/shard_map/ppermute | solution.py:468
  27.4 2.2 %fetch.6.refs_2_.rest_2_ = bf16[1024,2048]{1,0:T(8,128)(2,1)S(1)} custom-call(bf16[4096,2048]{1,0:T(8,128)(2,1)} %weight_ref.7, bf16[2,64,128]{2,1,0:T(8,128)(2,1)S(1)} %get-tuple-element.34.rest_0_.refs_0_), custom_call_target="tpu_custom_call" | custom-call | bytes 4194304 | tf_op jit(solution)/shard_map/fetch/pallas_call | solution.py:245
  29.6 0.0 collective-permute-done.7.refs_1_
  29.6 2.6 %collective-permute-start.10 = (bf16[4,64,128]{2,1,0:T(8,128)(2,1)S(1)}, bf16[4,64,128]{2,1,0:T(8,128)(2,1)S(1)}, u32[]{:S(2)}, u32[]{:S(2)}) collective-permute-start(bf16[4,64,128]{2,1,0:T(8,128)(2,1)S(1)} %local.1.rest_0_.rest_4_), channel_id=1, source_target_pairs={{0,6},{1,7},{2,4},{3,5},{4,2},{5,3},{6,0},{7,1},{8,14},{9,15},{10,... | collective-permute-start | bytes 196616 | tf_op jit(solution)/shard_map/ppermute | solution.py:468
  32.2 0.6 %collective-permute-start.9 = (bf16[4,64,128]{2,1,0:T(8,128)(2,1)S(1)}, bf16[4,64,128]{2,1,0:T(8,128)(2,1)S(1)}, u32[]{:S(2)}, u32[]{:S(2)}) collective-permute-start(bf16[4,64,128]{2,1,0:T(8,128)(2,1)S(1)} %local.1.rest_0_.rest_4_), channel_id=1, source_target_pairs={{0,2},{1,3},{2,0},{3,1},{4,6},{5,7},{6,4},{7,5},{8,10},{9,11},{10,... | collective-permute-start | bytes 196616 | tf_op jit(solution)/shard_map/ppermute | solution.py:468
  32.8 0.3 collective-permute-start.8
  33.2 2.9 %fetch.7.rest_3_ = bf16[1536,2048]{1,0:T(8,128)(2,1)S(1)} custom-call(bf16[4096,2048]{1,0:T(8,128)(2,1)} %weight_ref.7, bf16[4,64,128]{2,1,0:T(8,128)(2,1)S(1)} %local.1.rest_0_.rest_4_), custom_call_target="tpu_custom_call" | custom-call | bytes 6291456 | tf_op jit(solution)/shard_map/fetch/pallas_call | solution.py:245
  36.0 0.0 collective-permute-done.10.rest_7_
  36.0 0.4 %collective-permute-done.9.rest_6_ = bf16[4,64,128]{2,1,0:T(8,128)(2,1)S(1)} collective-permute-done((bf16[4,64,128]{2,1,0:T(8,128)(2,1)S(1)}, bf16[4,64,128]{2,1,0:T(8,128)(2,1)S(1)}, u32[]{:S(2)}, u32[]{:S(2)}) %collective-permute-start.9) | collective-permute-done | bytes 65568 | tf_op jit(solution)/shard_map/ppermute | solution.py:468
  36.5 0.6 %collective-permute-done.8.rest_5_ = bf16[4,64,128]{2,1,0:T(8,128)(2,1)S(1)} collective-permute-done((bf16[4,64,128]{2,1,0:T(8,128)(2,1)S(1)}, bf16[4,64,128]{2,1,0:T(8,128)(2,1)S(1)}, u32[]{:S(2)}, u32[]{:S(2)}) %collective-permute-start.8) | collective-permute-done | bytes 65568 | tf_op jit(solution)/shard_map/ppermute | solution.py:468
  37.1 3.1 %output.1 = (f32[16,2048]{1,0:T(8,128)S(1)}, bf16[32,2048]{1,0:T(8,128)(2,1)S(1)}) custom-call(s32[1]{0:T(128)} %bitcast.place_ref, bf16[16,256]{1,0:T(8,128)(2,1)S(1)} %get-tuple-element.33.fresh_ref, bf16[1024,2048]{1,0:T(8,128)(2,1)S(1)} %fetch.4.refs_5_.rest_0_, bf16[512,2048]{1,0:T(8,128)(2,1)S(1)} %fetch.5.rest_0_.rest_1_, ...), custom_call_target="tpu_custom_call" | custom-call | flops 536870912 | bytes 16777216 | tf_op jit(solution)/shard_map/output/pallas_call | solution.py:411
  40.2 0.0 collective-permute-start.11
  40.2 1.3 %collective-permute-done.11.came_ref = bf16[32,2048]{1,0:T(8,128)(2,1)S(1)} collective-permute-done((bf16[32,2048]{1,0:T(8,128)(2,1)S(1)}, bf16[32,2048]{1,0:T(8,128)(2,1)S(1)}, u32[]{:S(2)}, u32[]{:S(2)}) %collective-permute-start.11) | collective-permute-done | bytes 131104 | tf_op jit(solution)/shard_map/ppermute | solution.py:468
  41.6 0.7 %finish.1 = (bf16[16,2048]{1,0:T(8,128)(2,1)}, bf16[2,512]{1,0:T(2,128)(2,1)}, bf16[2,512]{1,0:T(2,128)(2,1)}) custom-call(s32[1]{0:T(128)} %bitcast.place_ref, f32[16,2048]{1,0:T(8,128)S(1)} %get-tuple-element.35.mine_ref, bf16[32,2048]{1,0:T(8,128)(2,1)S(1)} %collective-permute-done.11.came_ref, bf16[16,256]{1,0:T(8,128)(2,1)S(1)} %get-tuple-element.37.fresh_ref), custom_call_target="tpu_custom_call" | custom-call | tf_op jit(solution)/shard_map/finish/pallas_call | solution.py:446
  (2 shorter events, 0.0 us)
Async XLA Ops:
  0.6 2.8 %collective-permute-start = (bf16[16,2048]{1,0:T(8,128)(2,1)}, bf16[16,2048]{1,0:T(8,128)(2,1)S(1)}, u32[]{:S(2)}, u32[]{:S(2)}) collective-permute-start(bf16[16,2048]{1,0:T(8,128)(2,1)} %bitcast.10), channel_id=1, source_target_pairs={{0,1},{1,0},{2,3},{3,2},{4,5},{5,4},{6,7},{7,6},{8,9},{9,8},{10,11... | collective-permute-start | bytes 196616 | tf_op jit(solution)/shard_map/ppermute | solution.py:468
  9.5 14.2 %collective-permute-start.2 = (bf16[768,256]{1,0:T(8,128)(2,1)S(1)}, bf16[768,256]{1,0:T(8,128)(2,1)S(1)}, u32[]{:S(2)}, u32[]{:S(2)}) collective-permute-start(bf16[768,256]{1,0:T(8,128)(2,1)S(1)} %get-tuple-element.27), channel_id=1, source_target_pairs={{0,1},{1,0},{2,3},{3,2},{4,5},{5,4},{6,7},{7,6},{8,9},{9,8},{10,11... | collective-permute-start | bytes 1179656 | tf_op jit(solution)/shard_map/ppermute | solution.py:468
  9.6 8.1 %collective-permute-start.4 = (bf16[4,80,128]{2,1,0:T(8,128)(2,1)S(1)}, bf16[4,80,128]{2,1,0:T(8,128)(2,1)S(1)}, u32[]{:S(2)}, u32[]{:S(2)}) collective-permute-start(bf16[4,80,128]{2,1,0:T(8,128)(2,1)S(1)} %get-tuple-element.29), channel_id=1, source_target_pairs={{0,2},{1,3},{2,0},{3,1},{4,6},{5,7},{6,4},{7,5},{8,10},{9,11},{10,... | collective-permute-start | bytes 245768 | tf_op jit(solution)/shard_map/ppermute | solution.py:468
  12.5 6.1 %collective-permute-start.5 = (bf16[4,80,128]{2,1,0:T(8,128)(2,1)S(1)}, bf16[4,80,128]{2,1,0:T(8,128)(2,1)S(1)}, u32[]{:S(2)}, u32[]{:S(2)}) collective-permute-start(bf16[4,80,128]{2,1,0:T(8,128)(2,1)S(1)} %get-tuple-element.30), channel_id=1, source_target_pairs={{0,6},{1,7},{2,4},{3,5},{4,2},{5,3},{6,0},{7,1},{8,14},{9,15},{10,... | collective-permute-start | bytes 245768 | tf_op jit(solution)/shard_map/ppermute | solution.py:468
  14.1 4.5 %collective-permute-start.3 = (bf16[4,80,128]{2,1,0:T(8,128)(2,1)S(1)}, bf16[4,80,128]{2,1,0:T(8,128)(2,1)S(1)}, u32[]{:S(2)}, u32[]{:S(2)}) collective-permute-start(bf16[4,80,128]{2,1,0:T(8,128)(2,1)S(1)} %get-tuple-element.25.after_ref.rest_0_), channel_id=1, source_target_pairs={{0,4},{1,5},{2,6},{3,7},{4,0},{5,1},{6,2},{7,3},{8,12},{9,13},{10,... | collective-permute-start | bytes 245768 | tf_op jit(solution)/shard_map/ppermute | solution.py:468
  18.7 5.0 %collective-permute-start.6 = (bf16[2,80,128]{2,1,0:T(8,128)(2,1)S(1)}, bf16[2,80,128]{2,1,0:T(8,128)(2,1)S(1)}, u32[]{:S(2)}, u32[]{:S(2)}) collective-permute-start(bf16[2,80,128]{2,1,0:T(8,128)(2,1)S(1)} %get-tuple-element.31.rest_0_), channel_id=1, source_target_pairs={{0,8},{1,9},{2,10},{3,11},{4,12},{5,13},{6,14},{7,15},{8,0},{9,1},... | collective-permute-start | bytes 122888 | tf_op jit(solution)/shard_map/ppermute | solution.py:468
  21.4 1.6 %collective-permute-start.1 = (f32[8,128]{1,0:T(8,128)S(1)}, f32[8,128]{1,0:T(8,128)S(1)}, u32[]{:S(2)}, u32[]{:S(2)}) collective-permute-start(f32[8,128]{1,0:T(8,128)S(1)} %notes.1.rest_1_.refs_4_.notes_ref), channel_id=1, source_target_pairs={{0,1},{1,0},{2,3},{3,2},{4,5},{5,4},{6,7},{7,6},{8,9},{9,8},{10,11... | collective-permute-start | bytes 12296 | tf_op jit(solution)/shard_map/ppermute | solution.py:468
  24.5 5.0 %collective-permute-start.7 = (bf16[2,64,128]{2,1,0:T(8,128)(2,1)S(1)}, bf16[2,64,128]{2,1,0:T(8,128)(2,1)S(1)}, u32[]{:S(2)}, u32[]{:S(2)}) collective-permute-start(bf16[2,64,128]{2,1,0:T(8,128)(2,1)S(1)} %get-tuple-element.34.rest_0_.refs_0_), channel_id=1, source_target_pairs={{0,8},{1,9},{2,10},{3,11},{4,12},{5,13},{6,14},{7,15},{8,0},{9,1},... | collective-permute-start | bytes 98312 | tf_op jit(solution)/shard_map/ppermute | solution.py:468
  29.6 6.4 %collective-permute-start.10 = (bf16[4,64,128]{2,1,0:T(8,128)(2,1)S(1)}, bf16[4,64,128]{2,1,0:T(8,128)(2,1)S(1)}, u32[]{:S(2)}, u32[]{:S(2)}) collective-permute-start(bf16[4,64,128]{2,1,0:T(8,128)(2,1)S(1)} %local.1.rest_0_.rest_4_), channel_id=1, source_target_pairs={{0,6},{1,7},{2,4},{3,5},{4,2},{5,3},{6,0},{7,1},{8,14},{9,15},{10,... | collective-permute-start | bytes 196616 | tf_op jit(solution)/shard_map/ppermute | solution.py:468
  32.2 4.3 %collective-permute-start.9 = (bf16[4,64,128]{2,1,0:T(8,128)(2,1)S(1)}, bf16[4,64,128]{2,1,0:T(8,128)(2,1)S(1)}, u32[]{:S(2)}, u32[]{:S(2)}) collective-permute-start(bf16[4,64,128]{2,1,0:T(8,128)(2,1)S(1)} %local.1.rest_0_.rest_4_), channel_id=1, source_target_pairs={{0,2},{1,3},{2,0},{3,1},{4,6},{5,7},{6,4},{7,5},{8,10},{9,11},{10,... | collective-permute-start | bytes 196616 | tf_op jit(solution)/shard_map/ppermute | solution.py:468
  32.8 4.3 %collective-permute-start.8 = (bf16[4,64,128]{2,1,0:T(8,128)(2,1)S(1)}, bf16[4,64,128]{2,1,0:T(8,128)(2,1)S(1)}, u32[]{:S(2)}, u32[]{:S(2)}) collective-permute-start(bf16[4,64,128]{2,1,0:T(8,128)(2,1)S(1)} %local.1.rest_0_.rest_4_), channel_id=1, source_target_pairs={{0,4},{1,5},{2,6},{3,7},{4,0},{5,1},{6,2},{7,3},{8,12},{9,13},{10,... | collective-permute-start | bytes 196616 | tf_op jit(solution)/shard_map/ppermute | solution.py:468
  40.2 1.4 %collective-permute-start.11 = (bf16[32,2048]{1,0:T(8,128)(2,1)S(1)}, bf16[32,2048]{1,0:T(8,128)(2,1)S(1)}, u32[]{:S(2)}, u32[]{:S(2)}) collective-permute-start(bf16[32,2048]{1,0:T(8,128)(2,1)S(1)} %get-tuple-element.36), channel_id=1, source_target_pairs={{0,1},{1,0},{2,3},{3,2},{4,5},{5,4},{6,7},{7,6},{8,9},{9,8},{10,11... | collective-permute-start | bytes 393224 | tf_op jit(solution)/shard_map/ppermute | solution.py:468

commit v13 on v12

--- a/solution.py
+++ b/solution.py
@@ -501,6 +501,7 @@
     patterns = [0, 1]
     for i, stage in enumerate(stages[::-1]):
         moves = slot_patterns(stage)
+        moves = moves[:1] + moves[2:] + moves[1:2]
         came = [partner(context, move) for move in moves[1:]]
         patterns = [p ^ move for move in moves for p in patterns]
         now = fetch_next(len(stages) + i, [context])

time: 42.4 us -> 42.5 us (level)
  transfers between devices with their start and end apart: 12 -> 12, of which waited for: 5 -> 5; matrix products, arithmetic and copies ran while one was open for 0% -> 0% of each run, Pallas kernels for 27% -> 26%
where the time goes in v13:
time: 42.5 us; the launch traced here: 42.3 us
  Pallas kernels  21.9 us (52%)
  starting transfers between devices  14.3 us (34%)
  waiting for transfers between devices  4.1 us (10%)
  between operations  2.06 us (5%)
    ppermute x12, starting transfers between devices, partner(): lax.ppermute(array, everyone, [(i, i ^ pattern) for i in range(devices)])  14.3 us
    pallas_call x4, Pallas kernels, fetch(): pl.pallas_call(functools.partial(fetch_kernel, first, parts), out_shape=p...  8.83 us
    pallas_call x1, Pallas kernels, project(): pl.pallas_call(functools.partial(project_kernel, steps, group, colors, or...  6.04 us
    ppermute x12, waiting for transfers between devices, partner(): lax.ppermute(array, everyone, [(i, i ^ pattern) for i in range(devices)])  4.1 us
    pallas_call x1, Pallas kernels, output(): pl.pallas_call(functools.partial(output_kernel, steps, colors, patterns,...  3.13 us
    pallas_call x1, Pallas kernels, fetch_first(): pl.pallas_call(fetch_first_kernel, out_shape=(pltpu.VMEM((depth, early),...  2.26 us
    pallas_call x1, Pallas kernels, attend(): pl.pallas_call(functools.partial(attend_kernel, steps, width, len(held)),...  0.88 us
  transfers between devices with their start and end apart: 12, of which 5 were waited for; matrix products, arithmetic and copies ran while one was open for 0% of the time, Pallas kernels for 26%

profile of v13, /device:TPU:0, one launch (start us, length us, event | category | flops | bytes accessed | tf_op | source)
XLA Modules:
  0.0 42.3 jit_solution(3367509085602286876)
XLA Ops:
  0.6 0.5 %collective-permute-start = (bf16[16,2048]{1,0:T(8,128)(2,1)}, bf16[16,2048]{1,0:T(8,128)(2,1)S(1)}, u32[]{:S(2)}, u32[]{:S(2)}) collective-permute-start(bf16[16,2048]{1,0:T(8,128)(2,1)} %bitcast.10), channel_id=1, source_target_pairs={{0,1},{1,0},{2,3},{3,2},{4,5},{5,4},{6,7},{7,6},{8,9},{9,8},{10,11... | collective-permute-start | bytes 196616 | tf_op jit(solution)/shard_map/ppermute | solution.py:468
  1.1 2.3 %fetch_first.1 = (bf16[2048,512]{1,0:T(8,128)(2,1)S(1)}, bf16[2048,256]{1,0:T(8,128)(2,1)S(1)}, bf16[2048,256]{1,0:T(8,128)(2,1)S(1)}) custom-call(bf16[2048,4096]{1,0:T(8,128)(2,1)} %wq_ref.3, bf16[2048,256]{1,0:T(8,128)(2,1)} %wk_ref.1, bf16[2048,256]{1,0:T(8,128)(2,1)} %wv_ref.1), custom_call_target="tpu_custom_call" | custom-call | bytes 4194304 | tf_op jit(solution)/shard_map/fetch_first/pallas_call | solution.py:169
  3.4 0.0 collective-permute-done.other_ref
  3.4 6.0 %project.1 = (bf16[768,256]{1,0:T(8,128)(2,1)S(1)}, bf16[768,256]{1,0:T(8,128)(2,1)S(1)}, f32[4,80,128]{2,1,0:T(8,128)S(1)}, bf16[4,80,128]{2,1,0:T(8,128)(2,1)S...) custom-call(s32[1]{0:T(128)} %bitcast.place_ref, bf16[16,2048]{1,0:T(8,128)(2,1)} %bitcast.11, ...), custom_call_target="tpu_custom_call" | custom-call | flops 603979776 | bytes 18874368 | tf_op jit(solution)/shard_map/project/pallas_call | solution.py:133
  9.5 0.1 collective-permute-start.2
  9.6 2.9 %collective-permute-start.4 = (bf16[4,80,128]{2,1,0:T(8,128)(2,1)S(1)}, bf16[4,80,128]{2,1,0:T(8,128)(2,1)S(1)}, u32[]{:S(2)}, u32[]{:S(2)}) collective-permute-start(bf16[4,80,128]{2,1,0:T(8,128)(2,1)S(1)} %get-tuple-element.29), channel_id=1, source_target_pairs={{0,2},{1,3},{2,0},{3,1},{4,6},{5,7},{6,4},{7,5},{8,10},{9,11},{10,... | collective-permute-start | bytes 245768 | tf_op jit(solution)/shard_map/ppermute | solution.py:468
  12.5 1.5 %collective-permute-start.5 = (bf16[4,80,128]{2,1,0:T(8,128)(2,1)S(1)}, bf16[4,80,128]{2,1,0:T(8,128)(2,1)S(1)}, u32[]{:S(2)}, u32[]{:S(2)}) collective-permute-start(bf16[4,80,128]{2,1,0:T(8,128)(2,1)S(1)} %get-tuple-element.30), channel_id=1, source_target_pairs={{0,6},{1,7},{2,4},{3,5},{4,2},{5,3},{6,0},{7,1},{8,14},{9,15},{10,... | collective-permute-start | bytes 245768 | tf_op jit(solution)/shard_map/ppermute | solution.py:468
  14.1 0.0 collective-permute-start.3
  15.4 0.1 notes.1.rest_1_.refs_4_.notes_ref
  15.5 2.2 %fetch.4.refs_5_.rest_0_ = bf16[1024,2048]{1,0:T(8,128)(2,1)S(1)} custom-call(bf16[4096,2048]{1,0:T(8,128)(2,1)} %weight_ref.7, bf16[4,80,128]{2,1,0:T(8,128)(2,1)S(1)} %get-tuple-element.25.after_ref.rest_0_, f32[8,128]{1,0:T(8,128)S(1)} %notes.1.rest_1_.refs_4_.notes_ref), custom_call_target="tpu_custom_call" | custom-call | bytes 4194304 | tf_op jit(solution)/shard_map/fetch/pallas_call | solution.py:245
  17.7 0.0 collective-permute-done.4.refs_2_
  17.7 0.9 %collective-permute-done.5.refs_3_ = bf16[4,80,128]{2,1,0:T(8,128)(2,1)S(1)} collective-permute-done((bf16[4,80,128]{2,1,0:T(8,128)(2,1)S(1)}, bf16[4,80,128]{2,1,0:T(8,128)(2,1)S(1)}, u32[]{:S(2)}, u32[]{:S(2)}) %collective-permute-start.5) | collective-permute-done | bytes 81952 | tf_op jit(solution)/shard_map/ppermute | solution.py:468
  18.6 0.0 collective-permute-done.3.refs_1_
  18.7 2.7 %collective-permute-start.6 = (bf16[2,80,128]{2,1,0:T(8,128)(2,1)S(1)}, bf16[2,80,128]{2,1,0:T(8,128)(2,1)S(1)}, u32[]{:S(2)}, u32[]{:S(2)}) collective-permute-start(bf16[2,80,128]{2,1,0:T(8,128)(2,1)S(1)} %get-tuple-element.31.rest_0_), channel_id=1, source_target_pairs={{0,8},{1,9},{2,10},{3,11},{4,12},{5,13},{6,14},{7,15},{8,0},{9,1},... | collective-permute-start | bytes 122888 | tf_op jit(solution)/shard_map/ppermute | solution.py:468
  21.4 0.0 collective-permute-start.1
  21.4 1.5 %fetch.5.rest_0_.rest_1_ = bf16[512,2048]{1,0:T(8,128)(2,1)S(1)} custom-call(bf16[4096,2048]{1,0:T(8,128)(2,1)} %weight_ref.7, bf16[2,80,128]{2,1,0:T(8,128)(2,1)S(1)} %get-tuple-element.31.rest_0_, f32[8,128]{1,0:T(8,128)S(1)} %notes.1.rest_1_.refs_4_.notes_ref), custom_call_target="tpu_custom_call" | custom-call | bytes 2097152 | tf_op jit(solution)/shard_map/fetch/pallas_call | solution.py:245
  23.0 0.0 collective-permute-done.1.came_notes_ref
  23.0 0.7 %collective-permute-done.6.rest_2_ = bf16[2,80,128]{2,1,0:T(8,128)(2,1)S(1)} collective-permute-done((bf16[2,80,128]{2,1,0:T(8,128)(2,1)S(1)}, bf16[2,80,128]{2,1,0:T(8,128)(2,1)S(1)}, u32[]{:S(2)}, u32[]{:S(2)}) %collective-permute-start.6) | collective-permute-done | bytes 40992 | tf_op jit(solution)/shard_map/ppermute | solution.py:468
  23.6 0.0 collective-permute-done.2.came_ref
  23.6 0.9 %attend.1 = (bf16[2,64,128]{2,1,0:T(8,128)(2,1)S(1)}, bf16[16,256]{1,0:T(8,128)(2,1)S(1)}, bf16[16,256]{1,0:T(8,128)(2,1)S(1)}) custom-call(f32[8,128]{1,0:T(8,128)S(1)} %notes.1.rest_1_.refs_4_.notes_ref, f32[8,128]{1,0:T(8,128)S(1)} %collective-permute-done.1.came_notes_ref, bf16[768,256]{1,0:T(8,128)(2,1)S(1)} %get-tuple-element.26.own_ref, ...), custom_call_target="tpu_custom_call" | custom-call | tf_op jit(solution)/shard_map/attend/pallas_call | solution.py:334
  24.5 2.8 %collective-permute-start.7 = (bf16[2,64,128]{2,1,0:T(8,128)(2,1)S(1)}, bf16[2,64,128]{2,1,0:T(8,128)(2,1)S(1)}, u32[]{:S(2)}, u32[]{:S(2)}) collective-permute-start(bf16[2,64,128]{2,1,0:T(8,128)(2,1)S(1)} %get-tuple-element.34.rest_0_.refs_0_), channel_id=1, source_target_pairs={{0,8},{1,9},{2,10},{3,11},{4,12},{5,13},{6,14},{7,15},{8,0},{9,1},... | collective-permute-start | bytes 98312 | tf_op jit(solution)/shard_map/ppermute | solution.py:468
  27.4 2.2 %fetch.6.refs_2_.rest_2_ = bf16[1024,2048]{1,0:T(8,128)(2,1)S(1)} custom-call(bf16[4096,2048]{1,0:T(8,128)(2,1)} %weight_ref.7, bf16[2,64,128]{2,1,0:T(8,128)(2,1)S(1)} %get-tuple-element.34.rest_0_.refs_0_), custom_call_target="tpu_custom_call" | custom-call | bytes 4194304 | tf_op jit(solution)/shard_map/fetch/pallas_call | solution.py:245
  29.6 0.0 collective-permute-done.7.refs_1_
  29.6 1.7 %collective-permute-start.10 = (bf16[4,64,128]{2,1,0:T(8,128)(2,1)S(1)}, bf16[4,64,128]{2,1,0:T(8,128)(2,1)S(1)}, u32[]{:S(2)}, u32[]{:S(2)}) collective-permute-start(bf16[4,64,128]{2,1,0:T(8,128)(2,1)S(1)} %local.1.rest_0_.rest_4_), channel_id=1, source_target_pairs={{0,4},{1,5},{2,6},{3,7},{4,0},{5,1},{6,2},{7,3},{8,12},{9,13},{10,... | collective-permute-start | bytes 196616 | tf_op jit(solution)/shard_map/ppermute | solution.py:468
  31.3 1.3 %collective-permute-start.9 = (bf16[4,64,128]{2,1,0:T(8,128)(2,1)S(1)}, bf16[4,64,128]{2,1,0:T(8,128)(2,1)S(1)}, u32[]{:S(2)}, u32[]{:S(2)}) collective-permute-start(bf16[4,64,128]{2,1,0:T(8,128)(2,1)S(1)} %local.1.rest_0_.rest_4_), channel_id=1, source_target_pairs={{0,6},{1,7},{2,4},{3,5},{4,2},{5,3},{6,0},{7,1},{8,14},{9,15},{10,... | collective-permute-start | bytes 196616 | tf_op jit(solution)/shard_map/ppermute | solution.py:468
  32.6 0.5 %collective-permute-start.8 = (bf16[4,64,128]{2,1,0:T(8,128)(2,1)S(1)}, bf16[4,64,128]{2,1,0:T(8,128)(2,1)S(1)}, u32[]{:S(2)}, u32[]{:S(2)}) collective-permute-start(bf16[4,64,128]{2,1,0:T(8,128)(2,1)S(1)} %local.1.rest_0_.rest_4_), channel_id=1, source_target_pairs={{0,2},{1,3},{2,0},{3,1},{4,6},{5,7},{6,4},{7,5},{8,10},{9,11},{10,... | collective-permute-start | bytes 196616 | tf_op jit(solution)/shard_map/ppermute | solution.py:468
  33.2 2.9 %fetch.7.rest_3_ = bf16[1536,2048]{1,0:T(8,128)(2,1)S(1)} custom-call(bf16[4096,2048]{1,0:T(8,128)(2,1)} %weight_ref.7, bf16[4,64,128]{2,1,0:T(8,128)(2,1)S(1)} %local.1.rest_0_.rest_4_), custom_call_target="tpu_custom_call" | custom-call | bytes 6291456 | tf_op jit(solution)/shard_map/fetch/pallas_call | solution.py:245
  36.0 0.0 collective-permute-done.10.rest_7_
  36.0 0.5 %collective-permute-done.9.rest_6_ = bf16[4,64,128]{2,1,0:T(8,128)(2,1)S(1)} collective-permute-done((bf16[4,64,128]{2,1,0:T(8,128)(2,1)S(1)}, bf16[4,64,128]{2,1,0:T(8,128)(2,1)S(1)}, u32[]{:S(2)}, u32[]{:S(2)}) %collective-permute-start.9) | collective-permute-done | bytes 65568 | tf_op jit(solution)/shard_map/ppermute | solution.py:468
  36.5 0.7 %collective-permute-done.8.rest_5_ = bf16[4,64,128]{2,1,0:T(8,128)(2,1)S(1)} collective-permute-done((bf16[4,64,128]{2,1,0:T(8,128)(2,1)S(1)}, bf16[4,64,128]{2,1,0:T(8,128)(2,1)S(1)}, u32[]{:S(2)}, u32[]{:S(2)}) %collective-permute-start.8) | collective-permute-done | bytes 65568 | tf_op jit(solution)/shard_map/ppermute | solution.py:468
  37.2 3.1 %output.1 = (f32[16,2048]{1,0:T(8,128)S(1)}, bf16[32,2048]{1,0:T(8,128)(2,1)S(1)}) custom-call(s32[1]{0:T(128)} %bitcast.place_ref, bf16[16,256]{1,0:T(8,128)(2,1)S(1)} %get-tuple-element.33.fresh_ref, bf16[1024,2048]{1,0:T(8,128)(2,1)S(1)} %fetch.4.refs_5_.rest_0_, bf16[512,2048]{1,0:T(8,128)(2,1)S(1)} %fetch.5.rest_0_.rest_1_, ...), custom_call_target="tpu_custom_call" | custom-call | flops 536870912 | bytes 16777216 | tf_op jit(solution)/shard_map/output/pallas_call | solution.py:411
  40.3 0.0 collective-permute-start.11
  40.4 1.3 %collective-permute-done.11.came_ref = bf16[32,2048]{1,0:T(8,128)(2,1)S(1)} collective-permute-done((bf16[32,2048]{1,0:T(8,128)(2,1)S(1)}, bf16[32,2048]{1,0:T(8,128)(2,1)S(1)}, u32[]{:S(2)}, u32[]{:S(2)}) %collective-permute-start.11) | collective-permute-done | bytes 131104 | tf_op jit(solution)/shard_map/ppermute | solution.py:468
  41.7 0.7 %finish.1 = (bf16[16,2048]{1,0:T(8,128)(2,1)}, bf16[2,512]{1,0:T(2,128)(2,1)}, bf16[2,512]{1,0:T(2,128)(2,1)}) custom-call(s32[1]{0:T(128)} %bitcast.place_ref, f32[16,2048]{1,0:T(8,128)S(1)} %get-tuple-element.35.mine_ref, bf16[32,2048]{1,0:T(8,128)(2,1)S(1)} %collective-permute-done.11.came_ref, bf16[16,256]{1,0:T(8,128)(2,1)S(1)} %get-tuple-element.37.fresh_ref), custom_call_target="tpu_custom_call" | custom-call | tf_op jit(solution)/shard_map/finish/pallas_call | solution.py:446
  (2 shorter events, 0.0 us)
Async XLA Ops:
  0.6 2.8 %collective-permute-start = (bf16[16,2048]{1,0:T(8,128)(2,1)}, bf16[16,2048]{1,0:T(8,128)(2,1)S(1)}, u32[]{:S(2)}, u32[]{:S(2)}) collective-permute-start(bf16[16,2048]{1,0:T(8,128)(2,1)} %bitcast.10), channel_id=1, source_target_pairs={{0,1},{1,0},{2,3},{3,2},{4,5},{5,4},{6,7},{7,6},{8,9},{9,8},{10,11... | collective-permute-start | bytes 196616 | tf_op jit(solution)/shard_map/ppermute | solution.py:468
  9.5 14.2 %collective-permute-start.2 = (bf16[768,256]{1,0:T(8,128)(2,1)S(1)}, bf16[768,256]{1,0:T(8,128)(2,1)S(1)}, u32[]{:S(2)}, u32[]{:S(2)}) collective-permute-start(bf16[768,256]{1,0:T(8,128)(2,1)S(1)} %get-tuple-element.27), channel_id=1, source_target_pairs={{0,1},{1,0},{2,3},{3,2},{4,5},{5,4},{6,7},{7,6},{8,9},{9,8},{10,11... | collective-permute-start | bytes 1179656 | tf_op jit(solution)/shard_map/ppermute | solution.py:468
  9.6 8.1 %collective-permute-start.4 = (bf16[4,80,128]{2,1,0:T(8,128)(2,1)S(1)}, bf16[4,80,128]{2,1,0:T(8,128)(2,1)S(1)}, u32[]{:S(2)}, u32[]{:S(2)}) collective-permute-start(bf16[4,80,128]{2,1,0:T(8,128)(2,1)S(1)} %get-tuple-element.29), channel_id=1, source_target_pairs={{0,2},{1,3},{2,0},{3,1},{4,6},{5,7},{6,4},{7,5},{8,10},{9,11},{10,... | collective-permute-start | bytes 245768 | tf_op jit(solution)/shard_map/ppermute | solution.py:468
  12.5 6.1 %collective-permute-start.5 = (bf16[4,80,128]{2,1,0:T(8,128)(2,1)S(1)}, bf16[4,80,128]{2,1,0:T(8,128)(2,1)S(1)}, u32[]{:S(2)}, u32[]{:S(2)}) collective-permute-start(bf16[4,80,128]{2,1,0:T(8,128)(2,1)S(1)} %get-tuple-element.30), channel_id=1, source_target_pairs={{0,6},{1,7},{2,4},{3,5},{4,2},{5,3},{6,0},{7,1},{8,14},{9,15},{10,... | collective-permute-start | bytes 245768 | tf_op jit(solution)/shard_map/ppermute | solution.py:468
  14.1 4.5 %collective-permute-start.3 = (bf16[4,80,128]{2,1,0:T(8,128)(2,1)S(1)}, bf16[4,80,128]{2,1,0:T(8,128)(2,1)S(1)}, u32[]{:S(2)}, u32[]{:S(2)}) collective-permute-start(bf16[4,80,128]{2,1,0:T(8,128)(2,1)S(1)} %get-tuple-element.25.after_ref.rest_0_), channel_id=1, source_target_pairs={{0,4},{1,5},{2,6},{3,7},{4,0},{5,1},{6,2},{7,3},{8,12},{9,13},{10,... | collective-permute-start | bytes 245768 | tf_op jit(solution)/shard_map/ppermute | solution.py:468
  18.7 5.0 %collective-permute-start.6 = (bf16[2,80,128]{2,1,0:T(8,128)(2,1)S(1)}, bf16[2,80,128]{2,1,0:T(8,128)(2,1)S(1)}, u32[]{:S(2)}, u32[]{:S(2)}) collective-permute-start(bf16[2,80,128]{2,1,0:T(8,128)(2,1)S(1)} %get-tuple-element.31.rest_0_), channel_id=1, source_target_pairs={{0,8},{1,9},{2,10},{3,11},{4,12},{5,13},{6,14},{7,15},{8,0},{9,1},... | collective-permute-start | bytes 122888 | tf_op jit(solution)/shard_map/ppermute | solution.py:468
  21.4 1.6 %collective-permute-start.1 = (f32[8,128]{1,0:T(8,128)S(1)}, f32[8,128]{1,0:T(8,128)S(1)}, u32[]{:S(2)}, u32[]{:S(2)}) collective-permute-start(f32[8,128]{1,0:T(8,128)S(1)} %notes.1.rest_1_.refs_4_.notes_ref), channel_id=1, source_target_pairs={{0,1},{1,0},{2,3},{3,2},{4,5},{5,4},{6,7},{7,6},{8,9},{9,8},{10,11... | collective-permute-start | bytes 12296 | tf_op jit(solution)/shard_map/ppermute | solution.py:468
  24.5 5.0 %collective-permute-start.7 = (bf16[2,64,128]{2,1,0:T(8,128)(2,1)S(1)}, bf16[2,64,128]{2,1,0:T(8,128)(2,1)S(1)}, u32[]{:S(2)}, u32[]{:S(2)}) collective-permute-start(bf16[2,64,128]{2,1,0:T(8,128)(2,1)S(1)} %get-tuple-element.34.rest_0_.refs_0_), channel_id=1, source_target_pairs={{0,8},{1,9},{2,10},{3,11},{4,12},{5,13},{6,14},{7,15},{8,0},{9,1},... | collective-permute-start | bytes 98312 | tf_op jit(solution)/shard_map/ppermute | solution.py:468
  29.6 6.4 %collective-permute-start.10 = (bf16[4,64,128]{2,1,0:T(8,128)(2,1)S(1)}, bf16[4,64,128]{2,1,0:T(8,128)(2,1)S(1)}, u32[]{:S(2)}, u32[]{:S(2)}) collective-permute-start(bf16[4,64,128]{2,1,0:T(8,128)(2,1)S(1)} %local.1.rest_0_.rest_4_), channel_id=1, source_target_pairs={{0,4},{1,5},{2,6},{3,7},{4,0},{5,1},{6,2},{7,3},{8,12},{9,13},{10,... | collective-permute-start | bytes 196616 | tf_op jit(solution)/shard_map/ppermute | solution.py:468
  31.3 5.2 %collective-permute-start.9 = (bf16[4,64,128]{2,1,0:T(8,128)(2,1)S(1)}, bf16[4,64,128]{2,1,0:T(8,128)(2,1)S(1)}, u32[]{:S(2)}, u32[]{:S(2)}) collective-permute-start(bf16[4,64,128]{2,1,0:T(8,128)(2,1)S(1)} %local.1.rest_0_.rest_4_), channel_id=1, source_target_pairs={{0,6},{1,7},{2,4},{3,5},{4,2},{5,3},{6,0},{7,1},{8,14},{9,15},{10,... | collective-permute-start | bytes 196616 | tf_op jit(solution)/shard_map/ppermute | solution.py:468
  32.6 4.6 %collective-permute-start.8 = (bf16[4,64,128]{2,1,0:T(8,128)(2,1)S(1)}, bf16[4,64,128]{2,1,0:T(8,128)(2,1)S(1)}, u32[]{:S(2)}, u32[]{:S(2)}) collective-permute-start(bf16[4,64,128]{2,1,0:T(8,128)(2,1)S(1)} %local.1.rest_0_.rest_4_), channel_id=1, source_target_pairs={{0,2},{1,3},{2,0},{3,1},{4,6},{5,7},{6,4},{7,5},{8,10},{9,11},{10,... | collective-permute-start | bytes 196616 | tf_op jit(solution)/shard_map/ppermute | solution.py:468
  40.3 1.4 %collective-permute-start.11 = (bf16[32,2048]{1,0:T(8,128)(2,1)S(1)}, bf16[32,2048]{1,0:T(8,128)(2,1)S(1)}, u32[]{:S(2)}, u32[]{:S(2)}) collective-permute-start(bf16[32,2048]{1,0:T(8,128)(2,1)S(1)} %get-tuple-element.36), channel_id=1, source_target_pairs={{0,1},{1,0},{2,3},{3,2},{4,5},{5,4},{6,7},{7,6},{8,9},{9,8},{10,11... | collective-permute-start | bytes 393224 | tf_op jit(solution)/shard_map/ppermute | solution.py:468

commit v14 on v12

--- a/solution.py
+++ b/solution.py
@@ -256,7 +256,7 @@
 
 
 def attend_kernel(steps, width, unused, notes_ref, came_notes_ref, own_ref, came_ref, *rest):
-    part_refs, (context_ref, fresh_ref, fresh_send_ref) = rest[unused:-3], rest[-3:]
+    part_refs, (context_ref, fresh_ref, fresh_send_ref, rows_buf) = rest[unused:-4], rest[-4:]
     slots = own_ref.shape[0] // 2
     half_kv = own_ref.shape[1] // HD
     total = functools.reduce(jnp.add, [ref[...].astype(jnp.float32) for ref in part_refs])
@@ -322,10 +322,16 @@
     fresh = (fresh * inverse).astype(jnp.bfloat16)
     mixed = lax.dot_general(weights, values, over_first, preferred_element_type=jnp.float32)
     mixed = mixed + lax.dot_general(fresh, values_now, over_first, preferred_element_type=jnp.float32)
+    half_heads = half_kv * group
     for index in range(groups):
         seq, k = index // half_kv, index % half_kv
-        context_ref[seq, k * per_head:(k + 1) * per_head, :] = mixed[
-            index * per_head:(index + 1) * per_head, index * HD:(index + 1) * HD].astype(jnp.bfloat16)
+        for t in range(steps):
+            first = index * per_head + t * group
+            start = (seq * steps + t) * half_heads + k * group
+            rows_buf[start:start + group, :] = mixed[first:first + group, index * HD:(index + 1) * HD]
+    context_ref[...] = jnp.concatenate([
+        rows_buf[pl.ds(head, 2 * steps, stride=half_heads), :] for head in range(half_heads)],
+        axis=1).astype(jnp.bfloat16)
 
 
 def attend(notes, came_notes, own, came, parts, held, steps, width, half_heads):
@@ -333,19 +339,18 @@
     fresh = jax.ShapeDtypeStruct((16, own.shape[1]), jnp.bfloat16)
     return pl.pallas_call(
         functools.partial(attend_kernel, steps, width, len(held)),
-        out_shape=(jax.ShapeDtypeStruct((2, steps * half_heads, HD), jnp.bfloat16), fresh, fresh),
+        out_shape=(jax.ShapeDtypeStruct((2 * steps, half_heads * HD), jnp.bfloat16), fresh, fresh),
         in_specs=[vmem] * 4 + [pl.BlockSpec(memory_space=pl.ANY)] * len(held) + [vmem] * len(parts),
         out_specs=(vmem,) * 3,
+        scratch_shapes=[pltpu.VMEM((2 * steps * half_heads, HD), jnp.float32)],
         compiler_params=pltpu.CompilerParams(vmem_limit_bytes=16 * MIB),
         name="attend",
     )(notes, came_notes, own, came, *[in_vmem(piece) for piece in held], *parts)
 
 
 def join_kernel(arrived, *refs):
-    out_ref = refs[-1]
-    for i, ref in enumerate(refs[:arrived + 1]):
-        count = ref.shape[0]
-        out_ref[i * count:(i + 1) * count] = ref[...]
+    refs[-1][...] = jnp.concatenate(
+        [ref[...].astype(jnp.float32) for ref in refs[:arrived + 1]], axis=0).astype(jnp.bfloat16)
 
 
 def local_call(kernel, shape, arrays, held=()):
@@ -360,26 +365,22 @@
     )(*arrays, *[in_vmem(piece) for piece in held])
 
 
-def output_kernel(steps, colors, patterns, pieces, place_ref, fresh_ref, *rest):
-    weight_refs, context_refs = rest[:pieces], rest[pieces:-4]
-    mine_ref, other_ref, wide_buf, rows_buf = rest[-4:]
+def output_kernel(steps, patterns, pieces, place_ref, fresh_ref, *rest):
+    weight_refs, context_refs = rest[:pieces], rest[pieces:-3]
+    mine_ref, other_ref, rows_buf = rest[-3:]
     device = place_ref[0]
-    devices = len(patterns)
-    half_seqs = devices // 2
-    count, block, _ = context_refs[0].shape
-    group = block // (steps * colors)
+    half_seqs = len(patterns) // 2
+    rows = jnp.concatenate([ref[...].astype(jnp.float32) for ref in context_refs], axis=0).astype(jnp.bfloat16)
+    total = rows.shape[0]
+    column = lax.broadcasted_iota(jnp.int32, (1, total), 1)
+    slot, step = column // steps, column % steps
+    difference = jnp.zeros((1, total), jnp.int32)
     for j, pattern in enumerate(patterns):
-        rows = context_refs[j // count][j % count]
-        start = pl.multiple_of((device ^ pattern) * block, 8)
-        wide_buf[pl.ds(start, block), :] = rows.astype(jnp.float32)
-    for head in range(colors * group):
-        color, h = head // group, head % group
-        lines = []
-        for g in range(2):
-            for t in range(steps):
-                start = g * half_seqs * block + (color * steps + t) * group + h
-                lines.append(wide_buf[pl.ds(start, half_seqs, stride=block), :])
-        rows_buf[:, head * HD:(head + 1) * HD] = jnp.concatenate(lines, axis=0).astype(jnp.bfloat16)
+        difference = jnp.where(slot == j, pattern, difference)
+    seq = difference ^ device
+    target = (seq // half_seqs * steps + step) * half_seqs + seq % half_seqs
+    move = (lax.broadcasted_iota(jnp.int32, (total, total), 0) == target).astype(jnp.float32).astype(jnp.bfloat16)
+    rows_buf[...] = jnp.dot(move, rows, preferred_element_type=jnp.float32).astype(jnp.bfloat16)
     low_side = device % 2 == 0
     half = rows_buf.shape[0] // 2
     other_ref[half:, :fresh_ref.shape[1]] = fresh_ref[...]
@@ -401,7 +402,7 @@
         other_ref[:half, span] = jnp.where(low_side, upper, lower).astype(jnp.bfloat16)
 
 
-def output(place, fresh, contexts, patterns, held, steps, colors):
+def output(place, fresh, contexts, patterns, held, steps):
     columns = held[0].shape[1]
     depth = sum(piece.shape[0] for piece in held)
     devices = len(patterns)
@@ -409,7 +410,7 @@
     vmem = pl.BlockSpec(memory_space=pltpu.VMEM)
     smem = pl.BlockSpec(memory_space=pltpu.SMEM)
     return pl.pallas_call(
-        functools.partial(output_kernel, steps, colors, patterns, len(held)),
+        functools.partial(output_kernel, steps, patterns, len(held)),
         out_shape=(
             jax.ShapeDtypeStruct((half, columns), jnp.float32),
             jax.ShapeDtypeStruct((half + fresh.shape[0], columns), jnp.bfloat16),
@@ -417,7 +418,6 @@
         in_specs=[smem, vmem] + [vmem] * (len(held) + len(contexts)),
         out_specs=(vmem, vmem),
         scratch_shapes=[
-            pltpu.VMEM((devices * contexts[0].shape[1], HD), jnp.float32),
             pltpu.VMEM((devices * steps, depth), jnp.bfloat16),
         ],
         compiler_params=pltpu.CompilerParams(vmem_limit_bytes=26 * MIB),
@@ -507,7 +507,7 @@
         if i < len(stages) - 1:
             shape = (len(moves) * context.shape[0],) + context.shape[1:]
             context = local_call(functools.partial(join_kernel, len(came)), shape, [context, *came], now)
-    mine, other = output(place, fresh_send, [context, *came], patterns, held, steps, colors)
+    mine, other = output(place, fresh_send, [context, *came], patterns, held, steps)
     result, new_keys, new_values = finish(place, mine, partner(other, 1), fresh, steps)
     return (
         result.reshape(steps, half_seqs, -1),

time: 42.4 us -> 42.5 us (level)
  transfers between devices with their start and end apart: 12 -> 12, of which waited for: 5 -> 5; matrix products, arithmetic and copies ran while one was open for 0% -> 0% of each run, Pallas kernels for 27% -> 26%
where the time goes in v14:
time: 42.5 us; the launch traced here: 42.3 us
  Pallas kernels  22 us (52%)
  starting transfers between devices  14.3 us (34%)
  waiting for transfers between devices  3.96 us (9%)
  between operations  2.06 us (5%)
    ppermute x12, starting transfers between devices, partner(): lax.ppermute(array, everyone, [(i, i ^ pattern) for i in range(devices)])  14.3 us
    pallas_call x4, Pallas kernels, fetch(): pl.pallas_call(functools.partial(fetch_kernel, first, parts), out_shape=p...  8.83 us
    pallas_call x1, Pallas kernels, project(): pl.pallas_call(functools.partial(project_kernel, steps, group, colors, or...  6.04 us
    ppermute x12, waiting for transfers between devices, partner(): lax.ppermute(array, everyone, [(i, i ^ pattern) for i in range(devices)])  3.96 us
    pallas_call x1, Pallas kernels, output(): pl.pallas_call(functools.partial(output_kernel, steps, patterns, len(held...  3.15 us
    pallas_call x1, Pallas kernels, fetch_first(): pl.pallas_call(fetch_first_kernel, out_shape=(pltpu.VMEM((depth, early),...  2.26 us
    pallas_call x1, Pallas kernels, attend(): pl.pallas_call(functools.partial(attend_kernel, steps, width, len(held)),...  0.91 us
  transfers between devices with their start and end apart: 12, of which 5 were waited for; matrix products, arithmetic and copies ran while one was open for 0% of the time, Pallas kernels for 26%

profile of v14, /device:TPU:0, one launch (start us, length us, event | category | flops | bytes accessed | tf_op | source)
XLA Modules:
  0.0 42.3 jit_solution(13096777653798357592)
XLA Ops:
  0.6 0.5 %collective-permute-start = (bf16[16,2048]{1,0:T(8,128)(2,1)}, bf16[16,2048]{1,0:T(8,128)(2,1)S(1)}, u32[]{:S(2)}, u32[]{:S(2)}) collective-permute-start(bf16[16,2048]{1,0:T(8,128)(2,1)} %bitcast.10), channel_id=1, source_target_pairs={{0,1},{1,0},{2,3},{3,2},{4,5},{5,4},{6,7},{7,6},{8,9},{9,8},{10,11... | collective-permute-start | bytes 196616 | tf_op jit(solution)/shard_map/ppermute | solution.py:468
  1.1 2.3 %fetch_first.1 = (bf16[2048,512]{1,0:T(8,128)(2,1)S(1)}, bf16[2048,256]{1,0:T(8,128)(2,1)S(1)}, bf16[2048,256]{1,0:T(8,128)(2,1)S(1)}) custom-call(bf16[2048,4096]{1,0:T(8,128)(2,1)} %wq_ref.3, bf16[2048,256]{1,0:T(8,128)(2,1)} %wk_ref.1, bf16[2048,256]{1,0:T(8,128)(2,1)} %wv_ref.1), custom_call_target="tpu_custom_call" | custom-call | bytes 4194304 | tf_op jit(solution)/shard_map/fetch_first/pallas_call | solution.py:169
  3.4 0.0 collective-permute-done.other_ref
  3.4 6.0 %project.1 = (bf16[768,256]{1,0:T(8,128)(2,1)S(1)}, bf16[768,256]{1,0:T(8,128)(2,1)S(1)}, f32[4,80,128]{2,1,0:T(8,128)S(1)}, bf16[4,80,128]{2,1,0:T(8,128)(2,1)S...) custom-call(s32[1]{0:T(128)} %bitcast.place_ref, bf16[16,2048]{1,0:T(8,128)(2,1)} %bitcast.11, ...), custom_call_target="tpu_custom_call" | custom-call | flops 603979776 | bytes 18874368 | tf_op jit(solution)/shard_map/project/pallas_call | solution.py:133
  9.5 0.1 collective-permute-start.2
  9.6 2.9 %collective-permute-start.4 = (bf16[4,80,128]{2,1,0:T(8,128)(2,1)S(1)}, bf16[4,80,128]{2,1,0:T(8,128)(2,1)S(1)}, u32[]{:S(2)}, u32[]{:S(2)}) collective-permute-start(bf16[4,80,128]{2,1,0:T(8,128)(2,1)S(1)} %get-tuple-element.29), channel_id=1, source_target_pairs={{0,2},{1,3},{2,0},{3,1},{4,6},{5,7},{6,4},{7,5},{8,10},{9,11},{10,... | collective-permute-start | bytes 245768 | tf_op jit(solution)/shard_map/ppermute | solution.py:468
  12.5 1.5 %collective-permute-start.5 = (bf16[4,80,128]{2,1,0:T(8,128)(2,1)S(1)}, bf16[4,80,128]{2,1,0:T(8,128)(2,1)S(1)}, u32[]{:S(2)}, u32[]{:S(2)}) collective-permute-start(bf16[4,80,128]{2,1,0:T(8,128)(2,1)S(1)} %get-tuple-element.30), channel_id=1, source_target_pairs={{0,6},{1,7},{2,4},{3,5},{4,2},{5,3},{6,0},{7,1},{8,14},{9,15},{10,... | collective-permute-start | bytes 245768 | tf_op jit(solution)/shard_map/ppermute | solution.py:468
  14.1 0.0 collective-permute-start.3
  15.4 0.1 notes.1.rest_1_.refs_4_.notes_ref
  15.5 2.2 %fetch.4.refs_5_.rest_0_ = bf16[1024,2048]{1,0:T(8,128)(2,1)S(1)} custom-call(bf16[4096,2048]{1,0:T(8,128)(2,1)} %weight_ref.7, bf16[4,80,128]{2,1,0:T(8,128)(2,1)S(1)} %get-tuple-element.25.after_ref.rest_0_, f32[8,128]{1,0:T(8,128)S(1)} %notes.1.rest_1_.refs_4_.notes_ref), custom_call_target="tpu_custom_call" | custom-call | bytes 4194304 | tf_op jit(solution)/shard_map/fetch/pallas_call | solution.py:245
  17.7 0.0 collective-permute-done.4.refs_2_
  17.7 0.9 %collective-permute-done.5.refs_3_ = bf16[4,80,128]{2,1,0:T(8,128)(2,1)S(1)} collective-permute-done((bf16[4,80,128]{2,1,0:T(8,128)(2,1)S(1)}, bf16[4,80,128]{2,1,0:T(8,128)(2,1)S(1)}, u32[]{:S(2)}, u32[]{:S(2)}) %collective-permute-start.5) | collective-permute-done | bytes 81952 | tf_op jit(solution)/shard_map/ppermute | solution.py:468
  18.6 0.0 collective-permute-done.3.refs_1_
  18.7 2.7 %collective-permute-start.6 = (bf16[2,80,128]{2,1,0:T(8,128)(2,1)S(1)}, bf16[2,80,128]{2,1,0:T(8,128)(2,1)S(1)}, u32[]{:S(2)}, u32[]{:S(2)}) collective-permute-start(bf16[2,80,128]{2,1,0:T(8,128)(2,1)S(1)} %get-tuple-element.31.rest_0_), channel_id=1, source_target_pairs={{0,8},{1,9},{2,10},{3,11},{4,12},{5,13},{6,14},{7,15},{8,0},{9,1},... | collective-permute-start | bytes 122888 | tf_op jit(solution)/shard_map/ppermute | solution.py:468
  21.4 0.0 collective-permute-start.1
  21.4 1.5 %fetch.5.rest_0_.rest_1_ = bf16[512,2048]{1,0:T(8,128)(2,1)S(1)} custom-call(bf16[4096,2048]{1,0:T(8,128)(2,1)} %weight_ref.7, bf16[2,80,128]{2,1,0:T(8,128)(2,1)S(1)} %get-tuple-element.31.rest_0_, f32[8,128]{1,0:T(8,128)S(1)} %notes.1.rest_1_.refs_4_.notes_ref), custom_call_target="tpu_custom_call" | custom-call | bytes 2097152 | tf_op jit(solution)/shard_map/fetch/pallas_call | solution.py:245
  23.0 0.0 collective-permute-done.1.came_notes_ref
  23.0 0.7 %collective-permute-done.6.rest_2_ = bf16[2,80,128]{2,1,0:T(8,128)(2,1)S(1)} collective-permute-done((bf16[2,80,128]{2,1,0:T(8,128)(2,1)S(1)}, bf16[2,80,128]{2,1,0:T(8,128)(2,1)S(1)}, u32[]{:S(2)}, u32[]{:S(2)}) %collective-permute-start.6) | collective-permute-done | bytes 40992 | tf_op jit(solution)/shard_map/ppermute | solution.py:468
  23.6 0.0 collective-permute-done.2.came_ref
  23.6 0.9 %attend.1 = (bf16[4,4096]{1,0:T(4,128)(2,1)S(1)}, bf16[16,256]{1,0:T(8,128)(2,1)S(1)}, bf16[16,256]{1,0:T(8,128)(2,1)S(1)}) custom-call(f32[8,128]{1,0:T(8,128)S(1)} %notes.1.rest_1_.refs_4_.notes_ref, f32[8,128]{1,0:T(8,128)S(1)} %collective-permute-done.1.came_notes_ref, bf16[768,256]{1,0:T(8,128)(2,1)S(1)} %get-tuple-element.26.own_ref, ...), custom_call_target="tpu_custom_call" | custom-call | tf_op jit(solution)/shard_map/attend/pallas_call | solution.py:340
  24.6 2.8 %collective-permute-start.7 = (bf16[4,4096]{1,0:T(4,128)(2,1)S(1)}, bf16[4,4096]{1,0:T(4,128)(2,1)S(1)}, u32[]{:S(2)}, u32[]{:S(2)}) collective-permute-start(bf16[4,4096]{1,0:T(4,128)(2,1)S(1)} %get-tuple-element.34.rest_0_.refs_0_), channel_id=1, source_target_pairs={{0,8},{1,9},{2,10},{3,11},{4,12},{5,13},{6,14},{7,15},{8,0},{9,1},... | collective-permute-start | bytes 98312 | tf_op jit(solution)/shard_map/ppermute | solution.py:468
  27.4 2.2 %fetch.6.refs_2_.rest_2_ = bf16[1024,2048]{1,0:T(8,128)(2,1)S(1)} custom-call(bf16[4096,2048]{1,0:T(8,128)(2,1)} %weight_ref.7, bf16[4,4096]{1,0:T(4,128)(2,1)S(1)} %get-tuple-element.34.rest_0_.refs_0_), custom_call_target="tpu_custom_call" | custom-call | bytes 4194304 | tf_op jit(solution)/shard_map/fetch/pallas_call | solution.py:245
  29.6 0.0 collective-permute-done.7.refs_1_
  29.6 2.6 %collective-permute-start.10 = (bf16[8,4096]{1,0:T(8,128)(2,1)S(1)}, bf16[8,4096]{1,0:T(8,128)(2,1)S(1)}, u32[]{:S(2)}, u32[]{:S(2)}) collective-permute-start(bf16[8,4096]{1,0:T(8,128)(2,1)S(1)} %local.1.rest_0_.rest_4_), channel_id=1, source_target_pairs={{0,6},{1,7},{2,4},{3,5},{4,2},{5,3},{6,0},{7,1},{8,14},{9,15},{10,... | collective-permute-start | bytes 196616 | tf_op jit(solution)/shard_map/ppermute | solution.py:468
  32.3 0.6 %collective-permute-start.9 = (bf16[8,4096]{1,0:T(8,128)(2,1)S(1)}, bf16[8,4096]{1,0:T(8,128)(2,1)S(1)}, u32[]{:S(2)}, u32[]{:S(2)}) collective-permute-start(bf16[8,4096]{1,0:T(8,128)(2,1)S(1)} %local.1.rest_0_.rest_4_), channel_id=1, source_target_pairs={{0,2},{1,3},{2,0},{3,1},{4,6},{5,7},{6,4},{7,5},{8,10},{9,11},{10,... | collective-permute-start | bytes 196616 | tf_op jit(solution)/shard_map/ppermute | solution.py:468
  32.8 0.3 collective-permute-start.8
  33.2 2.9 %fetch.7.rest_3_ = bf16[1536,2048]{1,0:T(8,128)(2,1)S(1)} custom-call(bf16[4096,2048]{1,0:T(8,128)(2,1)} %weight_ref.7, bf16[8,4096]{1,0:T(8,128)(2,1)S(1)} %local.1.rest_0_.rest_4_), custom_call_target="tpu_custom_call" | custom-call | bytes 6291456 | tf_op jit(solution)/shard_map/fetch/pallas_call | solution.py:245
  36.1 0.0 collective-permute-done.10.rest_7_
  36.1 0.4 %collective-permute-done.9.rest_6_ = bf16[8,4096]{1,0:T(8,128)(2,1)S(1)} collective-permute-done((bf16[8,4096]{1,0:T(8,128)(2,1)S(1)}, bf16[8,4096]{1,0:T(8,128)(2,1)S(1)}, u32[]{:S(2)}, u32[]{:S(2)}) %collective-permute-start.9) | collective-permute-done | bytes 65568 | tf_op jit(solution)/shard_map/ppermute | solution.py:468
  36.5 0.6 %collective-permute-done.8.rest_5_ = bf16[8,4096]{1,0:T(8,128)(2,1)S(1)} collective-permute-done((bf16[8,4096]{1,0:T(8,128)(2,1)S(1)}, bf16[8,4096]{1,0:T(8,128)(2,1)S(1)}, u32[]{:S(2)}, u32[]{:S(2)}) %collective-permute-start.8) | collective-permute-done | bytes 65568 | tf_op jit(solution)/shard_map/ppermute | solution.py:468
  37.1 3.2 %output.1 = (f32[16,2048]{1,0:T(8,128)S(1)}, bf16[32,2048]{1,0:T(8,128)(2,1)S(1)}) custom-call(s32[1]{0:T(128)} %bitcast.place_ref, bf16[16,256]{1,0:T(8,128)(2,1)S(1)} %get-tuple-element.33.fresh_ref, bf16[1024,2048]{1,0:T(8,128)(2,1)S(1)} %fetch.4.refs_5_.rest_0_, bf16[512,2048]{1,0:T(8,128)(2,1)S(1)} %fetch.5.rest_0_.rest_1_, ...), custom_call_target="tpu_custom_call" | custom-call | flops 536870912 | bytes 16777216 | tf_op jit(solution)/shard_map/output/pallas_call | solution.py:412
  40.3 0.0 collective-permute-start.11
  40.3 1.3 %collective-permute-done.11.came_ref = bf16[32,2048]{1,0:T(8,128)(2,1)S(1)} collective-permute-done((bf16[32,2048]{1,0:T(8,128)(2,1)S(1)}, bf16[32,2048]{1,0:T(8,128)(2,1)S(1)}, u32[]{:S(2)}, u32[]{:S(2)}) %collective-permute-start.11) | collective-permute-done | bytes 131104 | tf_op jit(solution)/shard_map/ppermute | solution.py:468
  41.6 0.7 %finish.1 = (bf16[16,2048]{1,0:T(8,128)(2,1)}, bf16[2,512]{1,0:T(2,128)(2,1)}, bf16[2,512]{1,0:T(2,128)(2,1)}) custom-call(s32[1]{0:T(128)} %bitcast.place_ref, f32[16,2048]{1,0:T(8,128)S(1)} %get-tuple-element.35.mine_ref, bf16[32,2048]{1,0:T(8,128)(2,1)S(1)} %collective-permute-done.11.came_ref, bf16[16,256]{1,0:T(8,128)(2,1)S(1)} %get-tuple-element.37.fresh_ref), custom_call_target="tpu_custom_call" | custom-call | tf_op jit(solution)/shard_map/finish/pallas_call | solution.py:446
  (2 shorter events, 0.1 us)
Async XLA Ops:
  0.6 2.8 %collective-permute-start = (bf16[16,2048]{1,0:T(8,128)(2,1)}, bf16[16,2048]{1,0:T(8,128)(2,1)S(1)}, u32[]{:S(2)}, u32[]{:S(2)}) collective-permute-start(bf16[16,2048]{1,0:T(8,128)(2,1)} %bitcast.10), channel_id=1, source_target_pairs={{0,1},{1,0},{2,3},{3,2},{4,5},{5,4},{6,7},{7,6},{8,9},{9,8},{10,11... | collective-permute-start | bytes 196616 | tf_op jit(solution)/shard_map/ppermute | solution.py:468
  9.5 14.2 %collective-permute-start.2 = (bf16[768,256]{1,0:T(8,128)(2,1)S(1)}, bf16[768,256]{1,0:T(8,128)(2,1)S(1)}, u32[]{:S(2)}, u32[]{:S(2)}) collective-permute-start(bf16[768,256]{1,0:T(8,128)(2,1)S(1)} %get-tuple-element.27), channel_id=1, source_target_pairs={{0,1},{1,0},{2,3},{3,2},{4,5},{5,4},{6,7},{7,6},{8,9},{9,8},{10,11... | collective-permute-start | bytes 1179656 | tf_op jit(solution)/shard_map/ppermute | solution.py:468
  9.6 8.1 %collective-permute-start.4 = (bf16[4,80,128]{2,1,0:T(8,128)(2,1)S(1)}, bf16[4,80,128]{2,1,0:T(8,128)(2,1)S(1)}, u32[]{:S(2)}, u32[]{:S(2)}) collective-permute-start(bf16[4,80,128]{2,1,0:T(8,128)(2,1)S(1)} %get-tuple-element.29), channel_id=1, source_target_pairs={{0,2},{1,3},{2,0},{3,1},{4,6},{5,7},{6,4},{7,5},{8,10},{9,11},{10,... | collective-permute-start | bytes 245768 | tf_op jit(solution)/shard_map/ppermute | solution.py:468
  12.5 6.1 %collective-permute-start.5 = (bf16[4,80,128]{2,1,0:T(8,128)(2,1)S(1)}, bf16[4,80,128]{2,1,0:T(8,128)(2,1)S(1)}, u32[]{:S(2)}, u32[]{:S(2)}) collective-permute-start(bf16[4,80,128]{2,1,0:T(8,128)(2,1)S(1)} %get-tuple-element.30), channel_id=1, source_target_pairs={{0,6},{1,7},{2,4},{3,5},{4,2},{5,3},{6,0},{7,1},{8,14},{9,15},{10,... | collective-permute-start | bytes 245768 | tf_op jit(solution)/shard_map/ppermute | solution.py:468
  14.1 4.5 %collective-permute-start.3 = (bf16[4,80,128]{2,1,0:T(8,128)(2,1)S(1)}, bf16[4,80,128]{2,1,0:T(8,128)(2,1)S(1)}, u32[]{:S(2)}, u32[]{:S(2)}) collective-permute-start(bf16[4,80,128]{2,1,0:T(8,128)(2,1)S(1)} %get-tuple-element.25.after_ref.rest_0_), channel_id=1, source_target_pairs={{0,4},{1,5},{2,6},{3,7},{4,0},{5,1},{6,2},{7,3},{8,12},{9,13},{10,... | collective-permute-start | bytes 245768 | tf_op jit(solution)/shard_map/ppermute | solution.py:468
  18.7 5.0 %collective-permute-start.6 = (bf16[2,80,128]{2,1,0:T(8,128)(2,1)S(1)}, bf16[2,80,128]{2,1,0:T(8,128)(2,1)S(1)}, u32[]{:S(2)}, u32[]{:S(2)}) collective-permute-start(bf16[2,80,128]{2,1,0:T(8,128)(2,1)S(1)} %get-tuple-element.31.rest_0_), channel_id=1, source_target_pairs={{0,8},{1,9},{2,10},{3,11},{4,12},{5,13},{6,14},{7,15},{8,0},{9,1},... | collective-permute-start | bytes 122888 | tf_op jit(solution)/shard_map/ppermute | solution.py:468
  21.4 1.6 %collective-permute-start.1 = (f32[8,128]{1,0:T(8,128)S(1)}, f32[8,128]{1,0:T(8,128)S(1)}, u32[]{:S(2)}, u32[]{:S(2)}) collective-permute-start(f32[8,128]{1,0:T(8,128)S(1)} %notes.1.rest_1_.refs_4_.notes_ref), channel_id=1, source_target_pairs={{0,1},{1,0},{2,3},{3,2},{4,5},{5,4},{6,7},{7,6},{8,9},{9,8},{10,11... | collective-permute-start | bytes 12296 | tf_op jit(solution)/shard_map/ppermute | solution.py:468
  24.6 5.0 %collective-permute-start.7 = (bf16[4,4096]{1,0:T(4,128)(2,1)S(1)}, bf16[4,4096]{1,0:T(4,128)(2,1)S(1)}, u32[]{:S(2)}, u32[]{:S(2)}) collective-permute-start(bf16[4,4096]{1,0:T(4,128)(2,1)S(1)} %get-tuple-element.34.rest_0_.refs_0_), channel_id=1, source_target_pairs={{0,8},{1,9},{2,10},{3,11},{4,12},{5,13},{6,14},{7,15},{8,0},{9,1},... | collective-permute-start | bytes 98312 | tf_op jit(solution)/shard_map/ppermute | solution.py:468
  29.6 6.4 %collective-permute-start.10 = (bf16[8,4096]{1,0:T(8,128)(2,1)S(1)}, bf16[8,4096]{1,0:T(8,128)(2,1)S(1)}, u32[]{:S(2)}, u32[]{:S(2)}) collective-permute-start(bf16[8,4096]{1,0:T(8,128)(2,1)S(1)} %local.1.rest_0_.rest_4_), channel_id=1, source_target_pairs={{0,6},{1,7},{2,4},{3,5},{4,2},{5,3},{6,0},{7,1},{8,14},{9,15},{10,... | collective-permute-start | bytes 196616 | tf_op jit(solution)/shard_map/ppermute | solution.py:468
  32.3 4.3 %collective-permute-start.9 = (bf16[8,4096]{1,0:T(8,128)(2,1)S(1)}, bf16[8,4096]{1,0:T(8,128)(2,1)S(1)}, u32[]{:S(2)}, u32[]{:S(2)}) collective-permute-start(bf16[8,4096]{1,0:T(8,128)(2,1)S(1)} %local.1.rest_0_.rest_4_), channel_id=1, source_target_pairs={{0,2},{1,3},{2,0},{3,1},{4,6},{5,7},{6,4},{7,5},{8,10},{9,11},{10,... | collective-permute-start | bytes 196616 | tf_op jit(solution)/shard_map/ppermute | solution.py:468
  32.8 4.3 %collective-permute-start.8 = (bf16[8,4096]{1,0:T(8,128)(2,1)S(1)}, bf16[8,4096]{1,0:T(8,128)(2,1)S(1)}, u32[]{:S(2)}, u32[]{:S(2)}) collective-permute-start(bf16[8,4096]{1,0:T(8,128)(2,1)S(1)} %local.1.rest_0_.rest_4_), channel_id=1, source_target_pairs={{0,4},{1,5},{2,6},{3,7},{4,0},{5,1},{6,2},{7,3},{8,12},{9,13},{10,... | collective-permute-start | bytes 196616 | tf_op jit(solution)/shard_map/ppermute | solution.py:468
  40.3 1.4 %collective-permute-start.11 = (bf16[32,2048]{1,0:T(8,128)(2,1)S(1)}, bf16[32,2048]{1,0:T(8,128)(2,1)S(1)}, u32[]{:S(2)}, u32[]{:S(2)}) collective-permute-start(bf16[32,2048]{1,0:T(8,128)(2,1)S(1)} %get-tuple-element.36), channel_id=1, source_target_pairs={{0,1},{1,0},{2,3},{3,2},{4,5},{5,4},{6,7},{7,6},{8,9},{9,8},{10,11... | collective-permute-start | bytes 393224 | tf_op jit(solution)/shard_map/ppermute | solution.py:468
